TPU v7x, 128 devices: a whole 4x4x4 slice. The times are simulated.
128 devices in a mesh: pair: 4 (over z), virt: 32 (over y, x, core).
Axes of the slice: x: 4, y: 4, z: 4, core: 2. Of those that a mesh axis runs over, the one named last changes fastest.
Arguments:
- amps: bfloat16 [16, 768, 768], P('pair', 'virt'), may hold values from -6 to 6
- domain: int32 [16, 6], replicated, may hold values from 0 to 31, as said below
- pair_mask: int32 [16, 6, 6], P('pair'), may hold values 0 or 1
- dfint: bfloat16 [32, 4096, 4096], P('virt', 'pair'), may hold values from -0.09375 to 0.09375
- coupling: float32 [16, 16], P('pair'), may hold values from -1.75 to 1.75
Outputs:
- residual: bfloat16 [16, 768, 768], P('pair', 'virt')
Inputs may be any that keep to these rules, and one draw needn't show every extreme that they name: `domain`: each row lists 6 different tiles; of the 4 blocks of 8 consecutive tiles, none holds more than 2 tiles of one row, and some block holds exactly 2.
All inputs are finite; a program needn't handle non-finite values. No bound on the sum of `pair_mask` on one device may be relied on, other than what follows from the above.
Results may differ from a plain program's by a relative error of at most 0.0038.
Values may be sent and summed in bfloat16 or wider, within the bound.
No kernel may reach another device: no remote copies, remote signals or barrier semaphores. Data moves between devices by JAX's collectives and lax.ppermute only.
A program may use at most 192 MiB of HBM per device.

v0:
```python
import jax
import jax.numpy as jnp
from jax import lax
from jax.sharding import PartitionSpec as P

TB = 128


def body(amps, domain, pair_mask, dfint, coupling):
    pair_dev, row_dev, block_len = amps.shape
    aux_dev = dfint.shape[0]
    tile_size = TB
    tile_count = dfint.shape[2] // tile_size
    quarter = dfint.shape[1] // tile_size
    all_pairs, dom_count = domain.shape
    pair_here = lax.axis_index("pair")
    virt_here = lax.axis_index("virt")
    local_ints = dfint.reshape(aux_dev, quarter, tile_size, tile_count, tile_size)
    column_sets = jax.vmap(lambda tiles: jnp.take(local_ints, tiles, axis=3))(domain)
    column_sets = column_sets.reshape(all_pairs, aux_dev, quarter, tile_size, block_len)
    tile_quarter = domain // quarter
    local_tile = jnp.clip(domain - pair_here * quarter, 0, quarter - 1)
    owned = tile_quarter == pair_here
    picked = jax.vmap(lambda sets, tiles: jnp.take(sets, tiles, axis=1))(column_sets, local_tile)
    weighted = picked.astype(jnp.float32) * owned.astype(jnp.float32)[:, None, :, None, None]
    fetched = lax.psum_scatter(
        weighted.astype(jnp.bfloat16), "pair", scatter_dimension=0, tiled=True
    )
    int_block = fetched.reshape(pair_dev, aux_dev, block_len, block_len)
    first_row = virt_here * row_dev
    row_slot = (first_row + jnp.arange(row_dev, dtype=jnp.int32)) // tile_size
    slot_pick = (row_slot[:, None] == jnp.arange(dom_count, dtype=jnp.int32)[None, :]).astype(
        jnp.bfloat16
    )
    row_tiles = jnp.einsum(
        "rs,pst->prt", slot_pick, pair_mask.astype(jnp.bfloat16), preferred_element_type=jnp.float32
    ).astype(jnp.bfloat16)
    masked = (
        amps.reshape(pair_dev, row_dev, dom_count, tile_size) * row_tiles[:, :, :, None]
    ).reshape(pair_dev, row_dev, block_len)
    piece = lax.all_gather(masked, "virt", axis=1, tiled=True)
    part_cols = jnp.einsum("pqbd,pcd->pqbc", int_block, piece, preferred_element_type=jnp.float32)
    half_acc = part_cols
    int_rows = int_block
    intersection_acc = jnp.einsum(
        "pqcd,pcd->pq", int_rows, piece, preferred_element_type=jnp.float32
    )
    half_acc, intersection_acc = (half_acc, intersection_acc)
    half_ladder = half_acc.astype(jnp.bfloat16)
    intersections = lax.all_gather(intersection_acc, "pair", axis=0, tiled=True)
    dressing = jnp.dot(coupling, intersections, precision=lax.Precision.HIGHEST)
    int_rows = int_block
    ladder = jnp.einsum("pqac,pqbc->apb", int_rows, half_ladder, preferred_element_type=jnp.float32)
    cycle_term = jnp.einsum(
        "pq,pqab->apb", dressing, int_rows.astype(jnp.float32), precision=lax.Precision.HIGHEST
    )
    own_rows = lax.psum_scatter(ladder + cycle_term, "virt", scatter_dimension=0, tiled=True)
    return jnp.transpose(own_rows, (1, 0, 2)).astype(jnp.bfloat16)


def solution(mesh):
    return jax.shard_map(
        body,
        mesh=mesh,
        in_specs=(
            P("pair", "virt", None),
            P(),
            P("pair", None, None),
            P("virt", "pair", None),
            P("pair", None),
        ),
        out_specs=P("pair", "virt", None),
        check_vma=False,
    )
```

profile of v0, /device:TPU:1, one launch (start us, length us, event | category | flops | bytes accessed | tf_op | source)
XLA Modules:
  0.0 564.7 jit_solution(10132100058145658020)
XLA Ops:
  7.4 0.7 add_select_fusion.1
  8.1 0.7 compare_and_fusion.1
  8.8 0.7 bitcast_or_fusion
  9.6 9.4 %copy.57 = bf16[128,8,32,128]{3,2,1,0:T(8,128)(2,1)} copy(bf16[128,8,32,128]{3,1,2,0:T(8,128)(2,1)} %bitcast.49) | data formatting | bytes 16777216
  19.0 9.8 %copy.41 = bf16[8,128,32,128]{3,1,2,0:T(8,128)(2,1)} copy(bf16[8,128,32,128]{3,2,1,0:T(8,128)(2,1)} %bitcast.45) | data formatting | bytes 16777216 | tf_op jit(solution)/shard_map/reshape | solution.py:18
  29.0 13.6 %gather_fusion = bf16[96,8,128,128]{3,2,1,0:T(8,128)(2,1)} fusion(bf16[8,128,32,128]{3,1,2,0:T(8,128)(2,1)} %copy.41, s32[1024]{0:T(1024)S(1)} %pad_clamp_fusion), kind=kCustom, calls=%fused_computation | custom fusion | bytes 50332032 | tf_op jit(solution)/shard_map/vmap(jit(_take))/gather | solution.py:19
  42.6 32.7 %copy.42 = bf16[16,8,128,6,128]{2,4,3,1,0:T(8,128)(2,1)} copy(bf16[16,8,128,6,128]{4,2,1,3,0:T(8,128)(2,1)} %bitcast.42) | data formatting | bytes 50331648 | tf_op jit(solution)/shard_map/vmap(jit(_take))/gather | solution.py:19
  75.3 32.6 %copy.43 = bf16[16,1,8,128,768]{4,3,2,0,1:T(8,128)(2,1)} copy(bf16[16,1,8,128,768]{3,4,2,0,1:T(8,128)(2,1)} %bitcast.43) | data formatting | bytes 50331648 | tf_op jit(solution)/shard_map/vmap(jit(_take))/gather | solution.py:19
  108.3 0.1 copy.38
  108.4 21.0 %select_bitcast_fusion = bf16[16,8,128,768]{3,2,1,0:T(8,128)(2,1)} fusion(bf16[16,1,8,128,768]{4,3,2,0,1:T(8,128)(2,1)} %copy.43, pred[16,768]{1,0:T(8,128)(4,1)S(1)} %bitcast.51), kind=kLoop, calls=%fused_computation.3 | loop fusion | flops 12582912 | bytes 50343936 | tf_op jit(solution)/shard_map/vmap(jit(_take))/select_n | solution.py:19
  129.4 17.7 %gather_fusion.1 = bf16[96,128,768]{2,1,0:T(8,128)(2,1)} fusion(bf16[16,8,128,768]{3,2,1,0:T(8,128)(2,1)} %select_bitcast_fusion, s32[96]{0:T(128)S(1)} %reshape.110), kind=kCustom, calls=%fused_computation.1 | custom fusion | bytes 37749504 | tf_op jit(solution)/shard_map/vmap(jit(_take))/gather | solution.py:24
  147.1 20.5 %multiply_convert_fusion = bf16[16,1,6,128,768]{4,3,2,0,1:T(8,128)(2,1)} fusion(f32[16,6]{1,0:T(8,128)S(1)} %copy.45, bf16[16,1,6,128,768]{4,3,2,0,1:T(8,128)(2,1)} %bitcast.44, pred[16,6]{1,0:T(8,128)(4,1)S(1)} %copy.38), kind=kLoop, calls=%fused_computation.2 | loop fusion | flops 37748736 | bytes 37749216 | tf_op jit(solution)/shard_map/convert_element_type | solution.py:27
  167.6 0.2 all-gather.3.cloned.1.call-start
  167.9 0.4 copy-done.2
  168.3 0.2 fusion.7
  168.5 0.1 copy.47
  168.6 0.2 mul.37
  168.8 0.2 mul.38
  169.0 0.7 mul.39
  169.8 0.6 dynamic-slice
  171.0 0.7 dynamic-slice.1
  172.3 163.9 %reduce-scatter.2.cloned.1.call-done = bf16[4,1,6,128,768]{4,3,2,0,1:T(8,128)(2,1)} async-done(((bf16[16,1,6,128,768]{4,3,2,0,1:T(8,128)(2,1)}), bf16[4,1,6,128,768]{4,3,2,0,1:T(8,128)(2,1)}) %reduce-scatter.2.cloned.1.call-update) | async-done | bytes 4718608 | tf_op jit(solution)/shard_map/reduce_scatter | solution.py:26
  336.1 6.7 %copy.48 = bf16[4,768,768]{1,2,0:T(8,128)(2,1)} copy(bf16[4,768,768]{2,1,0:T(8,128)(2,1)} %bitcast.46) | data formatting | bytes 9437184 | tf_op jit(solution)/shard_map/reshape.3
  342.8 5.1 fusion
  347.9 0.2 dynamic-update-slice
  348.1 6.4 %all-reduce = f32[16]{0:T(128)S(1)} all-reduce(f32[16]{0:T(128)S(1)} %dynamic-update-slice), channel_id=2, replica_groups=mesh['pair'=4,'virt'=32] {'pair'}, use_global_device_ids=true, to_apply=%add | all-reduce | flops 16 | bytes 128
  354.6 0.1 convolution_bitcast_fusion
  354.7 14.9 %bitcast_add_fusion = f32[768,4,768]{0,2,1:T(8,128)} fusion(bf16[4,768,768]{1,2,0:T(8,128)(2,1)} %copy.48, f32[4]{0:T(128)S(1)} %convolution_bitcast_fusion, bf16[4,768,768]{2,1,0:T(8,128)(2,1)} %bitcast.48, bf16[4,768,768]{2,1,0:T(8,128)(2,1)} %all-gather.3.cloned.1.call-done), kind=kOutput, calls=%fused_computation.4 | convolution fusion | flops 7257194496 | bytes 23592976 | tf_op jit(solution)/shard_map/pqac,pqbc->apb/dot_general | solution.py:53
  369.6 12.1 %copy.49 = f32[768,4,768]{2,1,0:T(4,128)} copy(f32[768,4,768]{0,2,1:T(8,128)} %bitcast_add_fusion) | data formatting | bytes 18874368 | tf_op jit(solution)/shard_map/add | solution.py:57
  381.7 174.0 %all-reduce.3 = bf16[768,4,768]{2,1,0:T(4,128)(2,1)} all-reduce(f32[768,4,768]{2,1,0:T(4,128)} %copy.49), channel_id=4, replica_groups=mesh['pair'=4,'virt'=32] {'virt'}, use_global_device_ids=true, to_apply=%region_1.2.clone | all-reduce | flops 2359296 | bytes 14155776
  555.6 1.0 fusion.8
  556.6 0.7 copy.50
  (25 shorter events, 0.7 us)
Async XLA Ops:
  7.4 347.2 %copy-start = (f32[4,16]{1,0:T(4,128)S(1)}, f32[4,16]{1,0:T(4,128)}, u32[]{:S(2)}) copy-start(f32[4,16]{1,0:T(4,128)} %param.9) | copy-start | bytes 772
  7.4 328.8 %reduce-scatter.2.cloned.1.call-start = ((), (), s32[]{:S(2)}) async-start(), calls=%async_computation.1 | async-start | bytes 23592960 | tf_op jit(solution)/shard_map/reduce_scatter | solution.py:26
  167.6 0.7 copy-start.2
  167.6 1.4 copy-start.1
  167.6 2.2 copy-start.4
  167.6 3.4 copy-start.3
  167.6 175.2 %all-gather.3.cloned.1.call-start = ((), (), s32[]{:S(2)}) async-start(), calls=%async_computation.2 | async-start | bytes 4866048 | tf_op jit(solution)/shard_map/all_gather | solution.py:41
Sparse Core Ops, SparseCore 0:
  167.7 168.3 reduce-scatter.1
Sparse Core Ops, SparseCore 1:
  170.7 50.4 all-gather.2
where the time goes:
time: 572 us; the launch traced here: 565 us
  blocking collectives  180 us (31%)
  waiting for transfers between devices  164 us (29%)
  local copies, waits for them, and re-layouts  139 us (24%)
  other arithmetic  49.5 us (9%)
  between operations  16.2 us (3%)
  matrix products  15.2 us (3%)
    unnamed x2, blocking collectives  180 us
    reduce_scatter x1, waiting for transfers between devices, body(): lax.psum_scatter(weighted.astype(jnp.bfloat16), 'pair', scatter_dimension...  164 us
    gather x3, local copies, waits for them, and re-layouts, body(): jnp.take(local_ints, tiles, axis=3)  78.9 us
    select_n x2, other arithmetic, body(): jnp.take(local_ints, tiles, axis=3)  21.7 us
    convert_element_type x1, other arithmetic, body(): weighted.astype(jnp.bfloat16)  20.5 us
    gather x3, local copies, waits for them, and re-layouts, body(): jnp.take(sets, tiles, axis=1)  17.8 us
    dot_general x1, matrix products, body(): jnp.einsum('pqac,pqbc->apb', int_rows, half_ladder, preferred_element_typ...  14.9 us
    add x1, local copies, waits for them, and re-layouts, body(): ladder + cycle_term  12.1 us
  transfers between devices with their start and end apart: 2, of which 1 were waited for; matrix products, arithmetic and copies ran while one was open for 2% of the time, Pallas kernels for 0%

commit v1 on v0

v1 whole, which is shorter than its diff:
```python
import functools

import jax
import jax.numpy as jnp
from jax import lax
from jax.experimental import pallas as pl
from jax.experimental.pallas import tpu as pltpu
from jax.sharding import Mesh
from jax.sharding import PartitionSpec as P

TB = 128
BLOCKS = 4
SLOTS = 2
BF16 = jnp.bfloat16
F32 = jnp.float32
NT = (((1,), (1,)), ((), ()))


def ring(axis, shift, size):
    return functools.partial(
        lax.ppermute, axis_name=axis, perm=[(i, (i + shift) % size) for i in range(size)]
    )


def block_slots(domain_ref, pair, block, quarter, dom):
    found = jnp.int32(0)
    first = jnp.int32(0)
    second = jnp.int32(0)
    for s in range(dom):
        inside = domain_ref[pair, s] // quarter == block
        first = jnp.where(inside & (found == 0), s, first)
        second = jnp.where(inside & (found == 1), s, second)
        found = found + inside.astype(jnp.int32)
    return first, second


def pack_kernel(quarter, dom, domain_ref, here_ref, dfint_ref, *out_and_sem):
    outs, sem = out_and_sem[:-1], out_and_sem[-1]
    here = here_ref[0]
    pairs = outs[0].shape[0]
    for shift in (1, 2, 3, 0):
        target = lax.rem(here + shift, BLOCKS)

        def one_pair(k, carry):
            pair = target * pairs + k
            for j, slot in enumerate(block_slots(domain_ref, pair, here, quarter, dom)):
                row = jnp.clip(domain_ref[pair, slot] - here * quarter, 0, quarter - 1)
                for t in range(dom):
                    column = domain_ref[pair, t]
                    pltpu.make_async_copy(
                        dfint_ref.at[
                            0,
                            pl.ds(pl.multiple_of(row * TB, TB), TB),
                            pl.ds(pl.multiple_of(column * TB, TB), TB),
                        ],
                        outs[shift].at[k, j, :, pl.ds(t * TB, TB)],
                        sem.at[shift],
                    ).start()
            return carry

        lax.fori_loop(0, pairs, one_pair, 0)
    for shift in range(BLOCKS):
        pltpu.make_async_copy(outs[shift], outs[shift], sem.at[shift]).wait()


def pack(dfint, domain, here, pairs, quarter):
    dom = domain.shape[1]
    out = jax.ShapeDtypeStruct((pairs, SLOTS, TB, dom * TB), BF16)
    return pl.pallas_call(
        functools.partial(pack_kernel, quarter, dom),
        out_shape=[out] * BLOCKS,
        grid_spec=pltpu.PrefetchScalarGridSpec(
            num_scalar_prefetch=2,
            grid=(1,),
            in_specs=[pl.BlockSpec(memory_space=pl.ANY)],
            out_specs=[pl.BlockSpec(memory_space=pl.ANY)] * BLOCKS,
            scratch_shapes=[pltpu.SemaphoreType.DMA((BLOCKS,))],
        ),
        name="pack_tiles",
    )(domain, here, dfint)


def fetch_rows(quarter, dom, domain_ref, here, k, pairs, parts, block, sem):
    pair = here * pairs + k
    for s in range(dom):
        owner = domain_ref[pair, s] // quarter
        rank = jnp.int32(0)
        for before in range(s):
            rank = rank + (domain_ref[pair, before] // quarter == owner).astype(jnp.int32)
        shift = lax.rem(here - owner + BLOCKS, BLOCKS)
        for option in range(BLOCKS):

            @pl.when(shift == option)
            def _(option=option):
                pltpu.make_async_copy(
                    parts[option].at[k, rank], block.at[k, pl.ds(s * TB, TB), :], sem.at[k]
                ).start()


def gather_start(quarter, dom, domain_ref, here, parts, block, sem):
    pairs = block.shape[0]

    @pl.when(pl.program_id(0) == 0)
    def _():
        for k in range(pairs):
            fetch_rows(quarter, dom, domain_ref, here, k, pairs, parts, block, sem)

    k = pl.program_id(0)
    pltpu.make_async_copy(block.at[k], block.at[k], sem.at[k]).wait()


def half_kernel(quarter, dom, domain_ref, here_ref, amp_ref, p0, p1, p2, p3, half_ref, inter_ref, block, sem):
    k = pl.program_id(0)
    gather_start(quarter, dom, domain_ref, here_ref[0], (p0, p1, p2, p3), block, sem)
    amp = amp_ref[0]
    total = jnp.float32(0)
    rows = 2 * TB
    for r in range(0, dom * TB, rows):
        half = lax.dot_general(block[k, pl.ds(r, rows), :], amp, NT, preferred_element_type=F32)
        half_ref[0, pl.ds(r, rows), :] = half.astype(BF16)
        corner = half[:, r : r + rows]
        diagonal = lax.broadcasted_iota(jnp.int32, (rows, rows), 0) == lax.broadcasted_iota(
            jnp.int32, (rows, rows), 1
        )
        total = total + jnp.sum(jnp.where(diagonal, corner, 0.0))
    inter_ref[0, k] = total


def half_ladders(amp, parts, domain, here, quarter):
    pairs, length = amp.shape[0], amp.shape[1]
    dom = domain.shape[1]
    return pl.pallas_call(
        functools.partial(half_kernel, quarter, dom),
        out_shape=[
            jax.ShapeDtypeStruct((pairs, length, length), BF16),
            jax.ShapeDtypeStruct((1, pairs), F32),
        ],
        grid_spec=pltpu.PrefetchScalarGridSpec(
            num_scalar_prefetch=2,
            grid=(pairs,),
            in_specs=[pl.BlockSpec((1, length, length), lambda k, *_: (k, 0, 0))]
            + [pl.BlockSpec(memory_space=pl.ANY)] * BLOCKS,
            out_specs=[
                pl.BlockSpec((1, length, length), lambda k, *_: (k, 0, 0)),
                pl.BlockSpec(memory_space=pltpu.SMEM),
            ],
            scratch_shapes=[
                pltpu.VMEM((pairs, length, length), BF16),
                pltpu.SemaphoreType.DMA((pairs,)),
            ],
        ),
        compiler_params=pltpu.CompilerParams(vmem_limit_bytes=40 * 2**20),
        name="half_ladder",
    )(domain, here, amp, *parts)


def ladder_kernel(
    quarter, dom, ny, nx, domain_ref, here_ref, coupling_ref, i0, i1, i2, i3, half_ref, p0, p1, p2, p3,
    keep_ref, send_ref, block, sem,
):
    k = pl.program_id(0)
    pairs = block.shape[0]
    here, y, x, core = here_ref[0], here_ref[1], here_ref[2], here_ref[3]
    gather_start(quarter, dom, domain_ref, here, (p0, p1, p2, p3), block, sem)
    dressing = jnp.float32(0)
    for shift, inter in enumerate((i0, i1, i2, i3)):
        owner = lax.rem(here - shift + BLOCKS, BLOCKS)
        for other in range(pairs):
            dressing = dressing + coupling_ref[k, owner * pairs + other] * inter[0, other]
    half = half_ref[0]
    own = keep_ref.shape[3]
    groups = 2 * nx
    rows = groups * own
    for yy in range(ny):
        mine = block[k, pl.ds(yy * rows, rows), :]
        acc = lax.dot_general(mine, half, NT, preferred_element_type=F32)
        acc = acc + dressing * mine.astype(F32)
        sy = lax.rem(yy - y + ny, ny)
        for xx in range(nx):
            sx = lax.rem(xx - x + nx, nx)
            low = acc[(2 * xx) * own : (2 * xx + 1) * own]
            high = acc[(2 * xx + 1) * own : (2 * xx + 2) * own]
            keep_ref[0, sy, sx] = jnp.where(core == 0, low, high)
            send_ref[0, sy, sx] = jnp.where(core == 0, high, low).astype(BF16)


def ladders(half, parts, inters, coupling, domain, here, quarter, ny, nx, own):
    pairs, length = half.shape[0], half.shape[1]
    dom = domain.shape[1]
    shape = (pairs, ny, nx, own, length)
    spec = pl.BlockSpec((1,) + shape[1:], lambda k, *_: (k, 0, 0, 0, 0))
    smem = pl.BlockSpec(memory_space=pltpu.SMEM)
    return pl.pallas_call(
        functools.partial(ladder_kernel, quarter, dom, ny, nx),
        out_shape=[jax.ShapeDtypeStruct(shape, F32), jax.ShapeDtypeStruct(shape, BF16)],
        grid_spec=pltpu.PrefetchScalarGridSpec(
            num_scalar_prefetch=2,
            grid=(pairs,),
            in_specs=[smem] * 5
            + [pl.BlockSpec((1, length, length), lambda k, *_: (k, 0, 0))]
            + [pl.BlockSpec(memory_space=pl.ANY)] * BLOCKS,
            out_specs=[spec, spec],
            scratch_shapes=[
                pltpu.VMEM((pairs, length, length), BF16),
                pltpu.SemaphoreType.DMA((pairs,)),
            ],
        ),
        compiler_params=pltpu.CompilerParams(vmem_limit_bytes=40 * 2**20),
        name="ladder_and_cycle",
    )(domain, here, coupling, *inters, half, *parts)


def masked_amps(amps, pair_mask, first_row, dom):
    pairs, rows, length = amps.shape
    row_slot = (first_row + jnp.arange(rows, dtype=jnp.int32)) // TB
    slot_pick = row_slot[:, None] == jnp.arange(dom, dtype=jnp.int32)[None, :]
    row_tiles = jnp.sum(
        jnp.where(slot_pick[None, :, :, None], pair_mask[:, None, :, :], 0), axis=2
    ).astype(BF16)
    tiles = amps.reshape(pairs, rows, dom, TB) * row_tiles[:, :, :, None]
    return tiles.reshape(pairs, rows, length)


def make_body(ny, nx):
    def body(amps, domain, pair_mask, dfint, coupling):
        pairs, own, length = amps.shape
        dom = domain.shape[1]
        quarter = dfint.shape[1] // TB
        z, y, x, c = (lax.axis_index(name).astype(jnp.int32) for name in ("z", "y", "x", "c"))
        here = jnp.stack([z, y, x, c])
        packed = pack(dfint, domain, here, pairs, quarter)
        parts = [packed[0]] + [ring("z", s, BLOCKS)(packed[s]) for s in (1, 2, 3)]
        first_row = ((y * nx + x) * 2 + c) * own
        masked = masked_amps(amps, pair_mask, first_row, dom)
        amp = lax.all_gather(masked, ("y", "x", "c"), axis=1, tiled=True)
        half, inter = half_ladders(amp, parts, domain, here, quarter)
        inters = [inter] + [ring("z", s, BLOCKS)(inter) for s in (1, 2, 3)]
        keep, send = ladders(half, parts, inters, coupling, domain, here, quarter, ny, nx, own)
        summed = keep + ring("c", 1, 2)(send).astype(F32)
        cut = pairs // 2
        ends = []
        for part, axes in ((summed[:cut], "xy"), (summed[cut:], "yx")):
            first = part if axes == "xy" else jnp.swapaxes(part, 1, 2)
            n1, n2 = (nx, ny) if axes == "xy" else (ny, nx)
            stage = first[:, :, 0]
            for s in range(1, n1):
                stage = stage + ring(axes[0], s, n1)(first[:, :, s].astype(BF16)).astype(F32)
            last = stage[:, 0]
            for s in range(1, n2):
                last = last + ring(axes[1], s, n2)(stage[:, s].astype(BF16)).astype(F32)
            ends.append(last)
        return jnp.concatenate(ends, axis=0).astype(BF16)

    return body


def solution(mesh):
    ny = nx = 4
    grid = Mesh(mesh.devices.reshape(BLOCKS, ny, nx, 2), ("z", "y", "x", "c"))
    virt = ("y", "x", "c")
    return jax.shard_map(
        make_body(ny, nx),
        mesh=grid,
        in_specs=(P("z", virt, None), P(), P("z", None, None), P(virt, "z", None), P("z", None)),
        out_specs=P("z", virt, None),
        check_vma=False,
    )
```

time: 572 us -> 369 us (0.65)
  Pallas kernels: 0 us -> 224 us
  blocking collectives: 180 us -> 0 us
  local copies, waits for them, and re-layouts: 139 us -> 9.23 us
  waiting for transfers between devices: 164 us -> 85.3 us
  other arithmetic: 49.5 us -> 4.06 us
  starting transfers between devices: 0.23 us -> 31 us
  matrix products: 15.2 us -> 0 us
    pallas_call x0 -> x3, Pallas kernels: none -> 224 us  [the longest x1 193 us: pack(): pl.pallas_call(functools.partial(pack_kernel, quarter, dom), out_shape=[o...]
    unnamed x2 -> x0, blocking collectives: 180 us -> none
    reduce_scatter x1 -> x0, waiting for transfers between devices: 164 us -> none  [body(): lax.psum_scatter(weighted.astype(jnp.bfloat16), 'pair', scatter_dimension...]
    gather x6 -> x0, local copies, waits for them, and re-layouts: 96.8 us -> none  [the longest x3 78.9 us: body(): jnp.take(local_ints, tiles, axis=3)]
    ppermute x0 -> x19, waiting for transfers between devices: none -> 85.3 us  [the longest x3 67 us: body(): parts = [packed[0]] + [ring('z', s, BLOCKS)(packed[s]) for s in (1, 2, 3)]]
    ppermute x0 -> x19, starting transfers between devices: none -> 31 us  [the longest x6 10.1 us: body(): ring(axes[0], s, n1)(first[:, :, s].astype(BF16)).astype(F32)]
    select_n x3 -> x1, other arithmetic: 21.7 us -> 0.01 us  [masked_amps(): row_slot = (first_row + jnp.arange(rows, dtype=jnp.int32)) // TB]
    convert_element_type x2 -> x1, other arithmetic: 20.5 us -> 0.01 us  [masked_amps(): row_tiles = jnp.sum(jnp.where(slot_pick[None, :, :, None], pair_mask[:, N...]
  transfers between devices with their start and end apart: 2 -> 20, of which waited for: 1 -> 11; matrix products, arithmetic and copies ran while one was open for 2% -> 1% of each run, Pallas kernels for 0% -> 53%
where the time goes in v1:
time: 369 us; the launch traced here: 367 us
  Pallas kernels  224 us (61%)
  waiting for transfers between devices  85.3 us (23%)
  starting transfers between devices  31 us (8%)
  between operations  13.6 us (4%)
  local copies, waits for them, and re-layouts  9.23 us (3%)
  other arithmetic  4.06 us (1%)
    pallas_call x1, Pallas kernels, pack(): pl.pallas_call(functools.partial(pack_kernel, quarter, dom), out_shape=[o...  193 us
    ppermute x3, waiting for transfers between devices, body(): parts = [packed[0]] + [ring('z', s, BLOCKS)(packed[s]) for s in (1, 2, 3)]  67 us
    pallas_call x1, Pallas kernels, ladders(): pl.pallas_call(functools.partial(ladder_kernel, quarter, dom, ny, nx), ou...  16.3 us
    pallas_call x1, Pallas kernels, half_ladders(): pl.pallas_call(functools.partial(half_kernel, quarter, dom), out_shape=[j...  14.7 us
    ppermute x6, starting transfers between devices, body(): ring(axes[0], s, n1)(first[:, :, s].astype(BF16)).astype(F32)  10.1 us
    unnamed x16, local copies, waits for them, and re-layouts  8.3 us
    ppermute x6, starting transfers between devices, body(): last = last + ring(axes[1], s, n2)(stage[:, s].astype(BF16)).astype(F32)  8.2 us
  transfers between devices with their start and end apart: 20, of which 11 were waited for; matrix products, arithmetic and copies ran while one was open for 1% of the time, Pallas kernels for 53%

profile of v1, /device:TPU:1, one launch (start us, length us, event | category | flops | bytes accessed | tf_op | source)
XLA Modules:
  0.0 366.9 jit_solution(8970209667485252271)
XLA Ops:
  8.0 1.6 mul.25
  9.6 1.4 copy.34.domain_ref
  11.6 192.7 %pack_tiles.1 = (bf16[4,2,128,768]{3,2,1,0:T(8,128)(2,1)}, bf16[4,2,128,768]{3,2,1,0:T(8,128)(2,1)}, bf16[4,2,128,768]{3,2,1,0:T(8,128)(2,1)}, bf16[4,2,128,768]{3,2,1,0:T(8,128)(2,1)}) custom-call(s32[16,6]{1,0:T(8,128)} %copy.34.domain_ref, s32[4]{0:T(128)} %pad_add_fusion.here_ref, bf16[1,1024,4096]{2,1,0:T(8,128)(2,1)} %dfint_ref.1), custom_call_target="tpu_custom_call" | custom-call | tf_op jit(solution)/shard_map/pack_tiles/pallas_call | solution.py:69
  204.3 2.5 collective-permute-start
  206.8 3.3 collective-permute-start.1
  210.9 32.4 %collective-permute-done.p1 = bf16[4,2,128,768]{3,2,1,0:T(8,128)(2,1)S(1)} collective-permute-done((bf16[4,2,128,768]{3,2,1,0:T(8,128)(2,1)}, bf16[4,2,128,768]{3,2,1,0:T(8,128)(2,1)S(1)}, u32[]{:S(2)}, u32[]{:S(2)}) %collective-permute-start) | collective-permute-done | bytes 1572896 | tf_op jit(solution)/shard_map/ppermute | solution.py:232
  243.3 34.6 %collective-permute-done.1.p2 = bf16[4,2,128,768]{3,2,1,0:T(8,128)(2,1)S(1)} collective-permute-done((bf16[4,2,128,768]{3,2,1,0:T(8,128)(2,1)}, bf16[4,2,128,768]{3,2,1,0:T(8,128)(2,1)S(1)}, u32[]{:S(2)}, u32[]{:S(2)}) %collective-permute-start.1) | collective-permute-done | bytes 1572896 | tf_op jit(solution)/shard_map/ppermute | solution.py:232
  277.8 1.2 copy-done.1
  279.0 1.4 copy-done
  280.4 1.4 copy-done.2
  281.8 14.7 %half_ladder.1 = (bf16[4,768,768]{2,1,0:T(8,128)(2,1)S(1)}, f32[1,4]{1,0:T(1,128)S(1)}) custom-call(s32[16,6]{1,0:T(8,128)S(1)} %copy-done.4, s32[4]{0:T(128)S(1)} %copy-done.5, bf16[4,768,768]{2,1,0:T(8,128)(2,1)} %all-gather.2.cloned.1.call-done.amp_ref, bf16[4,2,128,768]{3,2,1,0:T(8,128)(2,1)S(1)} %copy-done, ...), custom_call_target="tpu_custom_call" | custom-call | tf_op jit(solution)/shard_map/half_ladder/pallas_call | solution.py:132
  296.6 2.1 copy-done.3
  298.7 2.9 collective-permute-start.5
  302.4 3.2 collective-permute-done.4.i2
  305.7 16.3 %ladder_and_cycle.1 = (f32[4,4,4,24,768]{4,3,2,1,0:T(8,128)S(1)}, bf16[4,4,4,24,768]{4,3,2,1,0:T(8,128)(2,1)S(1)}) custom-call(s32[16,6]{1,0:T(8,128)S(1)} %copy-done.4, s32[4]{0:T(128)S(1)} %copy-done.5, f32[4,16]{1,0:T(4,128)S(1)} %copy-done.6, f32[1,4]{1,0:T(1,128)S(1)} %get-tuple-element.17.i0, f32[1,4]{1,0:T(1,128)S(1)} %collective-permute-done.3.i1, ...), custom_call_target="tpu_custom_call" | custom-call | tf_op jit(solution)/shard_map/ladder_and_cycle/pallas_call | solution.py:193
  322.0 2.7 collective-permute-start.6
  324.7 4.2 %collective-permute-done.6 = bf16[4,4,4,24,768]{4,3,2,1,0:T(8,128)(2,1)S(1)} collective-permute-done((bf16[4,4,4,24,768]{4,3,2,1,0:T(8,128)(2,1)S(1)}, bf16[4,4,4,24,768]{4,3,2,1,0:T(8,128)(2,1)S(1)}, u32[]{:S(2)}, u32[]{:S(2)}) %collective-permute-start.6) | collective-permute-done | bytes 2359328 | tf_op jit(solution)/shard_map/ppermute | solution.py:239
  329.7 1.3 collective-permute-start.7
  331.0 1.5 collective-permute-start.9
  332.5 1.5 collective-permute-start.8
  334.1 1.4 collective-permute-start.13
  335.5 1.5 collective-permute-start.15
  337.1 2.1 collective-permute-done.7
  339.3 2.9 collective-permute-start.14
  342.2 4.4 %collective-permute-done.8 = bf16[2,4,24,768]{3,2,0,1:T(8,128)(2,1)S(1)} collective-permute-done((bf16[2,4,24,768]{3,2,0,1:T(8,128)(2,1)S(1)}, bf16[2,4,24,768]{3,2,0,1:T(8,128)(2,1)S(1)}, u32[]{:S(2)}, u32[]{:S(2)}) %collective-permute-start.8) | collective-permute-done | bytes 294944 | tf_op jit(solution)/shard_map/ppermute | solution.py:247
  346.7 1.4 collective-permute-start.10
  348.1 1.5 collective-permute-start.12
  349.6 1.6 collective-permute-start.11
  352.0 2.1 collective-permute-start.18
  354.1 1.0 collective-permute-start.17
  355.2 1.0 collective-permute-done.16
  356.2 3.1 collective-permute-done.17
  (49 shorter events, 6.5 us)
Async XLA Ops:
  6.5 272.5 %all-gather.2.cloned.1.call-start = ((), (), s32[]{:S(2)}) async-start(), calls=%async_computation | async-start | bytes 4866048 | tf_op jit(solution)/shard_map/all_gather | solution.py:235
  11.6 267.4 %copy-start.4 = (s32[16,6]{1,0:T(8,128)S(1)}, s32[16,6]{1,0:T(8,128)}, u32[]{:S(2)}) copy-start(s32[16,6]{1,0:T(8,128)} %copy.34.domain_ref) | copy-start | bytes 1156
  11.6 267.4 %copy-start.5 = (s32[4]{0:T(128)S(1)}, s32[4]{0:T(128)}, u32[]{:S(2)}) copy-start(s32[4]{0:T(128)} %pad_add_fusion.here_ref) | copy-start | bytes 52
  204.3 39.0 %collective-permute-start = (bf16[4,2,128,768]{3,2,1,0:T(8,128)(2,1)}, bf16[4,2,128,768]{3,2,1,0:T(8,128)(2,1)S(1)}, u32[]{:S(2)}, u32[]{:S(2)}) collective-permute-start(bf16[4,2,128,768]{3,2,1,0:T(8,128)(2,1)} %get-tuple-element.14), channel_id=1, source_target_pairs={{0,32},{32,64},{64,96},{96,0},{1,33},{33,65},{65,97},{97,1},{2,34}... | collective-permute-start | bytes 4718600 | tf_op jit(solution)/shard_map/ppermute | solution.py:232
  206.8 71.0 %collective-permute-start.1 = (bf16[4,2,128,768]{3,2,1,0:T(8,128)(2,1)}, bf16[4,2,128,768]{3,2,1,0:T(8,128)(2,1)S(1)}, u32[]{:S(2)}, u32[]{:S(2)}) collective-permute-start(bf16[4,2,128,768]{3,2,1,0:T(8,128)(2,1)} %get-tuple-element.15), channel_id=1, source_target_pairs={{0,64},{32,96},{64,0},{96,32},{1,65},{33,97},{65,1},{97,33},{2,66}... | collective-permute-start | bytes 4718600 | tf_op jit(solution)/shard_map/ppermute | solution.py:232
  210.1 67.7 %collective-permute-start.2 = (bf16[4,2,128,768]{3,2,1,0:T(8,128)(2,1)}, bf16[4,2,128,768]{3,2,1,0:T(8,128)(2,1)S(1)}, u32[]{:S(2)}, u32[]{:S(2)}) collective-permute-start(bf16[4,2,128,768]{3,2,1,0:T(8,128)(2,1)} %get-tuple-element.16), channel_id=1, source_target_pairs={{0,96},{32,0},{64,32},{96,64},{1,97},{33,1},{65,33},{97,65},{2,98}... | collective-permute-start | bytes 4718600 | tf_op jit(solution)/shard_map/ppermute | solution.py:232
  277.8 1.2 copy-start.1
  279.0 1.4 copy-start
  280.4 1.4 copy-start.2
  281.8 23.9 %copy-start.6 = (f32[4,16]{1,0:T(4,128)S(1)}, f32[4,16]{1,0:T(4,128)}, u32[]{:S(2)}) copy-start(f32[4,16]{1,0:T(4,128)} %coupling_ref.1) | copy-start | bytes 772
  296.6 2.1 copy-start.3
  298.7 3.7 collective-permute-start.5
  301.6 3.9 %collective-permute-start.4 = (f32[1,4]{1,0:T(1,128)S(1)}, f32[1,4]{1,0:T(1,128)S(1)}, u32[]{:S(2)}, u32[]{:S(2)}) collective-permute-start(f32[1,4]{1,0:T(1,128)S(1)} %get-tuple-element.17.i0), channel_id=1, source_target_pairs={{0,64},{32,96},{64,0},{96,32},{1,65},{33,97},{65,1},{97,33},{2,66}... | collective-permute-start | bytes 56 | tf_op jit(solution)/shard_map/ppermute | solution.py:237
  302.1 3.6 collective-permute-start.3
  322.0 6.8 %collective-permute-start.6 = (bf16[4,4,4,24,768]{4,3,2,1,0:T(8,128)(2,1)S(1)}, bf16[4,4,4,24,768]{4,3,2,1,0:T(8,128)(2,1)S(1)}, u32[]{:S(2)}, u32[]{:S(2)}) collective-permute-start(bf16[4,4,4,24,768]{4,3,2,1,0:T(8,128)(2,1)S(1)} %get-tuple-element.20), channel_id=1, source_target_pairs={{0,1},{1,0},{2,3},{3,2},{4,5},{5,4},{6,7},{7,6},{8,9},{9,8},{10,11... | collective-permute-start | bytes 7077896 | tf_op jit(solution)/shard_map/ppermute | solution.py:239
  329.7 9.5 %collective-permute-start.7 = (bf16[2,4,24,768]{3,2,0,1:T(8,128)(2,1)S(1)}, bf16[2,4,24,768]{3,2,0,1:T(8,128)(2,1)S(1)}, u32[]{:S(2)}, u32[]{:S(2)}) collective-permute-start(bf16[2,4,24,768]{3,2,0,1:T(8,128)(2,1)S(1)} %get-tuple-element.25), channel_id=1, source_target_pairs={{0,2},{2,4},{4,6},{6,0},{1,3},{3,5},{5,7},{7,1},{8,10},{10,12},{12... | collective-permute-start | bytes 884744 | tf_op jit(solution)/shard_map/ppermute | solution.py:247
  331.0 11.1 %collective-permute-start.9 = (bf16[2,4,24,768]{3,2,0,1:T(8,128)(2,1)S(1)}, bf16[2,4,24,768]{3,2,0,1:T(8,128)(2,1)S(1)}, u32[]{:S(2)}, u32[]{:S(2)}) collective-permute-start(bf16[2,4,24,768]{3,2,0,1:T(8,128)(2,1)S(1)} %get-tuple-element.26), channel_id=1, source_target_pairs={{0,6},{2,0},{4,2},{6,4},{1,7},{3,1},{5,3},{7,5},{8,14},{10,8},{12,... | collective-permute-start | bytes 884744 | tf_op jit(solution)/shard_map/ppermute | solution.py:247
  332.5 14.1 %collective-permute-start.8 = (bf16[2,4,24,768]{3,2,0,1:T(8,128)(2,1)S(1)}, bf16[2,4,24,768]{3,2,0,1:T(8,128)(2,1)S(1)}, u32[]{:S(2)}, u32[]{:S(2)}) collective-permute-start(bf16[2,4,24,768]{3,2,0,1:T(8,128)(2,1)S(1)} %get-tuple-element.27), channel_id=1, source_target_pairs={{0,4},{2,6},{4,0},{6,2},{1,5},{3,7},{5,1},{7,3},{8,12},{10,14},{12... | collective-permute-start | bytes 884744 | tf_op jit(solution)/shard_map/ppermute | solution.py:247
  334.1 15.5 %collective-permute-start.13 = (bf16[2,4,24,768]{3,2,1,0:T(8,128)(2,1)S(1)}, bf16[2,4,24,768]{3,2,1,0:T(8,128)(2,1)S(1)}, u32[]{:S(2)}, u32[]{:S(2)}) collective-permute-start(bf16[2,4,24,768]{3,2,1,0:T(8,128)(2,1)S(1)} %get-tuple-element.28), channel_id=1, source_target_pairs={{0,8},{8,16},{16,24},{24,0},{1,9},{9,17},{17,25},{25,1},{2,10},{10... | collective-permute-start | bytes 884744 | tf_op jit(solution)/shard_map/ppermute | solution.py:247
  335.5 15.8 %collective-permute-start.15 = (bf16[2,4,24,768]{3,2,1,0:T(8,128)(2,1)S(1)}, bf16[2,4,24,768]{3,2,1,0:T(8,128)(2,1)S(1)}, u32[]{:S(2)}, u32[]{:S(2)}) collective-permute-start(bf16[2,4,24,768]{3,2,1,0:T(8,128)(2,1)S(1)} %get-tuple-element.29), channel_id=1, source_target_pairs={{0,24},{8,0},{16,8},{24,16},{1,25},{9,1},{17,9},{25,17},{2,26},{10... | collective-permute-start | bytes 884744 | tf_op jit(solution)/shard_map/ppermute | solution.py:247
  339.3 12.0 %collective-permute-start.14 = (bf16[2,4,24,768]{3,2,1,0:T(8,128)(2,1)S(1)}, bf16[2,4,24,768]{3,2,1,0:T(8,128)(2,1)S(1)}, u32[]{:S(2)}, u32[]{:S(2)}) collective-permute-start(bf16[2,4,24,768]{3,2,1,0:T(8,128)(2,1)S(1)} %get-tuple-element.30), channel_id=1, source_target_pairs={{0,16},{8,24},{16,0},{24,8},{1,17},{9,25},{17,1},{25,9},{2,18},{10... | collective-permute-start | bytes 884744 | tf_op jit(solution)/shard_map/ppermute | solution.py:247
  346.7 7.4 %collective-permute-start.10 = (bf16[2,24,768]{2,1,0:T(8,128)(2,1)S(1)}, bf16[2,24,768]{2,1,0:T(8,128)(2,1)S(1)}, u32[]{:S(2)}, u32[]{:S(2)}) collective-permute-start(bf16[2,24,768]{2,1,0:T(8,128)(2,1)S(1)} %get-tuple-element.31), channel_id=1, source_target_pairs={{0,8},{8,16},{16,24},{24,0},{1,9},{9,17},{17,25},{25,1},{2,10},{10... | collective-permute-start | bytes 221192 | tf_op jit(solution)/shard_map/ppermute | solution.py:250
  348.1 7.0 %collective-permute-start.12 = (bf16[2,24,768]{2,1,0:T(8,128)(2,1)S(1)}, bf16[2,24,768]{2,1,0:T(8,128)(2,1)S(1)}, u32[]{:S(2)}, u32[]{:S(2)}) collective-permute-start(bf16[2,24,768]{2,1,0:T(8,128)(2,1)S(1)} %get-tuple-element.32), channel_id=1, source_target_pairs={{0,24},{8,0},{16,8},{24,16},{1,25},{9,1},{17,9},{25,17},{2,26},{10... | collective-permute-start | bytes 221192 | tf_op jit(solution)/shard_map/ppermute | solution.py:250
  349.6 5.5 %collective-permute-start.11 = (bf16[2,24,768]{2,1,0:T(8,128)(2,1)S(1)}, bf16[2,24,768]{2,1,0:T(8,128)(2,1)S(1)}, u32[]{:S(2)}, u32[]{:S(2)}) collective-permute-start(bf16[2,24,768]{2,1,0:T(8,128)(2,1)S(1)} %get-tuple-element.33), channel_id=1, source_target_pairs={{0,16},{8,24},{16,0},{24,8},{1,17},{9,25},{17,1},{25,9},{2,18},{10... | collective-permute-start | bytes 221192 | tf_op jit(solution)/shard_map/ppermute | solution.py:250
  351.4 4.8 %collective-permute-start.16 = (bf16[2,24,768]{2,1,0:T(8,128)(2,1)S(1)}, bf16[2,24,768]{2,1,0:T(8,128)(2,1)S(1)}, u32[]{:S(2)}, u32[]{:S(2)}) collective-permute-start(bf16[2,24,768]{2,1,0:T(8,128)(2,1)S(1)} %get-tuple-element.34), channel_id=1, source_target_pairs={{0,2},{2,4},{4,6},{6,0},{1,3},{3,5},{5,7},{7,1},{8,10},{10,12},{12... | collective-permute-start | bytes 221192 | tf_op jit(solution)/shard_map/ppermute | solution.py:250
  352.0 4.2 %collective-permute-start.18 = (bf16[2,24,768]{2,1,0:T(8,128)(2,1)S(1)}, bf16[2,24,768]{2,1,0:T(8,128)(2,1)S(1)}, u32[]{:S(2)}, u32[]{:S(2)}) collective-permute-start(bf16[2,24,768]{2,1,0:T(8,128)(2,1)S(1)} %get-tuple-element.35), channel_id=1, source_target_pairs={{0,6},{2,0},{4,2},{6,4},{1,7},{3,1},{5,3},{7,5},{8,14},{10,8},{12,... | collective-permute-start | bytes 221192 | tf_op jit(solution)/shard_map/ppermute | solution.py:250
  354.1 5.2 %collective-permute-start.17 = (bf16[2,24,768]{2,1,0:T(8,128)(2,1)S(1)}, bf16[2,24,768]{2,1,0:T(8,128)(2,1)S(1)}, u32[]{:S(2)}, u32[]{:S(2)}) collective-permute-start(bf16[2,24,768]{2,1,0:T(8,128)(2,1)S(1)} %get-tuple-element.36), channel_id=1, source_target_pairs={{0,4},{2,6},{4,0},{6,2},{1,5},{3,7},{5,1},{7,3},{8,12},{10,14},{12... | collective-permute-start | bytes 221192 | tf_op jit(solution)/shard_map/ppermute | solution.py:250
Sparse Core Ops, SparseCore 0:
  9.8 50.3 all-gather.1

commit v2 on v0

v2 whole, which is shorter than its diff:
```python
import functools

import jax
import jax.numpy as jnp
from jax import lax
from jax.experimental import pallas as pl
from jax.experimental.pallas import tpu as pltpu
from jax.sharding import Mesh
from jax.sharding import PartitionSpec as P

TB = 128
BLOCKS = 4
CORES = 2
SLOTS = 2
BF16 = jnp.bfloat16
F32 = jnp.float32
NT = (((1,), (1,)), ((), ()))
FLOWS = ((1, 0), (3, 0), (1, 1), (3, 1), (2, 0), (2, 1), (0, 1), (0, 0))


def hop(shift, flip):
    perm = [
        (z * CORES + c, (z + shift) % BLOCKS * CORES + (c ^ flip))
        for z in range(BLOCKS)
        for c in range(CORES)
    ]
    return functools.partial(lax.ppermute, axis_name=("z", "c"), perm=perm)


def swap_cores(value):
    return lax.ppermute(value, "c", [(0, 1), (1, 0)])


def block_slots(domain_ref, pair, block, quarter, dom):
    found = jnp.int32(0)
    first = jnp.int32(0)
    second = jnp.int32(0)
    for s in range(dom):
        inside = domain_ref[pair, s] // quarter == block
        first = jnp.where(inside & (found == 0), s, first)
        second = jnp.where(inside & (found == 1), s, second)
        found = found + inside.astype(jnp.int32)
    return first, second


def pack_kernel(quarter, dom, which, domain_ref, here_ref, dfint_ref, *rest):
    count = len(FLOWS)
    outs, (buffer, in_sem, out_sem) = rest[:count], rest[count:]
    here, core = here_ref[0], here_ref[3]
    for flow, (shift, flip) in enumerate(FLOWS):
        target = lax.rem(here + shift, BLOCKS)
        pair = (target * CORES + (core ^ flip)) * CORES + which
        for j, slot in enumerate(block_slots(domain_ref, pair, here, quarter, dom)):
            row = jnp.clip(domain_ref[pair, slot] - here * quarter, 0, quarter - 1)
            for t in range(dom):
                column = domain_ref[pair, t]
                pltpu.make_async_copy(
                    dfint_ref.at[
                        0,
                        pl.ds(pl.multiple_of(row * TB, TB), TB),
                        pl.ds(pl.multiple_of(column * TB, TB), TB),
                    ],
                    buffer.at[flow, j, :, pl.ds(t * TB, TB)],
                    in_sem.at[flow],
                ).start()
    for flow in range(count):
        pltpu.make_async_copy(buffer.at[flow], buffer.at[flow], in_sem.at[flow]).wait()
        pltpu.make_async_copy(buffer.at[flow], outs[flow], out_sem.at[flow]).start()
    for flow in range(count):
        pltpu.make_async_copy(buffer.at[flow], outs[flow], out_sem.at[flow]).wait()


def pack(dfint, domain, here, which, quarter):
    dom = domain.shape[1]
    count = len(FLOWS)
    tile_rows = (SLOTS, TB, dom * TB)
    return pl.pallas_call(
        functools.partial(pack_kernel, quarter, dom, which),
        out_shape=[jax.ShapeDtypeStruct(tile_rows, BF16)] * count,
        grid_spec=pltpu.PrefetchScalarGridSpec(
            num_scalar_prefetch=2,
            grid=(1,),
            in_specs=[pl.BlockSpec(memory_space=pl.ANY)],
            out_specs=[pl.BlockSpec(memory_space=pl.ANY)] * count,
            scratch_shapes=[
                pltpu.VMEM((count,) + tile_rows, BF16),
                pltpu.SemaphoreType.DMA((count,)),
                pltpu.SemaphoreType.DMA((count,)),
            ],
        ),
        compiler_params=pltpu.CompilerParams(vmem_limit_bytes=16 * 2**20),
        cost_estimate=pl.CostEstimate(flops=0, bytes_accessed=13 * 2**20, transcendentals=0),
        name="pack_tiles",
    )(domain, here, dfint)


def ladder_kernel(quarter, dom, which, domain_ref, here_ref, amp_ref, *rest):
    count = len(FLOWS)
    parts, (int_ref, ladder_ref, inter_ref, half, sem) = rest[:count], rest[count:]
    here, core = here_ref[0], here_ref[3]
    pair = (here * CORES + core) * CORES + which
    for f in range(CORES):
        for s in range(dom):
            owner = domain_ref[pair, s] // quarter
            rank = jnp.int32(0)
            for before in range(s):
                rank = rank + (domain_ref[pair, before] // quarter == owner).astype(jnp.int32)
            shift = lax.rem(here - owner + BLOCKS, BLOCKS)
            for flow, (flow_shift, flip) in enumerate(FLOWS):
                if flip == f:

                    @pl.when(shift == flow_shift)
                    def _(flow=flow, rank=rank, f=f, s=s):
                        pltpu.make_async_copy(
                            parts[flow].at[rank], int_ref.at[f, pl.ds(s * TB, TB), :], sem.at[f]
                        ).start()

    rows = 2 * TB
    diagonal = lax.broadcasted_iota(jnp.int32, (rows, rows), 0) == lax.broadcasted_iota(
        jnp.int32, (rows, rows), 1
    )
    for f in range(CORES):
        pltpu.make_async_copy(int_ref.at[f], int_ref.at[f], sem.at[f]).wait()
        total = jnp.zeros((rows, rows), F32)
        for r in range(0, dom * TB, rows):
            acc = lax.dot_general(
                int_ref[f, pl.ds(r, rows), :], amp_ref[which], NT, preferred_element_type=F32
            )
            half[f, pl.ds(r, rows), :] = acc.astype(BF16)
            total = total + acc[:, r : r + rows]
        inter_ref[0, f] = jnp.sum(jnp.where(diagonal, total, 0.0))
    for r in range(0, dom * TB, rows):
        acc = None
        for f in range(CORES):
            term = lax.dot_general(
                int_ref[f, pl.ds(r, rows), :], half[f], NT, preferred_element_type=F32
            )
            acc = term if acc is None else acc + term
        ladder_ref[pl.ds(r, rows), :] = acc


def half_and_ladder(amp, parts, domain, here, which, quarter):
    length = amp.shape[1]
    dom = domain.shape[1]
    vmem = pl.BlockSpec(memory_space=pltpu.VMEM)
    return pl.pallas_call(
        functools.partial(ladder_kernel, quarter, dom, which),
        out_shape=[
            jax.ShapeDtypeStruct((CORES, length, length), BF16),
            jax.ShapeDtypeStruct((length, length), F32),
            jax.ShapeDtypeStruct((1, CORES), F32),
        ],
        grid_spec=pltpu.PrefetchScalarGridSpec(
            num_scalar_prefetch=2,
            grid=(1,),
            in_specs=[vmem] + [pl.BlockSpec(memory_space=pl.ANY)] * len(parts),
            out_specs=[vmem, vmem, pl.BlockSpec(memory_space=pltpu.SMEM)],
            scratch_shapes=[
                pltpu.VMEM((CORES, length, length), BF16),
                pltpu.SemaphoreType.DMA((CORES,)),
            ],
        ),
        compiler_params=pltpu.CompilerParams(vmem_limit_bytes=32 * 2**20),
        cost_estimate=pl.CostEstimate(
            flops=8 * length**3, bytes_accessed=10 * 2**20, transcendentals=0
        ),
        name="half_and_ladder",
    )(domain, here, amp, *parts)


def masked_amps(amps, pair_mask, first_row, dom):
    pairs, rows, length = amps.shape
    row_slot = (first_row + jnp.arange(rows, dtype=jnp.int32)) // TB
    slot_pick = row_slot[:, None] == jnp.arange(dom, dtype=jnp.int32)[None, :]
    row_tiles = jnp.sum(
        jnp.where(slot_pick[None, :, :, None], pair_mask[:, None, :, :], 0), axis=2
    ).astype(BF16)
    tiles = amps.reshape(pairs, rows, dom, TB) * row_tiles[:, :, :, None]
    return tiles.reshape(pairs, rows, length)


def by_core(core, mine, other, axis):
    return jnp.where(
        core == 0,
        jnp.concatenate([mine, other], axis=axis),
        jnp.concatenate([other, mine], axis=axis),
    )


def make_body(ny, nx):
    def body(amps, domain, pair_mask, dfint, coupling):
        pairs, own, length = amps.shape
        dom = domain.shape[1]
        quarter = dfint.shape[1] // TB
        each = pairs // CORES
        z, y, x, c = (lax.axis_index(name).astype(jnp.int32) for name in ("z", "y", "x", "c"))
        here = jnp.stack([z, y, x, c])
        parts = []
        for which in range(each):
            packed = pack(dfint, domain, here, which, quarter)
            parts.append([hop(*flow)(part) for flow, part in zip(FLOWS[:-1], packed)] + [packed[-1]])
        masked = masked_amps(amps, pair_mask, ((y * nx + x) * CORES + c) * own, dom)
        mine = lax.dynamic_slice_in_dim(masked, c * each, each, axis=0)
        other = swap_cores(lax.dynamic_slice_in_dim(masked, (1 - c) * each, each, axis=0))
        amp = lax.all_gather(by_core(c, mine, other, 1), ("y", "x"), axis=1, tiled=True)
        blocks, sums, inters = zip(
            *(half_and_ladder(amp, parts[which], domain, here, which, quarter) for which in range(each))
        )
        inter = jnp.concatenate(inters, axis=0)
        inter = jnp.where(c == 0, inter, inter[:, ::-1])
        spread = jnp.broadcast_to(inter.reshape(1, each * CORES), (BLOCKS * CORES, each * CORES))
        every = lax.all_to_all(spread, ("z", "c"), 0, 0, tiled=True)
        every = every.reshape(BLOCKS * pairs, CORES)
        rows = lax.dynamic_slice_in_dim(coupling, c * each, each, axis=0)
        dressing = jnp.sum(rows[:, :, None] * every[None], axis=1)
        dressing = jnp.where(c == 0, dressing, dressing[:, ::-1])
        chips = ny * nx
        totals = []
        for which in range(each):
            total = sums[which]
            for f in range(CORES):
                total = total + dressing[which, f] * blocks[which][f].astype(F32)
            totals.append(total.astype(BF16).reshape(chips, 1, length // chips, length))
        sent = jnp.concatenate(totals, axis=1)
        got = lax.all_to_all(sent, ("y", "x"), 0, 0, tiled=True)
        result = jnp.sum(got.astype(F32), axis=0).astype(BF16)
        mine = lax.dynamic_slice_in_dim(result, c * own, own, axis=1)
        other = swap_cores(lax.dynamic_slice_in_dim(result, (1 - c) * own, own, axis=1))
        return by_core(c, mine, other, 0)

    return body


def solution(mesh):
    ny = nx = 4
    grid = Mesh(mesh.devices.reshape(BLOCKS, ny, nx, CORES), ("z", "y", "x", "c"))
    virt = ("y", "x", "c")
    return jax.shard_map(
        make_body(ny, nx),
        mesh=grid,
        in_specs=(P("z", virt, None), P(), P("z", None, None), P(virt, "z", None), P("z", None)),
        out_specs=P("z", virt, None),
        check_vma=False,
    )
```

time: 572 us -> 178 us (0.31); the launches traced: 565 us -> 178 us
  blocking collectives: 180 us -> 0 us
  waiting for transfers between devices: 164 us -> 49.5 us
  local copies, waits for them, and re-layouts: 139 us -> 27.5 us
  starting transfers between devices: 0.23 us -> 51.6 us
  other arithmetic: 49.5 us -> 11 us
  Pallas kernels: 0 us -> 24.6 us
  matrix products: 15.2 us -> 0 us
    unnamed x2 -> x0, blocking collectives: 180 us -> none
    reduce_scatter x1 -> x0, waiting for transfers between devices: 164 us -> none  [body(): lax.psum_scatter(weighted.astype(jnp.bfloat16), 'pair', scatter_dimension...]
    gather x6 -> x0, local copies, waits for them, and re-layouts: 96.8 us -> none  [the longest x3 78.9 us: body(): jnp.take(local_ints, tiles, axis=3)]
    all_to_all x0 -> x2, waiting for transfers between devices: none -> 39 us  [the longest x1 34.6 us: body(): got = lax.all_to_all(sent, ('y', 'x'), 0, 0, tiled=True)]
    ppermute x0 -> x16, starting transfers between devices: none -> 37.4 us  [the longest x14 33.9 us: body(): hop(*flow)(part)]
    pallas_call x0 -> x4, Pallas kernels: none -> 24.6 us  [the longest x2 15.7 us: half_and_ladder(): pl.pallas_call(functools.partial(ladder_kernel, quarter, dom, which), out...]
    select_n x3 -> x5, other arithmetic: 21.7 us -> 1.39 us  [the longest x2 1.36 us: by_core(): jnp.where(core == 0, jnp.concatenate([mine, other], axis=axis), jnp.conca...]
    dot_general x3 -> x0, matrix products: 15.2 us -> none  [the longest x1 14.9 us: body(): jnp.einsum('pqac,pqbc->apb', int_rows, half_ladder, preferred_element_typ...]
  transfers between devices with their start and end apart: 2 -> 19, of which waited for: 1 -> 8; matrix products, arithmetic and copies ran while one was open for 2% -> 0% of each run, Pallas kernels for 0% -> 10%
where the time goes in v2:
time: 178 us
  starting transfers between devices  51.6 us (29%)
  waiting for transfers between devices  49.5 us (28%)
  local copies, waits for them, and re-layouts  27.5 us (15%)
  Pallas kernels  24.6 us (14%)
  between operations  13.6 us (8%)
  other arithmetic  11 us (6%)
    all_to_all x1, waiting for transfers between devices, body(): got = lax.all_to_all(sent, ('y', 'x'), 0, 0, tiled=True)  34.6 us
    ppermute x14, starting transfers between devices, body(): hop(*flow)(part)  33.9 us
    unnamed x54, local copies, waits for them, and re-layouts  24.8 us
    pallas_call x2, Pallas kernels, half_and_ladder(): pl.pallas_call(functools.partial(ladder_kernel, quarter, dom, which), out...  15.7 us
    pallas_call x2, Pallas kernels, pack(): pl.pallas_call(functools.partial(pack_kernel, quarter, dom, which), out_s...  8.91 us
    ppermute x14, waiting for transfers between devices, body(): hop(*flow)(part)  8.63 us
    all_to_all x1, starting transfers between devices, body(): every = lax.all_to_all(spread, ('z', 'c'), 0, 0, tiled=True)  7.53 us
    all_to_all x1, starting transfers between devices, body(): got = lax.all_to_all(sent, ('y', 'x'), 0, 0, tiled=True)  6.71 us
  transfers between devices with their start and end apart: 19, of which 8 were waited for; matrix products, arithmetic and copies ran while one was open for 0% of the time, Pallas kernels for 10%

profile of v2, /device:TPU:1, one launch (start us, length us, event | category | flops | bytes accessed | tf_op | source)
XLA Modules:
  0.0 177.8 jit_solution(17555163748336528284)
XLA Ops:
  9.0 1.5 collective-permute-start
  13.0 3.4 %copy-done.1 = bf16[1,1024,4096]{2,1,0:T(8,128)(2,1)S(1)} copy-done((bf16[1,1024,4096]{2,1,0:T(8,128)(2,1)S(1)}, bf16[1,1024,4096]{2,1,0:T(8,128)(2,1)}, u32[]{:S(2)}) %copy-start.1) | copy-done | bytes 8388632
  16.4 4.5 %pack_tiles.3 = (bf16[2,128,768]{2,1,0:T(8,128)(2,1)S(1)}, bf16[2,128,768]{2,1,0:T(8,128)(2,1)S(1)}, bf16[2,128,768]{2,1,0:T(8,128)(2,1)S(1)}, bf16[2,128,768]{2...) custom-call(s32[16,6]{1,0:T(8,128)S(1)} %copy.26.domain_ref, ...), custom_call_target="tpu_custom_call" | custom-call | bytes 13631488 | tf_op jit(solution)/shard_map/pack_tiles/pallas_call | solution.py:77
  20.8 1.8 %collective-permute-start.8 = (bf16[2,128,768]{2,1,0:T(8,128)(2,1)S(1)}, bf16[2,128,768]{2,1,0:T(8,128)(2,1)S(1)}, u32[]{:S(2)}, u32[]{:S(2)}) collective-permute-start(bf16[2,128,768]{2,1,0:T(8,128)(2,1)S(1)} %get-tuple-element.37), channel_id=1, source_target_pairs={{0,32},{1,33},{32,64},{33,65},{64,96},{65,97},{96,0},{97,1},{2,34}... | collective-permute-start | bytes 1179656 | tf_op jit(solution)/shard_map/ppermute | solution.py:201
  22.6 2.2 %collective-permute-start.9 = (bf16[2,128,768]{2,1,0:T(8,128)(2,1)S(1)}, bf16[2,128,768]{2,1,0:T(8,128)(2,1)S(1)}, u32[]{:S(2)}, u32[]{:S(2)}) collective-permute-start(bf16[2,128,768]{2,1,0:T(8,128)(2,1)S(1)} %get-tuple-element.38), channel_id=1, source_target_pairs={{0,96},{1,97},{32,0},{33,1},{64,32},{65,33},{96,64},{97,65},{2,98}... | collective-permute-start | bytes 1179656 | tf_op jit(solution)/shard_map/ppermute | solution.py:201
  24.9 2.9 %collective-permute-start.11 = (bf16[2,128,768]{2,1,0:T(8,128)(2,1)S(1)}, bf16[2,128,768]{2,1,0:T(8,128)(2,1)S(1)}, u32[]{:S(2)}, u32[]{:S(2)}) collective-permute-start(bf16[2,128,768]{2,1,0:T(8,128)(2,1)S(1)} %get-tuple-element.40), channel_id=1, source_target_pairs={{0,97},{1,96},{32,1},{33,0},{64,33},{65,32},{96,65},{97,64},{2,99}... | collective-permute-start | bytes 1179656 | tf_op jit(solution)/shard_map/ppermute | solution.py:201
  28.2 4.4 %pack_tiles.2 = (bf16[2,128,768]{2,1,0:T(8,128)(2,1)S(1)}, bf16[2,128,768]{2,1,0:T(8,128)(2,1)S(1)}, bf16[2,128,768]{2,1,0:T(8,128)(2,1)}, bf16[2,128,768]{2,1,0...) custom-call(s32[16,6]{1,0:T(8,128)S(1)} %copy.26.domain_ref, ...), custom_call_target="tpu_custom_call" | custom-call | bytes 13631488 | tf_op jit(solution)/shard_map/pack_tiles/pallas_call | solution.py:77
  32.7 1.4 collective-permute-done.8.rest_0_
  34.8 2.7 %collective-permute-start.13 = (bf16[2,128,768]{2,1,0:T(8,128)(2,1)S(1)}, bf16[2,128,768]{2,1,0:T(8,128)(2,1)S(1)}, u32[]{:S(2)}, u32[]{:S(2)}) collective-permute-start(bf16[2,128,768]{2,1,0:T(8,128)(2,1)S(1)} %get-tuple-element.42), channel_id=1, source_target_pairs={{0,65},{1,64},{32,97},{33,96},{64,1},{65,0},{96,33},{97,32},{2,67}... | collective-permute-start | bytes 1179656 | tf_op jit(solution)/shard_map/ppermute | solution.py:201
  38.4 4.2 %collective-permute-done.10.rest_2_ = bf16[2,128,768]{2,1,0:T(8,128)(2,1)S(1)} collective-permute-done((bf16[2,128,768]{2,1,0:T(8,128)(2,1)S(1)}, bf16[2,128,768]{2,1,0:T(8,128)(2,1)S(1)}, u32[]{:S(2)}, u32[]{:S(2)}) %collective-permute-start.10) | collective-permute-done | bytes 393248 | tf_op jit(solution)/shard_map/ppermute | solution.py:201
  44.3 19.1 %collective-permute-start.2 = (bf16[2,128,768]{2,1,0:T(8,128)(2,1)S(1)}, bf16[2,128,768]{2,1,0:T(8,128)(2,1)S(1)}, u32[]{:S(2)}, u32[]{:S(2)}) collective-permute-start(bf16[2,128,768]{2,1,0:T(8,128)(2,1)S(1)} %get-tuple-element.28), channel_id=1, source_target_pairs={{0,96},{1,97},{32,0},{33,1},{64,32},{65,33},{96,64},{97,65},{2,98}... | collective-permute-start | bytes 1179656 | tf_op jit(solution)/shard_map/ppermute | solution.py:201
  64.9 3.0 %collective-permute-start.4 = (bf16[2,128,768]{2,1,0:T(8,128)(2,1)}, bf16[2,128,768]{2,1,0:T(8,128)(2,1)}, u32[]{:S(2)}, u32[]{:S(2)}) collective-permute-start(bf16[2,128,768]{2,1,0:T(8,128)(2,1)} %get-tuple-element.30), channel_id=1, source_target_pairs={{0,97},{1,96},{32,1},{33,0},{64,33},{65,32},{96,65},{97,64},{2,99}... | collective-permute-start | bytes 1179656 | tf_op jit(solution)/shard_map/ppermute | solution.py:201
  70.0 2.3 %collective-permute-done.2.rest_1_ = bf16[2,128,768]{2,1,0:T(8,128)(2,1)S(1)} collective-permute-done((bf16[2,128,768]{2,1,0:T(8,128)(2,1)S(1)}, bf16[2,128,768]{2,1,0:T(8,128)(2,1)S(1)}, u32[]{:S(2)}, u32[]{:S(2)}) %collective-permute-start.2) | collective-permute-done | bytes 393248 | tf_op jit(solution)/shard_map/ppermute | solution.py:201
  73.1 1.6 collective-permute-start.7
  74.7 1.7 copy-done.7
  76.4 1.0 copy-done.9
  77.4 1.0 copy-done.11
  78.4 1.0 copy-done.13
  81.4 1.0 copy-done.23
  83.4 8.8 %half_and_ladder.3 = (bf16[2,768,768]{2,1,0:T(8,128)(2,1)S(1)}, f32[768,768]{1,0:T(8,128)S(1)}, f32[1,2]{1,0:T(1,128)S(1)}) custom-call(s32[16,6]{1,0:T(8,128)S(1)} %copy.26.domain_ref, s32[4]{0:T(128)S(1)} %pad_add_fusion.here_ref, bf16[2,768,768]{2,1,0:T(8,128)(2,1)S(1)} %copy-done.7, bf16[2,128,768]{2,1,0:T(8,128)(2,1)S(1)} %copy-done.9, ...), custom_call_target="tpu_custom_call" | custom-call | flops 3623878656 | bytes 10485760 | tf_op jit(solution)/shard_map/half_and_ladder/pallas_call | solution.py:146
  92.1 1.4 copy-done.2
  93.6 6.9 %half_and_ladder.2 = (bf16[2,768,768]{2,1,0:T(8,128)(2,1)S(1)}, f32[768,768]{1,0:T(8,128)S(1)}, f32[1,2]{1,0:T(1,128)S(1)}) custom-call(s32[16,6]{1,0:T(8,128)S(1)} %copy.26.domain_ref, s32[4]{0:T(128)S(1)} %pad_add_fusion.here_ref, bf16[2,768,768]{2,1,0:T(8,128)(2,1)S(1)} %copy-done.7, bf16[2,128,768]{2,1,0:T(8,128)(2,1)S(1)} %copy-done.19, ...), custom_call_target="tpu_custom_call" | custom-call | flops 3623878656 | bytes 10485760 | tf_op jit(solution)/shard_map/half_and_ladder/pallas_call | solution.py:146
  100.6 1.4 copy-done.3
  102.0 1.4 copy-done.5
  104.2 7.5 %all-to-all-start = ((f32[8,1,4]{2,1,0:T(1,128)}), f32[8,1,4]{2,1,0:T(1,128)S(1)}, u32[]{:S(2)}, u32[]{:S(2)}) async-start(f32[8,1,4]{2,1,0:T(1,128)} %broadcast_in_dim.37), calls=%async_computation | async-start | bytes 8192 | tf_op jit(solution)/shard_map/all_to_all | solution.py:212
  111.8 4.5 %all-to-all-done = f32[8,1,4]{2,1,0:T(1,128)S(1)} async-done(((f32[8,1,4]{2,1,0:T(1,128)}), f32[8,1,4]{2,1,0:T(1,128)S(1)}, u32[]{:S(2)}, u32[]{:S(2)}) %all-to-all-start) | async-done | bytes 160 | tf_op jit(solution)/shard_map/all_to_all | solution.py:212
  118.4 3.9 %fusion = bf16[768,768]{1,0:T(8,128)(2,1)S(1)} fusion(f32[768,768]{1,0:T(8,128)} %copy-done.2, bf16[2,768,768]{2,1,0:T(8,128)(2,1)S(1)} %get-tuple-element.48, f32[]{:T(128)} %bitcast.12, f32[]{:T(128)} %bitcast.10), kind=kLoop, calls=%fused_computation.2 | loop fusion | flops 4128768 | bytes 5898248 | tf_op jit(solution)/shard_map/convert_element_type | solution.py:223
  122.4 1.8 fusion.1
  124.1 1.6 pad_maximum_fusion
  125.8 6.7 %all-to-all-start.1 = ((bf16[16,2,48,768]{3,2,1,0:T(8,128)(2,1)}), bf16[16,2,48,768]{3,2,1,0:T(8,128)(2,1)S(1)}, u32[]{:S(2)}, u32[]{:S(2)}) async-start(bf16[16,2,48,768]{3,2,1,0:T(8,128)(2,1)} %pad_maximum_fusion), calls=%async_computation.1 | async-start | bytes 4718592 | tf_op jit(solution)/shard_map/all_to_all | solution.py:225
  132.5 34.6 %all-to-all-done.1 = bf16[16,2,48,768]{3,2,1,0:T(8,128)(2,1)S(1)} async-done(((bf16[16,2,48,768]{3,2,1,0:T(8,128)(2,1)}), bf16[16,2,48,768]{3,2,1,0:T(8,128)(2,1)S(1)}, u32[]{:S(2)}, u32[]{:S(2)}) %all-to-all-start.1) | async-done | bytes 2359328 | tf_op jit(solution)/shard_map/all_to_all | solution.py:225
  167.4 1.9 %collective-permute-start.15 = (bf16[2,24,768]{2,1,0:T(8,128)(2,1)S(1)}, bf16[2,24,768]{2,1,0:T(8,128)(2,1)S(1)}, u32[]{:S(2)}, u32[]{:S(2)}) collective-permute-start(bf16[2,24,768]{2,1,0:T(8,128)(2,1)S(1)} %get-tuple-element.50), channel_id=1, source_target_pairs={{0,1},{1,0},{2,3},{3,2},{4,5},{5,4},{6,7},{7,6},{8,9},{9,8},{10,11... | collective-permute-start | bytes 221192 | tf_op jit(solution)/shard_map/ppermute | solution.py:31
  (96 shorter events, 21.0 us)
Async XLA Ops:
  6.5 105.2 %copy-start = (f32[4,16]{1,0:T(4,128)S(1)}, f32[4,16]{1,0:T(4,128)}, u32[]{:S(2)}) copy-start(f32[4,16]{1,0:T(4,128)} %param.9) | copy-start | bytes 772
  6.5 68.2 %all-gather.2.cloned.1.call-start = ((), (), s32[]{:S(2)}) async-start(), calls=%async_computation.2 | async-start | bytes 2506752 | tf_op jit(solution)/shard_map/all_gather | solution.py:205
  9.0 2.4 %collective-permute-start = (bf16[2,24,768]{2,1,0:T(8,128)(2,1)S(1)}, bf16[2,24,768]{2,1,0:T(8,128)(2,1)S(1)}, u32[]{:S(2)}, u32[]{:S(2)}) collective-permute-start(bf16[2,24,768]{2,1,0:T(8,128)(2,1)S(1)} %get-tuple-element.52), channel_id=1, source_target_pairs={{0,1},{1,0},{2,3},{3,2},{4,5},{5,4},{6,7},{7,6},{8,9},{9,8},{10,11... | collective-permute-start | bytes 221192 | tf_op jit(solution)/shard_map/ppermute | solution.py:31
  13.0 3.4 %copy-start.1 = (bf16[1,1024,4096]{2,1,0:T(8,128)(2,1)S(1)}, bf16[1,1024,4096]{2,1,0:T(8,128)(2,1)}, u32[]{:S(2)}) copy-start(bf16[1,1024,4096]{2,1,0:T(8,128)(2,1)} %dfint_ref.3) | copy-start | bytes 25165828
  20.8 13.2 %collective-permute-start.8 = (bf16[2,128,768]{2,1,0:T(8,128)(2,1)S(1)}, bf16[2,128,768]{2,1,0:T(8,128)(2,1)S(1)}, u32[]{:S(2)}, u32[]{:S(2)}) collective-permute-start(bf16[2,128,768]{2,1,0:T(8,128)(2,1)S(1)} %get-tuple-element.37), channel_id=1, source_target_pairs={{0,32},{1,33},{32,64},{33,65},{64,96},{65,97},{96,0},{97,1},{2,34}... | collective-permute-start | bytes 1179656 | tf_op jit(solution)/shard_map/ppermute | solution.py:201
  22.6 14.9 %collective-permute-start.9 = (bf16[2,128,768]{2,1,0:T(8,128)(2,1)S(1)}, bf16[2,128,768]{2,1,0:T(8,128)(2,1)S(1)}, u32[]{:S(2)}, u32[]{:S(2)}) collective-permute-start(bf16[2,128,768]{2,1,0:T(8,128)(2,1)S(1)} %get-tuple-element.38), channel_id=1, source_target_pairs={{0,96},{1,97},{32,0},{33,1},{64,32},{65,33},{96,64},{97,65},{2,98}... | collective-permute-start | bytes 1179656 | tf_op jit(solution)/shard_map/ppermute | solution.py:201
  24.8 17.7 %collective-permute-start.10 = (bf16[2,128,768]{2,1,0:T(8,128)(2,1)S(1)}, bf16[2,128,768]{2,1,0:T(8,128)(2,1)S(1)}, u32[]{:S(2)}, u32[]{:S(2)}) collective-permute-start(bf16[2,128,768]{2,1,0:T(8,128)(2,1)S(1)} %get-tuple-element.39), channel_id=1, source_target_pairs={{0,33},{1,32},{32,65},{33,64},{64,97},{65,96},{96,1},{97,0},{2,35}... | collective-permute-start | bytes 1179656 | tf_op jit(solution)/shard_map/ppermute | solution.py:201
  24.9 18.6 %collective-permute-start.11 = (bf16[2,128,768]{2,1,0:T(8,128)(2,1)S(1)}, bf16[2,128,768]{2,1,0:T(8,128)(2,1)S(1)}, u32[]{:S(2)}, u32[]{:S(2)}) collective-permute-start(bf16[2,128,768]{2,1,0:T(8,128)(2,1)S(1)} %get-tuple-element.40), channel_id=1, source_target_pairs={{0,97},{1,96},{32,1},{33,0},{64,33},{65,32},{96,65},{97,64},{2,99}... | collective-permute-start | bytes 1179656 | tf_op jit(solution)/shard_map/ppermute | solution.py:201
  27.8 35.6 %collective-permute-start.12 = (bf16[2,128,768]{2,1,0:T(8,128)(2,1)S(1)}, bf16[2,128,768]{2,1,0:T(8,128)(2,1)S(1)}, u32[]{:S(2)}, u32[]{:S(2)}) collective-permute-start(bf16[2,128,768]{2,1,0:T(8,128)(2,1)S(1)} %get-tuple-element.41), channel_id=1, source_target_pairs={{0,64},{1,65},{32,96},{33,97},{64,0},{65,1},{96,32},{97,33},{2,66}... | collective-permute-start | bytes 1179656 | tf_op jit(solution)/shard_map/ppermute | solution.py:201
  34.8 29.3 %collective-permute-start.13 = (bf16[2,128,768]{2,1,0:T(8,128)(2,1)S(1)}, bf16[2,128,768]{2,1,0:T(8,128)(2,1)S(1)}, u32[]{:S(2)}, u32[]{:S(2)}) collective-permute-start(bf16[2,128,768]{2,1,0:T(8,128)(2,1)S(1)} %get-tuple-element.42), channel_id=1, source_target_pairs={{0,65},{1,64},{32,97},{33,96},{64,1},{65,0},{96,33},{97,32},{2,67}... | collective-permute-start | bytes 1179656 | tf_op jit(solution)/shard_map/ppermute | solution.py:201
  38.3 29.5 %collective-permute-start.14 = (bf16[2,128,768]{2,1,0:T(8,128)(2,1)S(1)}, bf16[2,128,768]{2,1,0:T(8,128)(2,1)S(1)}, u32[]{:S(2)}, u32[]{:S(2)}) collective-permute-start(bf16[2,128,768]{2,1,0:T(8,128)(2,1)S(1)} %get-tuple-element.43), channel_id=1, source_target_pairs={{0,1},{1,0},{32,33},{33,32},{64,65},{65,64},{96,97},{97,96},{2,3},... | collective-permute-start | bytes 1179656 | tf_op jit(solution)/shard_map/ppermute | solution.py:201
  43.3 25.9 %collective-permute-start.1 = (bf16[2,128,768]{2,1,0:T(8,128)(2,1)S(1)}, bf16[2,128,768]{2,1,0:T(8,128)(2,1)S(1)}, u32[]{:S(2)}, u32[]{:S(2)}) collective-permute-start(bf16[2,128,768]{2,1,0:T(8,128)(2,1)S(1)} %get-tuple-element.27), channel_id=1, source_target_pairs={{0,32},{1,33},{32,64},{33,65},{64,96},{65,97},{96,0},{97,1},{2,34}... | collective-permute-start | bytes 1179656 | tf_op jit(solution)/shard_map/ppermute | solution.py:201
  44.3 28.1 %collective-permute-start.2 = (bf16[2,128,768]{2,1,0:T(8,128)(2,1)S(1)}, bf16[2,128,768]{2,1,0:T(8,128)(2,1)S(1)}, u32[]{:S(2)}, u32[]{:S(2)}) collective-permute-start(bf16[2,128,768]{2,1,0:T(8,128)(2,1)S(1)} %get-tuple-element.28), channel_id=1, source_target_pairs={{0,96},{1,97},{32,0},{33,1},{64,32},{65,33},{96,64},{97,65},{2,98}... | collective-permute-start | bytes 1179656 | tf_op jit(solution)/shard_map/ppermute | solution.py:201
  64.1 29.5 %collective-permute-start.3 = (bf16[2,128,768]{2,1,0:T(8,128)(2,1)}, bf16[2,128,768]{2,1,0:T(8,128)(2,1)}, u32[]{:S(2)}, u32[]{:S(2)}) collective-permute-start(bf16[2,128,768]{2,1,0:T(8,128)(2,1)} %get-tuple-element.29), channel_id=1, source_target_pairs={{0,33},{1,32},{32,65},{33,64},{64,97},{65,96},{96,1},{97,0},{2,35}... | collective-permute-start | bytes 1179656 | tf_op jit(solution)/shard_map/ppermute | solution.py:201
  64.9 28.7 %collective-permute-start.4 = (bf16[2,128,768]{2,1,0:T(8,128)(2,1)}, bf16[2,128,768]{2,1,0:T(8,128)(2,1)}, u32[]{:S(2)}, u32[]{:S(2)}) collective-permute-start(bf16[2,128,768]{2,1,0:T(8,128)(2,1)} %get-tuple-element.30), channel_id=1, source_target_pairs={{0,97},{1,96},{32,1},{33,0},{64,33},{65,32},{96,65},{97,64},{2,99}... | collective-permute-start | bytes 1179656 | tf_op jit(solution)/shard_map/ppermute | solution.py:201
  68.6 25.0 %collective-permute-start.5 = (bf16[2,128,768]{2,1,0:T(8,128)(2,1)}, bf16[2,128,768]{2,1,0:T(8,128)(2,1)}, u32[]{:S(2)}, u32[]{:S(2)}) collective-permute-start(bf16[2,128,768]{2,1,0:T(8,128)(2,1)} %get-tuple-element.31), channel_id=1, source_target_pairs={{0,64},{1,65},{32,96},{33,97},{64,0},{65,1},{96,32},{97,33},{2,66}... | collective-permute-start | bytes 1179656 | tf_op jit(solution)/shard_map/ppermute | solution.py:201
  70.0 23.6 %collective-permute-start.6 = (bf16[2,128,768]{2,1,0:T(8,128)(2,1)}, bf16[2,128,768]{2,1,0:T(8,128)(2,1)}, u32[]{:S(2)}, u32[]{:S(2)}) collective-permute-start(bf16[2,128,768]{2,1,0:T(8,128)(2,1)} %get-tuple-element.32), channel_id=1, source_target_pairs={{0,65},{1,64},{32,97},{33,96},{64,1},{65,0},{96,33},{97,32},{2,67}... | collective-permute-start | bytes 1179656 | tf_op jit(solution)/shard_map/ppermute | solution.py:201
  73.1 20.5 %collective-permute-start.7 = (bf16[2,128,768]{2,1,0:T(8,128)(2,1)}, bf16[2,128,768]{2,1,0:T(8,128)(2,1)}, u32[]{:S(2)}, u32[]{:S(2)}) collective-permute-start(bf16[2,128,768]{2,1,0:T(8,128)(2,1)} %get-tuple-element.33), channel_id=1, source_target_pairs={{0,1},{1,0},{32,33},{33,32},{64,65},{65,64},{96,97},{97,96},{2,3},... | collective-permute-start | bytes 1179656 | tf_op jit(solution)/shard_map/ppermute | solution.py:201
  74.7 1.7 copy-start.7
  76.4 1.0 copy-start.9
  79.4 1.0 copy-start.15
  80.4 1.0 copy-start.17
  83.4 10.2 %copy-start.19 = (bf16[2,128,768]{2,1,0:T(8,128)(2,1)S(1)}, bf16[2,128,768]{2,1,0:T(8,128)(2,1)}, u32[]{:S(2)}) copy-start(bf16[2,128,768]{2,1,0:T(8,128)(2,1)} %copy-done.18) | copy-start | bytes 1179652
  83.4 10.2 %copy-start.21 = (bf16[2,128,768]{2,1,0:T(8,128)(2,1)S(1)}, bf16[2,128,768]{2,1,0:T(8,128)(2,1)}, u32[]{:S(2)}) copy-start(bf16[2,128,768]{2,1,0:T(8,128)(2,1)} %copy-done.20) | copy-start | bytes 1179652
  92.1 1.4 copy-start.2
  100.5 1.4 copy-start.3
  102.0 1.4 copy-start.5
  104.2 12.0 %all-to-all-start = ((f32[8,1,4]{2,1,0:T(1,128)}), f32[8,1,4]{2,1,0:T(1,128)S(1)}, u32[]{:S(2)}, u32[]{:S(2)}) async-start(f32[8,1,4]{2,1,0:T(1,128)} %broadcast_in_dim.37), calls=%async_computation | async-start | bytes 8192 | tf_op jit(solution)/shard_map/all_to_all | solution.py:212
  118.4 3.9 %copy-start.4 = (bf16[2,768,768]{2,1,0:T(8,128)(2,1)S(1)}, bf16[2,768,768]{2,1,0:T(8,128)(2,1)}, u32[]{:S(2)}) copy-start(bf16[2,768,768]{2,1,0:T(8,128)(2,1)} %copy-done.3) | copy-start | bytes 7077892
  118.4 3.9 %copy-start.6 = (f32[768,768]{1,0:T(8,128)S(1)}, f32[768,768]{1,0:T(8,128)}, u32[]{:S(2)}) copy-start(f32[768,768]{1,0:T(8,128)} %copy-done.5) | copy-start | bytes 7077892
  125.8 41.3 %all-to-all-start.1 = ((bf16[16,2,48,768]{3,2,1,0:T(8,128)(2,1)}), bf16[16,2,48,768]{3,2,1,0:T(8,128)(2,1)S(1)}, u32[]{:S(2)}, u32[]{:S(2)}) async-start(bf16[16,2,48,768]{3,2,1,0:T(8,128)(2,1)} %pad_maximum_fusion), calls=%async_computation.1 | async-start | bytes 4718592 | tf_op jit(solution)/shard_map/all_to_all | solution.py:225
  167.4 2.8 %collective-permute-start.15 = (bf16[2,24,768]{2,1,0:T(8,128)(2,1)S(1)}, bf16[2,24,768]{2,1,0:T(8,128)(2,1)S(1)}, u32[]{:S(2)}, u32[]{:S(2)}) collective-permute-start(bf16[2,24,768]{2,1,0:T(8,128)(2,1)S(1)} %get-tuple-element.50), channel_id=1, source_target_pairs={{0,1},{1,0},{2,3},{3,2},{4,5},{5,4},{6,7},{7,6},{8,9},{9,8},{10,11... | collective-permute-start | bytes 221192 | tf_op jit(solution)/shard_map/ppermute | solution.py:31
  (13 other events, 10.9 us)
Sparse Core Ops, SparseCore 0:
  12.3 46.7 all-gather.1

commit v3 on v2

v3 whole, which is shorter than its diff:
```python
import functools

import jax
import jax.numpy as jnp
from jax import lax
from jax.experimental import pallas as pl
from jax.experimental.pallas import tpu as pltpu
from jax.sharding import Mesh
from jax.sharding import PartitionSpec as P

TB = 128
BLOCKS = 4
CORES = 2
SLOTS = 2
VMEM_LIMIT = 56 * 2**20
BF16 = jnp.bfloat16
F32 = jnp.float32
NT = (((1,), (1,)), ((), ()))
SHIFTS = (1, 3, 2, 0)


def hop(shift, flip):
    perm = [
        (z * CORES + c, (z + shift) % BLOCKS * CORES + (c ^ flip))
        for z in range(BLOCKS)
        for c in range(CORES)
    ]
    return functools.partial(lax.ppermute, axis_name=("z", "c"), perm=perm)


def swap_cores(value):
    return lax.ppermute(value, "c", [(0, 1), (1, 0)])


def block_slots(domain_ref, pair, block, quarter, dom):
    found = jnp.int32(0)
    first = jnp.int32(0)
    second = jnp.int32(0)
    for s in range(dom):
        inside = domain_ref[pair, s] // quarter == block
        first = jnp.where(inside & (found == 0), s, first)
        second = jnp.where(inside & (found == 1), s, second)
        found = found + inside.astype(jnp.int32)
    return first, second


def pack_kernel(quarter, dom, which, flip, domain_ref, here_ref, dfint_ref, *rest):
    count = len(SHIFTS)
    outs, (buffer, in_sem, out_sem) = rest[:count], rest[count:]
    here, core = here_ref[0], here_ref[3]
    for n, shift in enumerate(SHIFTS):
        target = lax.rem(here + shift, BLOCKS)
        pair = (target * CORES + (core ^ flip)) * CORES + which
        for j, slot in enumerate(block_slots(domain_ref, pair, here, quarter, dom)):
            row = jnp.clip(domain_ref[pair, slot] - here * quarter, 0, quarter - 1)
            for t in range(dom):
                column = domain_ref[pair, t]
                pltpu.make_async_copy(
                    dfint_ref.at[
                        0,
                        pl.ds(pl.multiple_of(row * TB, TB), TB),
                        pl.ds(pl.multiple_of(column * TB, TB), TB),
                    ],
                    buffer.at[n, j, :, pl.ds(t * TB, TB)],
                    in_sem.at[n],
                ).start()
    for n in range(count):
        pltpu.make_async_copy(buffer.at[n], buffer.at[n], in_sem.at[n]).wait()
        pltpu.make_async_copy(buffer.at[n], outs[n], out_sem.at[n]).start()
    for n in range(count):
        pltpu.make_async_copy(buffer.at[n], outs[n], out_sem.at[n]).wait()


def pack(dfint, domain, here, which, flip, quarter):
    dom = domain.shape[1]
    count = len(SHIFTS)
    tile_rows = (SLOTS, TB, dom * TB)
    return pl.pallas_call(
        functools.partial(pack_kernel, quarter, dom, which, flip),
        out_shape=[jax.ShapeDtypeStruct(tile_rows, BF16)] * count,
        grid_spec=pltpu.PrefetchScalarGridSpec(
            num_scalar_prefetch=2,
            grid=(1,),
            in_specs=[pl.BlockSpec(memory_space=pl.ANY)],
            out_specs=[pl.BlockSpec(memory_space=pl.ANY)] * count,
            scratch_shapes=[
                pltpu.VMEM((count,) + tile_rows, BF16),
                pltpu.SemaphoreType.DMA((count,)),
                pltpu.SemaphoreType.DMA((count,)),
            ],
        ),
        compiler_params=pltpu.CompilerParams(vmem_limit_bytes=VMEM_LIMIT),
        cost_estimate=pl.CostEstimate(flops=0, bytes_accessed=7 * 2**20, transcendentals=0),
        name="pack_tiles",
    )(domain, here, dfint)


def half_kernel(quarter, dom, which, flip, domain_ref, here_ref, amp_ref, before_ref, *rest):
    count = len(SHIFTS)
    parts, (int_ref, half_ref, inter_ref, sem) = rest[:count], rest[count:]
    here, core = here_ref[0], here_ref[3]
    pair = (here * CORES + core) * CORES + which
    for s in range(dom):
        owner = domain_ref[pair, s] // quarter
        rank = jnp.int32(0)
        for earlier in range(s):
            rank = rank + (domain_ref[pair, earlier] // quarter == owner).astype(jnp.int32)
        shift = lax.rem(here - owner + BLOCKS, BLOCKS)
        for n, flow_shift in enumerate(SHIFTS):

            @pl.when(shift == flow_shift)
            def _(n=n, rank=rank, s=s):
                pltpu.make_async_copy(
                    parts[n].at[rank], int_ref.at[pl.ds(s * TB, TB), :], sem.at[0]
                ).start()

    rows = 2 * TB
    pltpu.make_async_copy(int_ref, int_ref, sem.at[0]).wait()
    total = jnp.zeros((rows, rows), F32)
    for r in range(0, dom * TB, rows):
        acc = lax.dot_general(
            int_ref[pl.ds(r, rows), :], amp_ref[...], NT, preferred_element_type=F32
        )
        half_ref[pl.ds(r, rows), :] = acc.astype(BF16)
        total = total + acc[:, r : r + rows]
    diagonal = lax.broadcasted_iota(jnp.int32, (rows, rows), 0) == lax.broadcasted_iota(
        jnp.int32, (rows, rows), 1
    )
    trace = jnp.sum(jnp.where(diagonal, total, 0.0))
    lane = lax.broadcasted_iota(jnp.int32, inter_ref.shape, 1)
    inter_ref[...] = jnp.where(lane == which * CORES + flip, trace, before_ref[...])


def half_ladder(amp, before, parts, domain, here, which, flip, quarter):
    length = amp.shape[0]
    vmem = pl.BlockSpec(memory_space=pltpu.VMEM)
    square = jax.ShapeDtypeStruct((length, length), BF16)
    return pl.pallas_call(
        functools.partial(half_kernel, quarter, domain.shape[1], which, flip),
        out_shape=[square, square, jax.ShapeDtypeStruct(before.shape, F32)],
        grid_spec=pltpu.PrefetchScalarGridSpec(
            num_scalar_prefetch=2,
            grid=(1,),
            in_specs=[vmem, vmem] + [pl.BlockSpec(memory_space=pl.ANY)] * len(parts),
            out_specs=[vmem] * 3,
            scratch_shapes=[pltpu.SemaphoreType.DMA((1,))],
        ),
        compiler_params=pltpu.CompilerParams(vmem_limit_bytes=VMEM_LIMIT),
        cost_estimate=pl.CostEstimate(
            flops=2 * length**3, bytes_accessed=10 * length**2, transcendentals=0
        ),
        name="half_ladder",
    )(domain, here, amp, before, *parts)


def ladder_kernel(int_ref, half_ref, *rest):
    out_ref = rest[-1]
    acc = lax.dot_general(int_ref[...], half_ref[...], NT, preferred_element_type=F32)
    out_ref[...] = acc if len(rest) == 1 else acc + rest[0][...]


def ladder(ints, half, *before):
    length = half.shape[0]
    rows = length // 3
    block = pl.BlockSpec((rows, length), lambda i: (i, 0))
    return pl.pallas_call(
        ladder_kernel,
        out_shape=jax.ShapeDtypeStruct((length, length), F32),
        grid=(length // rows,),
        in_specs=[block, pl.BlockSpec((length, length), lambda i: (0, 0))] + [block] * len(before),
        out_specs=block,
        compiler_params=pltpu.CompilerParams(vmem_limit_bytes=VMEM_LIMIT),
        cost_estimate=pl.CostEstimate(
            flops=2 * length**3, bytes_accessed=12 * length**2, transcendentals=0
        ),
        name="ladder",
    )(ints, half, *before)


def cycle_kernel(which, ny, nx, here_ref, coupling_ref, inter_ref, *rest):
    ints, ladder_ref, outs = rest[:CORES], rest[CORES], rest[CORES + 1 :]
    y, x, core = here_ref[1], here_ref[2], here_ref[3]
    step = pl.program_id(0)
    dressing = []
    for f in range(CORES):
        total = jnp.float32(0)
        for source in range(BLOCKS * CORES):
            flip = (source % CORES) ^ core ^ f
            for w in range(CORES):
                total = total + coupling_ref[core * CORES + which, source * CORES + w] * (
                    inter_ref[source, w * CORES + flip]
                )
        dressing.append(total)
    rows = outs[0].shape[1]

    def chip_rows(xx):
        spot = pl.ds(pl.multiple_of(xx * rows, rows), rows)
        total = ladder_ref[spot, :]
        for f in range(CORES):
            total = total + dressing[f] * ints[f][spot, :].astype(F32)
        return total

    if which == 0:
        for s in range(nx):
            outs[s][0] = chip_rows(lax.rem(x + s, nx)).astype(outs[s].dtype)
    else:
        for s in range(ny):

            @pl.when(step == s)
            def _(s=s):
                for k in range(nx):
                    outs[s][k] = chip_rows(lax.rem(x + k, nx)).astype(outs[s].dtype)


def add_cycle(ladder_sum, ints, inter, coupling, here, which, ny, nx):
    length = ladder_sum.shape[0]
    rows = length // (ny * nx)
    smem = pl.BlockSpec(memory_space=pltpu.SMEM)
    block = pl.BlockSpec((nx * rows, length), lambda t, where: (lax.rem(where[1] + t, ny), 0))
    if which == 0:
        count, shape = nx, (ny, rows, length)
        out = pl.BlockSpec((1, rows, length), lambda t, where: (t, 0, 0))
    else:
        count, shape = ny, (nx, rows, length)
        out = pl.BlockSpec(shape, lambda t, where: (0, 0, 0))
    return pl.pallas_call(
        functools.partial(cycle_kernel, which, ny, nx),
        out_shape=[jax.ShapeDtypeStruct(shape, BF16 if s else F32) for s in range(count)],
        grid_spec=pltpu.PrefetchScalarGridSpec(
            num_scalar_prefetch=1,
            grid=(ny,),
            in_specs=[smem, smem] + [block] * (CORES + 1),
            out_specs=[out] * count,
        ),
        compiler_params=pltpu.CompilerParams(vmem_limit_bytes=VMEM_LIMIT),
        cost_estimate=pl.CostEstimate(
            flops=6 * length**2, bytes_accessed=12 * length**2, transcendentals=0
        ),
        name="add_cycle",
    )(here, coupling, inter, *ints, ladder_sum)


def sum_over(axis, size, parts):
    total = parts[0].astype(F32)
    for s in (1, 3, 2):
        perm = [(i, (i + s) % size) for i in range(size)]
        total = total + lax.ppermute(parts[s].astype(BF16), axis, perm).astype(F32)
    return total


def masked_amps(amps, pair_mask, first_row, dom):
    pairs, rows, length = amps.shape
    row_slot = (first_row + jnp.arange(rows, dtype=jnp.int32)) // TB
    slot_pick = row_slot[:, None] == jnp.arange(dom, dtype=jnp.int32)[None, :]
    row_tiles = jnp.sum(
        jnp.where(slot_pick[None, :, :, None], pair_mask[:, None, :, :], 0), axis=2
    ).astype(BF16)
    tiles = amps.reshape(pairs, rows, dom, TB) * row_tiles[:, :, :, None]
    return tiles.reshape(pairs, rows, length)


def by_core(core, mine, other, axis):
    return jnp.where(
        core == 0,
        jnp.concatenate([mine, other], axis=axis),
        jnp.concatenate([other, mine], axis=axis),
    )


def make_body(ny, nx):
    def gather(rows, chips):
        return lax.all_to_all(
            jnp.broadcast_to(rows[None], (chips,) + rows.shape), ("y", "x"), 0, 0, tiled=True
        ).reshape(chips * rows.shape[0], rows.shape[1])

    def body(amps, domain, pair_mask, dfint, coupling):
        pairs, own, length = amps.shape
        dom = domain.shape[1]
        quarter = dfint.shape[1] // TB
        each = pairs // CORES
        chips = ny * nx
        z, y, x, c = (lax.axis_index(name).astype(jnp.int32) for name in ("z", "y", "x", "c"))
        here = jnp.stack([z, y, x, c])
        order = [(which, f) for which in range(each) for f in range(CORES)]
        packed = {key: pack(dfint, domain, here, *key, quarter) for key in order[:1]}
        packed[order[0]], amps = lax.optimization_barrier((packed[order[0]], amps))
        for key in order[1:]:
            packed[key] = pack(dfint, domain, here, *key, quarter)
        parts = {
            (which, f): [
                part if (s, f) == (0, 0) else hop(s, f)(part)
                for s, part in zip(SHIFTS, packed[which, f])
            ]
            for which, f in order
        }
        masked = masked_amps(amps, pair_mask, ((y * nx + x) * CORES + c) * own, dom)
        mine = lax.dynamic_slice_in_dim(masked, c * each, each, axis=0)
        other = swap_cores(lax.dynamic_slice_in_dim(masked, (1 - c) * each, each, axis=0))
        both = by_core(c, mine, other, 1)
        inter = jnp.zeros((BLOCKS * CORES, TB), F32)
        sums, blocks = [None] * each, [[] for _ in range(each)]
        for which in range(each):
            amp = gather(both[which], chips)
            for f in range(CORES):
                ints, half, inter = half_ladder(
                    amp, inter, parts[which, f], domain, here, which, f, quarter
                )
                blocks[which].append(ints)
                sums[which] = ladder(ints, half, *([] if f == 0 else [sums[which]]))
        every = lax.all_to_all(inter, ("z", "c"), 0, 0, tiled=True)
        ends = []
        for which in range(each):
            (first, n1), (second, n2) = (("x", nx), ("y", ny))[:: 1 if which == 0 else -1]
            parts_out = add_cycle(
                sums[which], blocks[which], every, coupling, here, which, ny, nx
            )
            stage = sum_over(first, n1, parts_out)
            ends.append(sum_over(second, n2, [stage[s] for s in range(n2)]))
        result = jnp.stack(ends).astype(BF16)
        mine = lax.dynamic_slice_in_dim(result, c * own, own, axis=1)
        other = swap_cores(lax.dynamic_slice_in_dim(result, (1 - c) * own, own, axis=1))
        return by_core(c, mine, other, 0)

    return body


def solution(mesh):
    ny = nx = 4
    grid = Mesh(mesh.devices.reshape(BLOCKS, ny, nx, CORES), ("z", "y", "x", "c"))
    virt = ("y", "x", "c")
    return jax.shard_map(
        make_body(ny, nx),
        mesh=grid,
        in_specs=(P("z", virt, None), P(), P("z", None, None), P(virt, "z", None), P("z", None)),
        out_specs=P("z", virt, None),
        check_vma=False,
    )
```

time: 178 us -> 197 us (1.11)
  Pallas kernels: 24.6 us -> 65.5 us
  waiting for transfers between devices: 49.5 us -> 22.2 us
  blocking collectives: 0 us -> 24.8 us
  starting transfers between devices: 51.6 us -> 72.5 us
  local copies, waits for them, and re-layouts: 27.5 us -> 7.55 us
  between operations: 13.6 us -> 0.4 us
  other arithmetic: 11 us -> 1.9 us
    pallas_call x4 -> x14, Pallas kernels: 24.6 us -> 65.5 us  [the longest x4 22.4 us: half_ladder(): pl.pallas_call(functools.partial(half_kernel, quarter, domain.shape[1], w...]
    all_to_all x2, waiting for transfers between devices: 39 us -> 0.01 us  [the longest x1 0.01 us: gather(): lax.all_to_all(jnp.broadcast_to(rows[None], (chips,) + rows.shape), ('y',...]
    all_to_all x0 -> x1, blocking collectives: none -> 24.8 us  [gather(): lax.all_to_all(jnp.broadcast_to(rows[None], (chips,) + rows.shape), ('y',...]
    ppermute x14 -> x26, starting transfers between devices: 33.9 us -> 57.7 us  [the longest x14 42.7 us: body(): hop(s, f)(part)]
    unnamed x54 -> x48, local copies, waits for them, and re-layouts: 24.8 us -> 5.15 us
    ppermute x14 -> x26, waiting for transfers between devices: 8.63 us -> 20.4 us  [the longest x12 10.9 us: sum_over(): total = total + lax.ppermute(parts[s].astype(BF16), axis, perm).astype(F32)]
    convert_element_type x2 -> x0, other arithmetic: 5.69 us -> none  [body(): totals.append(total.astype(BF16).reshape(chips, 1, length // chips, length))]
    all_to_all x2, starting transfers between devices: 14.2 us -> 8.72 us  [the longest x1 5.03 us: body(): every = lax.all_to_all(inter, ('z', 'c'), 0, 0, tiled=True)]
  transfers between devices with their start and end apart: 19 -> 30, of which waited for: 8 -> 8; matrix products, arithmetic and copies ran while one was open for 0% -> 1% of each run, Pallas kernels for 10% -> 26%
where the time goes in v3:
time: 197 us; the launch traced here: 195 us
  starting transfers between devices  72.5 us (37%)
  Pallas kernels  65.5 us (33%)
  blocking collectives  24.8 us (13%)
  waiting for transfers between devices  22.2 us (11%)
  local copies, waits for them, and re-layouts  7.55 us (4%)
    ppermute x14, starting transfers between devices, body(): hop(s, f)(part)  42.7 us
    all_to_all x1, blocking collectives, gather(): lax.all_to_all(jnp.broadcast_to(rows[None], (chips,) + rows.shape), ('y',...  24.8 us
    pallas_call x4, Pallas kernels, half_ladder(): pl.pallas_call(functools.partial(half_kernel, quarter, domain.shape[1], w...  22.4 us
    pallas_call x4, Pallas kernels, ladder(): pl.pallas_call(ladder_kernel, out_shape=jax.ShapeDtypeStruct((length, len...  20.1 us
    ppermute x12, starting transfers between devices, sum_over(): total = total + lax.ppermute(parts[s].astype(BF16), axis, perm).astype(F32)  15 us
    pallas_call x4, Pallas kernels, pack(): pl.pallas_call(functools.partial(pack_kernel, quarter, dom, which, flip),...  12.6 us
    ppermute x12, waiting for transfers between devices, sum_over(): total = total + lax.ppermute(parts[s].astype(BF16), axis, perm).astype(F32)  10.9 us
    pallas_call x2, Pallas kernels, add_cycle(): pl.pallas_call(functools.partial(cycle_kernel, which, ny, nx), out_shape=...  10.4 us
  transfers between devices with their start and end apart: 30, of which 8 were waited for; matrix products, arithmetic and copies ran while one was open for 1% of the time, Pallas kernels for 26%

profile of v3, /device:TPU:1, one launch (start us, length us, event | category | flops | bytes accessed | tf_op | source)
XLA Modules:
  0.0 194.9 jit_solution(13872692468369291021)
XLA Ops:
  3.5 3.3 %pack_tiles.4 = (bf16[2,128,768]{2,1,0:T(8,128)(2,1)}, bf16[2,128,768]{2,1,0:T(8,128)(2,1)}, bf16[2,128,768]{2,1,0:T(8,128)(2,1)}, bf16[2,128,768]{2,1,0:T(8,128)(2,1)}) custom-call(s32[16,6]{1,0:T(8,128)} %copy.43.domain_ref, s32[4]{0:T(128)} %pad_add_fusion.here_ref, bf16[1,1024,4096]{2,1,0:T(8,128)(2,1)} %dfint_ref.7), custom_call_target="tpu_custom_call" | custom-call | bytes 7340032 | tf_op jit(solution)/shard_map/pack_tiles/pallas_call | solution.py:78
  9.4 24.8 %all_to_all.21 = bf16[16,48,768]{2,1,0:T(8,128)(2,1)} all-to-all(bf16[16,48,768]{2,1,0:T(8,128)(2,1)S(1)} %broadcast_in_dim.48), channel_id=1, replica_groups=mesh['z'=4,'y'=4,'x'=4,'c'=2] {'y','x'}, dimensions={0} | all-to-all | bytes 2359296 | tf_op jit(solution)/shard_map/all_to_all | solution.py:272
  35.3 3.7 %all-to-all-start = ((bf16[16,48,768]{2,1,0:T(8,128)(2,1)}), bf16[16,48,768]{2,1,0:T(8,128)(2,1)S(1)}, u32[]{:S(2)}, u32[]{:S(2)}) async-start(bf16[16,48,768]{2,1,0:T(8,128)(2,1)} %broadcast_in_dim.46), calls=%async_computation | async-start | bytes 2359296 | tf_op jit(solution)/shard_map/all_to_all | solution.py:272
  39.0 3.1 %pack_tiles.6 = (bf16[2,128,768]{2,1,0:T(8,128)(2,1)}, bf16[2,128,768]{2,1,0:T(8,128)(2,1)}, bf16[2,128,768]{2,1,0:T(8,128)(2,1)}, bf16[2,128,768]{2,1,0:T(8,128)(2,1)}) custom-call(s32[16,6]{1,0:T(8,128)} %copy.43.domain_ref, s32[4]{0:T(128)} %pad_add_fusion.here_ref, bf16[1,1024,4096]{2,1,0:T(8,128)(2,1)} %dfint_ref.7), custom_call_target="tpu_custom_call" | custom-call | bytes 7340032 | tf_op jit(solution)/shard_map/pack_tiles/pallas_call | solution.py:78
  42.1 1.7 collective-permute-start.8
  43.9 2.3 %collective-permute-start.9 = (bf16[2,128,768]{2,1,0:T(8,128)(2,1)}, bf16[2,128,768]{2,1,0:T(8,128)(2,1)S(1)}, u32[]{:S(2)}, u32[]{:S(2)}) collective-permute-start(bf16[2,128,768]{2,1,0:T(8,128)(2,1)} %get-tuple-element.62), channel_id=1, source_target_pairs={{0,96},{1,97},{32,0},{33,1},{64,32},{65,33},{96,64},{97,65},{2,98}... | collective-permute-start | bytes 1179656 | tf_op jit(solution)/shard_map/ppermute | solution.py:291
  46.2 3.1 %pack_tiles.5 = (bf16[2,128,768]{2,1,0:T(8,128)(2,1)}, bf16[2,128,768]{2,1,0:T(8,128)(2,1)}, bf16[2,128,768]{2,1,0:T(8,128)(2,1)}, bf16[2,128,768]{2,1,0:T(8,128)(2,1)}) custom-call(s32[16,6]{1,0:T(8,128)} %copy.43.domain_ref, s32[4]{0:T(128)} %pad_add_fusion.here_ref, bf16[1,1024,4096]{2,1,0:T(8,128)(2,1)} %dfint_ref.7), custom_call_target="tpu_custom_call" | custom-call | bytes 7340032 | tf_op jit(solution)/shard_map/pack_tiles/pallas_call | solution.py:78
  50.6 2.1 %collective-permute-start.5 = (bf16[2,128,768]{2,1,0:T(8,128)(2,1)}, bf16[2,128,768]{2,1,0:T(8,128)(2,1)S(1)}, u32[]{:S(2)}, u32[]{:S(2)}) collective-permute-start(bf16[2,128,768]{2,1,0:T(8,128)(2,1)} %get-tuple-element.57), channel_id=1, source_target_pairs={{0,97},{1,96},{32,1},{33,0},{64,33},{65,32},{96,65},{97,64},{2,99}... | collective-permute-start | bytes 1179656 | tf_op jit(solution)/shard_map/ppermute | solution.py:291
  54.3 2.8 %collective-permute-start.7 = (bf16[2,128,768]{2,1,0:T(8,128)(2,1)}, bf16[2,128,768]{2,1,0:T(8,128)(2,1)S(1)}, u32[]{:S(2)}, u32[]{:S(2)}) collective-permute-start(bf16[2,128,768]{2,1,0:T(8,128)(2,1)} %get-tuple-element.59), channel_id=1, source_target_pairs={{0,1},{1,0},{32,33},{33,32},{64,65},{65,64},{96,97},{97,96},{2,3},... | collective-permute-start | bytes 1179656 | tf_op jit(solution)/shard_map/ppermute | solution.py:291
  57.3 9.3 %collective-permute-done.4.rest_0_ = bf16[2,128,768]{2,1,0:T(8,128)(2,1)S(1)} collective-permute-done((bf16[2,128,768]{2,1,0:T(8,128)(2,1)}, bf16[2,128,768]{2,1,0:T(8,128)(2,1)S(1)}, u32[]{:S(2)}, u32[]{:S(2)}) %collective-permute-start.4) | collective-permute-done | bytes 393248 | tf_op jit(solution)/shard_map/ppermute | solution.py:291
  67.6 8.4 %collective-permute-start.3 = (bf16[2,128,768]{2,1,0:T(8,128)(2,1)S(1)}, bf16[2,128,768]{2,1,0:T(8,128)(2,1)S(1)}, u32[]{:S(2)}, u32[]{:S(2)}) collective-permute-start(bf16[2,128,768]{2,1,0:T(8,128)(2,1)S(1)} %copy-done.5), channel_id=1, source_target_pairs={{0,64},{1,65},{32,96},{33,97},{64,0},{65,1},{96,32},{97,33},{2,66}... | collective-permute-start | bytes 1179656 | tf_op jit(solution)/shard_map/ppermute | solution.py:291
  76.2 3.1 %pack_tiles.7 = (bf16[2,128,768]{2,1,0:T(8,128)(2,1)}, bf16[2,128,768]{2,1,0:T(8,128)(2,1)}, bf16[2,128,768]{2,1,0:T(8,128)(2,1)}, bf16[2,128,768]{2,1,0:T(8,128)(2,1)}) custom-call(s32[16,6]{1,0:T(8,128)} %copy.43.domain_ref, s32[4]{0:T(128)} %pad_add_fusion.here_ref, bf16[1,1024,4096]{2,1,0:T(8,128)(2,1)} %dfint_ref.7), custom_call_target="tpu_custom_call" | custom-call | bytes 7340032 | tf_op jit(solution)/shard_map/pack_tiles/pallas_call | solution.py:78
  80.6 4.2 %collective-permute-start.12 = (bf16[2,128,768]{2,1,0:T(8,128)(2,1)}, bf16[2,128,768]{2,1,0:T(8,128)(2,1)S(1)}, u32[]{:S(2)}, u32[]{:S(2)}) collective-permute-start(bf16[2,128,768]{2,1,0:T(8,128)(2,1)} %get-tuple-element.67), channel_id=1, source_target_pairs={{0,97},{1,96},{32,1},{33,0},{64,33},{65,32},{96,65},{97,64},{2,99}... | collective-permute-start | bytes 1179656 | tf_op jit(solution)/shard_map/ppermute | solution.py:291
  84.8 15.8 %collective-permute-start.13 = (bf16[2,128,768]{2,1,0:T(8,128)(2,1)}, bf16[2,128,768]{2,1,0:T(8,128)(2,1)S(1)}, u32[]{:S(2)}, u32[]{:S(2)}) collective-permute-start(bf16[2,128,768]{2,1,0:T(8,128)(2,1)} %get-tuple-element.68), channel_id=1, source_target_pairs={{0,65},{1,64},{32,97},{33,96},{64,1},{65,0},{96,33},{97,32},{2,67}... | collective-permute-start | bytes 1179656 | tf_op jit(solution)/shard_map/ppermute | solution.py:291
  101.3 5.6 %half_ladder.4 = (bf16[768,768]{1,0:T(8,128)(2,1)}, bf16[768,768]{1,0:T(8,128)(2,1)}, f32[8,128]{1,0:T(8,128)}) custom-call(s32[16,6]{1,0:T(8,128)} %copy.43.domain_ref, s32[4]{0:T(128)} %pad_add_fusion.here_ref, bf16[768,768]{1,0:T(8,128)(2,1)} %bitcast.56, f32[8,128]{1,0:T(8,128)} %broadcast_in_dim.49.before_ref, bf16[2,128,768]{2,1,0:T(8,128)(2,1)} %copy-done.19, ...), custom_call_target="tpu_custom_call" | custom-call | flops 905969664 | bytes 5898240 | tf_op jit(solution)/shard_map/half_ladder/pallas_call | solution.py:138
  107.0 5.5 %half_ladder.5 = (bf16[768,768]{1,0:T(8,128)(2,1)}, bf16[768,768]{1,0:T(8,128)(2,1)}, f32[8,128]{1,0:T(8,128)}) custom-call(s32[16,6]{1,0:T(8,128)} %copy.43.domain_ref, s32[4]{0:T(128)} %pad_add_fusion.here_ref, bf16[768,768]{1,0:T(8,128)(2,1)} %bitcast.57, f32[8,128]{1,0:T(8,128)} %get-tuple-element.55.before_ref, bf16[2,128,768]{2,1,0:T(8,128)(2,1)} %copy-done.11, ...), custom_call_target="tpu_custom_call" | custom-call | flops 905969664 | bytes 5898240 | tf_op jit(solution)/shard_map/half_ladder/pallas_call | solution.py:138
  113.7 5.6 %half_ladder.6 = (bf16[768,768]{1,0:T(8,128)(2,1)}, bf16[768,768]{1,0:T(8,128)(2,1)}, f32[8,128]{1,0:T(8,128)}) custom-call(s32[16,6]{1,0:T(8,128)} %copy.43.domain_ref, s32[4]{0:T(128)} %pad_add_fusion.here_ref, bf16[768,768]{1,0:T(8,128)(2,1)} %bitcast.54, f32[8,128]{1,0:T(8,128)} %get-tuple-element.60.before_ref, bf16[2,128,768]{2,1,0:T(8,128)(2,1)} %copy-done.7, ...), custom_call_target="tpu_custom_call" | custom-call | flops 905969664 | bytes 5898240 | tf_op jit(solution)/shard_map/half_ladder/pallas_call | solution.py:138
  120.4 5.6 %half_ladder.7 = (bf16[768,768]{1,0:T(8,128)(2,1)}, bf16[768,768]{1,0:T(8,128)(2,1)}, f32[8,128]{1,0:T(8,128)}) custom-call(s32[16,6]{1,0:T(8,128)} %copy.43.domain_ref, s32[4]{0:T(128)} %pad_add_fusion.here_ref, bf16[768,768]{1,0:T(8,128)(2,1)} %bitcast.55, f32[8,128]{1,0:T(8,128)} %get-tuple-element.65.before_ref, bf16[2,128,768]{2,1,0:T(8,128)(2,1)} %copy-done.15, ...), custom_call_target="tpu_custom_call" | custom-call | flops 905969664 | bytes 5898240 | tf_op jit(solution)/shard_map/half_ladder/pallas_call | solution.py:138
  126.0 5.0 %all-to-all-start.2 = ((f32[8,1,128]{2,1,0:T(1,128)}), f32[8,1,128]{2,1,0:T(1,128)S(1)}, u32[]{:S(2)}, u32[]{:S(2)}) async-start(f32[8,1,128]{2,1,0:T(1,128)} %bitcast.60), calls=%async_computation.2 | async-start | bytes 8192 | tf_op jit(solution)/shard_map/all_to_all | solution.py:310
  131.1 4.6 %ladder.6.rest_0_ = f32[768,768]{1,0:T(8,128)} custom-call(bf16[768,768]{1,0:T(8,128)(2,1)} %get-tuple-element.79.int_ref.rest_0_, bf16[768,768]{1,0:T(8,128)(2,1)} %get-tuple-element.82.half_ref), custom_call_target="tpu_custom_call" | custom-call | flops 905969664 | bytes 7077888 | tf_op jit(solution)/shard_map/ladder/pallas_call | solution.py:166
  135.7 5.5 %ladder.7.rest_2_ = f32[768,768]{1,0:T(8,128)} custom-call(bf16[768,768]{1,0:T(8,128)(2,1)} %get-tuple-element.80.int_ref.rest_1_, bf16[768,768]{1,0:T(8,128)(2,1)} %get-tuple-element.81.half_ref, f32[768,768]{1,0:T(8,128)} %ladder.6.rest_0_), custom_call_target="tpu_custom_call" | custom-call | flops 905969664 | bytes 7077888 | tf_op jit(solution)/shard_map/ladder/pallas_call | solution.py:166
  141.7 5.3 %add_cycle.3 = (f32[4,48,768]{2,1,0:T(8,128)}, bf16[4,48,768]{2,1,0:T(8,128)(2,1)}, bf16[4,48,768]{2,1,0:T(8,128)(2,1)}, bf16[4,48,768]{2,1,0:T(8,128)(2,1)}) custom-call(s32[4]{0:T(128)} %pad_add_fusion.here_ref, f32[4,16]{1,0:T(4,128)} %coupling_ref.3, f32[8,128]{1,0:T(8,128)} %bitcast.58, bf16[768,768]{1,0:T(8,128)(2,1)} %get-tuple-element.79.int_ref.rest_0_, ...), custom_call_target="tpu_custom_call" | custom-call | flops 3538944 | bytes 7077888 | tf_op jit(solution)/shard_map/add_cycle/pallas_call | solution.py:226
  148.0 1.7 collective-permute-start.22
  151.0 4.6 %ladder.4.rest_0_ = f32[768,768]{1,0:T(8,128)} custom-call(bf16[768,768]{1,0:T(8,128)(2,1)} %get-tuple-element.71.int_ref.rest_0_, bf16[768,768]{1,0:T(8,128)(2,1)} %get-tuple-element.74.half_ref), custom_call_target="tpu_custom_call" | custom-call | flops 905969664 | bytes 7077888 | tf_op jit(solution)/shard_map/ladder/pallas_call | solution.py:166
  155.6 5.5 %ladder.5.rest_2_ = f32[768,768]{1,0:T(8,128)} custom-call(bf16[768,768]{1,0:T(8,128)(2,1)} %get-tuple-element.72.int_ref.rest_1_, bf16[768,768]{1,0:T(8,128)(2,1)} %get-tuple-element.73.half_ref, f32[768,768]{1,0:T(8,128)} %ladder.4.rest_0_), custom_call_target="tpu_custom_call" | custom-call | flops 905969664 | bytes 7077888 | tf_op jit(solution)/shard_map/ladder/pallas_call | solution.py:166
  161.0 5.2 %add_cycle.2 = (f32[4,48,768]{2,1,0:T(8,128)}, bf16[4,48,768]{2,1,0:T(8,128)(2,1)}, bf16[4,48,768]{2,1,0:T(8,128)(2,1)}, bf16[4,48,768]{2,1,0:T(8,128)(2,1)}) custom-call(s32[4]{0:T(128)} %pad_add_fusion.here_ref, f32[4,16]{1,0:T(4,128)} %coupling_ref.3, f32[8,128]{1,0:T(8,128)} %bitcast.59, bf16[768,768]{1,0:T(8,128)(2,1)} %get-tuple-element.71.int_ref.rest_0_, ...), custom_call_target="tpu_custom_call" | custom-call | flops 3538944 | bytes 7077888 | tf_op jit(solution)/shard_map/add_cycle/pallas_call | solution.py:226
  170.9 1.8 collective-permute-start.26
  172.7 2.6 %collective-permute-done.15 = bf16[4,48,768]{2,1,0:T(8,128)(2,1)S(1)} collective-permute-done((bf16[4,48,768]{2,1,0:T(8,128)(2,1)}, bf16[4,48,768]{2,1,0:T(8,128)(2,1)S(1)}, u32[]{:S(2)}, u32[]{:S(2)}) %collective-permute-start.15) | collective-permute-done | bytes 294944 | tf_op jit(solution)/shard_map/ppermute | solution.py:247
  176.5 6.1 %collective-permute-done.17 = bf16[4,48,768]{2,1,0:T(8,128)(2,1)S(1)} collective-permute-done((bf16[4,48,768]{2,1,0:T(8,128)(2,1)}, bf16[4,48,768]{2,1,0:T(8,128)(2,1)S(1)}, u32[]{:S(2)}, u32[]{:S(2)}) %collective-permute-start.17) | collective-permute-done | bytes 294944 | tf_op jit(solution)/shard_map/ppermute | solution.py:247
  183.2 1.7 collective-permute-start.20
  186.4 1.6 collective-permute-done.18
  188.7 4.6 %collective-permute-start.27 = (bf16[2,24,768]{2,1,0:T(8,128)(2,1)S(1)}, bf16[2,24,768]{2,1,0:T(8,128)(2,1)S(1)}, u32[]{:S(2)}, u32[]{:S(2)}) collective-permute-start(bf16[2,24,768]{2,1,0:T(8,128)(2,1)S(1)} %get-tuple-element.98), channel_id=1, source_target_pairs={{0,1},{1,0},{2,3},{3,2},{4,5},{5,4},{6,7},{7,6},{8,9},{9,8},{10,11... | collective-permute-start | bytes 221192 | tf_op jit(solution)/shard_map/ppermute | solution.py:32
  (114 shorter events, 28.7 us)
Async XLA Ops:
  6.8 2.4 %collective-permute-start = (bf16[2,24,768]{2,1,0:T(8,128)(2,1)S(1)}, bf16[2,24,768]{2,1,0:T(8,128)(2,1)S(1)}, u32[]{:S(2)}, u32[]{:S(2)}) collective-permute-start(bf16[2,24,768]{2,1,0:T(8,128)(2,1)S(1)} %get-tuple-element.102), channel_id=1, source_target_pairs={{0,1},{1,0},{2,3},{3,2},{4,5},{5,4},{6,7},{7,6},{8,9},{9,8},{10,11... | collective-permute-start | bytes 221192 | tf_op jit(solution)/shard_map/ppermute | solution.py:32
  35.3 77.2 %all-to-all-start = ((bf16[16,48,768]{2,1,0:T(8,128)(2,1)}), bf16[16,48,768]{2,1,0:T(8,128)(2,1)S(1)}, u32[]{:S(2)}, u32[]{:S(2)}) async-start(bf16[16,48,768]{2,1,0:T(8,128)(2,1)} %broadcast_in_dim.46), calls=%async_computation | async-start | bytes 2359296 | tf_op jit(solution)/shard_map/all_to_all | solution.py:272
  42.1 12.1 %collective-permute-start.8 = (bf16[2,128,768]{2,1,0:T(8,128)(2,1)}, bf16[2,128,768]{2,1,0:T(8,128)(2,1)S(1)}, u32[]{:S(2)}, u32[]{:S(2)}) collective-permute-start(bf16[2,128,768]{2,1,0:T(8,128)(2,1)} %get-tuple-element.61), channel_id=1, source_target_pairs={{0,32},{1,33},{32,64},{33,65},{64,96},{65,97},{96,0},{97,1},{2,34}... | collective-permute-start | bytes 1179656 | tf_op jit(solution)/shard_map/ppermute | solution.py:291
  43.9 32.2 %copy-start.10 = (bf16[2,128,768]{2,1,0:T(8,128)(2,1)S(1)}, bf16[2,128,768]{2,1,0:T(8,128)(2,1)}, u32[]{:S(2)}) copy-start(bf16[2,128,768]{2,1,0:T(8,128)(2,1)} %get-tuple-element.63) | copy-start | bytes 1179652
  43.9 13.3 %collective-permute-start.9 = (bf16[2,128,768]{2,1,0:T(8,128)(2,1)}, bf16[2,128,768]{2,1,0:T(8,128)(2,1)S(1)}, u32[]{:S(2)}, u32[]{:S(2)}) collective-permute-start(bf16[2,128,768]{2,1,0:T(8,128)(2,1)} %get-tuple-element.62), channel_id=1, source_target_pairs={{0,96},{1,97},{32,0},{33,1},{64,32},{65,33},{96,64},{97,65},{2,98}... | collective-permute-start | bytes 1179656 | tf_op jit(solution)/shard_map/ppermute | solution.py:291
  49.3 17.3 %collective-permute-start.4 = (bf16[2,128,768]{2,1,0:T(8,128)(2,1)}, bf16[2,128,768]{2,1,0:T(8,128)(2,1)S(1)}, u32[]{:S(2)}, u32[]{:S(2)}) collective-permute-start(bf16[2,128,768]{2,1,0:T(8,128)(2,1)} %get-tuple-element.56), channel_id=1, source_target_pairs={{0,33},{1,32},{32,65},{33,64},{64,97},{65,96},{96,1},{97,0},{2,35}... | collective-permute-start | bytes 1179656 | tf_op jit(solution)/shard_map/ppermute | solution.py:291
  50.6 17.0 %collective-permute-start.5 = (bf16[2,128,768]{2,1,0:T(8,128)(2,1)}, bf16[2,128,768]{2,1,0:T(8,128)(2,1)S(1)}, u32[]{:S(2)}, u32[]{:S(2)}) collective-permute-start(bf16[2,128,768]{2,1,0:T(8,128)(2,1)} %get-tuple-element.57), channel_id=1, source_target_pairs={{0,97},{1,96},{32,1},{33,0},{64,33},{65,32},{96,65},{97,64},{2,99}... | collective-permute-start | bytes 1179656 | tf_op jit(solution)/shard_map/ppermute | solution.py:291
  52.7 23.3 %collective-permute-start.6 = (bf16[2,128,768]{2,1,0:T(8,128)(2,1)}, bf16[2,128,768]{2,1,0:T(8,128)(2,1)S(1)}, u32[]{:S(2)}, u32[]{:S(2)}) collective-permute-start(bf16[2,128,768]{2,1,0:T(8,128)(2,1)} %get-tuple-element.58), channel_id=1, source_target_pairs={{0,65},{1,64},{32,97},{33,96},{64,1},{65,0},{96,33},{97,32},{2,67}... | collective-permute-start | bytes 1179656 | tf_op jit(solution)/shard_map/ppermute | solution.py:291
  54.3 25.0 %collective-permute-start.7 = (bf16[2,128,768]{2,1,0:T(8,128)(2,1)}, bf16[2,128,768]{2,1,0:T(8,128)(2,1)S(1)}, u32[]{:S(2)}, u32[]{:S(2)}) collective-permute-start(bf16[2,128,768]{2,1,0:T(8,128)(2,1)} %get-tuple-element.59), channel_id=1, source_target_pairs={{0,1},{1,0},{32,33},{33,32},{64,65},{65,64},{96,97},{97,96},{2,3},... | collective-permute-start | bytes 1179656 | tf_op jit(solution)/shard_map/ppermute | solution.py:291
  57.1 23.5 %collective-permute-start.1 = (bf16[2,128,768]{2,1,0:T(8,128)(2,1)S(1)}, bf16[2,128,768]{2,1,0:T(8,128)(2,1)S(1)}, u32[]{:S(2)}, u32[]{:S(2)}) collective-permute-start(bf16[2,128,768]{2,1,0:T(8,128)(2,1)S(1)} %copy-done.8), channel_id=1, source_target_pairs={{0,32},{1,33},{32,64},{33,65},{64,96},{65,97},{96,0},{97,1},{2,34}... | collective-permute-start | bytes 1179656 | tf_op jit(solution)/shard_map/ppermute | solution.py:291
  66.6 18.2 %collective-permute-start.2 = (bf16[2,128,768]{2,1,0:T(8,128)(2,1)S(1)}, bf16[2,128,768]{2,1,0:T(8,128)(2,1)S(1)}, u32[]{:S(2)}, u32[]{:S(2)}) collective-permute-start(bf16[2,128,768]{2,1,0:T(8,128)(2,1)S(1)} %copy-done.6), channel_id=1, source_target_pairs={{0,96},{1,97},{32,0},{33,1},{64,32},{65,33},{96,64},{97,65},{2,98}... | collective-permute-start | bytes 1179656 | tf_op jit(solution)/shard_map/ppermute | solution.py:291
  67.6 32.9 %collective-permute-start.3 = (bf16[2,128,768]{2,1,0:T(8,128)(2,1)S(1)}, bf16[2,128,768]{2,1,0:T(8,128)(2,1)S(1)}, u32[]{:S(2)}, u32[]{:S(2)}) collective-permute-start(bf16[2,128,768]{2,1,0:T(8,128)(2,1)S(1)} %copy-done.5), channel_id=1, source_target_pairs={{0,64},{1,65},{32,96},{33,97},{64,0},{65,1},{96,32},{97,33},{2,66}... | collective-permute-start | bytes 1179656 | tf_op jit(solution)/shard_map/ppermute | solution.py:291
  76.0 36.5 %collective-permute-start.10 = (bf16[2,128,768]{2,1,0:T(8,128)(2,1)S(1)}, bf16[2,128,768]{2,1,0:T(8,128)(2,1)S(1)}, u32[]{:S(2)}, u32[]{:S(2)}) collective-permute-start(bf16[2,128,768]{2,1,0:T(8,128)(2,1)S(1)} %copy-done.10), channel_id=1, source_target_pairs={{0,64},{1,65},{32,96},{33,97},{64,0},{65,1},{96,32},{97,33},{2,66}... | collective-permute-start | bytes 1179656 | tf_op jit(solution)/shard_map/ppermute | solution.py:291
  79.3 27.6 %copy-start.14 = (bf16[2,128,768]{2,1,0:T(8,128)(2,1)}, bf16[2,128,768]{2,1,0:T(8,128)(2,1)S(1)}, u32[]{:S(2)}) copy-start(bf16[2,128,768]{2,1,0:T(8,128)(2,1)S(1)} %collective-permute-done.7.rest_3_) | copy-start | bytes 1179652
  79.3 39.9 %collective-permute-start.11 = (bf16[2,128,768]{2,1,0:T(8,128)(2,1)}, bf16[2,128,768]{2,1,0:T(8,128)(2,1)S(1)}, u32[]{:S(2)}, u32[]{:S(2)}) collective-permute-start(bf16[2,128,768]{2,1,0:T(8,128)(2,1)} %get-tuple-element.66), channel_id=1, source_target_pairs={{0,33},{1,32},{32,65},{33,64},{64,97},{65,96},{96,1},{97,0},{2,35}... | collective-permute-start | bytes 1179656 | tf_op jit(solution)/shard_map/ppermute | solution.py:291
  80.6 38.7 %collective-permute-start.12 = (bf16[2,128,768]{2,1,0:T(8,128)(2,1)}, bf16[2,128,768]{2,1,0:T(8,128)(2,1)S(1)}, u32[]{:S(2)}, u32[]{:S(2)}) collective-permute-start(bf16[2,128,768]{2,1,0:T(8,128)(2,1)} %get-tuple-element.67), channel_id=1, source_target_pairs={{0,97},{1,96},{32,1},{33,0},{64,33},{65,32},{96,65},{97,64},{2,99}... | collective-permute-start | bytes 1179656 | tf_op jit(solution)/shard_map/ppermute | solution.py:291
  84.8 34.5 %collective-permute-start.13 = (bf16[2,128,768]{2,1,0:T(8,128)(2,1)}, bf16[2,128,768]{2,1,0:T(8,128)(2,1)S(1)}, u32[]{:S(2)}, u32[]{:S(2)}) collective-permute-start(bf16[2,128,768]{2,1,0:T(8,128)(2,1)} %get-tuple-element.68), channel_id=1, source_target_pairs={{0,65},{1,64},{32,97},{33,96},{64,1},{65,0},{96,33},{97,32},{2,67}... | collective-permute-start | bytes 1179656 | tf_op jit(solution)/shard_map/ppermute | solution.py:291
  100.6 18.8 %collective-permute-start.14 = (bf16[2,128,768]{2,1,0:T(8,128)(2,1)}, bf16[2,128,768]{2,1,0:T(8,128)(2,1)S(1)}, u32[]{:S(2)}, u32[]{:S(2)}) collective-permute-start(bf16[2,128,768]{2,1,0:T(8,128)(2,1)} %get-tuple-element.69), channel_id=1, source_target_pairs={{0,1},{1,0},{32,33},{33,32},{64,65},{65,64},{96,97},{97,96},{2,3},... | collective-permute-start | bytes 1179656 | tf_op jit(solution)/shard_map/ppermute | solution.py:291
  126.0 15.1 %all-to-all-start.2 = ((f32[8,1,128]{2,1,0:T(1,128)}), f32[8,1,128]{2,1,0:T(1,128)S(1)}, u32[]{:S(2)}, u32[]{:S(2)}) async-start(f32[8,1,128]{2,1,0:T(1,128)} %bitcast.60), calls=%async_computation.2 | async-start | bytes 8192 | tf_op jit(solution)/shard_map/all_to_all | solution.py:310
  147.0 21.9 %collective-permute-start.21 = (bf16[4,48,768]{2,1,0:T(8,128)(2,1)}, bf16[4,48,768]{2,1,0:T(8,128)(2,1)S(1)}, u32[]{:S(2)}, u32[]{:S(2)}) collective-permute-start(bf16[4,48,768]{2,1,0:T(8,128)(2,1)} %get-tuple-element.84), channel_id=1, source_target_pairs={{0,8},{8,16},{16,24},{24,0},{1,9},{9,17},{17,25},{25,1},{2,10},{10... | collective-permute-start | bytes 884744 | tf_op jit(solution)/shard_map/ppermute | solution.py:247
  148.0 22.4 %collective-permute-start.22 = (bf16[4,48,768]{2,1,0:T(8,128)(2,1)}, bf16[4,48,768]{2,1,0:T(8,128)(2,1)S(1)}, u32[]{:S(2)}, u32[]{:S(2)}) collective-permute-start(bf16[4,48,768]{2,1,0:T(8,128)(2,1)} %get-tuple-element.85), channel_id=1, source_target_pairs={{0,24},{8,0},{16,8},{24,16},{1,25},{9,1},{17,9},{25,17},{2,26},{10... | collective-permute-start | bytes 884744 | tf_op jit(solution)/shard_map/ppermute | solution.py:247
  149.7 20.7 %collective-permute-start.23 = (bf16[4,48,768]{2,1,0:T(8,128)(2,1)}, bf16[4,48,768]{2,1,0:T(8,128)(2,1)S(1)}, u32[]{:S(2)}, u32[]{:S(2)}) collective-permute-start(bf16[4,48,768]{2,1,0:T(8,128)(2,1)} %get-tuple-element.86), channel_id=1, source_target_pairs={{0,16},{8,24},{16,0},{24,8},{1,17},{9,25},{17,1},{25,9},{2,18},{10... | collective-permute-start | bytes 884744 | tf_op jit(solution)/shard_map/ppermute | solution.py:247
  166.2 9.1 %collective-permute-start.15 = (bf16[4,48,768]{2,1,0:T(8,128)(2,1)}, bf16[4,48,768]{2,1,0:T(8,128)(2,1)S(1)}, u32[]{:S(2)}, u32[]{:S(2)}) collective-permute-start(bf16[4,48,768]{2,1,0:T(8,128)(2,1)} %get-tuple-element.76), channel_id=1, source_target_pairs={{0,2},{2,4},{4,6},{6,0},{1,3},{3,5},{5,7},{7,1},{8,10},{10,12},{12... | collective-permute-start | bytes 884744 | tf_op jit(solution)/shard_map/ppermute | solution.py:247
  167.4 9.1 %collective-permute-start.16 = (bf16[4,48,768]{2,1,0:T(8,128)(2,1)}, bf16[4,48,768]{2,1,0:T(8,128)(2,1)S(1)}, u32[]{:S(2)}, u32[]{:S(2)}) collective-permute-start(bf16[4,48,768]{2,1,0:T(8,128)(2,1)} %get-tuple-element.77), channel_id=1, source_target_pairs={{0,6},{2,0},{4,2},{6,4},{1,7},{3,1},{5,3},{7,5},{8,14},{10,8},{12,... | collective-permute-start | bytes 884744 | tf_op jit(solution)/shard_map/ppermute | solution.py:247
  168.9 13.7 %collective-permute-start.17 = (bf16[4,48,768]{2,1,0:T(8,128)(2,1)}, bf16[4,48,768]{2,1,0:T(8,128)(2,1)S(1)}, u32[]{:S(2)}, u32[]{:S(2)}) collective-permute-start(bf16[4,48,768]{2,1,0:T(8,128)(2,1)} %get-tuple-element.78), channel_id=1, source_target_pairs={{0,4},{2,6},{4,0},{6,2},{1,5},{3,7},{5,1},{7,3},{8,12},{10,14},{12... | collective-permute-start | bytes 884744 | tf_op jit(solution)/shard_map/ppermute | solution.py:247
  170.6 14.3 %collective-permute-start.24 = (bf16[48,768]{1,0:T(8,128)(2,1)S(1)}, bf16[48,768]{1,0:T(8,128)(2,1)S(1)}, u32[]{:S(2)}, u32[]{:S(2)}) collective-permute-start(bf16[48,768]{1,0:T(8,128)(2,1)S(1)} %get-tuple-element.91), channel_id=1, source_target_pairs={{0,2},{2,4},{4,6},{6,0},{1,3},{3,5},{5,7},{7,1},{8,10},{10,12},{12... | collective-permute-start | bytes 221192 | tf_op jit(solution)/shard_map/ppermute | solution.py:247
  170.9 15.4 %collective-permute-start.26 = (bf16[48,768]{1,0:T(8,128)(2,1)S(1)}, bf16[48,768]{1,0:T(8,128)(2,1)S(1)}, u32[]{:S(2)}, u32[]{:S(2)}) collective-permute-start(bf16[48,768]{1,0:T(8,128)(2,1)S(1)} %get-tuple-element.92), channel_id=1, source_target_pairs={{0,4},{2,6},{4,0},{6,2},{1,5},{3,7},{5,1},{7,3},{8,12},{10,14},{12... | collective-permute-start | bytes 221192 | tf_op jit(solution)/shard_map/ppermute | solution.py:247
  175.3 11.0 %collective-permute-start.25 = (bf16[48,768]{1,0:T(8,128)(2,1)S(1)}, bf16[48,768]{1,0:T(8,128)(2,1)S(1)}, u32[]{:S(2)}, u32[]{:S(2)}) collective-permute-start(bf16[48,768]{1,0:T(8,128)(2,1)S(1)} %get-tuple-element.93), channel_id=1, source_target_pairs={{0,6},{2,0},{4,2},{6,4},{1,7},{3,1},{5,3},{7,5},{8,14},{10,8},{12,... | collective-permute-start | bytes 221192 | tf_op jit(solution)/shard_map/ppermute | solution.py:247
  182.8 5.3 %collective-permute-start.18 = (bf16[48,768]{1,0:T(8,128)(2,1)S(1)}, bf16[48,768]{1,0:T(8,128)(2,1)S(1)}, u32[]{:S(2)}, u32[]{:S(2)}) collective-permute-start(bf16[48,768]{1,0:T(8,128)(2,1)S(1)} %get-tuple-element.94), channel_id=1, source_target_pairs={{0,8},{8,16},{16,24},{24,0},{1,9},{9,17},{17,25},{25,1},{2,10},{10... | collective-permute-start | bytes 221192 | tf_op jit(solution)/shard_map/ppermute | solution.py:247
  183.2 4.9 %collective-permute-start.20 = (bf16[48,768]{1,0:T(8,128)(2,1)S(1)}, bf16[48,768]{1,0:T(8,128)(2,1)S(1)}, u32[]{:S(2)}, u32[]{:S(2)}) collective-permute-start(bf16[48,768]{1,0:T(8,128)(2,1)S(1)} %get-tuple-element.95), channel_id=1, source_target_pairs={{0,16},{8,24},{16,0},{24,8},{1,17},{9,25},{17,1},{25,9},{2,18},{10... | collective-permute-start | bytes 221192 | tf_op jit(solution)/shard_map/ppermute | solution.py:247
  184.9 3.7 %collective-permute-start.19 = (bf16[48,768]{1,0:T(8,128)(2,1)S(1)}, bf16[48,768]{1,0:T(8,128)(2,1)S(1)}, u32[]{:S(2)}, u32[]{:S(2)}) collective-permute-start(bf16[48,768]{1,0:T(8,128)(2,1)S(1)} %get-tuple-element.96), channel_id=1, source_target_pairs={{0,24},{8,0},{16,8},{24,16},{1,25},{9,1},{17,9},{25,17},{2,26},{10... | collective-permute-start | bytes 221192 | tf_op jit(solution)/shard_map/ppermute | solution.py:247
  188.7 5.5 %collective-permute-start.27 = (bf16[2,24,768]{2,1,0:T(8,128)(2,1)S(1)}, bf16[2,24,768]{2,1,0:T(8,128)(2,1)S(1)}, u32[]{:S(2)}, u32[]{:S(2)}) collective-permute-start(bf16[2,24,768]{2,1,0:T(8,128)(2,1)S(1)} %get-tuple-element.98), channel_id=1, source_target_pairs={{0,1},{1,0},{2,3},{3,2},{4,5},{5,4},{6,7},{7,6},{8,9},{9,8},{10,11... | collective-permute-start | bytes 221192 | tf_op jit(solution)/shard_map/ppermute | solution.py:32
  (21 other events, 203.4 us)

commit v4 on v3

--- a/solution.py
+++ b/solution.py
@@ -95,11 +95,14 @@
     )(domain, here, dfint)
 
 
-def half_kernel(quarter, dom, which, flip, domain_ref, here_ref, amp_ref, before_ref, *rest):
+def work_kernel(quarter, dom, which, flips, finish, domain_ref, here_ref, amp_ref, before_ref, *rest):
     count = len(SHIFTS)
-    parts, (int_ref, half_ref, inter_ref, sem) = rest[:count], rest[count:]
+    parts, rest = rest[: count * len(flips)], rest[count * len(flips) :]
+    int_out, out_ref, inter_ref, amp, ints, half, ladder, in_sem, out_sem = rest
     here, core = here_ref[0], here_ref[3]
     pair = (here * CORES + core) * CORES + which
+    load_amp = pltpu.make_async_copy(amp_ref, amp, in_sem.at[len(flips)])
+    load_amp.start()
     for s in range(dom):
         owner = domain_ref[pair, s] // quarter
         rank = jnp.int32(0)
@@ -110,94 +113,140 @@
 
             @pl.when(shift == flow_shift)
             def _(n=n, rank=rank, s=s):
-                pltpu.make_async_copy(
-                    parts[n].at[rank], int_ref.at[pl.ds(s * TB, TB), :], sem.at[0]
-                ).start()
-
+                for f in range(len(flips)):
+                    pltpu.make_async_copy(
+                        parts[f * count + n].at[rank],
+                        ints.at[f, pl.ds(s * TB, TB), :],
+                        in_sem.at[f],
+                    ).start()
+
+    load_amp.wait()
     rows = 2 * TB
-    pltpu.make_async_copy(int_ref, int_ref, sem.at[0]).wait()
-    total = jnp.zeros((rows, rows), F32)
-    for r in range(0, dom * TB, rows):
-        acc = lax.dot_general(
-            int_ref[pl.ds(r, rows), :], amp_ref[...], NT, preferred_element_type=F32
-        )
-        half_ref[pl.ds(r, rows), :] = acc.astype(BF16)
-        total = total + acc[:, r : r + rows]
     diagonal = lax.broadcasted_iota(jnp.int32, (rows, rows), 0) == lax.broadcasted_iota(
         jnp.int32, (rows, rows), 1
     )
-    trace = jnp.sum(jnp.where(diagonal, total, 0.0))
     lane = lax.broadcasted_iota(jnp.int32, inter_ref.shape, 1)
-    inter_ref[...] = jnp.where(lane == which * CORES + flip, trace, before_ref[...])
-
-
-def half_ladder(amp, before, parts, domain, here, which, flip, quarter):
+    inter = before_ref[...]
+    for f, flip in enumerate(flips):
+        pltpu.make_async_copy(ints.at[f], ints.at[f], in_sem.at[f]).wait()
+        pltpu.make_async_copy(ints.at[f], int_out.at[f], out_sem.at[f]).start()
+        total = jnp.zeros((rows, rows), F32)
+        for r in range(0, dom * TB, rows):
+            spot = pl.ds(r, rows)
+            acc = lax.dot_general(ints[f, spot, :], amp[...], NT, preferred_element_type=F32)
+            half[f, spot, :] = acc.astype(BF16)
+            total = total + acc[:, r : r + rows]
+            if not finish:
+                pltpu.make_async_copy(
+                    half.at[f, spot, :], out_ref.at[f, spot, :], out_sem.at[len(flips)]
+                ).start()
+        trace = jnp.sum(jnp.where(diagonal, total, 0.0))
+        inter = jnp.where(lane == which * CORES + flip, trace, inter)
+    inter_ref[...] = inter
+    if finish:
+        for r in range(0, dom * TB, rows):
+            spot = pl.ds(r, rows)
+            acc = None
+            for f in range(len(flips)):
+                term = lax.dot_general(ints[f, spot, :], half[f], NT, preferred_element_type=F32)
+                acc = term if acc is None else acc + term
+            ladder[spot, :] = acc
+            pltpu.make_async_copy(
+                ladder.at[spot, :], out_ref.at[spot, :], out_sem.at[len(flips)]
+            ).start()
+    for f in range(len(flips)):
+        pltpu.make_async_copy(ints.at[f], int_out.at[f], out_sem.at[f]).wait()
+    pltpu.make_async_copy(ladder if finish else half, out_ref, out_sem.at[len(flips)]).wait()
+
+
+def work(amp, before, parts, domain, here, which, flips, finish, quarter):
     length = amp.shape[0]
-    vmem = pl.BlockSpec(memory_space=pltpu.VMEM)
-    square = jax.ShapeDtypeStruct((length, length), BF16)
+    count = len(flips)
+    small = pl.BlockSpec(memory_space=pltpu.VMEM)
+    anywhere = pl.BlockSpec(memory_space=pl.ANY)
+    squares = (count, length, length)
     return pl.pallas_call(
-        functools.partial(half_kernel, quarter, domain.shape[1], which, flip),
-        out_shape=[square, square, jax.ShapeDtypeStruct(before.shape, F32)],
+        functools.partial(work_kernel, quarter, domain.shape[1], which, flips, finish),
+        out_shape=[
+            jax.ShapeDtypeStruct(squares, BF16),
+            jax.ShapeDtypeStruct((length, length), F32)
+            if finish
+            else jax.ShapeDtypeStruct(squares, BF16),
+            jax.ShapeDtypeStruct(before.shape, F32),
+        ],
         grid_spec=pltpu.PrefetchScalarGridSpec(
             num_scalar_prefetch=2,
             grid=(1,),
-            in_specs=[vmem, vmem] + [pl.BlockSpec(memory_space=pl.ANY)] * len(parts),
-            out_specs=[vmem] * 3,
-            scratch_shapes=[pltpu.SemaphoreType.DMA((1,))],
+            in_specs=[anywhere, small] + [anywhere] * len(parts),
+            out_specs=[anywhere, anywhere, small],
+            scratch_shapes=[
+                pltpu.VMEM((length, length), BF16),
+                pltpu.VMEM(squares, BF16),
+                pltpu.VMEM(squares, BF16),
+                pltpu.VMEM((length, length), F32),
+                pltpu.SemaphoreType.DMA((count + 1,)),
+                pltpu.SemaphoreType.DMA((count + 1,)),
+            ],
         ),
         compiler_params=pltpu.CompilerParams(vmem_limit_bytes=VMEM_LIMIT),
         cost_estimate=pl.CostEstimate(
-            flops=2 * length**3, bytes_accessed=10 * length**2, transcendentals=0
-        ),
-        name="half_ladder",
+            flops=(4 if finish else 2) * count * length**3,
+            bytes_accessed=10 * count * length**2,
+            transcendentals=0,
+        ),
+        name="half_and_ladder" if finish else "half_ladder",
     )(domain, here, amp, before, *parts)
 
 
 def ladder_kernel(int_ref, half_ref, *rest):
     out_ref = rest[-1]
-    acc = lax.dot_general(int_ref[...], half_ref[...], NT, preferred_element_type=F32)
-    out_ref[...] = acc if len(rest) == 1 else acc + rest[0][...]
-
-
-def ladder(ints, half, *before):
-    length = half.shape[0]
+    acc = lax.dot_general(int_ref[0], half_ref[0], NT, preferred_element_type=F32)
+    out_ref[...] = acc + rest[0][...]
+
+
+def ladder(ints, half, before):
+    length = before.shape[0]
     rows = length // 3
     block = pl.BlockSpec((rows, length), lambda i: (i, 0))
+    int_block = pl.BlockSpec((1, rows, length), lambda i: (0, i, 0))
     return pl.pallas_call(
         ladder_kernel,
         out_shape=jax.ShapeDtypeStruct((length, length), F32),
         grid=(length // rows,),
-        in_specs=[block, pl.BlockSpec((length, length), lambda i: (0, 0))] + [block] * len(before),
+        in_specs=[int_block, pl.BlockSpec((1, length, length), lambda i: (0, 0, 0)), block],
         out_specs=block,
         compiler_params=pltpu.CompilerParams(vmem_limit_bytes=VMEM_LIMIT),
         cost_estimate=pl.CostEstimate(
             flops=2 * length**3, bytes_accessed=12 * length**2, transcendentals=0
         ),
         name="ladder",
-    )(ints, half, *before)
+    )(ints, half, before)
 
 
 def cycle_kernel(which, ny, nx, here_ref, coupling_ref, inter_ref, *rest):
-    ints, ladder_ref, outs = rest[:CORES], rest[CORES], rest[CORES + 1 :]
+    ints, ladder_ref, outs, dressing = rest[:CORES], rest[CORES], rest[CORES + 1 : -1], rest[-1]
     y, x, core = here_ref[1], here_ref[2], here_ref[3]
     step = pl.program_id(0)
-    dressing = []
-    for f in range(CORES):
-        total = jnp.float32(0)
-        for source in range(BLOCKS * CORES):
-            flip = (source % CORES) ^ core ^ f
-            for w in range(CORES):
-                total = total + coupling_ref[core * CORES + which, source * CORES + w] * (
-                    inter_ref[source, w * CORES + flip]
-                )
-        dressing.append(total)
+
+    @pl.when(step == 0)
+    def _():
+        for f in range(CORES):
+            total = jnp.float32(0)
+            for source in range(BLOCKS * CORES):
+                flip = (source % CORES) ^ core ^ f
+                for w in range(CORES):
+                    total = total + coupling_ref[core * CORES + which, source * CORES + w] * (
+                        inter_ref[source, w * CORES + flip]
+                    )
+            dressing[f] = total
+
     rows = outs[0].shape[1]
 
     def chip_rows(xx):
         spot = pl.ds(pl.multiple_of(xx * rows, rows), rows)
         total = ladder_ref[spot, :]
         for f in range(CORES):
-            total = total + dressing[f] * ints[f][spot, :].astype(F32)
+            total = total + dressing[f] * ints[f][0, spot, :].astype(F32)
         return total
 
     if which == 0:
@@ -217,6 +266,12 @@
     rows = length // (ny * nx)
     smem = pl.BlockSpec(memory_space=pltpu.SMEM)
     block = pl.BlockSpec((nx * rows, length), lambda t, where: (lax.rem(where[1] + t, ny), 0))
+    int_blocks = [
+        pl.BlockSpec(
+            (1, nx * rows, length), lambda t, where, n=n: (n, lax.rem(where[1] + t, ny), 0)
+        )
+        for _, n in ints
+    ]
     if which == 0:
         count, shape = nx, (ny, rows, length)
         out = pl.BlockSpec((1, rows, length), lambda t, where: (t, 0, 0))
@@ -229,15 +284,16 @@
         grid_spec=pltpu.PrefetchScalarGridSpec(
             num_scalar_prefetch=1,
             grid=(ny,),
-            in_specs=[smem, smem] + [block] * (CORES + 1),
+            in_specs=[smem, smem] + int_blocks + [block],
             out_specs=[out] * count,
+            scratch_shapes=[pltpu.SMEM((CORES,), F32)],
         ),
         compiler_params=pltpu.CompilerParams(vmem_limit_bytes=VMEM_LIMIT),
         cost_estimate=pl.CostEstimate(
             flops=6 * length**2, bytes_accessed=12 * length**2, transcendentals=0
         ),
         name="add_cycle",
-    )(here, coupling, inter, *ints, ladder_sum)
+    )(here, coupling, inter, *(array for array, _ in ints), ladder_sum)
 
 
 def sum_over(axis, size, parts):
@@ -282,31 +338,35 @@
         z, y, x, c = (lax.axis_index(name).astype(jnp.int32) for name in ("z", "y", "x", "c"))
         here = jnp.stack([z, y, x, c])
         order = [(which, f) for which in range(each) for f in range(CORES)]
-        packed = {key: pack(dfint, domain, here, *key, quarter) for key in order[:1]}
-        packed[order[0]], amps = lax.optimization_barrier((packed[order[0]], amps))
-        for key in order[1:]:
-            packed[key] = pack(dfint, domain, here, *key, quarter)
-        parts = {
-            (which, f): [
-                part if (s, f) == (0, 0) else hop(s, f)(part)
-                for s, part in zip(SHIFTS, packed[which, f])
+        parts = {}
+        for which, f in order:
+            packed = pack(dfint, domain, here, which, f, quarter)
+            if not parts:
+                packed, amps = lax.optimization_barrier((packed, amps))
+            parts[which, f] = [
+                part if (s, f) == (0, 0) else hop(s, f)(part) for s, part in zip(SHIFTS, packed)
             ]
-            for which, f in order
-        }
         masked = masked_amps(amps, pair_mask, ((y * nx + x) * CORES + c) * own, dom)
         mine = lax.dynamic_slice_in_dim(masked, c * each, each, axis=0)
         other = swap_cores(lax.dynamic_slice_in_dim(masked, (1 - c) * each, each, axis=0))
-        both = by_core(c, mine, other, 1)
+        parts[order[0]], both = lax.optimization_barrier(
+            (parts[order[0]], by_core(c, mine, other, 1))
+        )
+        amp = [gather(both[0], chips), None]
+        amp[0], later = lax.optimization_barrier((amp[0], both[1]))
+        amp[1] = gather(later, chips)
         inter = jnp.zeros((BLOCKS * CORES, TB), F32)
-        sums, blocks = [None] * each, [[] for _ in range(each)]
-        for which in range(each):
-            amp = gather(both[which], chips)
-            for f in range(CORES):
-                ints, half, inter = half_ladder(
-                    amp, inter, parts[which, f], domain, here, which, f, quarter
-                )
-                blocks[which].append(ints)
-                sums[which] = ladder(ints, half, *([] if f == 0 else [sums[which]]))
+        ints0, ladder0, inter = work(
+            amp[0], inter, parts[0, 0] + parts[0, 1], domain, here, 0, (0, 1), True, quarter
+        )
+        ints1, ladder1, inter = work(
+            amp[1], inter, parts[1, 0], domain, here, 1, (0,), True, quarter
+        )
+        ints2, half, inter = work(
+            amp[1], inter, parts[1, 1], domain, here, 1, (1,), False, quarter
+        )
+        sums = [ladder0, ladder(ints2, half, ladder1)]
+        blocks = [[(ints0, 0), (ints0, 1)], [(ints1, 0), (ints2, 0)]]
         every = lax.all_to_all(inter, ("z", "c"), 0, 0, tiled=True)
         ends = []
         for which in range(each):

time: 197 us -> 179 us (0.909)
  blocking collectives: 24.8 us -> 0 us
  waiting for transfers between devices: 22.2 us -> 45.6 us
  Pallas kernels: 65.5 us -> 50.1 us
    all_to_all x1 -> x0, blocking collectives: 24.8 us -> none  [gather(): lax.all_to_all(jnp.broadcast_to(rows[None], (chips,) + rows.shape), ('y',...]
    pallas_call x4 -> x1, Pallas kernels: 20.1 us -> 5.46 us  [ladder(): pl.pallas_call(ladder_kernel, out_shape=jax.ShapeDtypeStruct((length, len...]
    all_to_all x1 -> x2, waiting for transfers between devices: 0.01 us -> 12.7 us  [gather(): lax.all_to_all(jnp.broadcast_to(rows[None], (chips,) + rows.shape), ('y',...]
    ppermute x14, waiting for transfers between devices: 9.42 us -> 21.9 us  [body(): hop(s, f)(part)]
    ppermute x14, starting transfers between devices: 42.7 us -> 32.4 us  [body(): hop(s, f)(part)]
    all_to_all x1 -> x2, starting transfers between devices: 3.7 us -> 11.7 us  [gather(): lax.all_to_all(jnp.broadcast_to(rows[None], (chips,) + rows.shape), ('y',...]
    pallas_call x4 -> x3, Pallas kernels: 22.4 us -> 21.3 us  [work(): pl.pallas_call(functools.partial(work_kernel, quarter, domain.shape[1], w...]
  transfers between devices with their start and end apart: 30 -> 31, of which waited for: 8 -> 12; matrix products, arithmetic and copies ran while one was open for 1% -> 2% of each run, Pallas kernels for 26% -> 20%
where the time goes in v4:
time: 179 us; the launch traced here: 177 us
  starting transfers between devices  71 us (40%)
  Pallas kernels  50.1 us (28%)
  waiting for transfers between devices  45.6 us (25%)
  local copies, waits for them, and re-layouts  8.27 us (5%)
  other arithmetic  1.9 us (1%)
    ppermute x14, starting transfers between devices, body(): hop(s, f)(part)  32.4 us
    ppermute x14, waiting for transfers between devices, body(): hop(s, f)(part)  21.9 us
    pallas_call x3, Pallas kernels, work(): pl.pallas_call(functools.partial(work_kernel, quarter, domain.shape[1], w...  21.3 us
    ppermute x12, starting transfers between devices, sum_over(): total = total + lax.ppermute(parts[s].astype(BF16), axis, perm).astype(F32)  16.8 us
    pallas_call x4, Pallas kernels, pack(): pl.pallas_call(functools.partial(pack_kernel, quarter, dom, which, flip),...  12.9 us
    all_to_all x2, waiting for transfers between devices, gather(): lax.all_to_all(jnp.broadcast_to(rows[None], (chips,) + rows.shape), ('y',...  12.7 us
    all_to_all x2, starting transfers between devices, gather(): lax.all_to_all(jnp.broadcast_to(rows[None], (chips,) + rows.shape), ('y',...  11.7 us
    pallas_call x2, Pallas kernels, add_cycle(): pl.pallas_call(functools.partial(cycle_kernel, which, ny, nx), out_shape=...  10.3 us
  transfers between devices with their start and end apart: 31, of which 12 were waited for; matrix products, arithmetic and copies ran while one was open for 2% of the time, Pallas kernels for 20%

profile of v4, /device:TPU:1, one launch (start us, length us, event | category | flops | bytes accessed | tf_op | source)
XLA Modules:
  0.0 177.2 jit_solution(5320949782550399055)
XLA Ops:
  2.0 3.3 %pack_tiles.4 = (bf16[2,128,768]{2,1,0:T(8,128)(2,1)}, bf16[2,128,768]{2,1,0:T(8,128)(2,1)}, bf16[2,128,768]{2,1,0:T(8,128)(2,1)}, bf16[2,128,768]{2,1,0:T(8,128)(2,1)}) custom-call(s32[16,6]{1,0:T(8,128)} %copy.39.domain_ref, s32[4]{0:T(128)} %pad_add_fusion.here_ref, bf16[1,1024,4096]{2,1,0:T(8,128)(2,1)} %dfint_ref.7), custom_call_target="tpu_custom_call" | custom-call | bytes 7340032 | tf_op jit(solution)/shard_map/pack_tiles/pallas_call | solution.py:78
  5.3 2.5 %collective-permute-start = (bf16[2,128,768]{2,1,0:T(8,128)(2,1)}, bf16[2,128,768]{2,1,0:T(8,128)(2,1)S(1)}, u32[]{:S(2)}, u32[]{:S(2)}) collective-permute-start(bf16[2,128,768]{2,1,0:T(8,128)(2,1)} %get-tuple-element.54), channel_id=1, source_target_pairs={{0,32},{1,33},{32,64},{33,65},{64,96},{65,97},{96,0},{97,1},{2,34}... | collective-permute-start | bytes 1179656 | tf_op jit(solution)/shard_map/ppermute | solution.py:347
  7.8 2.2 %collective-permute-start.1 = (bf16[2,128,768]{2,1,0:T(8,128)(2,1)}, bf16[2,128,768]{2,1,0:T(8,128)(2,1)S(1)}, u32[]{:S(2)}, u32[]{:S(2)}) collective-permute-start(bf16[2,128,768]{2,1,0:T(8,128)(2,1)} %get-tuple-element.55), channel_id=1, source_target_pairs={{0,96},{1,97},{32,0},{33,1},{64,32},{65,33},{96,64},{97,65},{2,98}... | collective-permute-start | bytes 1179656 | tf_op jit(solution)/shard_map/ppermute | solution.py:347
  12.1 1.6 collective-permute-start.3
  14.7 4.3 %collective-permute-done.rest_0_ = bf16[2,128,768]{2,1,0:T(8,128)(2,1)S(1)} collective-permute-done((bf16[2,128,768]{2,1,0:T(8,128)(2,1)}, bf16[2,128,768]{2,1,0:T(8,128)(2,1)S(1)}, u32[]{:S(2)}, u32[]{:S(2)}) %collective-permute-start) | collective-permute-done | bytes 393248 | tf_op jit(solution)/shard_map/ppermute | solution.py:347
  19.0 9.3 %collective-permute-done.2.rest_2_ = bf16[2,128,768]{2,1,0:T(8,128)(2,1)S(1)} collective-permute-done((bf16[2,128,768]{2,1,0:T(8,128)(2,1)}, bf16[2,128,768]{2,1,0:T(8,128)(2,1)S(1)}, u32[]{:S(2)}, u32[]{:S(2)}) %collective-permute-start.2) | collective-permute-done | bytes 393248 | tf_op jit(solution)/shard_map/ppermute | solution.py:347
  29.5 6.8 %all-to-all-start = ((bf16[16,48,768]{2,1,0:T(8,128)(2,1)}), bf16[16,48,768]{2,1,0:T(8,128)(2,1)S(1)}, u32[]{:S(2)}, u32[]{:S(2)}) async-start(bf16[16,48,768]{2,1,0:T(8,128)(2,1)} %broadcast_in_dim.45), calls=%async_computation | async-start | bytes 2359296 | tf_op jit(solution)/shard_map/all_to_all | solution.py:328
  36.3 3.1 %pack_tiles.6 = (bf16[2,128,768]{2,1,0:T(8,128)(2,1)}, bf16[2,128,768]{2,1,0:T(8,128)(2,1)}, bf16[2,128,768]{2,1,0:T(8,128)(2,1)}, bf16[2,128,768]{2,1,0:T(8,128)(2,1)}) custom-call(s32[16,6]{1,0:T(8,128)} %copy.39.domain_ref, s32[4]{0:T(128)} %pad_add_fusion.here_ref, bf16[1,1024,4096]{2,1,0:T(8,128)(2,1)} %dfint_ref.7), custom_call_target="tpu_custom_call" | custom-call | bytes 7340032 | tf_op jit(solution)/shard_map/pack_tiles/pallas_call | solution.py:78
  40.1 12.7 %all-to-all-done = bf16[16,48,768]{2,1,0:T(8,128)(2,1)S(1)} async-done(((bf16[16,48,768]{2,1,0:T(8,128)(2,1)}), bf16[16,48,768]{2,1,0:T(8,128)(2,1)S(1)}, u32[]{:S(2)}, u32[]{:S(2)}) %all-to-all-start) | async-done | bytes 1179680 | tf_op jit(solution)/shard_map/all_to_all | solution.py:328
  54.2 4.9 %all-to-all-start.1 = ((bf16[16,48,768]{2,1,0:T(8,128)(2,1)}), bf16[16,48,768]{2,1,0:T(8,128)(2,1)S(1)}, u32[]{:S(2)}, u32[]{:S(2)}) async-start(bf16[16,48,768]{2,1,0:T(8,128)(2,1)} %broadcast_in_dim.46), calls=%async_computation.1 | async-start | bytes 2359296 | tf_op jit(solution)/shard_map/all_to_all | solution.py:328
  59.3 3.3 %pack_tiles.5 = (bf16[2,128,768]{2,1,0:T(8,128)(2,1)}, bf16[2,128,768]{2,1,0:T(8,128)(2,1)}, bf16[2,128,768]{2,1,0:T(8,128)(2,1)}, bf16[2,128,768]{2,1,0:T(8,128)(2,1)}) custom-call(s32[16,6]{1,0:T(8,128)} %copy.39.domain_ref, s32[4]{0:T(128)} %pad_add_fusion.here_ref, bf16[1,1024,4096]{2,1,0:T(8,128)(2,1)} %dfint_ref.7), custom_call_target="tpu_custom_call" | custom-call | bytes 7340032 | tf_op jit(solution)/shard_map/pack_tiles/pallas_call | solution.py:78
  62.5 3.7 %collective-permute-start.4 = (bf16[2,128,768]{2,1,0:T(8,128)(2,1)}, bf16[2,128,768]{2,1,0:T(8,128)(2,1)S(1)}, u32[]{:S(2)}, u32[]{:S(2)}) collective-permute-start(bf16[2,128,768]{2,1,0:T(8,128)(2,1)} %get-tuple-element.66), channel_id=1, source_target_pairs={{0,33},{1,32},{32,65},{33,64},{64,97},{65,96},{96,1},{97,0},{2,35}... | collective-permute-start | bytes 1179656 | tf_op jit(solution)/shard_map/ppermute | solution.py:347
  66.2 2.6 %collective-permute-start.6 = (bf16[2,128,768]{2,1,0:T(8,128)(2,1)}, bf16[2,128,768]{2,1,0:T(8,128)(2,1)S(1)}, u32[]{:S(2)}, u32[]{:S(2)}) collective-permute-start(bf16[2,128,768]{2,1,0:T(8,128)(2,1)} %get-tuple-element.68), channel_id=1, source_target_pairs={{0,65},{1,64},{32,97},{33,96},{64,1},{65,0},{96,33},{97,32},{2,67}... | collective-permute-start | bytes 1179656 | tf_op jit(solution)/shard_map/ppermute | solution.py:347
  68.9 2.7 %collective-permute-start.10 = (bf16[2,128,768]{2,1,0:T(8,128)(2,1)S(1)}, bf16[2,128,768]{2,1,0:T(8,128)(2,1)S(1)}, u32[]{:S(2)}, u32[]{:S(2)}) collective-permute-start(bf16[2,128,768]{2,1,0:T(8,128)(2,1)S(1)} %copy-done.11), channel_id=1, source_target_pairs={{0,64},{1,65},{32,96},{33,97},{64,0},{65,1},{96,32},{97,33},{2,66}... | collective-permute-start | bytes 1179656 | tf_op jit(solution)/shard_map/ppermute | solution.py:347
  71.6 3.2 %pack_tiles.7 = (bf16[2,128,768]{2,1,0:T(8,128)(2,1)}, bf16[2,128,768]{2,1,0:T(8,128)(2,1)}, bf16[2,128,768]{2,1,0:T(8,128)(2,1)}, bf16[2,128,768]{2,1,0:T(8,128)(2,1)}) custom-call(s32[16,6]{1,0:T(8,128)} %copy.39.domain_ref, s32[4]{0:T(128)} %pad_add_fusion.here_ref, bf16[1,1024,4096]{2,1,0:T(8,128)(2,1)} %dfint_ref.7), custom_call_target="tpu_custom_call" | custom-call | bytes 7340032 | tf_op jit(solution)/shard_map/pack_tiles/pallas_call | solution.py:78
  75.4 2.4 %collective-permute-start.11 = (bf16[2,128,768]{2,1,0:T(8,128)(2,1)}, bf16[2,128,768]{2,1,0:T(8,128)(2,1)S(1)}, u32[]{:S(2)}, u32[]{:S(2)}) collective-permute-start(bf16[2,128,768]{2,1,0:T(8,128)(2,1)} %get-tuple-element.76), channel_id=1, source_target_pairs={{0,33},{1,32},{32,65},{33,64},{64,97},{65,96},{96,1},{97,0},{2,35}... | collective-permute-start | bytes 1179656 | tf_op jit(solution)/shard_map/ppermute | solution.py:347
  77.7 2.8 %collective-permute-done.5.rest_5_ = bf16[2,128,768]{2,1,0:T(8,128)(2,1)S(1)} collective-permute-done((bf16[2,128,768]{2,1,0:T(8,128)(2,1)}, bf16[2,128,768]{2,1,0:T(8,128)(2,1)S(1)}, u32[]{:S(2)}, u32[]{:S(2)}) %collective-permute-start.5) | collective-permute-done | bytes 393248 | tf_op jit(solution)/shard_map/ppermute | solution.py:347
  80.6 4.9 %collective-permute-done.6.rest_6_ = bf16[2,128,768]{2,1,0:T(8,128)(2,1)S(1)} collective-permute-done((bf16[2,128,768]{2,1,0:T(8,128)(2,1)}, bf16[2,128,768]{2,1,0:T(8,128)(2,1)S(1)}, u32[]{:S(2)}, u32[]{:S(2)}) %collective-permute-start.6) | collective-permute-done | bytes 393248 | tf_op jit(solution)/shard_map/ppermute | solution.py:347
  85.4 14.3 %collective-permute-start.13 = (bf16[2,128,768]{2,1,0:T(8,128)(2,1)}, bf16[2,128,768]{2,1,0:T(8,128)(2,1)S(1)}, u32[]{:S(2)}, u32[]{:S(2)}) collective-permute-start(bf16[2,128,768]{2,1,0:T(8,128)(2,1)} %get-tuple-element.78), channel_id=1, source_target_pairs={{0,65},{1,64},{32,97},{33,96},{64,1},{65,0},{96,33},{97,32},{2,67}... | collective-permute-start | bytes 1179656 | tf_op jit(solution)/shard_map/ppermute | solution.py:347
  100.5 9.2 %half_and_ladder.2 = (bf16[2,768,768]{2,1,0:T(8,128)(2,1)}, f32[768,768]{1,0:T(8,128)}, f32[8,128]{1,0:T(8,128)}) custom-call(s32[16,6]{1,0:T(8,128)} %copy.39.domain_ref, s32[4]{0:T(128)} %pad_add_fusion.here_ref, bf16[768,768]{1,0:T(8,128)(2,1)} %bitcast.56, f32[8,128]{1,0:T(8,128)} %broadcast_in_dim.47.before_ref, bf16[2,128,768]{2,1,0:T(8,128)(2,1)} %copy-done.7, ...), custom_call_target="tpu_custom_call" | custom-call | flops 3623878656 | bytes 11796480 | tf_op jit(solution)/shard_map/half_and_ladder/pallas_call | solution.py:168
  110.9 6.7 %half_and_ladder.3 = (bf16[1,768,768]{2,1,0:T(8,128)(2,1)}, f32[768,768]{1,0:T(8,128)}, f32[8,128]{1,0:T(8,128)}) custom-call(s32[16,6]{1,0:T(8,128)} %copy.39.domain_ref, s32[4]{0:T(128)} %pad_add_fusion.here_ref, bf16[768,768]{1,0:T(8,128)(2,1)} %bitcast.54, f32[8,128]{1,0:T(8,128)} %get-tuple-element.70.before_ref, bf16[2,128,768]{2,1,0:T(8,128)(2,1)} %copy-done.10, ...), custom_call_target="tpu_custom_call" | custom-call | flops 1811939328 | bytes 5898240 | tf_op jit(solution)/shard_map/half_and_ladder/pallas_call | solution.py:168
  118.7 5.5 %half_ladder.1 = (bf16[1,768,768]{2,1,0:T(8,128)(2,1)}, bf16[1,768,768]{2,1,0:T(8,128)(2,1)}, f32[8,128]{1,0:T(8,128)}) custom-call(s32[16,6]{1,0:T(8,128)} %copy.39.domain_ref, s32[4]{0:T(128)} %pad_add_fusion.here_ref, bf16[768,768]{1,0:T(8,128)(2,1)} %bitcast.55, f32[8,128]{1,0:T(8,128)} %get-tuple-element.75.before_ref, bf16[2,128,768]{2,1,0:T(8,128)(2,1)} %copy-done.13, ...), custom_call_target="tpu_custom_call" | custom-call | flops 905969664 | bytes 5898240 | tf_op jit(solution)/shard_map/half_ladder/pallas_call | solution.py:168
  124.3 3.6 %all-to-all-start.2 = ((f32[8,1,128]{2,1,0:T(1,128)}), f32[8,1,128]{2,1,0:T(1,128)S(1)}, u32[]{:S(2)}, u32[]{:S(2)}) async-start(f32[8,1,128]{2,1,0:T(1,128)} %bitcast.59), calls=%async_computation.2 | async-start | bytes 8192 | tf_op jit(solution)/shard_map/all_to_all | solution.py:370
  127.8 5.5 %ladder.1.rest_2_ = f32[768,768]{1,0:T(8,128)} custom-call(bf16[1,768,768]{2,1,0:T(8,128)(2,1)} %get-tuple-element.88.int_ref.rest_1_, bf16[1,768,768]{2,1,0:T(8,128)(2,1)} %get-tuple-element.89.half_ref, f32[768,768]{1,0:T(8,128)} %get-tuple-element.90.rest_0_), custom_call_target="tpu_custom_call" | custom-call | flops 905969664 | bytes 7077888 | tf_op jit(solution)/shard_map/ladder/pallas_call | solution.py:212
  133.9 5.2 %add_cycle.3 = (f32[4,48,768]{2,1,0:T(8,128)}, bf16[4,48,768]{2,1,0:T(8,128)(2,1)}, bf16[4,48,768]{2,1,0:T(8,128)(2,1)}, bf16[4,48,768]{2,1,0:T(8,128)(2,1)}) custom-call(s32[4]{0:T(128)} %pad_add_fusion.here_ref, f32[4,16]{1,0:T(4,128)} %coupling_ref.3, f32[8,128]{1,0:T(8,128)} %bitcast.57, bf16[1,768,768]{2,1,0:T(8,128)(2,1)} %get-tuple-element.87.rest_0_, ...), custom_call_target="tpu_custom_call" | custom-call | flops 3538944 | bytes 7077888 | tf_op jit(solution)/shard_map/add_cycle/pallas_call | solution.py:281
  143.2 5.2 %add_cycle.2 = (f32[4,48,768]{2,1,0:T(8,128)}, bf16[4,48,768]{2,1,0:T(8,128)(2,1)}, bf16[4,48,768]{2,1,0:T(8,128)(2,1)}, bf16[4,48,768]{2,1,0:T(8,128)(2,1)}) custom-call(s32[4]{0:T(128)} %pad_add_fusion.here_ref, f32[4,16]{1,0:T(4,128)} %coupling_ref.3, f32[8,128]{1,0:T(8,128)} %bitcast.58, bf16[2,768,768]{2,1,0:T(8,128)(2,1)} %get-tuple-element.81.rest_0_.rest_1_, ...), custom_call_target="tpu_custom_call" | custom-call | flops 3538944 | bytes 7077888 | tf_op jit(solution)/shard_map/add_cycle/pallas_call | solution.py:281
  152.5 3.6 %collective-permute-done.23 = bf16[4,48,768]{2,1,0:T(8,128)(2,1)S(1)} collective-permute-done((bf16[4,48,768]{2,1,0:T(8,128)(2,1)}, bf16[4,48,768]{2,1,0:T(8,128)(2,1)S(1)}, u32[]{:S(2)}, u32[]{:S(2)}) %collective-permute-start.23) | collective-permute-done | bytes 294944 | tf_op jit(solution)/shard_map/ppermute | solution.py:303
  157.5 2.4 %collective-permute-start.26 = (bf16[48,768]{1,0:T(8,128)(2,1)S(1)}, bf16[48,768]{1,0:T(8,128)(2,1)S(1)}, u32[]{:S(2)}, u32[]{:S(2)}) collective-permute-start(bf16[48,768]{1,0:T(8,128)(2,1)S(1)} %get-tuple-element.100), channel_id=1, source_target_pairs={{0,4},{2,6},{4,0},{6,2},{1,5},{3,7},{5,1},{7,3},{8,12},{10,14},{12... | collective-permute-start | bytes 221192 | tf_op jit(solution)/shard_map/ppermute | solution.py:303
  161.1 3.4 %collective-permute-done.17 = bf16[4,48,768]{2,1,0:T(8,128)(2,1)S(1)} collective-permute-done((bf16[4,48,768]{2,1,0:T(8,128)(2,1)}, bf16[4,48,768]{2,1,0:T(8,128)(2,1)S(1)}, u32[]{:S(2)}, u32[]{:S(2)}) %collective-permute-start.17) | collective-permute-done | bytes 294944 | tf_op jit(solution)/shard_map/ppermute | solution.py:303
  165.0 1.8 %collective-permute-start.20 = (bf16[48,768]{1,0:T(8,128)(2,1)S(1)}, bf16[48,768]{1,0:T(8,128)(2,1)S(1)}, u32[]{:S(2)}, u32[]{:S(2)}) collective-permute-start(bf16[48,768]{1,0:T(8,128)(2,1)S(1)} %get-tuple-element.103), channel_id=1, source_target_pairs={{0,16},{8,24},{16,0},{24,8},{1,17},{9,25},{17,1},{25,9},{2,18},{10... | collective-permute-start | bytes 221192 | tf_op jit(solution)/shard_map/ppermute | solution.py:303
  168.4 1.6 collective-permute-done.18
  170.6 5.0 %collective-permute-start.27 = (bf16[2,24,768]{2,1,0:T(8,128)(2,1)S(1)}, bf16[2,24,768]{2,1,0:T(8,128)(2,1)S(1)}, u32[]{:S(2)}, u32[]{:S(2)}) collective-permute-start(bf16[2,24,768]{2,1,0:T(8,128)(2,1)S(1)} %get-tuple-element.106), channel_id=1, source_target_pairs={{0,1},{1,0},{2,3},{3,2},{4,5},{5,4},{6,7},{7,6},{8,9},{9,8},{10,11... | collective-permute-start | bytes 221192 | tf_op jit(solution)/shard_map/ppermute | solution.py:32
  (111 shorter events, 27.7 us)
Async XLA Ops:
  5.3 13.7 %collective-permute-start = (bf16[2,128,768]{2,1,0:T(8,128)(2,1)}, bf16[2,128,768]{2,1,0:T(8,128)(2,1)S(1)}, u32[]{:S(2)}, u32[]{:S(2)}) collective-permute-start(bf16[2,128,768]{2,1,0:T(8,128)(2,1)} %get-tuple-element.54), channel_id=1, source_target_pairs={{0,32},{1,33},{32,64},{33,65},{64,96},{65,97},{96,0},{97,1},{2,34}... | collective-permute-start | bytes 1179656 | tf_op jit(solution)/shard_map/ppermute | solution.py:347
  7.8 11.2 %collective-permute-start.1 = (bf16[2,128,768]{2,1,0:T(8,128)(2,1)}, bf16[2,128,768]{2,1,0:T(8,128)(2,1)S(1)}, u32[]{:S(2)}, u32[]{:S(2)}) collective-permute-start(bf16[2,128,768]{2,1,0:T(8,128)(2,1)} %get-tuple-element.55), channel_id=1, source_target_pairs={{0,96},{1,97},{32,0},{33,1},{64,32},{65,33},{96,64},{97,65},{2,98}... | collective-permute-start | bytes 1179656 | tf_op jit(solution)/shard_map/ppermute | solution.py:347
  10.0 18.3 %collective-permute-start.2 = (bf16[2,128,768]{2,1,0:T(8,128)(2,1)}, bf16[2,128,768]{2,1,0:T(8,128)(2,1)S(1)}, u32[]{:S(2)}, u32[]{:S(2)}) collective-permute-start(bf16[2,128,768]{2,1,0:T(8,128)(2,1)} %get-tuple-element.56), channel_id=1, source_target_pairs={{0,64},{1,65},{32,96},{33,97},{64,0},{65,1},{96,32},{97,33},{2,66}... | collective-permute-start | bytes 1179656 | tf_op jit(solution)/shard_map/ppermute | solution.py:347
  12.1 2.5 %collective-permute-start.3 = (bf16[2,24,768]{2,1,0:T(8,128)(2,1)S(1)}, bf16[2,24,768]{2,1,0:T(8,128)(2,1)S(1)}, u32[]{:S(2)}, u32[]{:S(2)}) collective-permute-start(bf16[2,24,768]{2,1,0:T(8,128)(2,1)S(1)} %get-tuple-element.110), channel_id=1, source_target_pairs={{0,1},{1,0},{2,3},{3,2},{4,5},{5,4},{6,7},{7,6},{8,9},{9,8},{10,11... | collective-permute-start | bytes 221192 | tf_op jit(solution)/shard_map/ppermute | solution.py:32
  29.5 23.3 %all-to-all-start = ((bf16[16,48,768]{2,1,0:T(8,128)(2,1)}), bf16[16,48,768]{2,1,0:T(8,128)(2,1)S(1)}, u32[]{:S(2)}, u32[]{:S(2)}) async-start(bf16[16,48,768]{2,1,0:T(8,128)(2,1)} %broadcast_in_dim.45), calls=%async_computation | async-start | bytes 2359296 | tf_op jit(solution)/shard_map/all_to_all | solution.py:328
  39.4 29.4 %collective-permute-start.8 = (bf16[2,128,768]{2,1,0:T(8,128)(2,1)}, bf16[2,128,768]{2,1,0:T(8,128)(2,1)S(1)}, u32[]{:S(2)}, u32[]{:S(2)}) collective-permute-start(bf16[2,128,768]{2,1,0:T(8,128)(2,1)} %get-tuple-element.71), channel_id=1, source_target_pairs={{0,32},{1,33},{32,64},{33,65},{64,96},{65,97},{96,0},{97,1},{2,34}... | collective-permute-start | bytes 1179656 | tf_op jit(solution)/shard_map/ppermute | solution.py:347
  54.2 55.5 %all-to-all-start.1 = ((bf16[16,48,768]{2,1,0:T(8,128)(2,1)}), bf16[16,48,768]{2,1,0:T(8,128)(2,1)S(1)}, u32[]{:S(2)}, u32[]{:S(2)}) async-start(bf16[16,48,768]{2,1,0:T(8,128)(2,1)} %broadcast_in_dim.46), calls=%async_computation.1 | async-start | bytes 2359296 | tf_op jit(solution)/shard_map/all_to_all | solution.py:328
  59.2 9.7 %collective-permute-start.9 = (bf16[2,128,768]{2,1,0:T(8,128)(2,1)S(1)}, bf16[2,128,768]{2,1,0:T(8,128)(2,1)S(1)}, u32[]{:S(2)}, u32[]{:S(2)}) collective-permute-start(bf16[2,128,768]{2,1,0:T(8,128)(2,1)S(1)} %copy-done.22), channel_id=1, source_target_pairs={{0,96},{1,97},{32,0},{33,1},{64,32},{65,33},{96,64},{97,65},{2,98}... | collective-permute-start | bytes 1179656 | tf_op jit(solution)/shard_map/ppermute | solution.py:347
  62.5 12.8 %collective-permute-start.4 = (bf16[2,128,768]{2,1,0:T(8,128)(2,1)}, bf16[2,128,768]{2,1,0:T(8,128)(2,1)S(1)}, u32[]{:S(2)}, u32[]{:S(2)}) collective-permute-start(bf16[2,128,768]{2,1,0:T(8,128)(2,1)} %get-tuple-element.66), channel_id=1, source_target_pairs={{0,33},{1,32},{32,65},{33,64},{64,97},{65,96},{96,1},{97,0},{2,35}... | collective-permute-start | bytes 1179656 | tf_op jit(solution)/shard_map/ppermute | solution.py:347
  66.2 14.4 %collective-permute-start.5 = (bf16[2,128,768]{2,1,0:T(8,128)(2,1)}, bf16[2,128,768]{2,1,0:T(8,128)(2,1)S(1)}, u32[]{:S(2)}, u32[]{:S(2)}) collective-permute-start(bf16[2,128,768]{2,1,0:T(8,128)(2,1)} %get-tuple-element.67), channel_id=1, source_target_pairs={{0,97},{1,96},{32,1},{33,0},{64,33},{65,32},{96,65},{97,64},{2,99}... | collective-permute-start | bytes 1179656 | tf_op jit(solution)/shard_map/ppermute | solution.py:347
  66.2 19.2 %collective-permute-start.6 = (bf16[2,128,768]{2,1,0:T(8,128)(2,1)}, bf16[2,128,768]{2,1,0:T(8,128)(2,1)S(1)}, u32[]{:S(2)}, u32[]{:S(2)}) collective-permute-start(bf16[2,128,768]{2,1,0:T(8,128)(2,1)} %get-tuple-element.68), channel_id=1, source_target_pairs={{0,65},{1,64},{32,97},{33,96},{64,1},{65,0},{96,33},{97,32},{2,67}... | collective-permute-start | bytes 1179656 | tf_op jit(solution)/shard_map/ppermute | solution.py:347
  68.8 31.0 %collective-permute-start.7 = (bf16[2,128,768]{2,1,0:T(8,128)(2,1)}, bf16[2,128,768]{2,1,0:T(8,128)(2,1)S(1)}, u32[]{:S(2)}, u32[]{:S(2)}) collective-permute-start(bf16[2,128,768]{2,1,0:T(8,128)(2,1)} %get-tuple-element.69), channel_id=1, source_target_pairs={{0,1},{1,0},{32,33},{33,32},{64,65},{65,64},{96,97},{97,96},{2,3},... | collective-permute-start | bytes 1179656 | tf_op jit(solution)/shard_map/ppermute | solution.py:347
  68.9 40.8 %collective-permute-start.10 = (bf16[2,128,768]{2,1,0:T(8,128)(2,1)S(1)}, bf16[2,128,768]{2,1,0:T(8,128)(2,1)S(1)}, u32[]{:S(2)}, u32[]{:S(2)}) collective-permute-start(bf16[2,128,768]{2,1,0:T(8,128)(2,1)S(1)} %copy-done.11), channel_id=1, source_target_pairs={{0,64},{1,65},{32,96},{33,97},{64,0},{65,1},{96,32},{97,33},{2,66}... | collective-permute-start | bytes 1179656 | tf_op jit(solution)/shard_map/ppermute | solution.py:347
  75.3 25.1 %copy-start.15 = (bf16[2,128,768]{2,1,0:T(8,128)(2,1)}, bf16[2,128,768]{2,1,0:T(8,128)(2,1)S(1)}, u32[]{:S(2)}) copy-start(bf16[2,128,768]{2,1,0:T(8,128)(2,1)S(1)} %collective-permute-done.4.rest_4_) | copy-start | bytes 1179652
  75.4 42.3 %collective-permute-start.11 = (bf16[2,128,768]{2,1,0:T(8,128)(2,1)}, bf16[2,128,768]{2,1,0:T(8,128)(2,1)S(1)}, u32[]{:S(2)}, u32[]{:S(2)}) collective-permute-start(bf16[2,128,768]{2,1,0:T(8,128)(2,1)} %get-tuple-element.76), channel_id=1, source_target_pairs={{0,33},{1,32},{32,65},{33,64},{64,97},{65,96},{96,1},{97,0},{2,35}... | collective-permute-start | bytes 1179656 | tf_op jit(solution)/shard_map/ppermute | solution.py:347
  80.6 37.1 %collective-permute-start.12 = (bf16[2,128,768]{2,1,0:T(8,128)(2,1)}, bf16[2,128,768]{2,1,0:T(8,128)(2,1)S(1)}, u32[]{:S(2)}, u32[]{:S(2)}) collective-permute-start(bf16[2,128,768]{2,1,0:T(8,128)(2,1)} %get-tuple-element.77), channel_id=1, source_target_pairs={{0,97},{1,96},{32,1},{33,0},{64,33},{65,32},{96,65},{97,64},{2,99}... | collective-permute-start | bytes 1179656 | tf_op jit(solution)/shard_map/ppermute | solution.py:347
  85.4 32.2 %collective-permute-start.13 = (bf16[2,128,768]{2,1,0:T(8,128)(2,1)}, bf16[2,128,768]{2,1,0:T(8,128)(2,1)S(1)}, u32[]{:S(2)}, u32[]{:S(2)}) collective-permute-start(bf16[2,128,768]{2,1,0:T(8,128)(2,1)} %get-tuple-element.78), channel_id=1, source_target_pairs={{0,65},{1,64},{32,97},{33,96},{64,1},{65,0},{96,33},{97,32},{2,67}... | collective-permute-start | bytes 1179656 | tf_op jit(solution)/shard_map/ppermute | solution.py:347
  99.8 17.9 %collective-permute-start.14 = (bf16[2,128,768]{2,1,0:T(8,128)(2,1)}, bf16[2,128,768]{2,1,0:T(8,128)(2,1)S(1)}, u32[]{:S(2)}, u32[]{:S(2)}) collective-permute-start(bf16[2,128,768]{2,1,0:T(8,128)(2,1)} %get-tuple-element.79), channel_id=1, source_target_pairs={{0,1},{1,0},{32,33},{33,32},{64,65},{65,64},{96,97},{97,96},{2,3},... | collective-permute-start | bytes 1179656 | tf_op jit(solution)/shard_map/ppermute | solution.py:347
  124.3 9.0 %all-to-all-start.2 = ((f32[8,1,128]{2,1,0:T(1,128)}), f32[8,1,128]{2,1,0:T(1,128)S(1)}, u32[]{:S(2)}, u32[]{:S(2)}) async-start(f32[8,1,128]{2,1,0:T(1,128)} %bitcast.59), calls=%async_computation.2 | async-start | bytes 8192 | tf_op jit(solution)/shard_map/all_to_all | solution.py:370
  139.1 12.0 %collective-permute-start.21 = (bf16[4,48,768]{2,1,0:T(8,128)(2,1)}, bf16[4,48,768]{2,1,0:T(8,128)(2,1)S(1)}, u32[]{:S(2)}, u32[]{:S(2)}) collective-permute-start(bf16[4,48,768]{2,1,0:T(8,128)(2,1)} %get-tuple-element.92), channel_id=1, source_target_pairs={{0,8},{8,16},{16,24},{24,0},{1,9},{9,17},{17,25},{25,1},{2,10},{10... | collective-permute-start | bytes 884744 | tf_op jit(solution)/shard_map/ppermute | solution.py:303
  140.3 12.3 %collective-permute-start.22 = (bf16[4,48,768]{2,1,0:T(8,128)(2,1)}, bf16[4,48,768]{2,1,0:T(8,128)(2,1)S(1)}, u32[]{:S(2)}, u32[]{:S(2)}) collective-permute-start(bf16[4,48,768]{2,1,0:T(8,128)(2,1)} %get-tuple-element.93), channel_id=1, source_target_pairs={{0,24},{8,0},{16,8},{24,16},{1,25},{9,1},{17,9},{25,17},{2,26},{10... | collective-permute-start | bytes 884744 | tf_op jit(solution)/shard_map/ppermute | solution.py:303
  141.7 14.4 %collective-permute-start.23 = (bf16[4,48,768]{2,1,0:T(8,128)(2,1)}, bf16[4,48,768]{2,1,0:T(8,128)(2,1)S(1)}, u32[]{:S(2)}, u32[]{:S(2)}) collective-permute-start(bf16[4,48,768]{2,1,0:T(8,128)(2,1)} %get-tuple-element.94), channel_id=1, source_target_pairs={{0,16},{8,24},{16,0},{24,8},{1,17},{9,25},{17,1},{25,9},{2,18},{10... | collective-permute-start | bytes 884744 | tf_op jit(solution)/shard_map/ppermute | solution.py:303
  148.4 11.6 %collective-permute-start.15 = (bf16[4,48,768]{2,1,0:T(8,128)(2,1)}, bf16[4,48,768]{2,1,0:T(8,128)(2,1)S(1)}, u32[]{:S(2)}, u32[]{:S(2)}) collective-permute-start(bf16[4,48,768]{2,1,0:T(8,128)(2,1)} %get-tuple-element.84), channel_id=1, source_target_pairs={{0,2},{2,4},{4,6},{6,0},{1,3},{3,5},{5,7},{7,1},{8,10},{10,12},{12... | collective-permute-start | bytes 884744 | tf_op jit(solution)/shard_map/ppermute | solution.py:303
  149.5 11.6 %collective-permute-start.16 = (bf16[4,48,768]{2,1,0:T(8,128)(2,1)}, bf16[4,48,768]{2,1,0:T(8,128)(2,1)S(1)}, u32[]{:S(2)}, u32[]{:S(2)}) collective-permute-start(bf16[4,48,768]{2,1,0:T(8,128)(2,1)} %get-tuple-element.85), channel_id=1, source_target_pairs={{0,6},{2,0},{4,2},{6,4},{1,7},{3,1},{5,3},{7,5},{8,14},{10,8},{12,... | collective-permute-start | bytes 884744 | tf_op jit(solution)/shard_map/ppermute | solution.py:303
  151.1 13.5 %collective-permute-start.17 = (bf16[4,48,768]{2,1,0:T(8,128)(2,1)}, bf16[4,48,768]{2,1,0:T(8,128)(2,1)S(1)}, u32[]{:S(2)}, u32[]{:S(2)}) collective-permute-start(bf16[4,48,768]{2,1,0:T(8,128)(2,1)} %get-tuple-element.86), channel_id=1, source_target_pairs={{0,4},{2,6},{4,0},{6,2},{1,5},{3,7},{5,1},{7,3},{8,12},{10,14},{12... | collective-permute-start | bytes 884744 | tf_op jit(solution)/shard_map/ppermute | solution.py:303
  156.3 10.6 %collective-permute-start.24 = (bf16[48,768]{1,0:T(8,128)(2,1)S(1)}, bf16[48,768]{1,0:T(8,128)(2,1)S(1)}, u32[]{:S(2)}, u32[]{:S(2)}) collective-permute-start(bf16[48,768]{1,0:T(8,128)(2,1)S(1)} %get-tuple-element.99), channel_id=1, source_target_pairs={{0,2},{2,4},{4,6},{6,0},{1,3},{3,5},{5,7},{7,1},{8,10},{10,12},{12... | collective-permute-start | bytes 221192 | tf_op jit(solution)/shard_map/ppermute | solution.py:303
  157.5 10.8 %collective-permute-start.26 = (bf16[48,768]{1,0:T(8,128)(2,1)S(1)}, bf16[48,768]{1,0:T(8,128)(2,1)S(1)}, u32[]{:S(2)}, u32[]{:S(2)}) collective-permute-start(bf16[48,768]{1,0:T(8,128)(2,1)S(1)} %get-tuple-element.100), channel_id=1, source_target_pairs={{0,4},{2,6},{4,0},{6,2},{1,5},{3,7},{5,1},{7,3},{8,12},{10,14},{12... | collective-permute-start | bytes 221192 | tf_op jit(solution)/shard_map/ppermute | solution.py:303
  159.9 8.5 %collective-permute-start.25 = (bf16[48,768]{1,0:T(8,128)(2,1)S(1)}, bf16[48,768]{1,0:T(8,128)(2,1)S(1)}, u32[]{:S(2)}, u32[]{:S(2)}) collective-permute-start(bf16[48,768]{1,0:T(8,128)(2,1)S(1)} %get-tuple-element.101), channel_id=1, source_target_pairs={{0,6},{2,0},{4,2},{6,4},{1,7},{3,1},{5,3},{7,5},{8,14},{10,8},{12,... | collective-permute-start | bytes 221192 | tf_op jit(solution)/shard_map/ppermute | solution.py:303
  164.7 5.3 %collective-permute-start.18 = (bf16[48,768]{1,0:T(8,128)(2,1)S(1)}, bf16[48,768]{1,0:T(8,128)(2,1)S(1)}, u32[]{:S(2)}, u32[]{:S(2)}) collective-permute-start(bf16[48,768]{1,0:T(8,128)(2,1)S(1)} %get-tuple-element.102), channel_id=1, source_target_pairs={{0,8},{8,16},{16,24},{24,0},{1,9},{9,17},{17,25},{25,1},{2,10},{10... | collective-permute-start | bytes 221192 | tf_op jit(solution)/shard_map/ppermute | solution.py:303
  165.0 5.0 %collective-permute-start.20 = (bf16[48,768]{1,0:T(8,128)(2,1)S(1)}, bf16[48,768]{1,0:T(8,128)(2,1)S(1)}, u32[]{:S(2)}, u32[]{:S(2)}) collective-permute-start(bf16[48,768]{1,0:T(8,128)(2,1)S(1)} %get-tuple-element.103), channel_id=1, source_target_pairs={{0,16},{8,24},{16,0},{24,8},{1,17},{9,25},{17,1},{25,9},{2,18},{10... | collective-permute-start | bytes 221192 | tf_op jit(solution)/shard_map/ppermute | solution.py:303
  166.9 3.7 %collective-permute-start.19 = (bf16[48,768]{1,0:T(8,128)(2,1)S(1)}, bf16[48,768]{1,0:T(8,128)(2,1)S(1)}, u32[]{:S(2)}, u32[]{:S(2)}) collective-permute-start(bf16[48,768]{1,0:T(8,128)(2,1)S(1)} %get-tuple-element.104), channel_id=1, source_target_pairs={{0,24},{8,0},{16,8},{24,16},{1,25},{9,1},{17,9},{25,17},{2,26},{10... | collective-permute-start | bytes 221192 | tf_op jit(solution)/shard_map/ppermute | solution.py:303
  170.6 5.9 %collective-permute-start.27 = (bf16[2,24,768]{2,1,0:T(8,128)(2,1)S(1)}, bf16[2,24,768]{2,1,0:T(8,128)(2,1)S(1)}, u32[]{:S(2)}, u32[]{:S(2)}) collective-permute-start(bf16[2,24,768]{2,1,0:T(8,128)(2,1)S(1)} %get-tuple-element.106), channel_id=1, source_target_pairs={{0,1},{1,0},{2,3},{3,2},{4,5},{5,4},{6,7},{7,6},{8,9},{9,8},{10,11... | collective-permute-start | bytes 221192 | tf_op jit(solution)/shard_map/ppermute | solution.py:32
  (22 other events, 132.9 us)

commit v5 on v4

--- a/solution.py
+++ b/solution.py
@@ -17,6 +17,8 @@
 F32 = jnp.float32
 NT = (((1,), (1,)), ((), ()))
 SHIFTS = (1, 3, 2, 0)
+EARLY = 1
+FIRST = (((0, 0), 0), ((0, 0), 1), ((0, 0), 2))
 
 
 def hop(shift, flip):
@@ -98,11 +100,13 @@
 def work_kernel(quarter, dom, which, flips, finish, domain_ref, here_ref, amp_ref, before_ref, *rest):
     count = len(SHIFTS)
     parts, rest = rest[: count * len(flips)], rest[count * len(flips) :]
-    int_out, out_ref, inter_ref, amp, ints, half, ladder, in_sem, out_sem = rest
+    int_out, out_ref, inter_out, amp, ints, half, ladder, inter_ref, in_sem, out_sem = rest
     here, core = here_ref[0], here_ref[3]
     pair = (here * CORES + core) * CORES + which
     load_amp = pltpu.make_async_copy(amp_ref, amp, in_sem.at[len(flips)])
     load_amp.start()
+    load_inter = pltpu.make_async_copy(before_ref, inter_ref, in_sem.at[len(flips) + 1])
+    load_inter.start()
     for s in range(dom):
         owner = domain_ref[pair, s] // quarter
         rank = jnp.int32(0)
@@ -126,7 +130,7 @@
         jnp.int32, (rows, rows), 1
     )
     lane = lax.broadcasted_iota(jnp.int32, inter_ref.shape, 1)
-    inter = before_ref[...]
+    traces = []
     for f, flip in enumerate(flips):
         pltpu.make_async_copy(ints.at[f], ints.at[f], in_sem.at[f]).wait()
         pltpu.make_async_copy(ints.at[f], int_out.at[f], out_sem.at[f]).start()
@@ -141,8 +145,14 @@
                     half.at[f, spot, :], out_ref.at[f, spot, :], out_sem.at[len(flips)]
                 ).start()
         trace = jnp.sum(jnp.where(diagonal, total, 0.0))
-        inter = jnp.where(lane == which * CORES + flip, trace, inter)
+        traces.append((which * CORES + flip, trace))
+    load_inter.wait()
+    inter = inter_ref[...]
+    for place, trace in traces:
+        inter = jnp.where(lane == place, trace, inter)
     inter_ref[...] = inter
+    store_inter = pltpu.make_async_copy(inter_ref, inter_out, out_sem.at[len(flips) + 1])
+    store_inter.start()
     if finish:
         for r in range(0, dom * TB, rows):
             spot = pl.ds(r, rows)
@@ -157,12 +167,12 @@
     for f in range(len(flips)):
         pltpu.make_async_copy(ints.at[f], int_out.at[f], out_sem.at[f]).wait()
     pltpu.make_async_copy(ladder if finish else half, out_ref, out_sem.at[len(flips)]).wait()
+    store_inter.wait()
 
 
 def work(amp, before, parts, domain, here, which, flips, finish, quarter):
     length = amp.shape[0]
     count = len(flips)
-    small = pl.BlockSpec(memory_space=pltpu.VMEM)
     anywhere = pl.BlockSpec(memory_space=pl.ANY)
     squares = (count, length, length)
     return pl.pallas_call(
@@ -177,15 +187,16 @@
         grid_spec=pltpu.PrefetchScalarGridSpec(
             num_scalar_prefetch=2,
             grid=(1,),
-            in_specs=[anywhere, small] + [anywhere] * len(parts),
-            out_specs=[anywhere, anywhere, small],
+            in_specs=[anywhere] * (2 + len(parts)),
+            out_specs=[anywhere] * 3,
             scratch_shapes=[
                 pltpu.VMEM((length, length), BF16),
                 pltpu.VMEM(squares, BF16),
                 pltpu.VMEM(squares, BF16),
                 pltpu.VMEM((length, length), F32),
-                pltpu.SemaphoreType.DMA((count + 1,)),
-                pltpu.SemaphoreType.DMA((count + 1,)),
+                pltpu.VMEM(before.shape, F32),
+                pltpu.SemaphoreType.DMA((count + 2,)),
+                pltpu.SemaphoreType.DMA((count + 2,)),
             ],
         ),
         compiler_params=pltpu.CompilerParams(vmem_limit_bytes=VMEM_LIMIT),
@@ -198,23 +209,48 @@
     )(domain, here, amp, before, *parts)
 
 
-def ladder_kernel(int_ref, half_ref, *rest):
-    out_ref = rest[-1]
-    acc = lax.dot_general(int_ref[0], half_ref[0], NT, preferred_element_type=F32)
-    out_ref[...] = acc + rest[0][...]
+def ladder_kernel(int_ref, half_ref, before_ref, out_ref, ints, half, total, in_sem, out_sem):
+    length = total.shape[0]
+    rows = length // 3
+    spots = [pl.ds(r, rows) for r in range(0, length, rows)]
+    load_half = pltpu.make_async_copy(half_ref.at[0], half, in_sem.at[0])
+    load_half.start()
+    loads = []
+    for n, spot in enumerate(spots):
+        loads.append(
+            [
+                pltpu.make_async_copy(int_ref.at[0, spot, :], ints.at[spot, :], in_sem.at[2 * n + 1]),
+                pltpu.make_async_copy(before_ref.at[spot, :], total.at[spot, :], in_sem.at[2 * n + 2]),
+            ]
+        )
+        for load in loads[-1]:
+            load.start()
+    load_half.wait()
+    for spot, pair_of_loads in zip(spots, loads):
+        for load in pair_of_loads:
+            load.wait()
+        total[spot, :] += lax.dot_general(
+            ints[spot, :], half[...], NT, preferred_element_type=F32
+        )
+        pltpu.make_async_copy(total.at[spot, :], out_ref.at[spot, :], out_sem.at[0]).start()
+    pltpu.make_async_copy(total, out_ref, out_sem.at[0]).wait()
 
 
 def ladder(ints, half, before):
     length = before.shape[0]
-    rows = length // 3
-    block = pl.BlockSpec((rows, length), lambda i: (i, 0))
-    int_block = pl.BlockSpec((1, rows, length), lambda i: (0, i, 0))
+    anywhere = pl.BlockSpec(memory_space=pl.ANY)
     return pl.pallas_call(
         ladder_kernel,
         out_shape=jax.ShapeDtypeStruct((length, length), F32),
-        grid=(length // rows,),
-        in_specs=[int_block, pl.BlockSpec((1, length, length), lambda i: (0, 0, 0)), block],
-        out_specs=block,
+        in_specs=[anywhere] * 3,
+        out_specs=anywhere,
+        scratch_shapes=[
+            pltpu.VMEM((length, length), BF16),
+            pltpu.VMEM((length, length), BF16),
+            pltpu.VMEM((length, length), F32),
+            pltpu.SemaphoreType.DMA((7,)),
+            pltpu.SemaphoreType.DMA((1,)),
+        ],
         compiler_params=pltpu.CompilerParams(vmem_limit_bytes=VMEM_LIMIT),
         cost_estimate=pl.CostEstimate(
             flops=2 * length**3, bytes_accessed=12 * length**2, transcendentals=0
@@ -223,70 +259,80 @@
     )(ints, half, before)
 
 
-def cycle_kernel(which, ny, nx, here_ref, coupling_ref, inter_ref, *rest):
-    ints, ladder_ref, outs, dressing = rest[:CORES], rest[CORES], rest[CORES + 1 : -1], rest[-1]
+def cycle_kernel(which, places, here_ref, coupling_ref, inter_ref, *rest):
+    sources, rest = rest[: CORES + 1], rest[CORES + 1 :]
+    count = (len(rest) - 4) // 2
+    outs, kept, (ints, ladder, in_sem, out_sem) = rest[:count], rest[count : 2 * count], rest[2 * count :]
     y, x, core = here_ref[1], here_ref[2], here_ref[3]
-    step = pl.program_id(0)
-
-    @pl.when(step == 0)
-    def _():
-        for f in range(CORES):
-            total = jnp.float32(0)
-            for source in range(BLOCKS * CORES):
-                flip = (source % CORES) ^ core ^ f
-                for w in range(CORES):
-                    total = total + coupling_ref[core * CORES + which, source * CORES + w] * (
-                        inter_ref[source, w * CORES + flip]
-                    )
-            dressing[f] = total
-
     rows = outs[0].shape[1]
-
-    def chip_rows(xx):
-        spot = pl.ds(pl.multiple_of(xx * rows, rows), rows)
-        total = ladder_ref[spot, :]
-        for f in range(CORES):
-            total = total + dressing[f] * ints[f][0, spot, :].astype(F32)
-        return total
-
-    if which == 0:
-        for s in range(nx):
-            outs[s][0] = chip_rows(lax.rem(x + s, nx)).astype(outs[s].dtype)
-    else:
-        for s in range(ny):
-
-            @pl.when(step == s)
-            def _(s=s):
-                for k in range(nx):
-                    outs[s][k] = chip_rows(lax.rem(x + k, nx)).astype(outs[s].dtype)
+    ny, nx = (outs[0].shape[0], count) if which == 0 else (count, outs[0].shape[0])
+    group = nx * rows
+    loads = []
+    for t in range(ny):
+        spot = pl.ds(pl.multiple_of(lax.rem(y + t, ny) * group, group), group)
+        loads.append(
+            [
+                pltpu.make_async_copy(
+                    sources[f].at[places[f], spot, :], ints.at[f, t], in_sem.at[t * (CORES + 1) + f]
+                )
+                for f in range(CORES)
+            ]
+            + [
+                pltpu.make_async_copy(
+                    sources[CORES].at[spot, :], ladder.at[t], in_sem.at[t * (CORES + 1) + CORES]
+                )
+            ]
+        )
+        for load in loads[-1]:
+            load.start()
+    dressing = []
+    for f in range(CORES):
+        total = jnp.float32(0)
+        for source in range(BLOCKS * CORES):
+            flip = (source % CORES) ^ core ^ f
+            for w in range(CORES):
+                total = total + coupling_ref[core * CORES + which, source * CORES + w] * (
+                    inter_ref[source, w * CORES + flip]
+                )
+        dressing.append(total)
+    for t in range(ny):
+        for load in loads[t]:
+            load.wait()
+        for k in range(nx):
+            spot = pl.ds(pl.multiple_of(lax.rem(x + k, nx) * rows, rows), rows)
+            total = ladder[t, spot, :]
+            for f in range(CORES):
+                total = total + dressing[f] * ints[f, t, spot, :].astype(F32)
+            n, place = (k, t) if which == 0 else (t, k)
+            kept[n][place] = total.astype(kept[n].dtype)
+            if which == 0:
+                pltpu.make_async_copy(kept[n].at[place], outs[n].at[place], out_sem.at[n]).start()
+        if which == 1:
+            pltpu.make_async_copy(kept[t], outs[t], out_sem.at[t]).start()
+    for n in range(count):
+        pltpu.make_async_copy(kept[n], outs[n], out_sem.at[n]).wait()
 
 
 def add_cycle(ladder_sum, ints, inter, coupling, here, which, ny, nx):
     length = ladder_sum.shape[0]
     rows = length // (ny * nx)
-    smem = pl.BlockSpec(memory_space=pltpu.SMEM)
-    block = pl.BlockSpec((nx * rows, length), lambda t, where: (lax.rem(where[1] + t, ny), 0))
-    int_blocks = [
-        pl.BlockSpec(
-            (1, nx * rows, length), lambda t, where, n=n: (n, lax.rem(where[1] + t, ny), 0)
-        )
-        for _, n in ints
-    ]
-    if which == 0:
-        count, shape = nx, (ny, rows, length)
-        out = pl.BlockSpec((1, rows, length), lambda t, where: (t, 0, 0))
-    else:
-        count, shape = ny, (nx, rows, length)
-        out = pl.BlockSpec(shape, lambda t, where: (0, 0, 0))
+    anywhere = pl.BlockSpec(memory_space=pl.ANY)
+    count, shape = (nx, (ny, rows, length)) if which == 0 else (ny, (nx, rows, length))
     return pl.pallas_call(
-        functools.partial(cycle_kernel, which, ny, nx),
+        functools.partial(cycle_kernel, which, [place for _, place in ints]),
         out_shape=[jax.ShapeDtypeStruct(shape, BF16 if s else F32) for s in range(count)],
         grid_spec=pltpu.PrefetchScalarGridSpec(
-            num_scalar_prefetch=1,
-            grid=(ny,),
-            in_specs=[smem, smem] + int_blocks + [block],
-            out_specs=[out] * count,
-            scratch_shapes=[pltpu.SMEM((CORES,), F32)],
+            num_scalar_prefetch=3,
+            grid=(1,),
+            in_specs=[anywhere] * (CORES + 1),
+            out_specs=[anywhere] * count,
+            scratch_shapes=[pltpu.VMEM(shape, BF16 if s else F32) for s in range(count)]
+            + [
+                pltpu.VMEM((CORES, ny, nx * rows, length), BF16),
+                pltpu.VMEM((ny, nx * rows, length), F32),
+                pltpu.SemaphoreType.DMA((ny * (CORES + 1),)),
+                pltpu.SemaphoreType.DMA((count,)),
+            ],
         ),
         compiler_params=pltpu.CompilerParams(vmem_limit_bytes=VMEM_LIMIT),
         cost_estimate=pl.CostEstimate(
@@ -325,9 +371,16 @@
 
 def make_body(ny, nx):
     def gather(rows, chips):
-        return lax.all_to_all(
+        got = lax.all_to_all(
             jnp.broadcast_to(rows[None], (chips,) + rows.shape), ("y", "x"), 0, 0, tiled=True
-        ).reshape(chips * rows.shape[0], rows.shape[1])
+        )
+        return [got[:, i].reshape(chips * rows.shape[1], rows.shape[2]) for i in range(rows.shape[0])]
+
+    def send(key, packed):
+        return [
+            part if (s, key[1]) == (0, 0) else hop(s, key[1])(part)
+            for s, part in zip(SHIFTS, packed)
+        ]
 
     def body(amps, domain, pair_mask, dfint, coupling):
         pairs, own, length = amps.shape
@@ -338,23 +391,24 @@
         z, y, x, c = (lax.axis_index(name).astype(jnp.int32) for name in ("z", "y", "x", "c"))
         here = jnp.stack([z, y, x, c])
         order = [(which, f) for which in range(each) for f in range(CORES)]
-        parts = {}
-        for which, f in order:
-            packed = pack(dfint, domain, here, which, f, quarter)
-            if not parts:
-                packed, amps = lax.optimization_barrier((packed, amps))
-            parts[which, f] = [
-                part if (s, f) == (0, 0) else hop(s, f)(part) for s, part in zip(SHIFTS, packed)
-            ]
+        packed = {order[0]: pack(dfint, domain, here, *order[0], quarter)}
+        packed[order[0]], amps = lax.optimization_barrier((packed[order[0]], amps))
+        for key in order[1:]:
+            packed[key] = pack(dfint, domain, here, *key, quarter)
         masked = masked_amps(amps, pair_mask, ((y * nx + x) * CORES + c) * own, dom)
         mine = lax.dynamic_slice_in_dim(masked, c * each, each, axis=0)
         other = swap_cores(lax.dynamic_slice_in_dim(masked, (1 - c) * each, each, axis=0))
-        parts[order[0]], both = lax.optimization_barrier(
-            (parts[order[0]], by_core(c, mine, other, 1))
-        )
-        amp = [gather(both[0], chips), None]
-        amp[0], later = lax.optimization_barrier((amp[0], both[1]))
-        amp[1] = gather(later, chips)
+        both = by_core(c, mine, other, 1)
+        parts = {}
+        for key in order[:EARLY]:
+            parts[key] = send(key, packed.pop(key))
+        early = [parts[key][n] for key, n in FIRST]
+        early, packed, both = lax.optimization_barrier((early, packed, both))
+        for (key, n), part in zip(FIRST, early):
+            parts[key][n] = part
+        for key in order[EARLY:]:
+            parts[key] = send(key, packed[key])
+        amp = gather(both, chips)
         inter = jnp.zeros((BLOCKS * CORES, TB), F32)
         ints0, ladder0, inter = work(
             amp[0], inter, parts[0, 0] + parts[0, 1], domain, here, 0, (0, 1), True, quarter

time: 179 us -> 151 us (0.84)
  starting transfers between devices: 71 us -> 55.6 us
  Pallas kernels: 50.1 us -> 44 us
  waiting for transfers between devices: 45.6 us -> 39.8 us
    ppermute x14, starting transfers between devices: 32.4 us -> 17.6 us  [send(): hop(s, key[1])(part)]
    all_to_all x2 -> x1, starting transfers between devices: 11.7 us -> 6.76 us  [gather(): lax.all_to_all(jnp.broadcast_to(rows[None], (chips,) + rows.shape), ('y',...]
    all_to_all x2 -> x1, waiting for transfers between devices: 12.7 us -> 9.63 us  [gather(): lax.all_to_all(jnp.broadcast_to(rows[None], (chips,) + rows.shape), ('y',...]
    pallas_call x3, Pallas kernels: 21.3 us -> 18.7 us  [work(): pl.pallas_call(functools.partial(work_kernel, quarter, domain.shape[1], w...]
    all_to_all x1, starting transfers between devices: 3.56 us -> 5.63 us  [body(): every = lax.all_to_all(inter, ('z', 'c'), 0, 0, tiled=True)]
    pallas_call x2, Pallas kernels: 10.3 us -> 8.42 us  [add_cycle(): pl.pallas_call(functools.partial(cycle_kernel, which, [place for _, place...]
    unnamed x48 -> x38, local copies, waits for them, and re-layouts: 4.72 us -> 3.92 us
  transfers between devices with their start and end apart: 31 -> 30, of which waited for: 12 -> 10; matrix products, arithmetic and copies ran while one was open for 2% -> 2% of each run, Pallas kernels for 20% -> 22%
where the time goes in v5:
time: 151 us; the launch traced here: 150 us
  starting transfers between devices  55.6 us (37%)
  Pallas kernels  44 us (29%)
  waiting for transfers between devices  39.8 us (26%)
  local copies, waits for them, and re-layouts  8.31 us (6%)
  other arithmetic  1.91 us (1%)
    ppermute x14, waiting for transfers between devices, send(): hop(s, key[1])(part)  21.3 us
    pallas_call x3, Pallas kernels, work(): pl.pallas_call(functools.partial(work_kernel, quarter, domain.shape[1], w...  18.7 us
    ppermute x12, starting transfers between devices, sum_over(): total = total + lax.ppermute(parts[s].astype(BF16), axis, perm).astype(F32)  18.3 us
    ppermute x14, starting transfers between devices, send(): hop(s, key[1])(part)  17.6 us
    pallas_call x4, Pallas kernels, pack(): pl.pallas_call(functools.partial(pack_kernel, quarter, dom, which, flip),...  12.6 us
    all_to_all x1, waiting for transfers between devices, gather(): lax.all_to_all(jnp.broadcast_to(rows[None], (chips,) + rows.shape), ('y',...  9.63 us
    pallas_call x2, Pallas kernels, add_cycle(): pl.pallas_call(functools.partial(cycle_kernel, which, [place for _, place...  8.42 us
    ppermute x12, waiting for transfers between devices, sum_over(): total = total + lax.ppermute(parts[s].astype(BF16), axis, perm).astype(F32)  7.68 us
  transfers between devices with their start and end apart: 30, of which 10 were waited for; matrix products, arithmetic and copies ran while one was open for 2% of the time, Pallas kernels for 22%

profile of v5, /device:TPU:1, one launch (start us, length us, event | category | flops | bytes accessed | tf_op | source)
XLA Modules:
  0.0 149.9 jit_solution(14900360483246015369)
XLA Ops:
  2.0 3.2 %pack_tiles.4 = (bf16[2,128,768]{2,1,0:T(8,128)(2,1)}, bf16[2,128,768]{2,1,0:T(8,128)(2,1)}, bf16[2,128,768]{2,1,0:T(8,128)(2,1)}, bf16[2,128,768]{2,1,0:T(8,128)(2,1)}) custom-call(s32[16,6]{1,0:T(8,128)} %copy.39.domain_ref, s32[4]{0:T(128)} %pad_add_fusion.here_ref, bf16[1,1024,4096]{2,1,0:T(8,128)(2,1)} %dfint_ref.7), custom_call_target="tpu_custom_call" | custom-call | bytes 7340032 | tf_op jit(solution)/shard_map/pack_tiles/pallas_call | solution.py:80
  5.3 2.6 %collective-permute-start = (bf16[2,128,768]{2,1,0:T(8,128)(2,1)}, bf16[2,128,768]{2,1,0:T(8,128)(2,1)S(1)}, u32[]{:S(2)}, u32[]{:S(2)}) collective-permute-start(bf16[2,128,768]{2,1,0:T(8,128)(2,1)} %get-tuple-element.63), channel_id=1, source_target_pairs={{0,32},{1,33},{32,64},{33,65},{64,96},{65,97},{96,0},{97,1},{2,34}... | collective-permute-start | bytes 1179656 | tf_op jit(solution)/shard_map/ppermute | solution.py:381
  7.9 2.2 %collective-permute-start.1 = (bf16[2,128,768]{2,1,0:T(8,128)(2,1)}, bf16[2,128,768]{2,1,0:T(8,128)(2,1)S(1)}, u32[]{:S(2)}, u32[]{:S(2)}) collective-permute-start(bf16[2,128,768]{2,1,0:T(8,128)(2,1)} %get-tuple-element.64), channel_id=1, source_target_pairs={{0,96},{1,97},{32,0},{33,1},{64,32},{65,33},{96,64},{97,65},{2,98}... | collective-permute-start | bytes 1179656 | tf_op jit(solution)/shard_map/ppermute | solution.py:381
  12.1 1.6 %collective-permute-start.3 = (bf16[2,24,768]{2,1,0:T(8,128)(2,1)S(1)}, bf16[2,24,768]{2,1,0:T(8,128)(2,1)S(1)}, u32[]{:S(2)}, u32[]{:S(2)}) collective-permute-start(bf16[2,24,768]{2,1,0:T(8,128)(2,1)S(1)} %get-tuple-element.128), channel_id=1, source_target_pairs={{0,1},{1,0},{2,3},{3,2},{4,5},{5,4},{6,7},{7,6},{8,9},{9,8},{10,11... | collective-permute-start | bytes 221192 | tf_op jit(solution)/shard_map/ppermute | solution.py:34
  13.7 3.1 %pack_tiles.7 = (bf16[2,128,768]{2,1,0:T(8,128)(2,1)}, bf16[2,128,768]{2,1,0:T(8,128)(2,1)}, bf16[2,128,768]{2,1,0:T(8,128)(2,1)}, bf16[2,128,768]{2,1,0:T(8,128)(2,1)}) custom-call(s32[16,6]{1,0:T(8,128)} %copy.39.domain_ref, s32[4]{0:T(128)} %pad_add_fusion.here_ref, bf16[1,1024,4096]{2,1,0:T(8,128)(2,1)} %dfint_ref.7), custom_call_target="tpu_custom_call" | custom-call | bytes 7340032 | tf_op jit(solution)/shard_map/pack_tiles/pallas_call | solution.py:80
  16.8 3.1 %pack_tiles.6 = (bf16[2,128,768]{2,1,0:T(8,128)(2,1)}, bf16[2,128,768]{2,1,0:T(8,128)(2,1)}, bf16[2,128,768]{2,1,0:T(8,128)(2,1)}, bf16[2,128,768]{2,1,0:T(8,128)(2,1)}) custom-call(s32[16,6]{1,0:T(8,128)} %copy.39.domain_ref, s32[4]{0:T(128)} %pad_add_fusion.here_ref, bf16[1,1024,4096]{2,1,0:T(8,128)(2,1)} %dfint_ref.7), custom_call_target="tpu_custom_call" | custom-call | bytes 7340032 | tf_op jit(solution)/shard_map/pack_tiles/pallas_call | solution.py:80
  19.9 3.1 %pack_tiles.5 = (bf16[2,128,768]{2,1,0:T(8,128)(2,1)}, bf16[2,128,768]{2,1,0:T(8,128)(2,1)}, bf16[2,128,768]{2,1,0:T(8,128)(2,1)}, bf16[2,128,768]{2,1,0:T(8,128)(2,1)}) custom-call(s32[16,6]{1,0:T(8,128)} %copy.39.domain_ref, s32[4]{0:T(128)} %pad_add_fusion.here_ref, bf16[1,1024,4096]{2,1,0:T(8,128)(2,1)} %dfint_ref.7), custom_call_target="tpu_custom_call" | custom-call | bytes 7340032 | tf_op jit(solution)/shard_map/pack_tiles/pallas_call | solution.py:80
  23.2 5.1 %collective-permute-done.2.rest_2_ = bf16[2,128,768]{2,1,0:T(8,128)(2,1)S(1)} collective-permute-done((bf16[2,128,768]{2,1,0:T(8,128)(2,1)}, bf16[2,128,768]{2,1,0:T(8,128)(2,1)S(1)}, u32[]{:S(2)}, u32[]{:S(2)}) %collective-permute-start.2) | collective-permute-done | bytes 393248 | tf_op jit(solution)/shard_map/ppermute | solution.py:381
  28.3 1.6 %broadcast_in_dim.37 = bf16[16,2,48,768]{3,2,1,0:T(8,128)(2,1)} broadcast(bf16[2,48,768]{2,1,0:T(8,128)(2,1)S(1)} %maximum_select_fusion), dimensions={1,2,3} | broadcast | bytes 2506752 | tf_op jit(solution)/shard_map/broadcast_in_dim | solution.py:375
  29.9 6.8 %all-to-all-start = ((bf16[16,2,48,768]{3,2,1,0:T(8,128)(2,1)}), bf16[16,2,48,768]{3,2,1,0:T(8,128)(2,1)S(1)}, u32[]{:S(2)}, u32[]{:S(2)}) async-start(bf16[16,2,48,768]{3,2,1,0:T(8,128)(2,1)} %broadcast_in_dim.37), calls=%async_computation | async-start | bytes 4718592 | tf_op jit(solution)/shard_map/all_to_all | solution.py:374
  36.7 2.6 %collective-permute-start.4 = (bf16[2,128,768]{2,1,0:T(8,128)(2,1)}, bf16[2,128,768]{2,1,0:T(8,128)(2,1)S(1)}, u32[]{:S(2)}, u32[]{:S(2)}) collective-permute-start(bf16[2,128,768]{2,1,0:T(8,128)(2,1)} %get-tuple-element.84), channel_id=1, source_target_pairs={{0,33},{1,32},{32,65},{33,64},{64,97},{65,96},{96,1},{97,0},{2,35}... | collective-permute-start | bytes 1179656 | tf_op jit(solution)/shard_map/ppermute | solution.py:381
  42.4 13.8 %collective-permute-done.4.rest_4_ = bf16[2,128,768]{2,1,0:T(8,128)(2,1)S(1)} collective-permute-done((bf16[2,128,768]{2,1,0:T(8,128)(2,1)}, bf16[2,128,768]{2,1,0:T(8,128)(2,1)S(1)}, u32[]{:S(2)}, u32[]{:S(2)}) %collective-permute-start.4) | collective-permute-done | bytes 393248 | tf_op jit(solution)/shard_map/ppermute | solution.py:381
  56.3 1.8 %collective-permute-start.9 = (bf16[2,128,768]{2,1,0:T(8,128)(2,1)}, bf16[2,128,768]{2,1,0:T(8,128)(2,1)}, u32[]{:S(2)}, u32[]{:S(2)}) collective-permute-start(bf16[2,128,768]{2,1,0:T(8,128)(2,1)} %get-tuple-element.90), channel_id=1, source_target_pairs={{0,96},{1,97},{32,0},{33,1},{64,32},{65,33},{96,64},{97,65},{2,98}... | collective-permute-start | bytes 1179656 | tf_op jit(solution)/shard_map/ppermute | solution.py:381
  58.8 9.6 %all-to-all-done = bf16[16,2,48,768]{3,2,1,0:T(8,128)(2,1)S(1)} async-done(((bf16[16,2,48,768]{3,2,1,0:T(8,128)(2,1)}), bf16[16,2,48,768]{3,2,1,0:T(8,128)(2,1)S(1)}, u32[]{:S(2)}, u32[]{:S(2)}) %all-to-all-start) | async-done | bytes 2359328 | tf_op jit(solution)/shard_map/all_to_all | solution.py:374
  68.5 1.6 %fusion.14 = (bf16[16,1,48,768]{3,2,1,0:T(8,128)(2,1)}, bf16[16,1,48,768]{3,2,1,0:T(8,128)(2,1)}) fusion(bf16[16,2,48,768]{3,2,1,0:T(8,128)(2,1)S(1)} %all-to-all-done), kind=kLoop, calls=%fused_computation.39 | loop fusion | bytes 4718592 | tf_op jit(solution)/shard_map/slice | solution.py:377
  70.1 3.5 %collective-permute-start.11 = (bf16[2,128,768]{2,1,0:T(8,128)(2,1)S(1)}, bf16[2,128,768]{2,1,0:T(8,128)(2,1)S(1)}, u32[]{:S(2)}, u32[]{:S(2)}) collective-permute-start(bf16[2,128,768]{2,1,0:T(8,128)(2,1)S(1)} %copy-done.11), channel_id=1, source_target_pairs={{0,33},{1,32},{32,65},{33,64},{64,97},{65,96},{96,1},{97,0},{2,35}... | collective-permute-start | bytes 1179656 | tf_op jit(solution)/shard_map/ppermute | solution.py:381
  73.6 2.3 %collective-permute-done.8.rest_0_ = bf16[2,128,768]{2,1,0:T(8,128)(2,1)} collective-permute-done((bf16[2,128,768]{2,1,0:T(8,128)(2,1)}, bf16[2,128,768]{2,1,0:T(8,128)(2,1)}, u32[]{:S(2)}, u32[]{:S(2)}) %collective-permute-start.8) | collective-permute-done | bytes 393248 | tf_op jit(solution)/shard_map/ppermute | solution.py:381
  77.2 8.5 %half_and_ladder.2 = (bf16[2,768,768]{2,1,0:T(8,128)(2,1)}, f32[768,768]{1,0:T(8,128)}, f32[8,128]{1,0:T(8,128)}) custom-call(s32[16,6]{1,0:T(8,128)} %copy.39.domain_ref, s32[4]{0:T(128)} %pad_add_fusion.here_ref, bf16[768,768]{1,0:T(8,128)(2,1)} %bitcast.52, f32[8,128]{1,0:T(8,128)} %broadcast_in_dim.38.before_ref, bf16[2,128,768]{2,1,0:T(8,128)(2,1)} %copy-done.5, ...), custom_call_target="tpu_custom_call" | custom-call | flops 3623878656 | bytes 11796480 | tf_op jit(solution)/shard_map/half_and_ladder/pallas_call | solution.py:178
  85.6 5.9 %half_and_ladder.3 = (bf16[1,768,768]{2,1,0:T(8,128)(2,1)}, f32[768,768]{1,0:T(8,128)}, f32[8,128]{1,0:T(8,128)}) custom-call(s32[16,6]{1,0:T(8,128)} %copy.39.domain_ref, s32[4]{0:T(128)} %pad_add_fusion.here_ref, bf16[768,768]{1,0:T(8,128)(2,1)} %bitcast.50, f32[8,128]{1,0:T(8,128)} %get-tuple-element.88.before_ref, ...), custom_call_target="tpu_custom_call" | custom-call | flops 1811939328 | bytes 5898240 | tf_op jit(solution)/shard_map/half_and_ladder/pallas_call | solution.py:178
  92.7 4.3 %half_ladder.1 = (bf16[1,768,768]{2,1,0:T(8,128)(2,1)}, bf16[1,768,768]{2,1,0:T(8,128)(2,1)}, f32[8,128]{1,0:T(8,128)}) custom-call(s32[16,6]{1,0:T(8,128)} %copy.39.domain_ref, s32[4]{0:T(128)} %pad_add_fusion.here_ref, bf16[768,768]{1,0:T(8,128)(2,1)} %bitcast.51, f32[8,128]{1,0:T(8,128)} %get-tuple-element.93.before_ref, bf16[2,128,768]{2,1,0:T(8,128)(2,1)} %copy-done.14, ...), custom_call_target="tpu_custom_call" | custom-call | flops 905969664 | bytes 5898240 | tf_op jit(solution)/shard_map/half_ladder/pallas_call | solution.py:178
  97.0 5.6 %all-to-all-start.1 = ((f32[8,1,128]{2,1,0:T(1,128)}), f32[8,1,128]{2,1,0:T(1,128)S(1)}, u32[]{:S(2)}, u32[]{:S(2)}) async-start(f32[8,1,128]{2,1,0:T(1,128)} %bitcast.55), calls=%async_computation.1 | async-start | bytes 8192 | tf_op jit(solution)/shard_map/all_to_all | solution.py:424
  102.6 4.3 %ladder.1.rest_2_ = f32[768,768]{1,0:T(8,128)} custom-call(bf16[1,768,768]{2,1,0:T(8,128)(2,1)} %get-tuple-element.106.int_ref.rest_1_, bf16[1,768,768]{2,1,0:T(8,128)(2,1)} %get-tuple-element.107.half_ref, f32[768,768]{1,0:T(8,128)} %get-tuple-element.108.before_ref), custom_call_target="tpu_custom_call" | custom-call | flops 905969664 | bytes 7077888 | tf_op jit(solution)/shard_map/ladder/pallas_call | solution.py:242
  107.8 4.2 %add_cycle.3 = (f32[4,48,768]{2,1,0:T(8,128)}, bf16[4,48,768]{2,1,0:T(8,128)(2,1)}, bf16[4,48,768]{2,1,0:T(8,128)(2,1)}, bf16[4,48,768]{2,1,0:T(8,128)(2,1)}) custom-call(s32[4]{0:T(128)} %pad_add_fusion.here_ref, f32[4,16]{1,0:T(4,128)} %coupling_ref.3, f32[8,128]{1,0:T(8,128)} %bitcast.53, bf16[1,768,768]{2,1,0:T(8,128)(2,1)} %get-tuple-element.105.rest_0_, ...), custom_call_target="tpu_custom_call" | custom-call | flops 3538944 | bytes 7077888 | tf_op jit(solution)/shard_map/add_cycle/pallas_call | solution.py:321
  112.0 1.8 %collective-permute-start.21 = (bf16[4,48,768]{2,1,0:T(8,128)(2,1)}, bf16[4,48,768]{2,1,0:T(8,128)(2,1)S(1)}, u32[]{:S(2)}, u32[]{:S(2)}) collective-permute-start(bf16[4,48,768]{2,1,0:T(8,128)(2,1)} %get-tuple-element.110), channel_id=1, source_target_pairs={{0,8},{8,16},{16,24},{24,0},{1,9},{9,17},{17,25},{25,1},{2,10},{10... | collective-permute-start | bytes 884744 | tf_op jit(solution)/shard_map/ppermute | solution.py:349
  115.0 1.7 %collective-permute-start.23 = (bf16[4,48,768]{2,1,0:T(8,128)(2,1)}, bf16[4,48,768]{2,1,0:T(8,128)(2,1)S(1)}, u32[]{:S(2)}, u32[]{:S(2)}) collective-permute-start(bf16[4,48,768]{2,1,0:T(8,128)(2,1)} %get-tuple-element.112), channel_id=1, source_target_pairs={{0,16},{8,24},{16,0},{24,8},{1,17},{9,25},{17,1},{25,9},{2,18},{10... | collective-permute-start | bytes 884744 | tf_op jit(solution)/shard_map/ppermute | solution.py:349
  116.7 4.3 %add_cycle.2 = (f32[4,48,768]{2,1,0:T(8,128)}, bf16[4,48,768]{2,1,0:T(8,128)(2,1)}, bf16[4,48,768]{2,1,0:T(8,128)(2,1)}, bf16[4,48,768]{2,1,0:T(8,128)(2,1)}) custom-call(s32[4]{0:T(128)} %pad_add_fusion.here_ref, f32[4,16]{1,0:T(4,128)} %coupling_ref.3, f32[8,128]{1,0:T(8,128)} %bitcast.54, bf16[2,768,768]{2,1,0:T(8,128)(2,1)} %get-tuple-element.99.rest_0_.rest_1_, ...), custom_call_target="tpu_custom_call" | custom-call | flops 3538944 | bytes 7077888 | tf_op jit(solution)/shard_map/add_cycle/pallas_call | solution.py:321
  123.7 1.8 %collective-permute-start.17 = (bf16[4,48,768]{2,1,0:T(8,128)(2,1)}, bf16[4,48,768]{2,1,0:T(8,128)(2,1)S(1)}, u32[]{:S(2)}, u32[]{:S(2)}) collective-permute-start(bf16[4,48,768]{2,1,0:T(8,128)(2,1)} %get-tuple-element.104), channel_id=1, source_target_pairs={{0,4},{2,6},{4,0},{6,2},{1,5},{3,7},{5,1},{7,3},{8,12},{10,14},{12... | collective-permute-start | bytes 884744 | tf_op jit(solution)/shard_map/ppermute | solution.py:349
  125.6 3.5 %collective-permute-done.23 = bf16[4,48,768]{2,1,0:T(8,128)(2,1)S(1)} collective-permute-done((bf16[4,48,768]{2,1,0:T(8,128)(2,1)}, bf16[4,48,768]{2,1,0:T(8,128)(2,1)S(1)}, u32[]{:S(2)}, u32[]{:S(2)}) %collective-permute-start.23) | collective-permute-done | bytes 294944 | tf_op jit(solution)/shard_map/ppermute | solution.py:349
  130.7 2.3 %collective-permute-start.26 = (bf16[48,768]{1,0:T(8,128)(2,1)S(1)}, bf16[48,768]{1,0:T(8,128)(2,1)S(1)}, u32[]{:S(2)}, u32[]{:S(2)}) collective-permute-start(bf16[48,768]{1,0:T(8,128)(2,1)S(1)} %get-tuple-element.120), channel_id=1, source_target_pairs={{0,4},{2,6},{4,0},{6,2},{1,5},{3,7},{5,1},{7,3},{8,12},{10,14},{12... | collective-permute-start | bytes 221192 | tf_op jit(solution)/shard_map/ppermute | solution.py:349
  134.6 2.0 %collective-permute-done.17 = bf16[4,48,768]{2,1,0:T(8,128)(2,1)S(1)} collective-permute-done((bf16[4,48,768]{2,1,0:T(8,128)(2,1)}, bf16[4,48,768]{2,1,0:T(8,128)(2,1)S(1)}, u32[]{:S(2)}, u32[]{:S(2)}) %collective-permute-start.17) | collective-permute-done | bytes 294944 | tf_op jit(solution)/shard_map/ppermute | solution.py:349
  137.1 1.8 %collective-permute-start.20 = (bf16[48,768]{1,0:T(8,128)(2,1)S(1)}, bf16[48,768]{1,0:T(8,128)(2,1)S(1)}, u32[]{:S(2)}, u32[]{:S(2)}) collective-permute-start(bf16[48,768]{1,0:T(8,128)(2,1)S(1)} %get-tuple-element.123), channel_id=1, source_target_pairs={{0,16},{8,24},{16,0},{24,8},{1,17},{9,25},{17,1},{25,9},{2,18},{10... | collective-permute-start | bytes 221192 | tf_op jit(solution)/shard_map/ppermute | solution.py:349
  142.7 5.6 %collective-permute-start.27 = (bf16[2,24,768]{2,1,0:T(8,128)(2,1)S(1)}, bf16[2,24,768]{2,1,0:T(8,128)(2,1)S(1)}, u32[]{:S(2)}, u32[]{:S(2)}) collective-permute-start(bf16[2,24,768]{2,1,0:T(8,128)(2,1)S(1)} %get-tuple-element.126), channel_id=1, source_target_pairs={{0,1},{1,0},{2,3},{3,2},{4,5},{5,4},{6,7},{7,6},{8,9},{9,8},{10,11... | collective-permute-start | bytes 221192 | tf_op jit(solution)/shard_map/ppermute | solution.py:34
  (98 shorter events, 24.2 us)
Async XLA Ops:
  5.3 17.9 %collective-permute-start = (bf16[2,128,768]{2,1,0:T(8,128)(2,1)}, bf16[2,128,768]{2,1,0:T(8,128)(2,1)S(1)}, u32[]{:S(2)}, u32[]{:S(2)}) collective-permute-start(bf16[2,128,768]{2,1,0:T(8,128)(2,1)} %get-tuple-element.63), channel_id=1, source_target_pairs={{0,32},{1,33},{32,64},{33,65},{64,96},{65,97},{96,0},{97,1},{2,34}... | collective-permute-start | bytes 1179656 | tf_op jit(solution)/shard_map/ppermute | solution.py:381
  7.9 15.3 %collective-permute-start.1 = (bf16[2,128,768]{2,1,0:T(8,128)(2,1)}, bf16[2,128,768]{2,1,0:T(8,128)(2,1)S(1)}, u32[]{:S(2)}, u32[]{:S(2)}) collective-permute-start(bf16[2,128,768]{2,1,0:T(8,128)(2,1)} %get-tuple-element.64), channel_id=1, source_target_pairs={{0,96},{1,97},{32,0},{33,1},{64,32},{65,33},{96,64},{97,65},{2,98}... | collective-permute-start | bytes 1179656 | tf_op jit(solution)/shard_map/ppermute | solution.py:381
  10.0 18.3 %collective-permute-start.2 = (bf16[2,128,768]{2,1,0:T(8,128)(2,1)}, bf16[2,128,768]{2,1,0:T(8,128)(2,1)S(1)}, u32[]{:S(2)}, u32[]{:S(2)}) collective-permute-start(bf16[2,128,768]{2,1,0:T(8,128)(2,1)} %get-tuple-element.65), channel_id=1, source_target_pairs={{0,64},{1,65},{32,96},{33,97},{64,0},{65,1},{96,32},{97,33},{2,66}... | collective-permute-start | bytes 1179656 | tf_op jit(solution)/shard_map/ppermute | solution.py:381
  12.1 11.0 %collective-permute-start.3 = (bf16[2,24,768]{2,1,0:T(8,128)(2,1)S(1)}, bf16[2,24,768]{2,1,0:T(8,128)(2,1)S(1)}, u32[]{:S(2)}, u32[]{:S(2)}) collective-permute-start(bf16[2,24,768]{2,1,0:T(8,128)(2,1)S(1)} %get-tuple-element.128), channel_id=1, source_target_pairs={{0,1},{1,0},{2,3},{3,2},{4,5},{5,4},{6,7},{7,6},{8,9},{9,8},{10,11... | collective-permute-start | bytes 221192 | tf_op jit(solution)/shard_map/ppermute | solution.py:34
  29.9 38.6 %all-to-all-start = ((bf16[16,2,48,768]{3,2,1,0:T(8,128)(2,1)}), bf16[16,2,48,768]{3,2,1,0:T(8,128)(2,1)S(1)}, u32[]{:S(2)}, u32[]{:S(2)}) async-start(bf16[16,2,48,768]{3,2,1,0:T(8,128)(2,1)} %broadcast_in_dim.37), calls=%async_computation | async-start | bytes 4718592 | tf_op jit(solution)/shard_map/all_to_all | solution.py:374
  36.7 39.2 %copy-start.9 = (bf16[2,128,768]{2,1,0:T(8,128)(2,1)S(1)}, bf16[2,128,768]{2,1,0:T(8,128)(2,1)}, u32[]{:S(2)}) copy-start(bf16[2,128,768]{2,1,0:T(8,128)(2,1)} %get-tuple-element.96) | copy-start | bytes 1179652
  36.7 39.2 %copy-start.8 = (bf16[2,128,768]{2,1,0:T(8,128)(2,1)S(1)}, bf16[2,128,768]{2,1,0:T(8,128)(2,1)}, u32[]{:S(2)}) copy-start(bf16[2,128,768]{2,1,0:T(8,128)(2,1)} %get-tuple-element.97) | copy-start | bytes 1179652
  36.7 19.5 %collective-permute-start.4 = (bf16[2,128,768]{2,1,0:T(8,128)(2,1)}, bf16[2,128,768]{2,1,0:T(8,128)(2,1)S(1)}, u32[]{:S(2)}, u32[]{:S(2)}) collective-permute-start(bf16[2,128,768]{2,1,0:T(8,128)(2,1)} %get-tuple-element.84), channel_id=1, source_target_pairs={{0,33},{1,32},{32,65},{33,64},{64,97},{65,96},{96,1},{97,0},{2,35}... | collective-permute-start | bytes 1179656 | tf_op jit(solution)/shard_map/ppermute | solution.py:381
  39.4 18.7 %collective-permute-start.5 = (bf16[2,128,768]{2,1,0:T(8,128)(2,1)}, bf16[2,128,768]{2,1,0:T(8,128)(2,1)S(1)}, u32[]{:S(2)}, u32[]{:S(2)}) collective-permute-start(bf16[2,128,768]{2,1,0:T(8,128)(2,1)} %get-tuple-element.85), channel_id=1, source_target_pairs={{0,97},{1,96},{32,1},{33,0},{64,33},{65,32},{96,65},{97,64},{2,99}... | collective-permute-start | bytes 1179656 | tf_op jit(solution)/shard_map/ppermute | solution.py:381
  40.2 29.9 %collective-permute-start.6 = (bf16[2,128,768]{2,1,0:T(8,128)(2,1)}, bf16[2,128,768]{2,1,0:T(8,128)(2,1)}, u32[]{:S(2)}, u32[]{:S(2)}) collective-permute-start(bf16[2,128,768]{2,1,0:T(8,128)(2,1)} %get-tuple-element.86), channel_id=1, source_target_pairs={{0,65},{1,64},{32,97},{33,96},{64,1},{65,0},{96,33},{97,32},{2,67}... | collective-permute-start | bytes 1179656 | tf_op jit(solution)/shard_map/ppermute | solution.py:381
  40.5 33.1 %collective-permute-start.7 = (bf16[2,128,768]{2,1,0:T(8,128)(2,1)}, bf16[2,128,768]{2,1,0:T(8,128)(2,1)}, u32[]{:S(2)}, u32[]{:S(2)}) collective-permute-start(bf16[2,128,768]{2,1,0:T(8,128)(2,1)} %get-tuple-element.87), channel_id=1, source_target_pairs={{0,1},{1,0},{32,33},{33,32},{64,65},{65,64},{96,97},{97,96},{2,3},... | collective-permute-start | bytes 1179656 | tf_op jit(solution)/shard_map/ppermute | solution.py:381
  41.7 34.2 %collective-permute-start.8 = (bf16[2,128,768]{2,1,0:T(8,128)(2,1)}, bf16[2,128,768]{2,1,0:T(8,128)(2,1)}, u32[]{:S(2)}, u32[]{:S(2)}) collective-permute-start(bf16[2,128,768]{2,1,0:T(8,128)(2,1)} %get-tuple-element.89), channel_id=1, source_target_pairs={{0,32},{1,33},{32,64},{33,65},{64,96},{65,97},{96,0},{97,1},{2,34}... | collective-permute-start | bytes 1179656 | tf_op jit(solution)/shard_map/ppermute | solution.py:381
  56.3 19.6 %collective-permute-start.9 = (bf16[2,128,768]{2,1,0:T(8,128)(2,1)}, bf16[2,128,768]{2,1,0:T(8,128)(2,1)}, u32[]{:S(2)}, u32[]{:S(2)}) collective-permute-start(bf16[2,128,768]{2,1,0:T(8,128)(2,1)} %get-tuple-element.90), channel_id=1, source_target_pairs={{0,96},{1,97},{32,0},{33,1},{64,32},{65,33},{96,64},{97,65},{2,98}... | collective-permute-start | bytes 1179656 | tf_op jit(solution)/shard_map/ppermute | solution.py:381
  58.8 26.8 %collective-permute-start.10 = (bf16[2,128,768]{2,1,0:T(8,128)(2,1)}, bf16[2,128,768]{2,1,0:T(8,128)(2,1)}, u32[]{:S(2)}, u32[]{:S(2)}) collective-permute-start(bf16[2,128,768]{2,1,0:T(8,128)(2,1)} %get-tuple-element.91), channel_id=1, source_target_pairs={{0,64},{1,65},{32,96},{33,97},{64,0},{65,1},{96,32},{97,33},{2,66}... | collective-permute-start | bytes 1179656 | tf_op jit(solution)/shard_map/ppermute | solution.py:381
  70.1 21.4 %collective-permute-start.11 = (bf16[2,128,768]{2,1,0:T(8,128)(2,1)S(1)}, bf16[2,128,768]{2,1,0:T(8,128)(2,1)S(1)}, u32[]{:S(2)}, u32[]{:S(2)}) collective-permute-start(bf16[2,128,768]{2,1,0:T(8,128)(2,1)S(1)} %copy-done.11), channel_id=1, source_target_pairs={{0,33},{1,32},{32,65},{33,64},{64,97},{65,96},{96,1},{97,0},{2,35}... | collective-permute-start | bytes 1179656 | tf_op jit(solution)/shard_map/ppermute | solution.py:381
  73.6 18.0 %collective-permute-start.12 = (bf16[2,128,768]{2,1,0:T(8,128)(2,1)S(1)}, bf16[2,128,768]{2,1,0:T(8,128)(2,1)S(1)}, u32[]{:S(2)}, u32[]{:S(2)}) collective-permute-start(bf16[2,128,768]{2,1,0:T(8,128)(2,1)S(1)} %copy-done.10), channel_id=1, source_target_pairs={{0,97},{1,96},{32,1},{33,0},{64,33},{65,32},{96,65},{97,64},{2,99}... | collective-permute-start | bytes 1179656 | tf_op jit(solution)/shard_map/ppermute | solution.py:381
  75.9 15.7 %collective-permute-start.13 = (bf16[2,128,768]{2,1,0:T(8,128)(2,1)S(1)}, bf16[2,128,768]{2,1,0:T(8,128)(2,1)S(1)}, u32[]{:S(2)}, u32[]{:S(2)}) collective-permute-start(bf16[2,128,768]{2,1,0:T(8,128)(2,1)S(1)} %copy-done.9), channel_id=1, source_target_pairs={{0,65},{1,64},{32,97},{33,96},{64,1},{65,0},{96,33},{97,32},{2,67}... | collective-permute-start | bytes 1179656 | tf_op jit(solution)/shard_map/ppermute | solution.py:381
  75.9 15.7 %collective-permute-start.14 = (bf16[2,128,768]{2,1,0:T(8,128)(2,1)S(1)}, bf16[2,128,768]{2,1,0:T(8,128)(2,1)S(1)}, u32[]{:S(2)}, u32[]{:S(2)}) collective-permute-start(bf16[2,128,768]{2,1,0:T(8,128)(2,1)S(1)} %copy-done.8), channel_id=1, source_target_pairs={{0,1},{1,0},{32,33},{33,32},{64,65},{65,64},{96,97},{97,96},{2,3},... | collective-permute-start | bytes 1179656 | tf_op jit(solution)/shard_map/ppermute | solution.py:381
  97.0 10.2 %all-to-all-start.1 = ((f32[8,1,128]{2,1,0:T(1,128)}), f32[8,1,128]{2,1,0:T(1,128)S(1)}, u32[]{:S(2)}, u32[]{:S(2)}) async-start(f32[8,1,128]{2,1,0:T(1,128)} %bitcast.55), calls=%async_computation.1 | async-start | bytes 8192 | tf_op jit(solution)/shard_map/all_to_all | solution.py:424
  112.0 11.8 %collective-permute-start.21 = (bf16[4,48,768]{2,1,0:T(8,128)(2,1)}, bf16[4,48,768]{2,1,0:T(8,128)(2,1)S(1)}, u32[]{:S(2)}, u32[]{:S(2)}) collective-permute-start(bf16[4,48,768]{2,1,0:T(8,128)(2,1)} %get-tuple-element.110), channel_id=1, source_target_pairs={{0,8},{8,16},{16,24},{24,0},{1,9},{9,17},{17,25},{25,1},{2,10},{10... | collective-permute-start | bytes 884744 | tf_op jit(solution)/shard_map/ppermute | solution.py:349
  113.7 11.8 %collective-permute-start.22 = (bf16[4,48,768]{2,1,0:T(8,128)(2,1)}, bf16[4,48,768]{2,1,0:T(8,128)(2,1)S(1)}, u32[]{:S(2)}, u32[]{:S(2)}) collective-permute-start(bf16[4,48,768]{2,1,0:T(8,128)(2,1)} %get-tuple-element.111), channel_id=1, source_target_pairs={{0,24},{8,0},{16,8},{24,16},{1,25},{9,1},{17,9},{25,17},{2,26},{10... | collective-permute-start | bytes 884744 | tf_op jit(solution)/shard_map/ppermute | solution.py:349
  115.0 14.0 %collective-permute-start.23 = (bf16[4,48,768]{2,1,0:T(8,128)(2,1)}, bf16[4,48,768]{2,1,0:T(8,128)(2,1)S(1)}, u32[]{:S(2)}, u32[]{:S(2)}) collective-permute-start(bf16[4,48,768]{2,1,0:T(8,128)(2,1)} %get-tuple-element.112), channel_id=1, source_target_pairs={{0,16},{8,24},{16,0},{24,8},{1,17},{9,25},{17,1},{25,9},{2,18},{10... | collective-permute-start | bytes 884744 | tf_op jit(solution)/shard_map/ppermute | solution.py:349
  121.0 12.0 %collective-permute-start.15 = (bf16[4,48,768]{2,1,0:T(8,128)(2,1)}, bf16[4,48,768]{2,1,0:T(8,128)(2,1)S(1)}, u32[]{:S(2)}, u32[]{:S(2)}) collective-permute-start(bf16[4,48,768]{2,1,0:T(8,128)(2,1)} %get-tuple-element.102), channel_id=1, source_target_pairs={{0,2},{2,4},{4,6},{6,0},{1,3},{3,5},{5,7},{7,1},{8,10},{10,12},{12... | collective-permute-start | bytes 884744 | tf_op jit(solution)/shard_map/ppermute | solution.py:349
  122.3 12.3 %collective-permute-start.16 = (bf16[4,48,768]{2,1,0:T(8,128)(2,1)}, bf16[4,48,768]{2,1,0:T(8,128)(2,1)S(1)}, u32[]{:S(2)}, u32[]{:S(2)}) collective-permute-start(bf16[4,48,768]{2,1,0:T(8,128)(2,1)} %get-tuple-element.103), channel_id=1, source_target_pairs={{0,6},{2,0},{4,2},{6,4},{1,7},{3,1},{5,3},{7,5},{8,14},{10,8},{12,... | collective-permute-start | bytes 884744 | tf_op jit(solution)/shard_map/ppermute | solution.py:349
  123.7 12.9 %collective-permute-start.17 = (bf16[4,48,768]{2,1,0:T(8,128)(2,1)}, bf16[4,48,768]{2,1,0:T(8,128)(2,1)S(1)}, u32[]{:S(2)}, u32[]{:S(2)}) collective-permute-start(bf16[4,48,768]{2,1,0:T(8,128)(2,1)} %get-tuple-element.104), channel_id=1, source_target_pairs={{0,4},{2,6},{4,0},{6,2},{1,5},{3,7},{5,1},{7,3},{8,12},{10,14},{12... | collective-permute-start | bytes 884744 | tf_op jit(solution)/shard_map/ppermute | solution.py:349
  129.2 9.7 %collective-permute-start.24 = (bf16[48,768]{1,0:T(8,128)(2,1)S(1)}, bf16[48,768]{1,0:T(8,128)(2,1)S(1)}, u32[]{:S(2)}, u32[]{:S(2)}) collective-permute-start(bf16[48,768]{1,0:T(8,128)(2,1)S(1)} %get-tuple-element.119), channel_id=1, source_target_pairs={{0,2},{2,4},{4,6},{6,0},{1,3},{3,5},{5,7},{7,1},{8,10},{10,12},{12... | collective-permute-start | bytes 221192 | tf_op jit(solution)/shard_map/ppermute | solution.py:349
  130.7 9.8 %collective-permute-start.26 = (bf16[48,768]{1,0:T(8,128)(2,1)S(1)}, bf16[48,768]{1,0:T(8,128)(2,1)S(1)}, u32[]{:S(2)}, u32[]{:S(2)}) collective-permute-start(bf16[48,768]{1,0:T(8,128)(2,1)S(1)} %get-tuple-element.120), channel_id=1, source_target_pairs={{0,4},{2,6},{4,0},{6,2},{1,5},{3,7},{5,1},{7,3},{8,12},{10,14},{12... | collective-permute-start | bytes 221192 | tf_op jit(solution)/shard_map/ppermute | solution.py:349
  133.0 7.5 %collective-permute-start.25 = (bf16[48,768]{1,0:T(8,128)(2,1)S(1)}, bf16[48,768]{1,0:T(8,128)(2,1)S(1)}, u32[]{:S(2)}, u32[]{:S(2)}) collective-permute-start(bf16[48,768]{1,0:T(8,128)(2,1)S(1)} %get-tuple-element.121), channel_id=1, source_target_pairs={{0,6},{2,0},{4,2},{6,4},{1,7},{3,1},{5,3},{7,5},{8,14},{10,8},{12,... | collective-permute-start | bytes 221192 | tf_op jit(solution)/shard_map/ppermute | solution.py:349
  136.8 5.3 %collective-permute-start.18 = (bf16[48,768]{1,0:T(8,128)(2,1)S(1)}, bf16[48,768]{1,0:T(8,128)(2,1)S(1)}, u32[]{:S(2)}, u32[]{:S(2)}) collective-permute-start(bf16[48,768]{1,0:T(8,128)(2,1)S(1)} %get-tuple-element.122), channel_id=1, source_target_pairs={{0,8},{8,16},{16,24},{24,0},{1,9},{9,17},{17,25},{25,1},{2,10},{10... | collective-permute-start | bytes 221192 | tf_op jit(solution)/shard_map/ppermute | solution.py:349
  137.1 4.9 %collective-permute-start.20 = (bf16[48,768]{1,0:T(8,128)(2,1)S(1)}, bf16[48,768]{1,0:T(8,128)(2,1)S(1)}, u32[]{:S(2)}, u32[]{:S(2)}) collective-permute-start(bf16[48,768]{1,0:T(8,128)(2,1)S(1)} %get-tuple-element.123), channel_id=1, source_target_pairs={{0,16},{8,24},{16,0},{24,8},{1,17},{9,25},{17,1},{25,9},{2,18},{10... | collective-permute-start | bytes 221192 | tf_op jit(solution)/shard_map/ppermute | solution.py:349
  138.9 3.7 %collective-permute-start.19 = (bf16[48,768]{1,0:T(8,128)(2,1)S(1)}, bf16[48,768]{1,0:T(8,128)(2,1)S(1)}, u32[]{:S(2)}, u32[]{:S(2)}) collective-permute-start(bf16[48,768]{1,0:T(8,128)(2,1)S(1)} %get-tuple-element.124), channel_id=1, source_target_pairs={{0,24},{8,0},{16,8},{24,16},{1,25},{9,1},{17,9},{25,17},{2,26},{10... | collective-permute-start | bytes 221192 | tf_op jit(solution)/shard_map/ppermute | solution.py:349
  142.7 6.5 %collective-permute-start.27 = (bf16[2,24,768]{2,1,0:T(8,128)(2,1)S(1)}, bf16[2,24,768]{2,1,0:T(8,128)(2,1)S(1)}, u32[]{:S(2)}, u32[]{:S(2)}) collective-permute-start(bf16[2,24,768]{2,1,0:T(8,128)(2,1)S(1)} %get-tuple-element.126), channel_id=1, source_target_pairs={{0,1},{1,0},{2,3},{3,2},{4,5},{5,4},{6,7},{7,6},{8,9},{9,8},{10,11... | collective-permute-start | bytes 221192 | tf_op jit(solution)/shard_map/ppermute | solution.py:34
  (16 other events, 107.8 us)

commit v6 on v5

--- a/solution.py
+++ b/solution.py
@@ -92,7 +92,7 @@
             ],
         ),
         compiler_params=pltpu.CompilerParams(vmem_limit_bytes=VMEM_LIMIT),
-        cost_estimate=pl.CostEstimate(flops=0, bytes_accessed=7 * 2**20, transcendentals=0),
+        cost_estimate=pl.CostEstimate(flops=12000000000, bytes_accessed=1, transcendentals=0),
         name="pack_tiles",
     )(domain, here, dfint)
 
@@ -200,11 +200,7 @@
             ],
         ),
         compiler_params=pltpu.CompilerParams(vmem_limit_bytes=VMEM_LIMIT),
-        cost_estimate=pl.CostEstimate(
-            flops=(4 if finish else 2) * count * length**3,
-            bytes_accessed=10 * count * length**2,
-            transcendentals=0,
-        ),
+        cost_estimate=pl.CostEstimate(flops=1, bytes_accessed=1, transcendentals=0),
         name="half_and_ladder" if finish else "half_ladder",
     )(domain, here, amp, before, *parts)
 
@@ -252,9 +248,7 @@
             pltpu.SemaphoreType.DMA((1,)),
         ],
         compiler_params=pltpu.CompilerParams(vmem_limit_bytes=VMEM_LIMIT),
-        cost_estimate=pl.CostEstimate(
-            flops=2 * length**3, bytes_accessed=12 * length**2, transcendentals=0
-        ),
+        cost_estimate=pl.CostEstimate(flops=1, bytes_accessed=1, transcendentals=0),
         name="ladder",
     )(ints, half, before)
 
@@ -335,9 +329,7 @@
             ],
         ),
         compiler_params=pltpu.CompilerParams(vmem_limit_bytes=VMEM_LIMIT),
-        cost_estimate=pl.CostEstimate(
-            flops=6 * length**2, bytes_accessed=12 * length**2, transcendentals=0
-        ),
+        cost_estimate=pl.CostEstimate(flops=1, bytes_accessed=1, transcendentals=0),
         name="add_cycle",
     )(here, coupling, inter, *(array for array, _ in ints), ladder_sum)
 
@@ -392,7 +384,6 @@
         here = jnp.stack([z, y, x, c])
         order = [(which, f) for which in range(each) for f in range(CORES)]
         packed = {order[0]: pack(dfint, domain, here, *order[0], quarter)}
-        packed[order[0]], amps = lax.optimization_barrier((packed[order[0]], amps))
         for key in order[1:]:
             packed[key] = pack(dfint, domain, here, *key, quarter)
         masked = masked_amps(amps, pair_mask, ((y * nx + x) * CORES + c) * own, dom)
@@ -403,7 +394,7 @@
         for key in order[:EARLY]:
             parts[key] = send(key, packed.pop(key))
         early = [parts[key][n] for key, n in FIRST]
-        early, packed, both = lax.optimization_barrier((early, packed, both))
+        early = early
         for (key, n), part in zip(FIRST, early):
             parts[key][n] = part
         for key in order[EARLY:]:

time: 151 us -> 142 us (0.940)
  waiting for transfers between devices: 39.8 us -> 13 us
  starting transfers between devices: 55.6 us -> 72 us
    ppermute x14, starting transfers between devices: 17.6 us -> 36.3 us  [send(): hop(s, key[1])(part)]
    ppermute x14, waiting for transfers between devices: 21.3 us -> 2.86 us  [send(): hop(s, key[1])(part)]
    all_to_all x1, waiting for transfers between devices: 9.63 us -> 0.01 us  [gather(): lax.all_to_all(jnp.broadcast_to(rows[None], (chips,) + rows.shape), ('y',...]
    unnamed x38 -> x30, local copies, waits for them, and re-layouts: 3.92 us -> 4.5 us
  transfers between devices with their start and end apart: 30 -> 30, of which waited for: 10 -> 8; matrix products, arithmetic and copies ran while one was open for 2% -> 4% of each run, Pallas kernels for 22% -> 25%
where the time goes in v6:
time: 142 us; the launch traced here: 141 us
  starting transfers between devices  72 us (51%)
  Pallas kernels  44.1 us (31%)
  waiting for transfers between devices  13 us (9%)
  local copies, waits for them, and re-layouts  8.89 us (6%)
  other arithmetic  2.82 us (2%)
    ppermute x14, starting transfers between devices, send(): hop(s, key[1])(part)  36.3 us
    pallas_call x3, Pallas kernels, work(): pl.pallas_call(functools.partial(work_kernel, quarter, domain.shape[1], w...  18.7 us
    ppermute x12, starting transfers between devices, sum_over(): total = total + lax.ppermute(parts[s].astype(BF16), axis, perm).astype(F32)  16.9 us
    pallas_call x4, Pallas kernels, pack(): pl.pallas_call(functools.partial(pack_kernel, quarter, dom, which, flip),...  12.7 us
    ppermute x12, waiting for transfers between devices, sum_over(): total = total + lax.ppermute(parts[s].astype(BF16), axis, perm).astype(F32)  8.94 us
    pallas_call x2, Pallas kernels, add_cycle(): pl.pallas_call(functools.partial(cycle_kernel, which, [place for _, place...  8.43 us
    ppermute x2, starting transfers between devices, swap_cores(): return lax.ppermute(value, 'c', [(0, 1), (1, 0)])  7.1 us
    all_to_all x1, starting transfers between devices, gather(): lax.all_to_all(jnp.broadcast_to(rows[None], (chips,) + rows.shape), ('y',...  6.75 us
  transfers between devices with their start and end apart: 30, of which 8 were waited for; matrix products, arithmetic and copies ran while one was open for 4% of the time, Pallas kernels for 25%

profile of v6, /device:TPU:1, one launch (start us, length us, event | category | flops | bytes accessed | tf_op | source)
XLA Modules:
  0.0 141.1 jit_solution(1634897618346149227)
XLA Ops:
  2.5 1.5 %collective-permute-start = (bf16[2,24,768]{2,1,0:T(8,128)(2,1)S(1)}, bf16[2,24,768]{2,1,0:T(8,128)(2,1)S(1)}, u32[]{:S(2)}, u32[]{:S(2)}) collective-permute-start(bf16[2,24,768]{2,1,0:T(8,128)(2,1)S(1)} %get-tuple-element.86), channel_id=1, source_target_pairs={{0,1},{1,0},{2,3},{3,2},{4,5},{5,4},{6,7},{7,6},{8,9},{9,8},{10,11... | collective-permute-start | bytes 221192 | tf_op jit(solution)/shard_map/ppermute | solution.py:34
  6.0 3.1 %pack_tiles.6 = (bf16[2,128,768]{2,1,0:T(8,128)(2,1)}, bf16[2,128,768]{2,1,0:T(8,128)(2,1)}, bf16[2,128,768]{2,1,0:T(8,128)(2,1)}, bf16[2,128,768]{2,1,0:T(8,128)(2,1)}) custom-call(s32[16,6]{1,0:T(8,128)} %copy.39.domain_ref, s32[4]{0:T(128)} %pad_add_fusion.here_ref, bf16[1,1024,4096]{2,1,0:T(8,128)(2,1)} %dfint_ref.7), custom_call_target="tpu_custom_call" | custom-call | flops 12000000000 | bytes 1 | tf_op jit(solution)/shard_map/pack_tiles/pallas_call | solution.py:80
  9.1 1.8 %collective-permute-start.8 = (bf16[2,128,768]{2,1,0:T(8,128)(2,1)}, bf16[2,128,768]{2,1,0:T(8,128)(2,1)S(1)}, u32[]{:S(2)}, u32[]{:S(2)}) collective-permute-start(bf16[2,128,768]{2,1,0:T(8,128)(2,1)} %get-tuple-element.47), channel_id=1, source_target_pairs={{0,32},{1,33},{32,64},{33,65},{64,96},{65,97},{96,0},{97,1},{2,34}... | collective-permute-start | bytes 1179656 | tf_op jit(solution)/shard_map/ppermute | solution.py:373
  10.9 2.2 %collective-permute-start.9 = (bf16[2,128,768]{2,1,0:T(8,128)(2,1)}, bf16[2,128,768]{2,1,0:T(8,128)(2,1)S(1)}, u32[]{:S(2)}, u32[]{:S(2)}) collective-permute-start(bf16[2,128,768]{2,1,0:T(8,128)(2,1)} %get-tuple-element.48), channel_id=1, source_target_pairs={{0,96},{1,97},{32,0},{33,1},{64,32},{65,33},{96,64},{97,65},{2,98}... | collective-permute-start | bytes 1179656 | tf_op jit(solution)/shard_map/ppermute | solution.py:373
  13.1 3.2 %pack_tiles.5 = (bf16[2,128,768]{2,1,0:T(8,128)(2,1)}, bf16[2,128,768]{2,1,0:T(8,128)(2,1)}, bf16[2,128,768]{2,1,0:T(8,128)(2,1)}, bf16[2,128,768]{2,1,0:T(8,128)(2,1)}) custom-call(s32[16,6]{1,0:T(8,128)} %copy.39.domain_ref, s32[4]{0:T(128)} %pad_add_fusion.here_ref, bf16[1,1024,4096]{2,1,0:T(8,128)(2,1)} %dfint_ref.7), custom_call_target="tpu_custom_call" | custom-call | flops 12000000000 | bytes 1 | tf_op jit(solution)/shard_map/pack_tiles/pallas_call | solution.py:80
  16.4 2.9 %collective-permute-start.5 = (bf16[2,128,768]{2,1,0:T(8,128)(2,1)}, bf16[2,128,768]{2,1,0:T(8,128)(2,1)}, u32[]{:S(2)}, u32[]{:S(2)}) collective-permute-start(bf16[2,128,768]{2,1,0:T(8,128)(2,1)} %get-tuple-element.43), channel_id=1, source_target_pairs={{0,97},{1,96},{32,1},{33,0},{64,33},{65,32},{96,65},{97,64},{2,99}... | collective-permute-start | bytes 1179656 | tf_op jit(solution)/shard_map/ppermute | solution.py:373
  19.8 1.6 %broadcast_in_dim.37 = bf16[16,2,48,768]{3,2,1,0:T(8,128)(2,1)} broadcast(bf16[2,48,768]{2,1,0:T(8,128)(2,1)S(1)} %maximum_select_fusion), dimensions={1,2,3} | broadcast | bytes 2506752 | tf_op jit(solution)/shard_map/broadcast_in_dim | solution.py:367
  21.5 6.8 %all-to-all-start = ((bf16[16,2,48,768]{3,2,1,0:T(8,128)(2,1)}), bf16[16,2,48,768]{3,2,1,0:T(8,128)(2,1)S(1)}, u32[]{:S(2)}, u32[]{:S(2)}) async-start(bf16[16,2,48,768]{3,2,1,0:T(8,128)(2,1)} %broadcast_in_dim.37), calls=%async_computation | async-start | bytes 4718592 | tf_op jit(solution)/shard_map/all_to_all | solution.py:366
  28.2 3.3 %pack_tiles.4 = (bf16[2,128,768]{2,1,0:T(8,128)(2,1)}, bf16[2,128,768]{2,1,0:T(8,128)(2,1)}, bf16[2,128,768]{2,1,0:T(8,128)(2,1)}, bf16[2,128,768]{2,1,0:T(8,128)(2,1)}) custom-call(s32[16,6]{1,0:T(8,128)} %copy.39.domain_ref, s32[4]{0:T(128)} %pad_add_fusion.here_ref, bf16[1,1024,4096]{2,1,0:T(8,128)(2,1)} %dfint_ref.7), custom_call_target="tpu_custom_call" | custom-call | flops 12000000000 | bytes 1 | tf_op jit(solution)/shard_map/pack_tiles/pallas_call | solution.py:80
  32.6 2.1 %collective-permute-start.2 = (bf16[2,128,768]{2,1,0:T(8,128)(2,1)}, bf16[2,128,768]{2,1,0:T(8,128)(2,1)S(1)}, u32[]{:S(2)}, u32[]{:S(2)}) collective-permute-start(bf16[2,128,768]{2,1,0:T(8,128)(2,1)} %get-tuple-element.39), channel_id=1, source_target_pairs={{0,96},{1,97},{32,0},{33,1},{64,32},{65,33},{96,64},{97,65},{2,98}... | collective-permute-start | bytes 1179656 | tf_op jit(solution)/shard_map/ppermute | solution.py:373
  34.6 6.8 %collective-permute-start.3 = (bf16[2,128,768]{2,1,0:T(8,128)(2,1)}, bf16[2,128,768]{2,1,0:T(8,128)(2,1)S(1)}, u32[]{:S(2)}, u32[]{:S(2)}) collective-permute-start(bf16[2,128,768]{2,1,0:T(8,128)(2,1)} %get-tuple-element.40), channel_id=1, source_target_pairs={{0,64},{1,65},{32,96},{33,97},{64,0},{65,1},{96,32},{97,33},{2,66}... | collective-permute-start | bytes 1179656 | tf_op jit(solution)/shard_map/ppermute | solution.py:373
  41.4 3.1 %pack_tiles.7 = (bf16[2,128,768]{2,1,0:T(8,128)(2,1)}, bf16[2,128,768]{2,1,0:T(8,128)(2,1)}, bf16[2,128,768]{2,1,0:T(8,128)(2,1)}, bf16[2,128,768]{2,1,0:T(8,128)(2,1)}) custom-call(s32[16,6]{1,0:T(8,128)} %copy.39.domain_ref, s32[4]{0:T(128)} %pad_add_fusion.here_ref, bf16[1,1024,4096]{2,1,0:T(8,128)(2,1)} %dfint_ref.7), custom_call_target="tpu_custom_call" | custom-call | flops 12000000000 | bytes 1 | tf_op jit(solution)/shard_map/pack_tiles/pallas_call | solution.py:80
  44.6 1.8 %collective-permute-start.11 = (bf16[2,128,768]{2,1,0:T(8,128)(2,1)}, bf16[2,128,768]{2,1,0:T(8,128)(2,1)S(1)}, u32[]{:S(2)}, u32[]{:S(2)}) collective-permute-start(bf16[2,128,768]{2,1,0:T(8,128)(2,1)} %get-tuple-element.52), channel_id=1, source_target_pairs={{0,33},{1,32},{32,65},{33,64},{64,97},{65,96},{96,1},{97,0},{2,35}... | collective-permute-start | bytes 1179656 | tf_op jit(solution)/shard_map/ppermute | solution.py:373
  46.8 2.8 %collective-permute-done.1.rest_0_ = bf16[2,128,768]{2,1,0:T(8,128)(2,1)S(1)} collective-permute-done((bf16[2,128,768]{2,1,0:T(8,128)(2,1)}, bf16[2,128,768]{2,1,0:T(8,128)(2,1)S(1)}, u32[]{:S(2)}, u32[]{:S(2)}) %collective-permute-start.1) | collective-permute-done | bytes 393248 | tf_op jit(solution)/shard_map/ppermute | solution.py:373
  50.4 15.9 %collective-permute-start.13 = (bf16[2,128,768]{2,1,0:T(8,128)(2,1)}, bf16[2,128,768]{2,1,0:T(8,128)(2,1)S(1)}, u32[]{:S(2)}, u32[]{:S(2)}) collective-permute-start(bf16[2,128,768]{2,1,0:T(8,128)(2,1)} %get-tuple-element.54), channel_id=1, source_target_pairs={{0,65},{1,64},{32,97},{33,96},{64,1},{65,0},{96,33},{97,32},{2,67}... | collective-permute-start | bytes 1179656 | tf_op jit(solution)/shard_map/ppermute | solution.py:373
  67.1 1.6 %fusion.14 = (bf16[16,1,48,768]{3,2,1,0:T(8,128)(2,1)}, bf16[16,1,48,768]{3,2,1,0:T(8,128)(2,1)}) fusion(bf16[16,2,48,768]{3,2,1,0:T(8,128)(2,1)S(1)} %all-to-all-done), kind=kLoop, calls=%fused_computation.39 | loop fusion | bytes 4718592 | tf_op jit(solution)/shard_map/slice | solution.py:369
  69.3 8.5 %half_and_ladder.2 = (bf16[2,768,768]{2,1,0:T(8,128)(2,1)}, f32[768,768]{1,0:T(8,128)}, f32[8,128]{1,0:T(8,128)}) custom-call(s32[16,6]{1,0:T(8,128)} %copy.39.domain_ref, s32[4]{0:T(128)} %pad_add_fusion.here_ref, bf16[768,768]{1,0:T(8,128)(2,1)} %bitcast.52, f32[8,128]{1,0:T(8,128)} %broadcast_in_dim.38.before_ref, bf16[2,128,768]{2,1,0:T(8,128)(2,1)} %copy-done.9, ...), custom_call_target="tpu_custom_call" | custom-call | flops 1 | bytes 1 | tf_op jit(solution)/shard_map/half_and_ladder/pallas_call | solution.py:178
  77.8 5.9 %half_and_ladder.3 = (bf16[1,768,768]{2,1,0:T(8,128)(2,1)}, f32[768,768]{1,0:T(8,128)}, f32[8,128]{1,0:T(8,128)}) custom-call(s32[16,6]{1,0:T(8,128)} %copy.39.domain_ref, s32[4]{0:T(128)} %pad_add_fusion.here_ref, bf16[768,768]{1,0:T(8,128)(2,1)} %bitcast.50, f32[8,128]{1,0:T(8,128)} %get-tuple-element.46.before_ref, bf16[2,128,768]{2,1,0:T(8,128)(2,1)} %copy-done.2, ...), custom_call_target="tpu_custom_call" | custom-call | flops 1 | bytes 1 | tf_op jit(solution)/shard_map/half_and_ladder/pallas_call | solution.py:178
  84.7 4.3 %half_ladder.1 = (bf16[1,768,768]{2,1,0:T(8,128)(2,1)}, bf16[1,768,768]{2,1,0:T(8,128)(2,1)}, f32[8,128]{1,0:T(8,128)}) custom-call(s32[16,6]{1,0:T(8,128)} %copy.39.domain_ref, s32[4]{0:T(128)} %pad_add_fusion.here_ref, bf16[768,768]{1,0:T(8,128)(2,1)} %bitcast.51, f32[8,128]{1,0:T(8,128)} %get-tuple-element.51.before_ref, bf16[2,128,768]{2,1,0:T(8,128)(2,1)} %copy-done.4, ...), custom_call_target="tpu_custom_call" | custom-call | flops 1 | bytes 1 | tf_op jit(solution)/shard_map/half_ladder/pallas_call | solution.py:178
  89.0 4.9 %all-to-all-start.1 = ((f32[8,1,128]{2,1,0:T(1,128)}), f32[8,1,128]{2,1,0:T(1,128)S(1)}, u32[]{:S(2)}, u32[]{:S(2)}) async-start(f32[8,1,128]{2,1,0:T(1,128)} %bitcast.55), calls=%async_computation.1 | async-start | bytes 8192 | tf_op jit(solution)/shard_map/all_to_all | solution.py:415
  94.0 4.3 %ladder.1.rest_2_ = f32[768,768]{1,0:T(8,128)} custom-call(bf16[1,768,768]{2,1,0:T(8,128)(2,1)} %get-tuple-element.64.int_ref.rest_1_, bf16[1,768,768]{2,1,0:T(8,128)(2,1)} %get-tuple-element.65.half_ref, f32[768,768]{1,0:T(8,128)} %get-tuple-element.66.before_ref), custom_call_target="tpu_custom_call" | custom-call | flops 1 | bytes 1 | tf_op jit(solution)/shard_map/ladder/pallas_call | solution.py:238
  99.2 4.2 %add_cycle.3 = (f32[4,48,768]{2,1,0:T(8,128)}, bf16[4,48,768]{2,1,0:T(8,128)(2,1)}, bf16[4,48,768]{2,1,0:T(8,128)(2,1)}, bf16[4,48,768]{2,1,0:T(8,128)(2,1)}) custom-call(s32[4]{0:T(128)} %pad_add_fusion.here_ref, f32[4,16]{1,0:T(4,128)} %coupling_ref.3, f32[8,128]{1,0:T(8,128)} %bitcast.53, bf16[1,768,768]{2,1,0:T(8,128)(2,1)} %get-tuple-element.63.rest_0_, ...), custom_call_target="tpu_custom_call" | custom-call | flops 1 | bytes 1 | tf_op jit(solution)/shard_map/add_cycle/pallas_call | solution.py:315
  104.7 1.5 %collective-permute-start.22 = (bf16[4,48,768]{2,1,0:T(8,128)(2,1)}, bf16[4,48,768]{2,1,0:T(8,128)(2,1)S(1)}, u32[]{:S(2)}, u32[]{:S(2)}) collective-permute-start(bf16[4,48,768]{2,1,0:T(8,128)(2,1)} %get-tuple-element.69), channel_id=1, source_target_pairs={{0,24},{8,0},{16,8},{24,16},{1,25},{9,1},{17,9},{25,17},{2,26},{10... | collective-permute-start | bytes 884744 | tf_op jit(solution)/shard_map/ppermute | solution.py:341
  106.2 1.6 %collective-permute-start.23 = (bf16[4,48,768]{2,1,0:T(8,128)(2,1)}, bf16[4,48,768]{2,1,0:T(8,128)(2,1)S(1)}, u32[]{:S(2)}, u32[]{:S(2)}) collective-permute-start(bf16[4,48,768]{2,1,0:T(8,128)(2,1)} %get-tuple-element.70), channel_id=1, source_target_pairs={{0,16},{8,24},{16,0},{24,8},{1,17},{9,25},{17,1},{25,9},{2,18},{10... | collective-permute-start | bytes 884744 | tf_op jit(solution)/shard_map/ppermute | solution.py:341
  107.8 4.3 %add_cycle.2 = (f32[4,48,768]{2,1,0:T(8,128)}, bf16[4,48,768]{2,1,0:T(8,128)(2,1)}, bf16[4,48,768]{2,1,0:T(8,128)(2,1)}, bf16[4,48,768]{2,1,0:T(8,128)(2,1)}) custom-call(s32[4]{0:T(128)} %pad_add_fusion.here_ref, f32[4,16]{1,0:T(4,128)} %coupling_ref.3, f32[8,128]{1,0:T(8,128)} %bitcast.54, bf16[2,768,768]{2,1,0:T(8,128)(2,1)} %get-tuple-element.57.rest_0_.rest_1_, ...), custom_call_target="tpu_custom_call" | custom-call | flops 1 | bytes 1 | tf_op jit(solution)/shard_map/add_cycle/pallas_call | solution.py:315
  113.3 1.5 %collective-permute-start.16 = (bf16[4,48,768]{2,1,0:T(8,128)(2,1)}, bf16[4,48,768]{2,1,0:T(8,128)(2,1)S(1)}, u32[]{:S(2)}, u32[]{:S(2)}) collective-permute-start(bf16[4,48,768]{2,1,0:T(8,128)(2,1)} %get-tuple-element.61), channel_id=1, source_target_pairs={{0,6},{2,0},{4,2},{6,4},{1,7},{3,1},{5,3},{7,5},{8,14},{10,8},{12,... | collective-permute-start | bytes 884744 | tf_op jit(solution)/shard_map/ppermute | solution.py:341
  114.8 1.5 %collective-permute-start.17 = (bf16[4,48,768]{2,1,0:T(8,128)(2,1)}, bf16[4,48,768]{2,1,0:T(8,128)(2,1)S(1)}, u32[]{:S(2)}, u32[]{:S(2)}) collective-permute-start(bf16[4,48,768]{2,1,0:T(8,128)(2,1)} %get-tuple-element.62), channel_id=1, source_target_pairs={{0,4},{2,6},{4,0},{6,2},{1,5},{3,7},{5,1},{7,3},{8,12},{10,14},{12... | collective-permute-start | bytes 884744 | tf_op jit(solution)/shard_map/ppermute | solution.py:341
  116.4 3.9 %collective-permute-done.23 = bf16[4,48,768]{2,1,0:T(8,128)(2,1)S(1)} collective-permute-done((bf16[4,48,768]{2,1,0:T(8,128)(2,1)}, bf16[4,48,768]{2,1,0:T(8,128)(2,1)S(1)}, u32[]{:S(2)}, u32[]{:S(2)}) %collective-permute-start.23) | collective-permute-done | bytes 294944 | tf_op jit(solution)/shard_map/ppermute | solution.py:341
  121.7 2.4 %collective-permute-start.26 = (bf16[48,768]{1,0:T(8,128)(2,1)S(1)}, bf16[48,768]{1,0:T(8,128)(2,1)S(1)}, u32[]{:S(2)}, u32[]{:S(2)}) collective-permute-start(bf16[48,768]{1,0:T(8,128)(2,1)S(1)} %get-tuple-element.78), channel_id=1, source_target_pairs={{0,4},{2,6},{4,0},{6,2},{1,5},{3,7},{5,1},{7,3},{8,12},{10,14},{12... | collective-permute-start | bytes 221192 | tf_op jit(solution)/shard_map/ppermute | solution.py:341
  125.3 2.6 %collective-permute-done.17 = bf16[4,48,768]{2,1,0:T(8,128)(2,1)S(1)} collective-permute-done((bf16[4,48,768]{2,1,0:T(8,128)(2,1)}, bf16[4,48,768]{2,1,0:T(8,128)(2,1)S(1)}, u32[]{:S(2)}, u32[]{:S(2)}) %collective-permute-start.17) | collective-permute-done | bytes 294944 | tf_op jit(solution)/shard_map/ppermute | solution.py:341
  128.5 1.6 %collective-permute-start.20 = (bf16[48,768]{1,0:T(8,128)(2,1)S(1)}, bf16[48,768]{1,0:T(8,128)(2,1)S(1)}, u32[]{:S(2)}, u32[]{:S(2)}) collective-permute-start(bf16[48,768]{1,0:T(8,128)(2,1)S(1)} %get-tuple-element.81), channel_id=1, source_target_pairs={{0,16},{8,24},{16,0},{24,8},{1,17},{9,25},{17,1},{25,9},{2,18},{10... | collective-permute-start | bytes 221192 | tf_op jit(solution)/shard_map/ppermute | solution.py:341
  133.9 5.6 %collective-permute-start.27 = (bf16[2,24,768]{2,1,0:T(8,128)(2,1)S(1)}, bf16[2,24,768]{2,1,0:T(8,128)(2,1)S(1)}, u32[]{:S(2)}, u32[]{:S(2)}) collective-permute-start(bf16[2,24,768]{2,1,0:T(8,128)(2,1)S(1)} %get-tuple-element.84), channel_id=1, source_target_pairs={{0,1},{1,0},{2,3},{3,2},{4,5},{5,4},{6,7},{7,6},{8,9},{9,8},{10,11... | collective-permute-start | bytes 221192 | tf_op jit(solution)/shard_map/ppermute | solution.py:34
  (90 shorter events, 21.7 us)
Async XLA Ops:
  2.5 16.9 %collective-permute-start = (bf16[2,24,768]{2,1,0:T(8,128)(2,1)S(1)}, bf16[2,24,768]{2,1,0:T(8,128)(2,1)S(1)}, u32[]{:S(2)}, u32[]{:S(2)}) collective-permute-start(bf16[2,24,768]{2,1,0:T(8,128)(2,1)S(1)} %get-tuple-element.86), channel_id=1, source_target_pairs={{0,1},{1,0},{2,3},{3,2},{4,5},{5,4},{6,7},{7,6},{8,9},{9,8},{10,11... | collective-permute-start | bytes 221192 | tf_op jit(solution)/shard_map/ppermute | solution.py:34
  9.1 22.4 %collective-permute-start.8 = (bf16[2,128,768]{2,1,0:T(8,128)(2,1)}, bf16[2,128,768]{2,1,0:T(8,128)(2,1)S(1)}, u32[]{:S(2)}, u32[]{:S(2)}) collective-permute-start(bf16[2,128,768]{2,1,0:T(8,128)(2,1)} %get-tuple-element.47), channel_id=1, source_target_pairs={{0,32},{1,33},{32,64},{33,65},{64,96},{65,97},{96,0},{97,1},{2,34}... | collective-permute-start | bytes 1179656 | tf_op jit(solution)/shard_map/ppermute | solution.py:373
  10.9 21.1 %collective-permute-start.9 = (bf16[2,128,768]{2,1,0:T(8,128)(2,1)}, bf16[2,128,768]{2,1,0:T(8,128)(2,1)S(1)}, u32[]{:S(2)}, u32[]{:S(2)}) collective-permute-start(bf16[2,128,768]{2,1,0:T(8,128)(2,1)} %get-tuple-element.48), channel_id=1, source_target_pairs={{0,96},{1,97},{32,0},{33,1},{64,32},{65,33},{96,64},{97,65},{2,98}... | collective-permute-start | bytes 1179656 | tf_op jit(solution)/shard_map/ppermute | solution.py:373
  16.3 16.3 %collective-permute-start.4 = (bf16[2,128,768]{2,1,0:T(8,128)(2,1)}, bf16[2,128,768]{2,1,0:T(8,128)(2,1)S(1)}, u32[]{:S(2)}, u32[]{:S(2)}) collective-permute-start(bf16[2,128,768]{2,1,0:T(8,128)(2,1)} %get-tuple-element.42), channel_id=1, source_target_pairs={{0,33},{1,32},{32,65},{33,64},{64,97},{65,96},{96,1},{97,0},{2,35}... | collective-permute-start | bytes 1179656 | tf_op jit(solution)/shard_map/ppermute | solution.py:373
  16.4 18.3 %collective-permute-start.5 = (bf16[2,128,768]{2,1,0:T(8,128)(2,1)}, bf16[2,128,768]{2,1,0:T(8,128)(2,1)}, u32[]{:S(2)}, u32[]{:S(2)}) collective-permute-start(bf16[2,128,768]{2,1,0:T(8,128)(2,1)} %get-tuple-element.43), channel_id=1, source_target_pairs={{0,97},{1,96},{32,1},{33,0},{64,33},{65,32},{96,65},{97,64},{2,99}... | collective-permute-start | bytes 1179656 | tf_op jit(solution)/shard_map/ppermute | solution.py:373
  19.3 25.3 %collective-permute-start.6 = (bf16[2,128,768]{2,1,0:T(8,128)(2,1)}, bf16[2,128,768]{2,1,0:T(8,128)(2,1)}, u32[]{:S(2)}, u32[]{:S(2)}) collective-permute-start(bf16[2,128,768]{2,1,0:T(8,128)(2,1)} %get-tuple-element.44), channel_id=1, source_target_pairs={{0,65},{1,64},{32,97},{33,96},{64,1},{65,0},{96,33},{97,32},{2,67}... | collective-permute-start | bytes 1179656 | tf_op jit(solution)/shard_map/ppermute | solution.py:373
  21.5 45.6 %all-to-all-start = ((bf16[16,2,48,768]{3,2,1,0:T(8,128)(2,1)}), bf16[16,2,48,768]{3,2,1,0:T(8,128)(2,1)S(1)}, u32[]{:S(2)}, u32[]{:S(2)}) async-start(bf16[16,2,48,768]{3,2,1,0:T(8,128)(2,1)} %broadcast_in_dim.37), calls=%async_computation | async-start | bytes 4718592 | tf_op jit(solution)/shard_map/all_to_all | solution.py:366
  31.5 14.9 %collective-permute-start.7 = (bf16[2,128,768]{2,1,0:T(8,128)(2,1)S(1)}, bf16[2,128,768]{2,1,0:T(8,128)(2,1)S(1)}, u32[]{:S(2)}, u32[]{:S(2)}) collective-permute-start(bf16[2,128,768]{2,1,0:T(8,128)(2,1)S(1)} %copy-done.13), channel_id=1, source_target_pairs={{0,1},{1,0},{32,33},{33,32},{64,65},{65,64},{96,97},{97,96},{2,3},... | collective-permute-start | bytes 1179656 | tf_op jit(solution)/shard_map/ppermute | solution.py:373
  32.0 17.6 %collective-permute-start.1 = (bf16[2,128,768]{2,1,0:T(8,128)(2,1)}, bf16[2,128,768]{2,1,0:T(8,128)(2,1)S(1)}, u32[]{:S(2)}, u32[]{:S(2)}) collective-permute-start(bf16[2,128,768]{2,1,0:T(8,128)(2,1)} %get-tuple-element.38), channel_id=1, source_target_pairs={{0,32},{1,33},{32,64},{33,65},{64,96},{65,97},{96,0},{97,1},{2,34}... | collective-permute-start | bytes 1179656 | tf_op jit(solution)/shard_map/ppermute | solution.py:373
  32.6 17.8 %collective-permute-start.2 = (bf16[2,128,768]{2,1,0:T(8,128)(2,1)}, bf16[2,128,768]{2,1,0:T(8,128)(2,1)S(1)}, u32[]{:S(2)}, u32[]{:S(2)}) collective-permute-start(bf16[2,128,768]{2,1,0:T(8,128)(2,1)} %get-tuple-element.39), channel_id=1, source_target_pairs={{0,96},{1,97},{32,0},{33,1},{64,32},{65,33},{96,64},{97,65},{2,98}... | collective-permute-start | bytes 1179656 | tf_op jit(solution)/shard_map/ppermute | solution.py:373
  34.6 31.7 %collective-permute-start.3 = (bf16[2,128,768]{2,1,0:T(8,128)(2,1)}, bf16[2,128,768]{2,1,0:T(8,128)(2,1)S(1)}, u32[]{:S(2)}, u32[]{:S(2)}) collective-permute-start(bf16[2,128,768]{2,1,0:T(8,128)(2,1)} %get-tuple-element.40), channel_id=1, source_target_pairs={{0,64},{1,65},{32,96},{33,97},{64,0},{65,1},{96,32},{97,33},{2,66}... | collective-permute-start | bytes 1179656 | tf_op jit(solution)/shard_map/ppermute | solution.py:373
  44.6 39.1 %collective-permute-start.11 = (bf16[2,128,768]{2,1,0:T(8,128)(2,1)}, bf16[2,128,768]{2,1,0:T(8,128)(2,1)S(1)}, u32[]{:S(2)}, u32[]{:S(2)}) collective-permute-start(bf16[2,128,768]{2,1,0:T(8,128)(2,1)} %get-tuple-element.52), channel_id=1, source_target_pairs={{0,33},{1,32},{32,65},{33,64},{64,97},{65,96},{96,1},{97,0},{2,35}... | collective-permute-start | bytes 1179656 | tf_op jit(solution)/shard_map/ppermute | solution.py:373
  46.4 19.9 %copy-start.8 = (bf16[2,128,768]{2,1,0:T(8,128)(2,1)}, bf16[2,128,768]{2,1,0:T(8,128)(2,1)S(1)}, u32[]{:S(2)}) copy-start(bf16[2,128,768]{2,1,0:T(8,128)(2,1)S(1)} %collective-permute-done.7.rest_7_) | copy-start | bytes 1179652
  46.4 31.3 %collective-permute-start.10 = (bf16[2,128,768]{2,1,0:T(8,128)(2,1)}, bf16[2,128,768]{2,1,0:T(8,128)(2,1)}, u32[]{:S(2)}, u32[]{:S(2)}) collective-permute-start(bf16[2,128,768]{2,1,0:T(8,128)(2,1)} %get-tuple-element.49), channel_id=1, source_target_pairs={{0,64},{1,65},{32,96},{33,97},{64,0},{65,1},{96,32},{97,33},{2,66}... | collective-permute-start | bytes 1179656 | tf_op jit(solution)/shard_map/ppermute | solution.py:373
  49.6 16.7 %copy-start.9 = (bf16[2,128,768]{2,1,0:T(8,128)(2,1)}, bf16[2,128,768]{2,1,0:T(8,128)(2,1)S(1)}, u32[]{:S(2)}) copy-start(bf16[2,128,768]{2,1,0:T(8,128)(2,1)S(1)} %collective-permute-done.1.rest_0_) | copy-start | bytes 1179652
  49.6 34.1 %collective-permute-start.12 = (bf16[2,128,768]{2,1,0:T(8,128)(2,1)}, bf16[2,128,768]{2,1,0:T(8,128)(2,1)S(1)}, u32[]{:S(2)}, u32[]{:S(2)}) collective-permute-start(bf16[2,128,768]{2,1,0:T(8,128)(2,1)} %get-tuple-element.53), channel_id=1, source_target_pairs={{0,97},{1,96},{32,1},{33,0},{64,33},{65,32},{96,65},{97,64},{2,99}... | collective-permute-start | bytes 1179656 | tf_op jit(solution)/shard_map/ppermute | solution.py:373
  50.4 33.4 %collective-permute-start.13 = (bf16[2,128,768]{2,1,0:T(8,128)(2,1)}, bf16[2,128,768]{2,1,0:T(8,128)(2,1)S(1)}, u32[]{:S(2)}, u32[]{:S(2)}) collective-permute-start(bf16[2,128,768]{2,1,0:T(8,128)(2,1)} %get-tuple-element.54), channel_id=1, source_target_pairs={{0,65},{1,64},{32,97},{33,96},{64,1},{65,0},{96,33},{97,32},{2,67}... | collective-permute-start | bytes 1179656 | tf_op jit(solution)/shard_map/ppermute | solution.py:373
  67.1 16.7 %collective-permute-start.14 = (bf16[2,128,768]{2,1,0:T(8,128)(2,1)}, bf16[2,128,768]{2,1,0:T(8,128)(2,1)}, u32[]{:S(2)}, u32[]{:S(2)}) collective-permute-start(bf16[2,128,768]{2,1,0:T(8,128)(2,1)} %get-tuple-element.55), channel_id=1, source_target_pairs={{0,1},{1,0},{32,33},{33,32},{64,65},{65,64},{96,97},{97,96},{2,3},... | collective-permute-start | bytes 1179656 | tf_op jit(solution)/shard_map/ppermute | solution.py:373
  89.0 9.5 %all-to-all-start.1 = ((f32[8,1,128]{2,1,0:T(1,128)}), f32[8,1,128]{2,1,0:T(1,128)S(1)}, u32[]{:S(2)}, u32[]{:S(2)}) async-start(f32[8,1,128]{2,1,0:T(1,128)} %bitcast.55), calls=%async_computation.1 | async-start | bytes 8192 | tf_op jit(solution)/shard_map/all_to_all | solution.py:415
  103.3 11.5 %collective-permute-start.21 = (bf16[4,48,768]{2,1,0:T(8,128)(2,1)}, bf16[4,48,768]{2,1,0:T(8,128)(2,1)S(1)}, u32[]{:S(2)}, u32[]{:S(2)}) collective-permute-start(bf16[4,48,768]{2,1,0:T(8,128)(2,1)} %get-tuple-element.68), channel_id=1, source_target_pairs={{0,8},{8,16},{16,24},{24,0},{1,9},{9,17},{17,25},{25,1},{2,10},{10... | collective-permute-start | bytes 884744 | tf_op jit(solution)/shard_map/ppermute | solution.py:341
  104.7 11.7 %collective-permute-start.22 = (bf16[4,48,768]{2,1,0:T(8,128)(2,1)}, bf16[4,48,768]{2,1,0:T(8,128)(2,1)S(1)}, u32[]{:S(2)}, u32[]{:S(2)}) collective-permute-start(bf16[4,48,768]{2,1,0:T(8,128)(2,1)} %get-tuple-element.69), channel_id=1, source_target_pairs={{0,24},{8,0},{16,8},{24,16},{1,25},{9,1},{17,9},{25,17},{2,26},{10... | collective-permute-start | bytes 884744 | tf_op jit(solution)/shard_map/ppermute | solution.py:341
  106.2 14.0 %collective-permute-start.23 = (bf16[4,48,768]{2,1,0:T(8,128)(2,1)}, bf16[4,48,768]{2,1,0:T(8,128)(2,1)S(1)}, u32[]{:S(2)}, u32[]{:S(2)}) collective-permute-start(bf16[4,48,768]{2,1,0:T(8,128)(2,1)} %get-tuple-element.70), channel_id=1, source_target_pairs={{0,16},{8,24},{16,0},{24,8},{1,17},{9,25},{17,1},{25,9},{2,18},{10... | collective-permute-start | bytes 884744 | tf_op jit(solution)/shard_map/ppermute | solution.py:341
  112.1 12.0 %collective-permute-start.15 = (bf16[4,48,768]{2,1,0:T(8,128)(2,1)}, bf16[4,48,768]{2,1,0:T(8,128)(2,1)S(1)}, u32[]{:S(2)}, u32[]{:S(2)}) collective-permute-start(bf16[4,48,768]{2,1,0:T(8,128)(2,1)} %get-tuple-element.60), channel_id=1, source_target_pairs={{0,2},{2,4},{4,6},{6,0},{1,3},{3,5},{5,7},{7,1},{8,10},{10,12},{12... | collective-permute-start | bytes 884744 | tf_op jit(solution)/shard_map/ppermute | solution.py:341
  113.3 11.9 %collective-permute-start.16 = (bf16[4,48,768]{2,1,0:T(8,128)(2,1)}, bf16[4,48,768]{2,1,0:T(8,128)(2,1)S(1)}, u32[]{:S(2)}, u32[]{:S(2)}) collective-permute-start(bf16[4,48,768]{2,1,0:T(8,128)(2,1)} %get-tuple-element.61), channel_id=1, source_target_pairs={{0,6},{2,0},{4,2},{6,4},{1,7},{3,1},{5,3},{7,5},{8,14},{10,8},{12,... | collective-permute-start | bytes 884744 | tf_op jit(solution)/shard_map/ppermute | solution.py:341
  114.8 13.0 %collective-permute-start.17 = (bf16[4,48,768]{2,1,0:T(8,128)(2,1)}, bf16[4,48,768]{2,1,0:T(8,128)(2,1)S(1)}, u32[]{:S(2)}, u32[]{:S(2)}) collective-permute-start(bf16[4,48,768]{2,1,0:T(8,128)(2,1)} %get-tuple-element.62), channel_id=1, source_target_pairs={{0,4},{2,6},{4,0},{6,2},{1,5},{3,7},{5,1},{7,3},{8,12},{10,14},{12... | collective-permute-start | bytes 884744 | tf_op jit(solution)/shard_map/ppermute | solution.py:341
  120.4 9.7 %collective-permute-start.24 = (bf16[48,768]{1,0:T(8,128)(2,1)S(1)}, bf16[48,768]{1,0:T(8,128)(2,1)S(1)}, u32[]{:S(2)}, u32[]{:S(2)}) collective-permute-start(bf16[48,768]{1,0:T(8,128)(2,1)S(1)} %get-tuple-element.77), channel_id=1, source_target_pairs={{0,2},{2,4},{4,6},{6,0},{1,3},{3,5},{5,7},{7,1},{8,10},{10,12},{12... | collective-permute-start | bytes 221192 | tf_op jit(solution)/shard_map/ppermute | solution.py:341
  121.7 9.7 %collective-permute-start.26 = (bf16[48,768]{1,0:T(8,128)(2,1)S(1)}, bf16[48,768]{1,0:T(8,128)(2,1)S(1)}, u32[]{:S(2)}, u32[]{:S(2)}) collective-permute-start(bf16[48,768]{1,0:T(8,128)(2,1)S(1)} %get-tuple-element.78), channel_id=1, source_target_pairs={{0,4},{2,6},{4,0},{6,2},{1,5},{3,7},{5,1},{7,3},{8,12},{10,14},{12... | collective-permute-start | bytes 221192 | tf_op jit(solution)/shard_map/ppermute | solution.py:341
  124.1 7.2 %collective-permute-start.25 = (bf16[48,768]{1,0:T(8,128)(2,1)S(1)}, bf16[48,768]{1,0:T(8,128)(2,1)S(1)}, u32[]{:S(2)}, u32[]{:S(2)}) collective-permute-start(bf16[48,768]{1,0:T(8,128)(2,1)S(1)} %get-tuple-element.79), channel_id=1, source_target_pairs={{0,6},{2,0},{4,2},{6,4},{1,7},{3,1},{5,3},{7,5},{8,14},{10,8},{12,... | collective-permute-start | bytes 221192 | tf_op jit(solution)/shard_map/ppermute | solution.py:341
  128.0 4.8 %collective-permute-start.18 = (bf16[48,768]{1,0:T(8,128)(2,1)S(1)}, bf16[48,768]{1,0:T(8,128)(2,1)S(1)}, u32[]{:S(2)}, u32[]{:S(2)}) collective-permute-start(bf16[48,768]{1,0:T(8,128)(2,1)S(1)} %get-tuple-element.80), channel_id=1, source_target_pairs={{0,8},{8,16},{16,24},{24,0},{1,9},{9,17},{17,25},{25,1},{2,10},{10... | collective-permute-start | bytes 221192 | tf_op jit(solution)/shard_map/ppermute | solution.py:341
  128.5 4.8 %collective-permute-start.20 = (bf16[48,768]{1,0:T(8,128)(2,1)S(1)}, bf16[48,768]{1,0:T(8,128)(2,1)S(1)}, u32[]{:S(2)}, u32[]{:S(2)}) collective-permute-start(bf16[48,768]{1,0:T(8,128)(2,1)S(1)} %get-tuple-element.81), channel_id=1, source_target_pairs={{0,16},{8,24},{16,0},{24,8},{1,17},{9,25},{17,1},{25,9},{2,18},{10... | collective-permute-start | bytes 221192 | tf_op jit(solution)/shard_map/ppermute | solution.py:341
  130.1 3.8 %collective-permute-start.19 = (bf16[48,768]{1,0:T(8,128)(2,1)S(1)}, bf16[48,768]{1,0:T(8,128)(2,1)S(1)}, u32[]{:S(2)}, u32[]{:S(2)}) collective-permute-start(bf16[48,768]{1,0:T(8,128)(2,1)S(1)} %get-tuple-element.82), channel_id=1, source_target_pairs={{0,24},{8,0},{16,8},{24,16},{1,25},{9,1},{17,9},{25,17},{2,26},{10... | collective-permute-start | bytes 221192 | tf_op jit(solution)/shard_map/ppermute | solution.py:341
  133.9 6.5 %collective-permute-start.27 = (bf16[2,24,768]{2,1,0:T(8,128)(2,1)S(1)}, bf16[2,24,768]{2,1,0:T(8,128)(2,1)S(1)}, u32[]{:S(2)}, u32[]{:S(2)}) collective-permute-start(bf16[2,24,768]{2,1,0:T(8,128)(2,1)S(1)} %get-tuple-element.84), channel_id=1, source_target_pairs={{0,1},{1,0},{2,3},{3,2},{4,5},{5,4},{6,7},{7,6},{8,9},{9,8},{10,11... | collective-permute-start | bytes 221192 | tf_op jit(solution)/shard_map/ppermute | solution.py:34
  (12 other events, 89.1 us)

commit v7 on v6

v7 whole, which is shorter than its diff:
```python
import functools

import jax
import jax.numpy as jnp
from jax import lax
from jax.experimental import pallas as pl
from jax.experimental.pallas import tpu as pltpu
from jax.sharding import Mesh
from jax.sharding import PartitionSpec as P

TB = 128
BLOCKS = 4
RING = 4
CORES = 2
SLOTS = 2
VMEM_LIMIT = 56 * 2**20
BF16 = jnp.bfloat16
F32 = jnp.float32
NT = (((1,), (1,)), ((), ()))
SHIFTS = (1, 3, 2, 0)


def hop(shift, flip):
    perm = [
        (z * CORES + c, (z + shift) % BLOCKS * CORES + (c ^ flip))
        for z in range(BLOCKS)
        for c in range(CORES)
    ]
    return functools.partial(lax.ppermute, axis_name=("z", "c"), perm=perm)


def swap_cores(value):
    return lax.ppermute(value, "c", [(0, 1), (1, 0)])


def block_slots(scalars_ref, pair, block, quarter, dom):
    found = jnp.int32(0)
    first = jnp.int32(0)
    second = jnp.int32(0)
    for s in range(dom):
        inside = scalars_ref[pair * dom + s] // quarter == block
        first = jnp.where(inside & (found == 0), s, first)
        second = jnp.where(inside & (found == 1), s, second)
        found = found + inside.astype(jnp.int32)
    return first, second


def pack_kernel(quarter, dom, which, flip, scalars_ref, dfint_ref, *rest):
    count = len(SHIFTS)
    outs, (buffer, in_sem, out_sem) = rest[:count], rest[count:]
    here, core = (scalars_ref[scalars_ref.shape[0] - n] for n in (4, 1))
    for n, shift in enumerate(SHIFTS):
        target = lax.rem(here + shift, BLOCKS)
        pair = (target * CORES + (core ^ flip)) * CORES + which
        for j, slot in enumerate(block_slots(scalars_ref, pair, here, quarter, dom)):
            row = jnp.clip(scalars_ref[pair * dom + slot] - here * quarter, 0, quarter - 1)
            for t in range(dom):
                column = scalars_ref[pair * dom + t]
                pltpu.make_async_copy(
                    dfint_ref.at[
                        0,
                        pl.ds(pl.multiple_of(row * TB, TB), TB),
                        pl.ds(pl.multiple_of(column * TB, TB), TB),
                    ],
                    buffer.at[n, j, :, pl.ds(t * TB, TB)],
                    in_sem.at[n],
                ).start()
    for n in range(count):
        pltpu.make_async_copy(buffer.at[n], buffer.at[n], in_sem.at[n]).wait()
        pltpu.make_async_copy(buffer.at[n], outs[n], out_sem.at[n]).start()
    for n in range(count):
        pltpu.make_async_copy(buffer.at[n], outs[n], out_sem.at[n]).wait()


def pack(dfint, scalars, which, flip, quarter, dom):
    count = len(SHIFTS)
    tile_rows = (SLOTS, TB, dom * TB)
    return pl.pallas_call(
        functools.partial(pack_kernel, quarter, dom, which, flip),
        out_shape=[jax.ShapeDtypeStruct(tile_rows, BF16)] * count,
        grid_spec=pltpu.PrefetchScalarGridSpec(
            num_scalar_prefetch=1,
            grid=(1,),
            in_specs=[pl.BlockSpec(memory_space=pl.ANY)],
            out_specs=[pl.BlockSpec(memory_space=pl.ANY)] * count,
            scratch_shapes=[
                pltpu.VMEM((count,) + tile_rows, BF16),
                pltpu.SemaphoreType.DMA((count,)),
                pltpu.SemaphoreType.DMA((count,)),
            ],
        ),
        compiler_params=pltpu.CompilerParams(vmem_limit_bytes=VMEM_LIMIT),
        cost_estimate=pl.CostEstimate(flops=12000000000, bytes_accessed=1, transcendentals=0),
        name="pack_tiles",
    )(scalars, dfint)


def work_kernel(quarter, dom, jobs, finish, first, scalars_ref, amp_ref, *rest):
    count = len(SHIFTS)
    slots = [(which, flip) for which, flips in jobs for flip in flips]
    before_ref, rest = (None, rest) if first else (rest[0], rest[1:])
    parts, rest = rest[: count * len(slots)], rest[count * len(slots) :]
    int_out, results, inter_out = rest[0], rest[1 : 1 + len(jobs)], rest[1 + len(jobs)]
    amp, ints, half, ladder, inter_ref, amp_sem, in_sem, out_sem, small_sem = rest[2 + len(jobs) :]
    here, core = (scalars_ref[scalars_ref.shape[0] - n] for n in (4, 1))
    chip_rows = amp_ref.shape[2]
    if not first:
        load_inter = pltpu.make_async_copy(before_ref, inter_ref, small_sem.at[0])
        load_inter.start()
    slot = 0
    for job, (which, flips) in enumerate(jobs):
        for chip in range(amp_ref.shape[0]):
            pltpu.make_async_copy(
                amp_ref.at[chip, which],
                amp.at[job, pl.ds(chip * chip_rows, chip_rows), :],
                amp_sem.at[job],
            ).start()
        pair = (here * CORES + core) * CORES + which
        for s in range(dom):
            owner = scalars_ref[pair * dom + s] // quarter
            rank = jnp.int32(0)
            for earlier in range(s):
                rank = rank + (scalars_ref[pair * dom + earlier] // quarter == owner).astype(jnp.int32)
            shift = lax.rem(here - owner + BLOCKS, BLOCKS)
            for n, flow_shift in enumerate(SHIFTS):

                @pl.when(shift == flow_shift)
                def _(n=n, rank=rank, s=s, slot=slot, flips=flips):
                    for f in range(len(flips)):
                        pltpu.make_async_copy(
                            parts[(slot + f) * count + n].at[rank],
                            ints.at[slot + f, pl.ds(s * TB, TB), :],
                            in_sem.at[slot + f],
                        ).start()

        slot += len(flips)
    rows = 2 * TB
    diagonal = lax.broadcasted_iota(jnp.int32, (rows, rows), 0) == lax.broadcasted_iota(
        jnp.int32, (rows, rows), 1
    )
    traces = []
    slot = 0
    for job, (which, flips) in enumerate(jobs):
        pltpu.make_async_copy(amp.at[job], amp.at[job], amp_sem.at[job]).wait()
        for f, flip in enumerate(flips):
            place = slot + f
            pltpu.make_async_copy(ints.at[place], ints.at[place], in_sem.at[place]).wait()
            pltpu.make_async_copy(ints.at[place], int_out.at[place], out_sem.at[place]).start()
            total = jnp.zeros((rows, rows), F32)
            for r in range(0, dom * TB, rows):
                spot = pl.ds(r, rows)
                acc = lax.dot_general(ints[place, spot, :], amp[job], NT, preferred_element_type=F32)
                half[place, spot, :] = acc.astype(BF16)
                total = total + acc[:, r : r + rows]
                if not finish:
                    pltpu.make_async_copy(
                        half.at[place, spot, :], results[job].at[f, spot, :], out_sem.at[len(slots) + job]
                    ).start()
            traces.append((which * CORES + flip, jnp.sum(jnp.where(diagonal, total, 0.0))))
        if finish:
            for r in range(0, dom * TB, rows):
                spot = pl.ds(r, rows)
                acc = None
                for place in range(slot, slot + len(flips)):
                    term = lax.dot_general(
                        ints[place, spot, :], half[place], NT, preferred_element_type=F32
                    )
                    acc = term if acc is None else acc + term
                ladder[job, spot, :] = acc
                pltpu.make_async_copy(
                    ladder.at[job, spot, :], results[job].at[spot, :], out_sem.at[len(slots) + job]
                ).start()
        slot += len(flips)
    if first:
        inter = jnp.zeros(inter_ref.shape, F32)
    else:
        load_inter.wait()
        inter = inter_ref[...]
    lane = lax.broadcasted_iota(jnp.int32, inter_ref.shape, 1)
    for place, trace in traces:
        inter = jnp.where(lane == place, trace, inter)
    inter_ref[...] = inter
    store_inter = pltpu.make_async_copy(inter_ref, inter_out, small_sem.at[1])
    store_inter.start()
    for place in range(len(slots)):
        pltpu.make_async_copy(ints.at[place], int_out.at[place], out_sem.at[place]).wait()
    for job in range(len(jobs)):
        done = ladder.at[job] if finish else half
        pltpu.make_async_copy(done, results[job], out_sem.at[len(slots) + job]).wait()
    store_inter.wait()


def work(amp, before, parts, scalars, jobs, finish, quarter, dom):
    length = amp.shape[-1]
    count = sum(len(flips) for _, flips in jobs)
    anywhere = pl.BlockSpec(memory_space=pl.ANY)
    squares = (count, length, length)
    inter_shape = (BLOCKS * CORES, TB)
    result = jax.ShapeDtypeStruct((length, length), F32) if finish else jax.ShapeDtypeStruct(squares, BF16)
    first = before is None
    operands = [amp] + ([] if first else [before]) + list(parts)
    return pl.pallas_call(
        functools.partial(work_kernel, quarter, dom, jobs, finish, first),
        out_shape=[jax.ShapeDtypeStruct(squares, BF16)]
        + [result] * len(jobs)
        + [jax.ShapeDtypeStruct(inter_shape, F32)],
        grid_spec=pltpu.PrefetchScalarGridSpec(
            num_scalar_prefetch=1,
            grid=(1,),
            in_specs=[anywhere] * len(operands),
            out_specs=[anywhere] * (2 + len(jobs)),
            scratch_shapes=[
                pltpu.VMEM((len(jobs), length, length), BF16),
                pltpu.VMEM(squares, BF16),
                pltpu.VMEM(squares, BF16),
                pltpu.VMEM((len(jobs), length, length) if finish else (1, 8, TB), F32),
                pltpu.VMEM(inter_shape, F32),
                pltpu.SemaphoreType.DMA((len(jobs),)),
                pltpu.SemaphoreType.DMA((count,)),
                pltpu.SemaphoreType.DMA((count + len(jobs),)),
                pltpu.SemaphoreType.DMA((2,)),
            ],
        ),
        compiler_params=pltpu.CompilerParams(vmem_limit_bytes=VMEM_LIMIT),
        cost_estimate=pl.CostEstimate(flops=1, bytes_accessed=1, transcendentals=0),
        name="half_and_ladder" if finish else "half_ladder",
    )(scalars, *operands)


def ladder_kernel(int_ref, half_ref, before_ref, out_ref, ints, half, total, in_sem, out_sem):
    length = total.shape[0]
    rows = length // 3
    spots = [pl.ds(r, rows) for r in range(0, length, rows)]
    load_half = pltpu.make_async_copy(half_ref.at[0], half, in_sem.at[0])
    load_half.start()
    loads = []
    for n, spot in enumerate(spots):
        loads.append(
            [
                pltpu.make_async_copy(int_ref.at[0, spot, :], ints.at[spot, :], in_sem.at[2 * n + 1]),
                pltpu.make_async_copy(before_ref.at[spot, :], total.at[spot, :], in_sem.at[2 * n + 2]),
            ]
        )
        for load in loads[-1]:
            load.start()
    load_half.wait()
    for spot, pair_of_loads in zip(spots, loads):
        for load in pair_of_loads:
            load.wait()
        total[spot, :] += lax.dot_general(
            ints[spot, :], half[...], NT, preferred_element_type=F32
        )
        pltpu.make_async_copy(total.at[spot, :], out_ref.at[spot, :], out_sem.at[0]).start()
    pltpu.make_async_copy(total, out_ref, out_sem.at[0]).wait()


def ladder(ints, half, before):
    length = before.shape[0]
    anywhere = pl.BlockSpec(memory_space=pl.ANY)
    return pl.pallas_call(
        ladder_kernel,
        out_shape=jax.ShapeDtypeStruct((length, length), F32),
        in_specs=[anywhere] * 3,
        out_specs=anywhere,
        scratch_shapes=[
            pltpu.VMEM((length, length), BF16),
            pltpu.VMEM((length, length), BF16),
            pltpu.VMEM((length, length), F32),
            pltpu.SemaphoreType.DMA((7,)),
            pltpu.SemaphoreType.DMA((1,)),
        ],
        compiler_params=pltpu.CompilerParams(vmem_limit_bytes=VMEM_LIMIT),
        cost_estimate=pl.CostEstimate(flops=1, bytes_accessed=1, transcendentals=0),
        name="ladder",
    )(ints, half, before)


def cycle_kernel(places, scalars_ref, coupling_ref, inter_ref, *rest):
    each = len(places)
    width = CORES + 1
    sources, rest = rest[: each * width], rest[each * width :]
    count = (len(rest) - 4) // 2
    outs, kept, (ints, ladder, in_sem, out_sem) = rest[:count], rest[count : 2 * count], rest[2 * count :]
    y, x, core = (scalars_ref[scalars_ref.shape[0] - n] for n in (3, 2, 1))
    rows = outs[0].shape[1]
    group = RING * rows
    loads = {}
    for which in range(each):
        for t in range(RING):
            spot = pl.ds(pl.multiple_of(lax.rem(y + t, RING) * group, group), group)
            sem = (which * RING + t) * width
            loads[which, t] = [
                pltpu.make_async_copy(
                    sources[which * width + f].at[places[which][f], spot, :],
                    ints.at[which, f, t],
                    in_sem.at[sem + f],
                )
                for f in range(CORES)
            ]
            loads[which, t].append(
                pltpu.make_async_copy(
                    sources[which * width + CORES].at[spot, :],
                    ladder.at[which, t],
                    in_sem.at[sem + CORES],
                )
            )
            for load in loads[which, t]:
                load.start()
    dressing = {}
    for which in range(each):
        for f in range(CORES):
            total = jnp.float32(0)
            for source in range(BLOCKS * CORES):
                flip = (source % CORES) ^ core ^ f
                for w in range(CORES):
                    total = total + coupling_ref[core * CORES + which, source * CORES + w] * (
                        inter_ref[source, w * CORES + flip]
                    )
            dressing[which, f] = total
    for which in range(each):
        for t in range(RING):
            for load in loads[which, t]:
                load.wait()
            for k in range(RING):
                spot = pl.ds(pl.multiple_of(lax.rem(x + k, RING) * rows, rows), rows)
                total = ladder[which, t, spot, :]
                for f in range(CORES):
                    total = total + dressing[which, f] * ints[which, f, t, spot, :].astype(F32)
                n, place = (k, t) if which == 0 else (RING + t, k)
                kept[n][place] = total.astype(kept[n].dtype)
                pltpu.make_async_copy(kept[n].at[place], outs[n].at[place], out_sem.at[n]).start()
    for n in range(count):
        pltpu.make_async_copy(kept[n], outs[n], out_sem.at[n]).wait()


def add_cycle(sums, blocks, inter, coupling, scalars):
    each = len(sums)
    length = sums[0].shape[0]
    rows = length // RING**2
    anywhere = pl.BlockSpec(memory_space=pl.ANY)
    shape = (RING, rows, length)
    dtypes = [BF16 if s else F32 for s in range(RING)] * each
    sources = []
    for ints, ladder_sum in zip(blocks, sums):
        sources += [array for array, _ in ints] + [ladder_sum]
    outs = pl.pallas_call(
        functools.partial(cycle_kernel, [[place for _, place in ints] for ints in blocks]),
        out_shape=[jax.ShapeDtypeStruct(shape, dtype) for dtype in dtypes],
        grid_spec=pltpu.PrefetchScalarGridSpec(
            num_scalar_prefetch=3,
            grid=(1,),
            in_specs=[anywhere] * len(sources),
            out_specs=[anywhere] * len(dtypes),
            scratch_shapes=[pltpu.VMEM(shape, dtype) for dtype in dtypes]
            + [
                pltpu.VMEM((each, CORES, RING, RING * rows, length), BF16),
                pltpu.VMEM((each, RING, RING * rows, length), F32),
                pltpu.SemaphoreType.DMA((each * RING * (CORES + 1),)),
                pltpu.SemaphoreType.DMA((len(dtypes),)),
            ],
        ),
        compiler_params=pltpu.CompilerParams(vmem_limit_bytes=VMEM_LIMIT),
        cost_estimate=pl.CostEstimate(flops=1, bytes_accessed=1, transcendentals=0),
        name="add_cycle",
    )(scalars, coupling, inter, *sources)
    return [outs[which * RING : (which + 1) * RING] for which in range(each)]


def sum_over(axis, parts):
    total = parts[0].astype(F32)
    for s in (1, 3, 2):
        perm = [(i, (i + s) % RING) for i in range(RING)]
        total = total + lax.ppermute(parts[s].astype(BF16), axis, perm).astype(F32)
    return total


def masked_amps(amps, pair_mask, first_row, dom):
    pairs, rows, length = amps.shape
    row_slot = (first_row + jnp.arange(rows, dtype=jnp.int32)) // TB
    slot_pick = row_slot[:, None] == jnp.arange(dom, dtype=jnp.int32)[None, :]
    row_tiles = jnp.sum(
        jnp.where(slot_pick[None, :, :, None], pair_mask[:, None, :, :], 0), axis=2
    ).astype(BF16)
    tiles = amps.reshape(pairs, rows, dom, TB) * row_tiles[:, :, :, None]
    return tiles.reshape(pairs, rows, length)


def by_core(core, mine, other, axis):
    return jnp.where(
        core == 0,
        jnp.concatenate([mine, other], axis=axis),
        jnp.concatenate([other, mine], axis=axis),
    )


def make_body(ny, nx):
    def send(key, packed):
        return [
            part if (s, key[1]) == (0, 0) else hop(s, key[1])(part)
            for s, part in zip(SHIFTS, packed)
        ]

    def body(amps, domain, pair_mask, dfint, coupling):
        pairs, own, length = amps.shape
        dom = domain.shape[1]
        quarter = dfint.shape[1] // TB
        each = pairs // CORES
        chips = ny * nx
        z, y, x, c = (lax.axis_index(name).astype(jnp.int32) for name in ("z", "y", "x", "c"))
        scalars = jnp.concatenate([domain.reshape(-1), jnp.stack([z, y, x, c])])
        order = [(which, f) for which in range(each) for f in range(CORES)]
        packed = {order[0]: pack(dfint, scalars, *order[0], quarter, dom)}
        for key in order[1:]:
            packed[key] = pack(dfint, scalars, *key, quarter, dom)
        (packed[1, 0], amps, pair_mask) = lax.optimization_barrier((packed[1, 0], amps, pair_mask))
        masked = masked_amps(amps, pair_mask, ((y * nx + x) * CORES + c) * own, dom)
        mine = lax.dynamic_slice_in_dim(masked, c * each, each, axis=0)
        other = swap_cores(lax.dynamic_slice_in_dim(masked, (1 - c) * each, each, axis=0))
        both = by_core(c, mine, other, 1)
        amp = lax.all_to_all(
            jnp.broadcast_to(both[None], (chips,) + both.shape), ("y", "x"), 0, 0, tiled=True
        )
        parts = {key: send(key, packed[key]) for key in order[:-1]}
        parts[order[-1]] = send(order[-1], packed[order[-1]])
        ints, ladder0, ladder1, inter = work(
            amp,
            None,
            parts[0, 0] + parts[0, 1] + parts[1, 0],
            scalars,
            ((0, (0, 1)), (1, (0,))),
            True,
            quarter,
            dom,
        )
        late, half, inter = work(
            amp, inter, parts[1, 1], scalars, ((1, (1,)),), False, quarter, dom
        )
        sums = [ladder0, ladder(late, half, ladder1)]
        blocks = [[(ints, 0), (ints, 1)], [(ints, 2), (late, 0)]]
        every = lax.all_to_all(inter, ("z", "c"), 0, 0, tiled=True)
        ends = []
        for ordered, (first, second) in zip(
            add_cycle(sums, blocks, every, coupling, scalars), (("x", "y"), ("y", "x"))
        ):
            stage = sum_over(first, ordered)
            ends.append(sum_over(second, [stage[s] for s in range(RING)]))
        result = jnp.stack(ends).astype(BF16)
        mine = lax.dynamic_slice_in_dim(result, c * own, own, axis=1)
        other = swap_cores(lax.dynamic_slice_in_dim(result, (1 - c) * own, own, axis=1))
        return by_core(c, mine, other, 0)

    return body


def solution(mesh):
    ny = nx = 4
    grid = Mesh(mesh.devices.reshape(BLOCKS, ny, nx, CORES), ("z", "y", "x", "c"))
    virt = ("y", "x", "c")
    return jax.shard_map(
        make_body(ny, nx),
        mesh=grid,
        in_specs=(P("z", virt, None), P(), P("z", None, None), P(virt, "z", None), P("z", None)),
        out_specs=P("z", virt, None),
        check_vma=False,
    )
```

time: 142 us -> 137 us (0.965)
  waiting for transfers between devices: 13 us -> 34.1 us
  starting transfers between devices: 72 us -> 55.3 us
  Pallas kernels: 44.1 us -> 37.6 us
  local copies, waits for them, and re-layouts: 8.89 us -> 6.44 us
    ppermute x14, waiting for transfers between devices: 2.86 us -> 21.1 us  [send(): hop(s, key[1])(part)]
    ppermute x14, starting transfers between devices: 36.3 us -> 21.1 us  [send(): hop(s, key[1])(part)]
    pallas_call x5 -> x3, Pallas kernels: 27.1 us -> 21.2 us  [the longest x2 14.9 us: work(): pl.pallas_call(functools.partial(work_kernel, quarter, dom, jobs, finish,...]
    ppermute x12, waiting for transfers between devices: 8.94 us -> 11.8 us  [sum_over(): total = total + lax.ppermute(parts[s].astype(BF16), axis, perm).astype(F32)]
    slice x1 -> x0, local copies, waits for them, and re-layouts: 1.65 us -> none  [gather(): got[:, i].reshape(chips * rows.shape[1], rows.shape[2])]
    ppermute x2, starting transfers between devices: 7.1 us -> 5.62 us  [swap_cores(): return lax.ppermute(value, 'c', [(0, 1), (1, 0)])]
    unnamed x30 -> x35, local copies, waits for them, and re-layouts: 4.5 us -> 3.4 us
  transfers between devices with their start and end apart: 30 -> 30, of which waited for: 8 -> 14; matrix products, arithmetic and copies ran while one was open for 4% -> 2% of each run, Pallas kernels for 25% -> 18%
where the time goes in v7:
time: 137 us; the launch traced here: 136 us
  starting transfers between devices  55.3 us (40%)
  Pallas kernels  37.6 us (27%)
  waiting for transfers between devices  34.1 us (25%)
  local copies, waits for them, and re-layouts  6.44 us (5%)
  other arithmetic  2.31 us (2%)
    ppermute x14, starting transfers between devices, send(): hop(s, key[1])(part)  21.1 us
    ppermute x14, waiting for transfers between devices, send(): hop(s, key[1])(part)  21.1 us
    ppermute x12, starting transfers between devices, sum_over(): total = total + lax.ppermute(parts[s].astype(BF16), axis, perm).astype(F32)  16.9 us
    pallas_call x2, Pallas kernels, work(): pl.pallas_call(functools.partial(work_kernel, quarter, dom, jobs, finish,...  14.9 us
    pallas_call x4, Pallas kernels, pack(): pl.pallas_call(functools.partial(pack_kernel, quarter, dom, which, flip),...  12.1 us
    ppermute x12, waiting for transfers between devices, sum_over(): total = total + lax.ppermute(parts[s].astype(BF16), axis, perm).astype(F32)  11.8 us
    all_to_all x1, starting transfers between devices, body(): lax.all_to_all(jnp.broadcast_to(both[None], (chips,) + both.shape), ('y',...  6.75 us
    pallas_call x1, Pallas kernels, add_cycle(): pl.pallas_call(functools.partial(cycle_kernel, [[place for _, place in in...  6.35 us
  transfers between devices with their start and end apart: 30, of which 14 were waited for; matrix products, arithmetic and copies ran while one was open for 2% of the time, Pallas kernels for 18%

profile of v7, /device:TPU:1, one launch (start us, length us, event | category | flops | bytes accessed | tf_op | source)
XLA Modules:
  0.0 136.2 jit_solution(5857669749091038167)
XLA Ops:
  1.5 3.1 %pack_tiles.4 = (bf16[2,128,768]{2,1,0:T(8,128)(2,1)}, bf16[2,128,768]{2,1,0:T(8,128)(2,1)}, bf16[2,128,768]{2,1,0:T(8,128)(2,1)}, bf16[2,128,768]{2,1,0:T(8,128)(2,1)}) custom-call(s32[100]{0:T(128)} %concatenate.23.scalars_ref, bf16[1,1024,4096]{2,1,0:T(8,128)(2,1)} %dfint_ref.7), custom_call_target="tpu_custom_call" | custom-call | flops 12000000000 | bytes 1 | tf_op jit(solution)/shard_map/pack_tiles/pallas_call | solution.py:78
  5.5 1.5 %collective-permute-start = (bf16[2,24,768]{2,1,0:T(8,128)(2,1)S(1)}, bf16[2,24,768]{2,1,0:T(8,128)(2,1)S(1)}, u32[]{:S(2)}, u32[]{:S(2)}) collective-permute-start(bf16[2,24,768]{2,1,0:T(8,128)(2,1)S(1)} %get-tuple-element.92), channel_id=1, source_target_pairs={{0,1},{1,0},{2,3},{3,2},{4,5},{5,4},{6,7},{7,6},{8,9},{9,8},{10,11... | collective-permute-start | bytes 221192 | tf_op jit(solution)/shard_map/ppermute | solution.py:33
  7.0 3.7 %collective-permute-start.10 = (bf16[2,128,768]{2,1,0:T(8,128)(2,1)}, bf16[2,128,768]{2,1,0:T(8,128)(2,1)S(1)}, u32[]{:S(2)}, u32[]{:S(2)}) collective-permute-start(bf16[2,128,768]{2,1,0:T(8,128)(2,1)} %get-tuple-element.58), channel_id=1, source_target_pairs={{0,64},{1,65},{32,96},{33,97},{64,0},{65,1},{96,32},{97,33},{2,66}... | collective-permute-start | bytes 1179656 | tf_op jit(solution)/shard_map/ppermute | solution.py:399
  11.4 1.9 %collective-permute-start.9 = (bf16[2,128,768]{2,1,0:T(8,128)(2,1)}, bf16[2,128,768]{2,1,0:T(8,128)(2,1)S(1)}, u32[]{:S(2)}, u32[]{:S(2)}) collective-permute-start(bf16[2,128,768]{2,1,0:T(8,128)(2,1)} %get-tuple-element.57), channel_id=1, source_target_pairs={{0,96},{1,97},{32,0},{33,1},{64,32},{65,33},{96,64},{97,65},{2,98}... | collective-permute-start | bytes 1179656 | tf_op jit(solution)/shard_map/ppermute | solution.py:399
  13.4 2.9 %pack_tiles.5 = (bf16[2,128,768]{2,1,0:T(8,128)(2,1)}, bf16[2,128,768]{2,1,0:T(8,128)(2,1)}, bf16[2,128,768]{2,1,0:T(8,128)(2,1)}, bf16[2,128,768]{2,1,0:T(8,128)(2,1)}) custom-call(s32[100]{0:T(128)} %concatenate.23.scalars_ref, bf16[1,1024,4096]{2,1,0:T(8,128)(2,1)} %dfint_ref.7), custom_call_target="tpu_custom_call" | custom-call | flops 12000000000 | bytes 1 | tf_op jit(solution)/shard_map/pack_tiles/pallas_call | solution.py:78
  16.4 2.6 %collective-permute-start.2 = (bf16[2,128,768]{2,1,0:T(8,128)(2,1)}, bf16[2,128,768]{2,1,0:T(8,128)(2,1)}, u32[]{:S(2)}, u32[]{:S(2)}) collective-permute-start(bf16[2,128,768]{2,1,0:T(8,128)(2,1)} %get-tuple-element.49), channel_id=1, source_target_pairs={{0,96},{1,97},{32,0},{33,1},{64,32},{65,33},{96,64},{97,65},{2,98}... | collective-permute-start | bytes 1179656 | tf_op jit(solution)/shard_map/ppermute | solution.py:399
  19.1 1.6 %broadcast_in_dim.34 = bf16[16,2,48,768]{3,2,1,0:T(8,128)(2,1)} broadcast(bf16[2,48,768]{2,1,0:T(8,128)(2,1)S(1)} %maximum_select_fusion), dimensions={1,2,3} | broadcast | bytes 2506752 | tf_op jit(solution)/shard_map/broadcast_in_dim | solution.py:421
  20.7 6.8 %all-to-all-start = ((bf16[16,2,48,768]{3,2,1,0:T(8,128)(2,1)}), bf16[16,2,48,768]{3,2,1,0:T(8,128)(2,1)S(1)}, u32[]{:S(2)}, u32[]{:S(2)}) async-start(bf16[16,2,48,768]{3,2,1,0:T(8,128)(2,1)} %broadcast_in_dim.34), calls=%async_computation | async-start | bytes 4718592 | tf_op jit(solution)/shard_map/all_to_all | solution.py:420
  27.5 3.1 %pack_tiles.6 = (bf16[2,128,768]{2,1,0:T(8,128)(2,1)}, bf16[2,128,768]{2,1,0:T(8,128)(2,1)}, bf16[2,128,768]{2,1,0:T(8,128)(2,1)}, bf16[2,128,768]{2,1,0:T(8,128)(2,1)}) custom-call(s32[100]{0:T(128)} %concatenate.23.scalars_ref, bf16[1,1024,4096]{2,1,0:T(8,128)(2,1)} %dfint_ref.7), custom_call_target="tpu_custom_call" | custom-call | flops 12000000000 | bytes 1 | tf_op jit(solution)/shard_map/pack_tiles/pallas_call | solution.py:78
  30.8 2.2 %collective-permute-start.4 = (bf16[2,128,768]{2,1,0:T(8,128)(2,1)}, bf16[2,128,768]{2,1,0:T(8,128)(2,1)S(1)}, u32[]{:S(2)}, u32[]{:S(2)}) collective-permute-start(bf16[2,128,768]{2,1,0:T(8,128)(2,1)} %get-tuple-element.52), channel_id=1, source_target_pairs={{0,33},{1,32},{32,65},{33,64},{64,97},{65,96},{96,1},{97,0},{2,35}... | collective-permute-start | bytes 1179656 | tf_op jit(solution)/shard_map/ppermute | solution.py:399
  33.8 3.8 %collective-permute-done.1.rest_0_ = bf16[2,128,768]{2,1,0:T(8,128)(2,1)} collective-permute-done((bf16[2,128,768]{2,1,0:T(8,128)(2,1)}, bf16[2,128,768]{2,1,0:T(8,128)(2,1)}, u32[]{:S(2)}, u32[]{:S(2)}) %collective-permute-start.1) | collective-permute-done | bytes 393248 | tf_op jit(solution)/shard_map/ppermute | solution.py:399
  37.6 3.6 %collective-permute-start.6 = (bf16[2,128,768]{2,1,0:T(8,128)(2,1)}, bf16[2,128,768]{2,1,0:T(8,128)(2,1)S(1)}, u32[]{:S(2)}, u32[]{:S(2)}) collective-permute-start(bf16[2,128,768]{2,1,0:T(8,128)(2,1)} %get-tuple-element.54), channel_id=1, source_target_pairs={{0,65},{1,64},{32,97},{33,96},{64,1},{65,0},{96,33},{97,32},{2,67}... | collective-permute-start | bytes 1179656 | tf_op jit(solution)/shard_map/ppermute | solution.py:399
  41.3 3.0 %pack_tiles.7 = (bf16[2,128,768]{2,1,0:T(8,128)(2,1)}, bf16[2,128,768]{2,1,0:T(8,128)(2,1)}, bf16[2,128,768]{2,1,0:T(8,128)(2,1)}, bf16[2,128,768]{2,1,0:T(8,128)(2,1)}) custom-call(s32[100]{0:T(128)} %concatenate.23.scalars_ref, bf16[1,1024,4096]{2,1,0:T(8,128)(2,1)} %dfint_ref.7), custom_call_target="tpu_custom_call" | custom-call | flops 12000000000 | bytes 1 | tf_op jit(solution)/shard_map/pack_tiles/pallas_call | solution.py:78
  45.7 2.1 %collective-permute-start.11 = (bf16[2,128,768]{2,1,0:T(8,128)(2,1)}, bf16[2,128,768]{2,1,0:T(8,128)(2,1)S(1)}, u32[]{:S(2)}, u32[]{:S(2)}) collective-permute-start(bf16[2,128,768]{2,1,0:T(8,128)(2,1)} %get-tuple-element.61), channel_id=1, source_target_pairs={{0,33},{1,32},{32,65},{33,64},{64,97},{65,96},{96,1},{97,0},{2,35}... | collective-permute-start | bytes 1179656 | tf_op jit(solution)/shard_map/ppermute | solution.py:399
  47.8 6.8 %collective-permute-done.4.rest_4_ = bf16[2,128,768]{2,1,0:T(8,128)(2,1)S(1)} collective-permute-done((bf16[2,128,768]{2,1,0:T(8,128)(2,1)}, bf16[2,128,768]{2,1,0:T(8,128)(2,1)S(1)}, u32[]{:S(2)}, u32[]{:S(2)}) %collective-permute-start.4) | collective-permute-done | bytes 393248 | tf_op jit(solution)/shard_map/ppermute | solution.py:399
  55.6 2.8 %collective-permute-start.13 = (bf16[2,128,768]{2,1,0:T(8,128)(2,1)}, bf16[2,128,768]{2,1,0:T(8,128)(2,1)}, u32[]{:S(2)}, u32[]{:S(2)}) collective-permute-start(bf16[2,128,768]{2,1,0:T(8,128)(2,1)} %get-tuple-element.63), channel_id=1, source_target_pairs={{0,65},{1,64},{32,97},{33,96},{64,1},{65,0},{96,33},{97,32},{2,67}... | collective-permute-start | bytes 1179656 | tf_op jit(solution)/shard_map/ppermute | solution.py:399
  58.4 4.4 %collective-permute-done.6.rest_6_ = bf16[2,128,768]{2,1,0:T(8,128)(2,1)S(1)} collective-permute-done((bf16[2,128,768]{2,1,0:T(8,128)(2,1)}, bf16[2,128,768]{2,1,0:T(8,128)(2,1)S(1)}, u32[]{:S(2)}, u32[]{:S(2)}) %collective-permute-start.6) | collective-permute-done | bytes 393248 | tf_op jit(solution)/shard_map/ppermute | solution.py:399
  65.1 10.5 %half_and_ladder.1 = (bf16[3,768,768]{2,1,0:T(8,128)(2,1)}, f32[768,768]{1,0:T(8,128)}, f32[768,768]{1,0:T(8,128)}, f32[8,128]{1,0:T(8,128)}) custom-call(s32[100]{0:T(128)} %concatenate.23.scalars_ref, bf16[16,2,48,768]{3,2,1,0:T(8,128)(2,1)} %copy-done, bf16[2,128,768]{2,1,0:T(8,128)(2,1)} %collective-permute-done.1.rest_0_, ...), custom_call_target="tpu_custom_call" | custom-call | flops 1 | bytes 1 | tf_op jit(solution)/shard_map/half_and_ladder/pallas_call | solution.py:202
  75.7 3.8 %collective-permute-done.13.rest_3_ = bf16[2,128,768]{2,1,0:T(8,128)(2,1)} collective-permute-done((bf16[2,128,768]{2,1,0:T(8,128)(2,1)}, bf16[2,128,768]{2,1,0:T(8,128)(2,1)}, u32[]{:S(2)}, u32[]{:S(2)}) %collective-permute-start.13) | collective-permute-done | bytes 393248 | tf_op jit(solution)/shard_map/ppermute | solution.py:399
  79.5 4.3 %half_ladder.1 = (bf16[1,768,768]{2,1,0:T(8,128)(2,1)}, bf16[1,768,768]{2,1,0:T(8,128)(2,1)}, f32[8,128]{1,0:T(8,128)}) custom-call(s32[100]{0:T(128)} %concatenate.23.scalars_ref, bf16[16,2,48,768]{3,2,1,0:T(8,128)(2,1)} %copy-done, f32[8,128]{1,0:T(8,128)} %get-tuple-element.60.rest_0_, bf16[2,128,768]{2,1,0:T(8,128)(2,1)} %copy-done.10, ...), custom_call_target="tpu_custom_call" | custom-call | flops 1 | bytes 1 | tf_op jit(solution)/shard_map/half_ladder/pallas_call | solution.py:202
  83.8 4.9 %all-to-all-start.1 = ((f32[8,1,128]{2,1,0:T(1,128)}), f32[8,1,128]{2,1,0:T(1,128)S(1)}, u32[]{:S(2)}, u32[]{:S(2)}) async-start(f32[8,1,128]{2,1,0:T(1,128)} %bitcast.49), calls=%async_computation.1 | async-start | bytes 8192 | tf_op jit(solution)/shard_map/all_to_all | solution.py:440
  88.7 4.3 %ladder.1.rest_5_ = f32[768,768]{1,0:T(8,128)} custom-call(bf16[1,768,768]{2,1,0:T(8,128)(2,1)} %get-tuple-element.68.int_ref.rest_4_, bf16[1,768,768]{2,1,0:T(8,128)(2,1)} %get-tuple-element.69.half_ref, f32[768,768]{1,0:T(8,128)} %get-tuple-element.70.before_ref), custom_call_target="tpu_custom_call" | custom-call | flops 1 | bytes 1 | tf_op jit(solution)/shard_map/ladder/pallas_call | solution.py:260
  93.9 6.4 %add_cycle.1 = (f32[4,48,768]{2,1,0:T(8,128)}, bf16[4,48,768]{2,1,0:T(8,128)(2,1)}, bf16[4,48,768]{2,1,0:T(8,128)(2,1)}, bf16[4,48,768]{2,1,0:T(8,128)(2,1)}, f3...) custom-call(s32[100]{0:T(128)} %concatenate.23.scalars_ref, ...), custom_call_target="tpu_custom_call" | custom-call | flops 1 | bytes 1 | tf_op jit(solution)/shard_map/add_cycle/pallas_call | solution.py:346
  101.7 1.5 %collective-permute-start.22 = (bf16[4,48,768]{2,1,0:T(8,128)(2,1)}, bf16[4,48,768]{2,1,0:T(8,128)(2,1)S(1)}, u32[]{:S(2)}, u32[]{:S(2)}) collective-permute-start(bf16[4,48,768]{2,1,0:T(8,128)(2,1)} %get-tuple-element.77), channel_id=1, source_target_pairs={{0,24},{8,0},{16,8},{24,16},{1,25},{9,1},{17,9},{25,17},{2,26},{10... | collective-permute-start | bytes 884744 | tf_op jit(solution)/shard_map/ppermute | solution.py:373
  103.2 1.6 %collective-permute-start.23 = (bf16[4,48,768]{2,1,0:T(8,128)(2,1)}, bf16[4,48,768]{2,1,0:T(8,128)(2,1)S(1)}, u32[]{:S(2)}, u32[]{:S(2)}) collective-permute-start(bf16[4,48,768]{2,1,0:T(8,128)(2,1)} %get-tuple-element.78), channel_id=1, source_target_pairs={{0,16},{8,24},{16,0},{24,8},{1,17},{9,25},{17,1},{25,9},{2,18},{10... | collective-permute-start | bytes 884744 | tf_op jit(solution)/shard_map/ppermute | solution.py:373
  107.4 2.4 %collective-permute-done.21 = bf16[4,48,768]{2,1,0:T(8,128)(2,1)S(1)} collective-permute-done((bf16[4,48,768]{2,1,0:T(8,128)(2,1)}, bf16[4,48,768]{2,1,0:T(8,128)(2,1)S(1)}, u32[]{:S(2)}, u32[]{:S(2)}) %collective-permute-start.21) | collective-permute-done | bytes 294944 | tf_op jit(solution)/shard_map/ppermute | solution.py:373
  109.8 2.7 %collective-permute-start.17 = (bf16[4,48,768]{2,1,0:T(8,128)(2,1)}, bf16[4,48,768]{2,1,0:T(8,128)(2,1)S(1)}, u32[]{:S(2)}, u32[]{:S(2)}) collective-permute-start(bf16[4,48,768]{2,1,0:T(8,128)(2,1)} %get-tuple-element.74), channel_id=1, source_target_pairs={{0,4},{2,6},{4,0},{6,2},{1,5},{3,7},{5,1},{7,3},{8,12},{10,14},{12... | collective-permute-start | bytes 884744 | tf_op jit(solution)/shard_map/ppermute | solution.py:373
  112.5 4.7 %collective-permute-done.23 = bf16[4,48,768]{2,1,0:T(8,128)(2,1)S(1)} collective-permute-done((bf16[4,48,768]{2,1,0:T(8,128)(2,1)}, bf16[4,48,768]{2,1,0:T(8,128)(2,1)S(1)}, u32[]{:S(2)}, u32[]{:S(2)}) %collective-permute-start.23) | collective-permute-done | bytes 294944 | tf_op jit(solution)/shard_map/ppermute | solution.py:373
  121.2 1.5 %collective-permute-start.26 = (bf16[48,768]{1,0:T(8,128)(2,1)S(1)}, bf16[48,768]{1,0:T(8,128)(2,1)S(1)}, u32[]{:S(2)}, u32[]{:S(2)}) collective-permute-start(bf16[48,768]{1,0:T(8,128)(2,1)S(1)} %get-tuple-element.84), channel_id=1, source_target_pairs={{0,4},{2,6},{4,0},{6,2},{1,5},{3,7},{5,1},{7,3},{8,12},{10,14},{12... | collective-permute-start | bytes 221192 | tf_op jit(solution)/shard_map/ppermute | solution.py:373
  123.5 2.1 %collective-permute-start.19 = (bf16[48,768]{1,0:T(8,128)(2,1)S(1)}, bf16[48,768]{1,0:T(8,128)(2,1)S(1)}, u32[]{:S(2)}, u32[]{:S(2)}) collective-permute-start(bf16[48,768]{1,0:T(8,128)(2,1)S(1)} %get-tuple-element.88), channel_id=1, source_target_pairs={{0,24},{8,0},{16,8},{24,16},{1,25},{9,1},{17,9},{25,17},{2,26},{10... | collective-permute-start | bytes 221192 | tf_op jit(solution)/shard_map/ppermute | solution.py:373
  127.7 2.7 %collective-permute-done.20 = bf16[48,768]{1,0:T(8,128)(2,1)S(1)} collective-permute-done((bf16[48,768]{1,0:T(8,128)(2,1)S(1)}, bf16[48,768]{1,0:T(8,128)(2,1)S(1)}, u32[]{:S(2)}, u32[]{:S(2)}) %collective-permute-start.20) | collective-permute-done | bytes 73760 | tf_op jit(solution)/shard_map/ppermute | solution.py:373
  130.5 4.1 %collective-permute-start.27 = (bf16[2,24,768]{2,1,0:T(8,128)(2,1)S(1)}, bf16[2,24,768]{2,1,0:T(8,128)(2,1)S(1)}, u32[]{:S(2)}, u32[]{:S(2)}) collective-permute-start(bf16[2,24,768]{2,1,0:T(8,128)(2,1)S(1)} %get-tuple-element.90), channel_id=1, source_target_pairs={{0,1},{1,0},{2,3},{3,2},{4,5},{5,4},{6,7},{7,6},{8,9},{9,8},{10,11... | collective-permute-start | bytes 221192 | tf_op jit(solution)/shard_map/ppermute | solution.py:33
  (93 shorter events, 22.1 us)
Async XLA Ops:
  5.5 10.9 %collective-permute-start = (bf16[2,24,768]{2,1,0:T(8,128)(2,1)S(1)}, bf16[2,24,768]{2,1,0:T(8,128)(2,1)S(1)}, u32[]{:S(2)}, u32[]{:S(2)}) collective-permute-start(bf16[2,24,768]{2,1,0:T(8,128)(2,1)S(1)} %get-tuple-element.92), channel_id=1, source_target_pairs={{0,1},{1,0},{2,3},{3,2},{4,5},{5,4},{6,7},{7,6},{8,9},{9,8},{10,11... | collective-permute-start | bytes 221192 | tf_op jit(solution)/shard_map/ppermute | solution.py:33
  7.0 23.6 %collective-permute-start.10 = (bf16[2,128,768]{2,1,0:T(8,128)(2,1)}, bf16[2,128,768]{2,1,0:T(8,128)(2,1)S(1)}, u32[]{:S(2)}, u32[]{:S(2)}) collective-permute-start(bf16[2,128,768]{2,1,0:T(8,128)(2,1)} %get-tuple-element.58), channel_id=1, source_target_pairs={{0,64},{1,65},{32,96},{33,97},{64,0},{65,1},{96,32},{97,33},{2,66}... | collective-permute-start | bytes 1179656 | tf_op jit(solution)/shard_map/ppermute | solution.py:399
  10.7 20.1 %collective-permute-start.8 = (bf16[2,128,768]{2,1,0:T(8,128)(2,1)}, bf16[2,128,768]{2,1,0:T(8,128)(2,1)S(1)}, u32[]{:S(2)}, u32[]{:S(2)}) collective-permute-start(bf16[2,128,768]{2,1,0:T(8,128)(2,1)} %get-tuple-element.56), channel_id=1, source_target_pairs={{0,32},{1,33},{32,64},{33,65},{64,96},{65,97},{96,0},{97,1},{2,34}... | collective-permute-start | bytes 1179656 | tf_op jit(solution)/shard_map/ppermute | solution.py:399
  11.4 21.5 %collective-permute-start.9 = (bf16[2,128,768]{2,1,0:T(8,128)(2,1)}, bf16[2,128,768]{2,1,0:T(8,128)(2,1)S(1)}, u32[]{:S(2)}, u32[]{:S(2)}) collective-permute-start(bf16[2,128,768]{2,1,0:T(8,128)(2,1)} %get-tuple-element.57), channel_id=1, source_target_pairs={{0,96},{1,97},{32,0},{33,1},{64,32},{65,33},{96,64},{97,65},{2,98}... | collective-permute-start | bytes 1179656 | tf_op jit(solution)/shard_map/ppermute | solution.py:399
  16.3 21.3 %collective-permute-start.1 = (bf16[2,128,768]{2,1,0:T(8,128)(2,1)}, bf16[2,128,768]{2,1,0:T(8,128)(2,1)}, u32[]{:S(2)}, u32[]{:S(2)}) collective-permute-start(bf16[2,128,768]{2,1,0:T(8,128)(2,1)} %get-tuple-element.48), channel_id=1, source_target_pairs={{0,32},{1,33},{32,64},{33,65},{64,96},{65,97},{96,0},{97,1},{2,34}... | collective-permute-start | bytes 1179656 | tf_op jit(solution)/shard_map/ppermute | solution.py:399
  16.4 27.8 %collective-permute-start.2 = (bf16[2,128,768]{2,1,0:T(8,128)(2,1)}, bf16[2,128,768]{2,1,0:T(8,128)(2,1)}, u32[]{:S(2)}, u32[]{:S(2)}) collective-permute-start(bf16[2,128,768]{2,1,0:T(8,128)(2,1)} %get-tuple-element.49), channel_id=1, source_target_pairs={{0,96},{1,97},{32,0},{33,1},{64,32},{65,33},{96,64},{97,65},{2,98}... | collective-permute-start | bytes 1179656 | tf_op jit(solution)/shard_map/ppermute | solution.py:399
  20.7 42.8 %all-to-all-start = ((bf16[16,2,48,768]{3,2,1,0:T(8,128)(2,1)}), bf16[16,2,48,768]{3,2,1,0:T(8,128)(2,1)S(1)}, u32[]{:S(2)}, u32[]{:S(2)}) async-start(bf16[16,2,48,768]{3,2,1,0:T(8,128)(2,1)} %broadcast_in_dim.34), calls=%async_computation | async-start | bytes 4718592 | tf_op jit(solution)/shard_map/all_to_all | solution.py:420
  30.7 15.0 %collective-permute-start.3 = (bf16[2,128,768]{2,1,0:T(8,128)(2,1)S(1)}, bf16[2,128,768]{2,1,0:T(8,128)(2,1)S(1)}, u32[]{:S(2)}, u32[]{:S(2)}) collective-permute-start(bf16[2,128,768]{2,1,0:T(8,128)(2,1)S(1)} %copy-done.16), channel_id=1, source_target_pairs={{0,64},{1,65},{32,96},{33,97},{64,0},{65,1},{96,32},{97,33},{2,66}... | collective-permute-start | bytes 1179656 | tf_op jit(solution)/shard_map/ppermute | solution.py:399
  30.8 23.8 %collective-permute-start.4 = (bf16[2,128,768]{2,1,0:T(8,128)(2,1)}, bf16[2,128,768]{2,1,0:T(8,128)(2,1)S(1)}, u32[]{:S(2)}, u32[]{:S(2)}) collective-permute-start(bf16[2,128,768]{2,1,0:T(8,128)(2,1)} %get-tuple-element.52), channel_id=1, source_target_pairs={{0,33},{1,32},{32,65},{33,64},{64,97},{65,96},{96,1},{97,0},{2,35}... | collective-permute-start | bytes 1179656 | tf_op jit(solution)/shard_map/ppermute | solution.py:399
  33.0 22.6 %collective-permute-start.5 = (bf16[2,128,768]{2,1,0:T(8,128)(2,1)}, bf16[2,128,768]{2,1,0:T(8,128)(2,1)S(1)}, u32[]{:S(2)}, u32[]{:S(2)}) collective-permute-start(bf16[2,128,768]{2,1,0:T(8,128)(2,1)} %get-tuple-element.53), channel_id=1, source_target_pairs={{0,97},{1,96},{32,1},{33,0},{64,33},{65,32},{96,65},{97,64},{2,99}... | collective-permute-start | bytes 1179656 | tf_op jit(solution)/shard_map/ppermute | solution.py:399
  37.6 25.2 %collective-permute-start.6 = (bf16[2,128,768]{2,1,0:T(8,128)(2,1)}, bf16[2,128,768]{2,1,0:T(8,128)(2,1)S(1)}, u32[]{:S(2)}, u32[]{:S(2)}) collective-permute-start(bf16[2,128,768]{2,1,0:T(8,128)(2,1)} %get-tuple-element.54), channel_id=1, source_target_pairs={{0,65},{1,64},{32,97},{33,96},{64,1},{65,0},{96,33},{97,32},{2,67}... | collective-permute-start | bytes 1179656 | tf_op jit(solution)/shard_map/ppermute | solution.py:399
  44.3 19.3 %collective-permute-start.7 = (bf16[2,128,768]{2,1,0:T(8,128)(2,1)S(1)}, bf16[2,128,768]{2,1,0:T(8,128)(2,1)S(1)}, u32[]{:S(2)}, u32[]{:S(2)}) collective-permute-start(bf16[2,128,768]{2,1,0:T(8,128)(2,1)S(1)} %copy-done.15), channel_id=1, source_target_pairs={{0,1},{1,0},{32,33},{33,32},{64,65},{65,64},{96,97},{97,96},{2,3},... | collective-permute-start | bytes 1179656 | tf_op jit(solution)/shard_map/ppermute | solution.py:399
  45.7 17.4 %copy-start.5 = (bf16[2,128,768]{2,1,0:T(8,128)(2,1)}, bf16[2,128,768]{2,1,0:T(8,128)(2,1)S(1)}, u32[]{:S(2)}) copy-start(bf16[2,128,768]{2,1,0:T(8,128)(2,1)S(1)} %collective-permute-done.3.rest_2_) | copy-start | bytes 1179652
  45.7 30.0 %collective-permute-start.11 = (bf16[2,128,768]{2,1,0:T(8,128)(2,1)}, bf16[2,128,768]{2,1,0:T(8,128)(2,1)S(1)}, u32[]{:S(2)}, u32[]{:S(2)}) collective-permute-start(bf16[2,128,768]{2,1,0:T(8,128)(2,1)} %get-tuple-element.61), channel_id=1, source_target_pairs={{0,33},{1,32},{32,65},{33,64},{64,97},{65,96},{96,1},{97,0},{2,35}... | collective-permute-start | bytes 1179656 | tf_op jit(solution)/shard_map/ppermute | solution.py:399
  54.6 21.1 %collective-permute-start.12 = (bf16[2,128,768]{2,1,0:T(8,128)(2,1)}, bf16[2,128,768]{2,1,0:T(8,128)(2,1)S(1)}, u32[]{:S(2)}, u32[]{:S(2)}) collective-permute-start(bf16[2,128,768]{2,1,0:T(8,128)(2,1)} %get-tuple-element.62), channel_id=1, source_target_pairs={{0,97},{1,96},{32,1},{33,0},{64,33},{65,32},{96,65},{97,64},{2,99}... | collective-permute-start | bytes 1179656 | tf_op jit(solution)/shard_map/ppermute | solution.py:399
  55.6 23.9 %collective-permute-start.13 = (bf16[2,128,768]{2,1,0:T(8,128)(2,1)}, bf16[2,128,768]{2,1,0:T(8,128)(2,1)}, u32[]{:S(2)}, u32[]{:S(2)}) collective-permute-start(bf16[2,128,768]{2,1,0:T(8,128)(2,1)} %get-tuple-element.63), channel_id=1, source_target_pairs={{0,65},{1,64},{32,97},{33,96},{64,1},{65,0},{96,33},{97,32},{2,67}... | collective-permute-start | bytes 1179656 | tf_op jit(solution)/shard_map/ppermute | solution.py:399
  62.8 16.7 %collective-permute-start.14 = (bf16[2,128,768]{2,1,0:T(8,128)(2,1)}, bf16[2,128,768]{2,1,0:T(8,128)(2,1)}, u32[]{:S(2)}, u32[]{:S(2)}) collective-permute-start(bf16[2,128,768]{2,1,0:T(8,128)(2,1)} %get-tuple-element.64), channel_id=1, source_target_pairs={{0,1},{1,0},{32,33},{33,32},{64,65},{65,64},{96,97},{97,96},{2,3},... | collective-permute-start | bytes 1179656 | tf_op jit(solution)/shard_map/ppermute | solution.py:399
  83.8 9.5 %all-to-all-start.1 = ((f32[8,1,128]{2,1,0:T(1,128)}), f32[8,1,128]{2,1,0:T(1,128)S(1)}, u32[]{:S(2)}, u32[]{:S(2)}) async-start(f32[8,1,128]{2,1,0:T(1,128)} %bitcast.49), calls=%async_computation.1 | async-start | bytes 8192 | tf_op jit(solution)/shard_map/all_to_all | solution.py:440
  100.3 22.4 %copy-start.1 = (f32[4,48,768]{2,1,0:T(8,128)S(1)}, f32[4,48,768]{2,1,0:T(8,128)}, u32[]{:S(2)}) copy-start(f32[4,48,768]{2,1,0:T(8,128)} %get-tuple-element.71) | copy-start | bytes 1769476
  100.3 9.5 %collective-permute-start.21 = (bf16[4,48,768]{2,1,0:T(8,128)(2,1)}, bf16[4,48,768]{2,1,0:T(8,128)(2,1)S(1)}, u32[]{:S(2)}, u32[]{:S(2)}) collective-permute-start(bf16[4,48,768]{2,1,0:T(8,128)(2,1)} %get-tuple-element.76), channel_id=1, source_target_pairs={{0,8},{8,16},{16,24},{24,0},{1,9},{9,17},{17,25},{25,1},{2,10},{10... | collective-permute-start | bytes 884744 | tf_op jit(solution)/shard_map/ppermute | solution.py:373
  101.7 10.9 %collective-permute-start.22 = (bf16[4,48,768]{2,1,0:T(8,128)(2,1)}, bf16[4,48,768]{2,1,0:T(8,128)(2,1)S(1)}, u32[]{:S(2)}, u32[]{:S(2)}) collective-permute-start(bf16[4,48,768]{2,1,0:T(8,128)(2,1)} %get-tuple-element.77), channel_id=1, source_target_pairs={{0,24},{8,0},{16,8},{24,16},{1,25},{9,1},{17,9},{25,17},{2,26},{10... | collective-permute-start | bytes 884744 | tf_op jit(solution)/shard_map/ppermute | solution.py:373
  103.2 14.0 %collective-permute-start.23 = (bf16[4,48,768]{2,1,0:T(8,128)(2,1)}, bf16[4,48,768]{2,1,0:T(8,128)(2,1)S(1)}, u32[]{:S(2)}, u32[]{:S(2)}) collective-permute-start(bf16[4,48,768]{2,1,0:T(8,128)(2,1)} %get-tuple-element.78), channel_id=1, source_target_pairs={{0,16},{8,24},{16,0},{24,8},{1,17},{9,25},{17,1},{25,9},{2,18},{10... | collective-permute-start | bytes 884744 | tf_op jit(solution)/shard_map/ppermute | solution.py:373
  104.7 16.4 %collective-permute-start.15 = (bf16[4,48,768]{2,1,0:T(8,128)(2,1)}, bf16[4,48,768]{2,1,0:T(8,128)(2,1)S(1)}, u32[]{:S(2)}, u32[]{:S(2)}) collective-permute-start(bf16[4,48,768]{2,1,0:T(8,128)(2,1)} %get-tuple-element.72), channel_id=1, source_target_pairs={{0,2},{2,4},{4,6},{6,0},{1,3},{3,5},{5,7},{7,1},{8,10},{10,12},{12... | collective-permute-start | bytes 884744 | tf_op jit(solution)/shard_map/ppermute | solution.py:373
  106.0 16.7 %collective-permute-start.16 = (bf16[4,48,768]{2,1,0:T(8,128)(2,1)}, bf16[4,48,768]{2,1,0:T(8,128)(2,1)S(1)}, u32[]{:S(2)}, u32[]{:S(2)}) collective-permute-start(bf16[4,48,768]{2,1,0:T(8,128)(2,1)} %get-tuple-element.73), channel_id=1, source_target_pairs={{0,6},{2,0},{4,2},{6,4},{1,7},{3,1},{5,3},{7,5},{8,14},{10,8},{12,... | collective-permute-start | bytes 884744 | tf_op jit(solution)/shard_map/ppermute | solution.py:373
  109.8 12.9 %collective-permute-start.17 = (bf16[4,48,768]{2,1,0:T(8,128)(2,1)}, bf16[4,48,768]{2,1,0:T(8,128)(2,1)S(1)}, u32[]{:S(2)}, u32[]{:S(2)}) collective-permute-start(bf16[4,48,768]{2,1,0:T(8,128)(2,1)} %get-tuple-element.74), channel_id=1, source_target_pairs={{0,4},{2,6},{4,0},{6,2},{1,5},{3,7},{5,1},{7,3},{8,12},{10,14},{12... | collective-permute-start | bytes 884744 | tf_op jit(solution)/shard_map/ppermute | solution.py:373
  118.4 7.2 %collective-permute-start.24 = (bf16[48,768]{1,0:T(8,128)(2,1)S(1)}, bf16[48,768]{1,0:T(8,128)(2,1)S(1)}, u32[]{:S(2)}, u32[]{:S(2)}) collective-permute-start(bf16[48,768]{1,0:T(8,128)(2,1)S(1)} %get-tuple-element.83), channel_id=1, source_target_pairs={{0,2},{2,4},{4,6},{6,0},{1,3},{3,5},{5,7},{7,1},{8,10},{10,12},{12... | collective-permute-start | bytes 221192 | tf_op jit(solution)/shard_map/ppermute | solution.py:373
  119.7 5.9 %collective-permute-start.25 = (bf16[48,768]{1,0:T(8,128)(2,1)S(1)}, bf16[48,768]{1,0:T(8,128)(2,1)S(1)}, u32[]{:S(2)}, u32[]{:S(2)}) collective-permute-start(bf16[48,768]{1,0:T(8,128)(2,1)S(1)} %get-tuple-element.85), channel_id=1, source_target_pairs={{0,6},{2,0},{4,2},{6,4},{1,7},{3,1},{5,3},{7,5},{8,14},{10,8},{12,... | collective-permute-start | bytes 221192 | tf_op jit(solution)/shard_map/ppermute | solution.py:373
  121.2 5.4 %collective-permute-start.26 = (bf16[48,768]{1,0:T(8,128)(2,1)S(1)}, bf16[48,768]{1,0:T(8,128)(2,1)S(1)}, u32[]{:S(2)}, u32[]{:S(2)}) collective-permute-start(bf16[48,768]{1,0:T(8,128)(2,1)S(1)} %get-tuple-element.84), channel_id=1, source_target_pairs={{0,4},{2,6},{4,0},{6,2},{1,5},{3,7},{5,1},{7,3},{8,12},{10,14},{12... | collective-permute-start | bytes 221192 | tf_op jit(solution)/shard_map/ppermute | solution.py:373
  122.9 4.5 %collective-permute-start.18 = (bf16[48,768]{1,0:T(8,128)(2,1)S(1)}, bf16[48,768]{1,0:T(8,128)(2,1)S(1)}, u32[]{:S(2)}, u32[]{:S(2)}) collective-permute-start(bf16[48,768]{1,0:T(8,128)(2,1)S(1)} %get-tuple-element.86), channel_id=1, source_target_pairs={{0,8},{8,16},{16,24},{24,0},{1,9},{9,17},{17,25},{25,1},{2,10},{10... | collective-permute-start | bytes 221192 | tf_op jit(solution)/shard_map/ppermute | solution.py:373
  123.5 4.2 %collective-permute-start.19 = (bf16[48,768]{1,0:T(8,128)(2,1)S(1)}, bf16[48,768]{1,0:T(8,128)(2,1)S(1)}, u32[]{:S(2)}, u32[]{:S(2)}) collective-permute-start(bf16[48,768]{1,0:T(8,128)(2,1)S(1)} %get-tuple-element.88), channel_id=1, source_target_pairs={{0,24},{8,0},{16,8},{24,16},{1,25},{9,1},{17,9},{25,17},{2,26},{10... | collective-permute-start | bytes 221192 | tf_op jit(solution)/shard_map/ppermute | solution.py:373
  125.6 4.8 %collective-permute-start.20 = (bf16[48,768]{1,0:T(8,128)(2,1)S(1)}, bf16[48,768]{1,0:T(8,128)(2,1)S(1)}, u32[]{:S(2)}, u32[]{:S(2)}) collective-permute-start(bf16[48,768]{1,0:T(8,128)(2,1)S(1)} %get-tuple-element.87), channel_id=1, source_target_pairs={{0,16},{8,24},{16,0},{24,8},{1,17},{9,25},{17,1},{25,9},{2,18},{10... | collective-permute-start | bytes 221192 | tf_op jit(solution)/shard_map/ppermute | solution.py:373
  130.5 5.0 %collective-permute-start.27 = (bf16[2,24,768]{2,1,0:T(8,128)(2,1)S(1)}, bf16[2,24,768]{2,1,0:T(8,128)(2,1)S(1)}, u32[]{:S(2)}, u32[]{:S(2)}) collective-permute-start(bf16[2,24,768]{2,1,0:T(8,128)(2,1)S(1)} %get-tuple-element.90), channel_id=1, source_target_pairs={{0,1},{1,0},{2,3},{3,2},{4,5},{5,4},{6,7},{7,6},{8,9},{9,8},{10,11... | collective-permute-start | bytes 221192 | tf_op jit(solution)/shard_map/ppermute | solution.py:33
  (15 other events, 82.5 us)

commit v8 on v7

--- a/solution.py
+++ b/solution.py
@@ -368,7 +368,7 @@
 
 def sum_over(axis, parts):
     total = parts[0].astype(F32)
-    for s in (1, 3, 2):
+    for s in (2, 1, 3):
         perm = [(i, (i + s) % RING) for i in range(RING)]
         total = total + lax.ppermute(parts[s].astype(BF16), axis, perm).astype(F32)
     return total

time: 137 us -> 137 us (level)
  waiting for transfers between devices: 34.1 us -> 31.3 us
  starting transfers between devices: 55.3 us -> 57.5 us
    ppermute x12, starting transfers between devices: 16.9 us -> 20.8 us  [sum_over(): total = total + lax.ppermute(parts[s].astype(BF16), axis, perm).astype(F32)]
    ppermute x12, waiting for transfers between devices: 11.8 us -> 9.03 us  [sum_over(): total = total + lax.ppermute(parts[s].astype(BF16), axis, perm).astype(F32)]
    ppermute x2, starting transfers between devices: 5.62 us -> 3.86 us  [swap_cores(): return lax.ppermute(value, 'c', [(0, 1), (1, 0)])]
  transfers between devices with their start and end apart: 30 -> 30, of which waited for: 14 -> 13; matrix products, arithmetic and copies ran while one was open for 2% -> 2% of each run, Pallas kernels for 18% -> 18%
where the time goes in v8:
time: 137 us; the launch traced here: 136 us
  starting transfers between devices  57.5 us (42%)
  Pallas kernels  37.7 us (28%)
  waiting for transfers between devices  31.3 us (23%)
  local copies, waits for them, and re-layouts  6.43 us (5%)
  other arithmetic  2.31 us (2%)
    ppermute x14, starting transfers between devices, send(): hop(s, key[1])(part)  21.1 us
    ppermute x14, waiting for transfers between devices, send(): hop(s, key[1])(part)  21.1 us
    ppermute x12, starting transfers between devices, sum_over(): total = total + lax.ppermute(parts[s].astype(BF16), axis, perm).astype(F32)  20.8 us
    pallas_call x2, Pallas kernels, work(): pl.pallas_call(functools.partial(work_kernel, quarter, dom, jobs, finish,...  14.9 us
    pallas_call x4, Pallas kernels, pack(): pl.pallas_call(functools.partial(pack_kernel, quarter, dom, which, flip),...  12.2 us
    ppermute x12, waiting for transfers between devices, sum_over(): total = total + lax.ppermute(parts[s].astype(BF16), axis, perm).astype(F32)  9.03 us
    all_to_all x1, starting transfers between devices, body(): lax.all_to_all(jnp.broadcast_to(both[None], (chips,) + both.shape), ('y',...  6.75 us
    pallas_call x1, Pallas kernels, add_cycle(): pl.pallas_call(functools.partial(cycle_kernel, [[place for _, place in in...  6.35 us
  transfers between devices with their start and end apart: 30, of which 13 were waited for; matrix products, arithmetic and copies ran while one was open for 2% of the time, Pallas kernels for 18%

profile of v8, /device:TPU:1, one launch (start us, length us, event | category | flops | bytes accessed | tf_op | source)
XLA Modules:
  0.0 135.6 jit_solution(7611952180258696093)
XLA Ops:
  1.5 3.1 %pack_tiles.4 = (bf16[2,128,768]{2,1,0:T(8,128)(2,1)}, bf16[2,128,768]{2,1,0:T(8,128)(2,1)}, bf16[2,128,768]{2,1,0:T(8,128)(2,1)}, bf16[2,128,768]{2,1,0:T(8,128)(2,1)}) custom-call(s32[100]{0:T(128)} %concatenate.23.scalars_ref, bf16[1,1024,4096]{2,1,0:T(8,128)(2,1)} %dfint_ref.7), custom_call_target="tpu_custom_call" | custom-call | flops 12000000000 | bytes 1 | tf_op jit(solution)/shard_map/pack_tiles/pallas_call | solution.py:78
  7.0 3.7 %collective-permute-start.10 = (bf16[2,128,768]{2,1,0:T(8,128)(2,1)}, bf16[2,128,768]{2,1,0:T(8,128)(2,1)S(1)}, u32[]{:S(2)}, u32[]{:S(2)}) collective-permute-start(bf16[2,128,768]{2,1,0:T(8,128)(2,1)} %get-tuple-element.58), channel_id=1, source_target_pairs={{0,64},{1,65},{32,96},{33,97},{64,0},{65,1},{96,32},{97,33},{2,66}... | collective-permute-start | bytes 1179656 | tf_op jit(solution)/shard_map/ppermute | solution.py:399
  11.4 1.9 %collective-permute-start.9 = (bf16[2,128,768]{2,1,0:T(8,128)(2,1)}, bf16[2,128,768]{2,1,0:T(8,128)(2,1)S(1)}, u32[]{:S(2)}, u32[]{:S(2)}) collective-permute-start(bf16[2,128,768]{2,1,0:T(8,128)(2,1)} %get-tuple-element.57), channel_id=1, source_target_pairs={{0,96},{1,97},{32,0},{33,1},{64,32},{65,33},{96,64},{97,65},{2,98}... | collective-permute-start | bytes 1179656 | tf_op jit(solution)/shard_map/ppermute | solution.py:399
  13.4 3.0 %pack_tiles.5 = (bf16[2,128,768]{2,1,0:T(8,128)(2,1)}, bf16[2,128,768]{2,1,0:T(8,128)(2,1)}, bf16[2,128,768]{2,1,0:T(8,128)(2,1)}, bf16[2,128,768]{2,1,0:T(8,128)(2,1)}) custom-call(s32[100]{0:T(128)} %concatenate.23.scalars_ref, bf16[1,1024,4096]{2,1,0:T(8,128)(2,1)} %dfint_ref.7), custom_call_target="tpu_custom_call" | custom-call | flops 12000000000 | bytes 1 | tf_op jit(solution)/shard_map/pack_tiles/pallas_call | solution.py:78
  16.5 2.6 %collective-permute-start.2 = (bf16[2,128,768]{2,1,0:T(8,128)(2,1)}, bf16[2,128,768]{2,1,0:T(8,128)(2,1)}, u32[]{:S(2)}, u32[]{:S(2)}) collective-permute-start(bf16[2,128,768]{2,1,0:T(8,128)(2,1)} %get-tuple-element.49), channel_id=1, source_target_pairs={{0,96},{1,97},{32,0},{33,1},{64,32},{65,33},{96,64},{97,65},{2,98}... | collective-permute-start | bytes 1179656 | tf_op jit(solution)/shard_map/ppermute | solution.py:399
  19.2 1.6 %broadcast_in_dim.34 = bf16[16,2,48,768]{3,2,1,0:T(8,128)(2,1)} broadcast(bf16[2,48,768]{2,1,0:T(8,128)(2,1)S(1)} %maximum_select_fusion), dimensions={1,2,3} | broadcast | bytes 2506752 | tf_op jit(solution)/shard_map/broadcast_in_dim | solution.py:421
  20.8 6.8 %all-to-all-start = ((bf16[16,2,48,768]{3,2,1,0:T(8,128)(2,1)}), bf16[16,2,48,768]{3,2,1,0:T(8,128)(2,1)S(1)}, u32[]{:S(2)}, u32[]{:S(2)}) async-start(bf16[16,2,48,768]{3,2,1,0:T(8,128)(2,1)} %broadcast_in_dim.34), calls=%async_computation | async-start | bytes 4718592 | tf_op jit(solution)/shard_map/all_to_all | solution.py:420
  27.6 3.1 %pack_tiles.6 = (bf16[2,128,768]{2,1,0:T(8,128)(2,1)}, bf16[2,128,768]{2,1,0:T(8,128)(2,1)}, bf16[2,128,768]{2,1,0:T(8,128)(2,1)}, bf16[2,128,768]{2,1,0:T(8,128)(2,1)}) custom-call(s32[100]{0:T(128)} %concatenate.23.scalars_ref, bf16[1,1024,4096]{2,1,0:T(8,128)(2,1)} %dfint_ref.7), custom_call_target="tpu_custom_call" | custom-call | flops 12000000000 | bytes 1 | tf_op jit(solution)/shard_map/pack_tiles/pallas_call | solution.py:78
  30.8 2.1 %collective-permute-start.4 = (bf16[2,128,768]{2,1,0:T(8,128)(2,1)}, bf16[2,128,768]{2,1,0:T(8,128)(2,1)S(1)}, u32[]{:S(2)}, u32[]{:S(2)}) collective-permute-start(bf16[2,128,768]{2,1,0:T(8,128)(2,1)} %get-tuple-element.52), channel_id=1, source_target_pairs={{0,33},{1,32},{32,65},{33,64},{64,97},{65,96},{96,1},{97,0},{2,35}... | collective-permute-start | bytes 1179656 | tf_op jit(solution)/shard_map/ppermute | solution.py:399
  33.9 3.7 %collective-permute-done.1.rest_0_ = bf16[2,128,768]{2,1,0:T(8,128)(2,1)} collective-permute-done((bf16[2,128,768]{2,1,0:T(8,128)(2,1)}, bf16[2,128,768]{2,1,0:T(8,128)(2,1)}, u32[]{:S(2)}, u32[]{:S(2)}) %collective-permute-start.1) | collective-permute-done | bytes 393248 | tf_op jit(solution)/shard_map/ppermute | solution.py:399
  37.6 3.7 %collective-permute-start.6 = (bf16[2,128,768]{2,1,0:T(8,128)(2,1)}, bf16[2,128,768]{2,1,0:T(8,128)(2,1)S(1)}, u32[]{:S(2)}, u32[]{:S(2)}) collective-permute-start(bf16[2,128,768]{2,1,0:T(8,128)(2,1)} %get-tuple-element.54), channel_id=1, source_target_pairs={{0,65},{1,64},{32,97},{33,96},{64,1},{65,0},{96,33},{97,32},{2,67}... | collective-permute-start | bytes 1179656 | tf_op jit(solution)/shard_map/ppermute | solution.py:399
  41.3 3.0 %pack_tiles.7 = (bf16[2,128,768]{2,1,0:T(8,128)(2,1)}, bf16[2,128,768]{2,1,0:T(8,128)(2,1)}, bf16[2,128,768]{2,1,0:T(8,128)(2,1)}, bf16[2,128,768]{2,1,0:T(8,128)(2,1)}) custom-call(s32[100]{0:T(128)} %concatenate.23.scalars_ref, bf16[1,1024,4096]{2,1,0:T(8,128)(2,1)} %dfint_ref.7), custom_call_target="tpu_custom_call" | custom-call | flops 12000000000 | bytes 1 | tf_op jit(solution)/shard_map/pack_tiles/pallas_call | solution.py:78
  45.7 2.1 %collective-permute-start.11 = (bf16[2,128,768]{2,1,0:T(8,128)(2,1)}, bf16[2,128,768]{2,1,0:T(8,128)(2,1)S(1)}, u32[]{:S(2)}, u32[]{:S(2)}) collective-permute-start(bf16[2,128,768]{2,1,0:T(8,128)(2,1)} %get-tuple-element.61), channel_id=1, source_target_pairs={{0,33},{1,32},{32,65},{33,64},{64,97},{65,96},{96,1},{97,0},{2,35}... | collective-permute-start | bytes 1179656 | tf_op jit(solution)/shard_map/ppermute | solution.py:399
  47.7 6.9 %collective-permute-done.4.rest_4_ = bf16[2,128,768]{2,1,0:T(8,128)(2,1)S(1)} collective-permute-done((bf16[2,128,768]{2,1,0:T(8,128)(2,1)}, bf16[2,128,768]{2,1,0:T(8,128)(2,1)S(1)}, u32[]{:S(2)}, u32[]{:S(2)}) %collective-permute-start.4) | collective-permute-done | bytes 393248 | tf_op jit(solution)/shard_map/ppermute | solution.py:399
  55.6 2.8 %collective-permute-start.13 = (bf16[2,128,768]{2,1,0:T(8,128)(2,1)}, bf16[2,128,768]{2,1,0:T(8,128)(2,1)}, u32[]{:S(2)}, u32[]{:S(2)}) collective-permute-start(bf16[2,128,768]{2,1,0:T(8,128)(2,1)} %get-tuple-element.63), channel_id=1, source_target_pairs={{0,65},{1,64},{32,97},{33,96},{64,1},{65,0},{96,33},{97,32},{2,67}... | collective-permute-start | bytes 1179656 | tf_op jit(solution)/shard_map/ppermute | solution.py:399
  58.4 4.4 %collective-permute-done.6.rest_6_ = bf16[2,128,768]{2,1,0:T(8,128)(2,1)S(1)} collective-permute-done((bf16[2,128,768]{2,1,0:T(8,128)(2,1)}, bf16[2,128,768]{2,1,0:T(8,128)(2,1)S(1)}, u32[]{:S(2)}, u32[]{:S(2)}) %collective-permute-start.6) | collective-permute-done | bytes 393248 | tf_op jit(solution)/shard_map/ppermute | solution.py:399
  65.1 10.5 %half_and_ladder.1 = (bf16[3,768,768]{2,1,0:T(8,128)(2,1)}, f32[768,768]{1,0:T(8,128)}, f32[768,768]{1,0:T(8,128)}, f32[8,128]{1,0:T(8,128)}) custom-call(s32[100]{0:T(128)} %concatenate.23.scalars_ref, bf16[16,2,48,768]{3,2,1,0:T(8,128)(2,1)} %copy-done, bf16[2,128,768]{2,1,0:T(8,128)(2,1)} %collective-permute-done.1.rest_0_, ...), custom_call_target="tpu_custom_call" | custom-call | flops 1 | bytes 1 | tf_op jit(solution)/shard_map/half_and_ladder/pallas_call | solution.py:202
  75.7 3.8 %collective-permute-done.13.rest_3_ = bf16[2,128,768]{2,1,0:T(8,128)(2,1)} collective-permute-done((bf16[2,128,768]{2,1,0:T(8,128)(2,1)}, bf16[2,128,768]{2,1,0:T(8,128)(2,1)}, u32[]{:S(2)}, u32[]{:S(2)}) %collective-permute-start.13) | collective-permute-done | bytes 393248 | tf_op jit(solution)/shard_map/ppermute | solution.py:399
  79.5 4.3 %half_ladder.1 = (bf16[1,768,768]{2,1,0:T(8,128)(2,1)}, bf16[1,768,768]{2,1,0:T(8,128)(2,1)}, f32[8,128]{1,0:T(8,128)}) custom-call(s32[100]{0:T(128)} %concatenate.23.scalars_ref, bf16[16,2,48,768]{3,2,1,0:T(8,128)(2,1)} %copy-done, f32[8,128]{1,0:T(8,128)} %get-tuple-element.60.rest_0_, bf16[2,128,768]{2,1,0:T(8,128)(2,1)} %copy-done.10, ...), custom_call_target="tpu_custom_call" | custom-call | flops 1 | bytes 1 | tf_op jit(solution)/shard_map/half_ladder/pallas_call | solution.py:202
  83.8 4.9 %all-to-all-start.1 = ((f32[8,1,128]{2,1,0:T(1,128)}), f32[8,1,128]{2,1,0:T(1,128)S(1)}, u32[]{:S(2)}, u32[]{:S(2)}) async-start(f32[8,1,128]{2,1,0:T(1,128)} %bitcast.49), calls=%async_computation.1 | async-start | bytes 8192 | tf_op jit(solution)/shard_map/all_to_all | solution.py:440
  88.7 4.3 %ladder.1.rest_5_ = f32[768,768]{1,0:T(8,128)} custom-call(bf16[1,768,768]{2,1,0:T(8,128)(2,1)} %get-tuple-element.68.int_ref.rest_4_, bf16[1,768,768]{2,1,0:T(8,128)(2,1)} %get-tuple-element.69.half_ref, f32[768,768]{1,0:T(8,128)} %get-tuple-element.70.before_ref), custom_call_target="tpu_custom_call" | custom-call | flops 1 | bytes 1 | tf_op jit(solution)/shard_map/ladder/pallas_call | solution.py:260
  93.9 6.4 %add_cycle.1 = (f32[4,48,768]{2,1,0:T(8,128)}, bf16[4,48,768]{2,1,0:T(8,128)(2,1)}, bf16[4,48,768]{2,1,0:T(8,128)(2,1)}, bf16[4,48,768]{2,1,0:T(8,128)(2,1)}, f3...) custom-call(s32[100]{0:T(128)} %concatenate.23.scalars_ref, ...), custom_call_target="tpu_custom_call" | custom-call | flops 1 | bytes 1 | tf_op jit(solution)/shard_map/add_cycle/pallas_call | solution.py:346
  100.3 3.0 %collective-permute-start.21 = (bf16[4,48,768]{2,1,0:T(8,128)(2,1)}, bf16[4,48,768]{2,1,0:T(8,128)(2,1)S(1)}, u32[]{:S(2)}, u32[]{:S(2)}) collective-permute-start(bf16[4,48,768]{2,1,0:T(8,128)(2,1)} %get-tuple-element.76), channel_id=1, source_target_pairs={{0,16},{8,24},{16,0},{24,8},{1,17},{9,25},{17,1},{25,9},{2,18},{10... | collective-permute-start | bytes 884744 | tf_op jit(solution)/shard_map/ppermute | solution.py:373
  103.7 2.3 %collective-permute-start.23 = (bf16[4,48,768]{2,1,0:T(8,128)(2,1)}, bf16[4,48,768]{2,1,0:T(8,128)(2,1)S(1)}, u32[]{:S(2)}, u32[]{:S(2)}) collective-permute-start(bf16[4,48,768]{2,1,0:T(8,128)(2,1)} %get-tuple-element.78), channel_id=1, source_target_pairs={{0,24},{8,0},{16,8},{24,16},{1,25},{9,1},{17,9},{25,17},{2,26},{10... | collective-permute-start | bytes 884744 | tf_op jit(solution)/shard_map/ppermute | solution.py:373
  106.0 2.7 %collective-permute-start.15 = (bf16[4,48,768]{2,1,0:T(8,128)(2,1)}, bf16[4,48,768]{2,1,0:T(8,128)(2,1)S(1)}, u32[]{:S(2)}, u32[]{:S(2)}) collective-permute-start(bf16[4,48,768]{2,1,0:T(8,128)(2,1)} %get-tuple-element.72), channel_id=1, source_target_pairs={{0,4},{2,6},{4,0},{6,2},{1,5},{3,7},{5,1},{7,3},{8,12},{10,14},{12... | collective-permute-start | bytes 884744 | tf_op jit(solution)/shard_map/ppermute | solution.py:373
  110.0 2.5 %collective-permute-start.17 = (bf16[4,48,768]{2,1,0:T(8,128)(2,1)}, bf16[4,48,768]{2,1,0:T(8,128)(2,1)S(1)}, u32[]{:S(2)}, u32[]{:S(2)}) collective-permute-start(bf16[4,48,768]{2,1,0:T(8,128)(2,1)} %get-tuple-element.74), channel_id=1, source_target_pairs={{0,6},{2,0},{4,2},{6,4},{1,7},{3,1},{5,3},{7,5},{8,14},{10,8},{12,... | collective-permute-start | bytes 884744 | tf_op jit(solution)/shard_map/ppermute | solution.py:373
  112.5 4.9 %collective-permute-done.22 = bf16[4,48,768]{2,1,0:T(8,128)(2,1)S(1)} collective-permute-done((bf16[4,48,768]{2,1,0:T(8,128)(2,1)}, bf16[4,48,768]{2,1,0:T(8,128)(2,1)S(1)}, u32[]{:S(2)}, u32[]{:S(2)}) %collective-permute-start.22) | collective-permute-done | bytes 294944 | tf_op jit(solution)/shard_map/ppermute | solution.py:373
  118.6 2.8 %collective-permute-start.24 = (bf16[48,768]{1,0:T(8,128)(2,1)S(1)}, bf16[48,768]{1,0:T(8,128)(2,1)S(1)}, u32[]{:S(2)}, u32[]{:S(2)}) collective-permute-start(bf16[48,768]{1,0:T(8,128)(2,1)S(1)} %get-tuple-element.83), channel_id=1, source_target_pairs={{0,4},{2,6},{4,0},{6,2},{1,5},{3,7},{5,1},{7,3},{8,12},{10,14},{12... | collective-permute-start | bytes 221192 | tf_op jit(solution)/shard_map/ppermute | solution.py:373
  121.7 2.3 %collective-permute-start.26 = (bf16[48,768]{1,0:T(8,128)(2,1)S(1)}, bf16[48,768]{1,0:T(8,128)(2,1)S(1)}, u32[]{:S(2)}, u32[]{:S(2)}) collective-permute-start(bf16[48,768]{1,0:T(8,128)(2,1)S(1)} %get-tuple-element.84), channel_id=1, source_target_pairs={{0,6},{2,0},{4,2},{6,4},{1,7},{3,1},{5,3},{7,5},{8,14},{10,8},{12,... | collective-permute-start | bytes 221192 | tf_op jit(solution)/shard_map/ppermute | solution.py:373
  125.6 2.0 %collective-permute-start.19 = (bf16[48,768]{1,0:T(8,128)(2,1)S(1)}, bf16[48,768]{1,0:T(8,128)(2,1)S(1)}, u32[]{:S(2)}, u32[]{:S(2)}) collective-permute-start(bf16[48,768]{1,0:T(8,128)(2,1)S(1)} %get-tuple-element.88), channel_id=1, source_target_pairs={{0,8},{8,16},{16,24},{24,0},{1,9},{9,17},{17,25},{25,1},{2,10},{10... | collective-permute-start | bytes 221192 | tf_op jit(solution)/shard_map/ppermute | solution.py:373
  130.1 1.5 %collective-permute-done.20 = bf16[48,768]{1,0:T(8,128)(2,1)S(1)} collective-permute-done((bf16[48,768]{1,0:T(8,128)(2,1)S(1)}, bf16[48,768]{1,0:T(8,128)(2,1)S(1)}, u32[]{:S(2)}, u32[]{:S(2)}) %collective-permute-start.20) | collective-permute-done | bytes 73760 | tf_op jit(solution)/shard_map/ppermute | solution.py:373
  131.7 2.4 %collective-permute-start.27 = (bf16[2,24,768]{2,1,0:T(8,128)(2,1)S(1)}, bf16[2,24,768]{2,1,0:T(8,128)(2,1)S(1)}, u32[]{:S(2)}, u32[]{:S(2)}) collective-permute-start(bf16[2,24,768]{2,1,0:T(8,128)(2,1)S(1)} %get-tuple-element.90), channel_id=1, source_target_pairs={{0,1},{1,0},{2,3},{3,2},{4,5},{5,4},{6,7},{7,6},{8,9},{9,8},{10,11... | collective-permute-start | bytes 221192 | tf_op jit(solution)/shard_map/ppermute | solution.py:33
  (93 shorter events, 20.1 us)
Async XLA Ops:
  5.5 11.0 %collective-permute-start = (bf16[2,24,768]{2,1,0:T(8,128)(2,1)S(1)}, bf16[2,24,768]{2,1,0:T(8,128)(2,1)S(1)}, u32[]{:S(2)}, u32[]{:S(2)}) collective-permute-start(bf16[2,24,768]{2,1,0:T(8,128)(2,1)S(1)} %get-tuple-element.92), channel_id=1, source_target_pairs={{0,1},{1,0},{2,3},{3,2},{4,5},{5,4},{6,7},{7,6},{8,9},{9,8},{10,11... | collective-permute-start | bytes 221192 | tf_op jit(solution)/shard_map/ppermute | solution.py:33
  7.0 23.7 %collective-permute-start.10 = (bf16[2,128,768]{2,1,0:T(8,128)(2,1)}, bf16[2,128,768]{2,1,0:T(8,128)(2,1)S(1)}, u32[]{:S(2)}, u32[]{:S(2)}) collective-permute-start(bf16[2,128,768]{2,1,0:T(8,128)(2,1)} %get-tuple-element.58), channel_id=1, source_target_pairs={{0,64},{1,65},{32,96},{33,97},{64,0},{65,1},{96,32},{97,33},{2,66}... | collective-permute-start | bytes 1179656 | tf_op jit(solution)/shard_map/ppermute | solution.py:399
  10.7 20.1 %collective-permute-start.8 = (bf16[2,128,768]{2,1,0:T(8,128)(2,1)}, bf16[2,128,768]{2,1,0:T(8,128)(2,1)S(1)}, u32[]{:S(2)}, u32[]{:S(2)}) collective-permute-start(bf16[2,128,768]{2,1,0:T(8,128)(2,1)} %get-tuple-element.56), channel_id=1, source_target_pairs={{0,32},{1,33},{32,64},{33,65},{64,96},{65,97},{96,0},{97,1},{2,34}... | collective-permute-start | bytes 1179656 | tf_op jit(solution)/shard_map/ppermute | solution.py:399
  11.4 21.5 %collective-permute-start.9 = (bf16[2,128,768]{2,1,0:T(8,128)(2,1)}, bf16[2,128,768]{2,1,0:T(8,128)(2,1)S(1)}, u32[]{:S(2)}, u32[]{:S(2)}) collective-permute-start(bf16[2,128,768]{2,1,0:T(8,128)(2,1)} %get-tuple-element.57), channel_id=1, source_target_pairs={{0,96},{1,97},{32,0},{33,1},{64,32},{65,33},{96,64},{97,65},{2,98}... | collective-permute-start | bytes 1179656 | tf_op jit(solution)/shard_map/ppermute | solution.py:399
  16.4 21.2 %collective-permute-start.1 = (bf16[2,128,768]{2,1,0:T(8,128)(2,1)}, bf16[2,128,768]{2,1,0:T(8,128)(2,1)}, u32[]{:S(2)}, u32[]{:S(2)}) collective-permute-start(bf16[2,128,768]{2,1,0:T(8,128)(2,1)} %get-tuple-element.48), channel_id=1, source_target_pairs={{0,32},{1,33},{32,64},{33,65},{64,96},{65,97},{96,0},{97,1},{2,34}... | collective-permute-start | bytes 1179656 | tf_op jit(solution)/shard_map/ppermute | solution.py:399
  16.5 27.8 %collective-permute-start.2 = (bf16[2,128,768]{2,1,0:T(8,128)(2,1)}, bf16[2,128,768]{2,1,0:T(8,128)(2,1)}, u32[]{:S(2)}, u32[]{:S(2)}) collective-permute-start(bf16[2,128,768]{2,1,0:T(8,128)(2,1)} %get-tuple-element.49), channel_id=1, source_target_pairs={{0,96},{1,97},{32,0},{33,1},{64,32},{65,33},{96,64},{97,65},{2,98}... | collective-permute-start | bytes 1179656 | tf_op jit(solution)/shard_map/ppermute | solution.py:399
  20.8 42.8 %all-to-all-start = ((bf16[16,2,48,768]{3,2,1,0:T(8,128)(2,1)}), bf16[16,2,48,768]{3,2,1,0:T(8,128)(2,1)S(1)}, u32[]{:S(2)}, u32[]{:S(2)}) async-start(bf16[16,2,48,768]{3,2,1,0:T(8,128)(2,1)} %broadcast_in_dim.34), calls=%async_computation | async-start | bytes 4718592 | tf_op jit(solution)/shard_map/all_to_all | solution.py:420
  30.7 14.9 %collective-permute-start.3 = (bf16[2,128,768]{2,1,0:T(8,128)(2,1)S(1)}, bf16[2,128,768]{2,1,0:T(8,128)(2,1)S(1)}, u32[]{:S(2)}, u32[]{:S(2)}) collective-permute-start(bf16[2,128,768]{2,1,0:T(8,128)(2,1)S(1)} %copy-done.16), channel_id=1, source_target_pairs={{0,64},{1,65},{32,96},{33,97},{64,0},{65,1},{96,32},{97,33},{2,66}... | collective-permute-start | bytes 1179656 | tf_op jit(solution)/shard_map/ppermute | solution.py:399
  30.8 23.8 %collective-permute-start.4 = (bf16[2,128,768]{2,1,0:T(8,128)(2,1)}, bf16[2,128,768]{2,1,0:T(8,128)(2,1)S(1)}, u32[]{:S(2)}, u32[]{:S(2)}) collective-permute-start(bf16[2,128,768]{2,1,0:T(8,128)(2,1)} %get-tuple-element.52), channel_id=1, source_target_pairs={{0,33},{1,32},{32,65},{33,64},{64,97},{65,96},{96,1},{97,0},{2,35}... | collective-permute-start | bytes 1179656 | tf_op jit(solution)/shard_map/ppermute | solution.py:399
  33.0 22.6 %collective-permute-start.5 = (bf16[2,128,768]{2,1,0:T(8,128)(2,1)}, bf16[2,128,768]{2,1,0:T(8,128)(2,1)S(1)}, u32[]{:S(2)}, u32[]{:S(2)}) collective-permute-start(bf16[2,128,768]{2,1,0:T(8,128)(2,1)} %get-tuple-element.53), channel_id=1, source_target_pairs={{0,97},{1,96},{32,1},{33,0},{64,33},{65,32},{96,65},{97,64},{2,99}... | collective-permute-start | bytes 1179656 | tf_op jit(solution)/shard_map/ppermute | solution.py:399
  37.6 25.2 %collective-permute-start.6 = (bf16[2,128,768]{2,1,0:T(8,128)(2,1)}, bf16[2,128,768]{2,1,0:T(8,128)(2,1)S(1)}, u32[]{:S(2)}, u32[]{:S(2)}) collective-permute-start(bf16[2,128,768]{2,1,0:T(8,128)(2,1)} %get-tuple-element.54), channel_id=1, source_target_pairs={{0,65},{1,64},{32,97},{33,96},{64,1},{65,0},{96,33},{97,32},{2,67}... | collective-permute-start | bytes 1179656 | tf_op jit(solution)/shard_map/ppermute | solution.py:399
  44.3 19.3 %collective-permute-start.7 = (bf16[2,128,768]{2,1,0:T(8,128)(2,1)S(1)}, bf16[2,128,768]{2,1,0:T(8,128)(2,1)S(1)}, u32[]{:S(2)}, u32[]{:S(2)}) collective-permute-start(bf16[2,128,768]{2,1,0:T(8,128)(2,1)S(1)} %copy-done.15), channel_id=1, source_target_pairs={{0,1},{1,0},{32,33},{33,32},{64,65},{65,64},{96,97},{97,96},{2,3},... | collective-permute-start | bytes 1179656 | tf_op jit(solution)/shard_map/ppermute | solution.py:399
  45.7 17.4 %copy-start.5 = (bf16[2,128,768]{2,1,0:T(8,128)(2,1)}, bf16[2,128,768]{2,1,0:T(8,128)(2,1)S(1)}, u32[]{:S(2)}) copy-start(bf16[2,128,768]{2,1,0:T(8,128)(2,1)S(1)} %collective-permute-done.3.rest_2_) | copy-start | bytes 1179652
  45.7 30.0 %collective-permute-start.11 = (bf16[2,128,768]{2,1,0:T(8,128)(2,1)}, bf16[2,128,768]{2,1,0:T(8,128)(2,1)S(1)}, u32[]{:S(2)}, u32[]{:S(2)}) collective-permute-start(bf16[2,128,768]{2,1,0:T(8,128)(2,1)} %get-tuple-element.61), channel_id=1, source_target_pairs={{0,33},{1,32},{32,65},{33,64},{64,97},{65,96},{96,1},{97,0},{2,35}... | collective-permute-start | bytes 1179656 | tf_op jit(solution)/shard_map/ppermute | solution.py:399
  54.6 21.1 %collective-permute-start.12 = (bf16[2,128,768]{2,1,0:T(8,128)(2,1)}, bf16[2,128,768]{2,1,0:T(8,128)(2,1)S(1)}, u32[]{:S(2)}, u32[]{:S(2)}) collective-permute-start(bf16[2,128,768]{2,1,0:T(8,128)(2,1)} %get-tuple-element.62), channel_id=1, source_target_pairs={{0,97},{1,96},{32,1},{33,0},{64,33},{65,32},{96,65},{97,64},{2,99}... | collective-permute-start | bytes 1179656 | tf_op jit(solution)/shard_map/ppermute | solution.py:399
  55.6 23.9 %collective-permute-start.13 = (bf16[2,128,768]{2,1,0:T(8,128)(2,1)}, bf16[2,128,768]{2,1,0:T(8,128)(2,1)}, u32[]{:S(2)}, u32[]{:S(2)}) collective-permute-start(bf16[2,128,768]{2,1,0:T(8,128)(2,1)} %get-tuple-element.63), channel_id=1, source_target_pairs={{0,65},{1,64},{32,97},{33,96},{64,1},{65,0},{96,33},{97,32},{2,67}... | collective-permute-start | bytes 1179656 | tf_op jit(solution)/shard_map/ppermute | solution.py:399
  62.8 16.7 %collective-permute-start.14 = (bf16[2,128,768]{2,1,0:T(8,128)(2,1)}, bf16[2,128,768]{2,1,0:T(8,128)(2,1)}, u32[]{:S(2)}, u32[]{:S(2)}) collective-permute-start(bf16[2,128,768]{2,1,0:T(8,128)(2,1)} %get-tuple-element.64), channel_id=1, source_target_pairs={{0,1},{1,0},{32,33},{33,32},{64,65},{65,64},{96,97},{97,96},{2,3},... | collective-permute-start | bytes 1179656 | tf_op jit(solution)/shard_map/ppermute | solution.py:399
  83.8 9.5 %all-to-all-start.1 = ((f32[8,1,128]{2,1,0:T(1,128)}), f32[8,1,128]{2,1,0:T(1,128)S(1)}, u32[]{:S(2)}, u32[]{:S(2)}) async-start(f32[8,1,128]{2,1,0:T(1,128)} %bitcast.49), calls=%async_computation.1 | async-start | bytes 8192 | tf_op jit(solution)/shard_map/all_to_all | solution.py:440
  100.3 23.8 %copy-start.1 = (f32[4,48,768]{2,1,0:T(8,128)S(1)}, f32[4,48,768]{2,1,0:T(8,128)}, u32[]{:S(2)}) copy-start(f32[4,48,768]{2,1,0:T(8,128)} %get-tuple-element.71) | copy-start | bytes 1769476
  100.3 9.7 %collective-permute-start.21 = (bf16[4,48,768]{2,1,0:T(8,128)(2,1)}, bf16[4,48,768]{2,1,0:T(8,128)(2,1)S(1)}, u32[]{:S(2)}, u32[]{:S(2)}) collective-permute-start(bf16[4,48,768]{2,1,0:T(8,128)(2,1)} %get-tuple-element.76), channel_id=1, source_target_pairs={{0,16},{8,24},{16,0},{24,8},{1,17},{9,25},{17,1},{25,9},{2,18},{10... | collective-permute-start | bytes 884744 | tf_op jit(solution)/shard_map/ppermute | solution.py:373
  103.3 14.0 %collective-permute-start.22 = (bf16[4,48,768]{2,1,0:T(8,128)(2,1)}, bf16[4,48,768]{2,1,0:T(8,128)(2,1)S(1)}, u32[]{:S(2)}, u32[]{:S(2)}) collective-permute-start(bf16[4,48,768]{2,1,0:T(8,128)(2,1)} %get-tuple-element.77), channel_id=1, source_target_pairs={{0,8},{8,16},{16,24},{24,0},{1,9},{9,17},{17,25},{25,1},{2,10},{10... | collective-permute-start | bytes 884744 | tf_op jit(solution)/shard_map/ppermute | solution.py:373
  103.7 13.7 %collective-permute-start.23 = (bf16[4,48,768]{2,1,0:T(8,128)(2,1)}, bf16[4,48,768]{2,1,0:T(8,128)(2,1)S(1)}, u32[]{:S(2)}, u32[]{:S(2)}) collective-permute-start(bf16[4,48,768]{2,1,0:T(8,128)(2,1)} %get-tuple-element.78), channel_id=1, source_target_pairs={{0,24},{8,0},{16,8},{24,16},{1,25},{9,1},{17,9},{25,17},{2,26},{10... | collective-permute-start | bytes 884744 | tf_op jit(solution)/shard_map/ppermute | solution.py:373
  106.0 15.8 %collective-permute-start.15 = (bf16[4,48,768]{2,1,0:T(8,128)(2,1)}, bf16[4,48,768]{2,1,0:T(8,128)(2,1)S(1)}, u32[]{:S(2)}, u32[]{:S(2)}) collective-permute-start(bf16[4,48,768]{2,1,0:T(8,128)(2,1)} %get-tuple-element.72), channel_id=1, source_target_pairs={{0,4},{2,6},{4,0},{6,2},{1,5},{3,7},{5,1},{7,3},{8,12},{10,14},{12... | collective-permute-start | bytes 884744 | tf_op jit(solution)/shard_map/ppermute | solution.py:373
  108.7 15.4 %collective-permute-start.16 = (bf16[4,48,768]{2,1,0:T(8,128)(2,1)}, bf16[4,48,768]{2,1,0:T(8,128)(2,1)S(1)}, u32[]{:S(2)}, u32[]{:S(2)}) collective-permute-start(bf16[4,48,768]{2,1,0:T(8,128)(2,1)} %get-tuple-element.73), channel_id=1, source_target_pairs={{0,2},{2,4},{4,6},{6,0},{1,3},{3,5},{5,7},{7,1},{8,10},{10,12},{12... | collective-permute-start | bytes 884744 | tf_op jit(solution)/shard_map/ppermute | solution.py:373
  110.0 14.1 %collective-permute-start.17 = (bf16[4,48,768]{2,1,0:T(8,128)(2,1)}, bf16[4,48,768]{2,1,0:T(8,128)(2,1)S(1)}, u32[]{:S(2)}, u32[]{:S(2)}) collective-permute-start(bf16[4,48,768]{2,1,0:T(8,128)(2,1)} %get-tuple-element.74), channel_id=1, source_target_pairs={{0,6},{2,0},{4,2},{6,4},{1,7},{3,1},{5,3},{7,5},{8,14},{10,8},{12,... | collective-permute-start | bytes 884744 | tf_op jit(solution)/shard_map/ppermute | solution.py:373
  118.6 9.1 %collective-permute-start.24 = (bf16[48,768]{1,0:T(8,128)(2,1)S(1)}, bf16[48,768]{1,0:T(8,128)(2,1)S(1)}, u32[]{:S(2)}, u32[]{:S(2)}) collective-permute-start(bf16[48,768]{1,0:T(8,128)(2,1)S(1)} %get-tuple-element.83), channel_id=1, source_target_pairs={{0,4},{2,6},{4,0},{6,2},{1,5},{3,7},{5,1},{7,3},{8,12},{10,14},{12... | collective-permute-start | bytes 221192 | tf_op jit(solution)/shard_map/ppermute | solution.py:373
  121.4 6.9 %collective-permute-start.25 = (bf16[48,768]{1,0:T(8,128)(2,1)S(1)}, bf16[48,768]{1,0:T(8,128)(2,1)S(1)}, u32[]{:S(2)}, u32[]{:S(2)}) collective-permute-start(bf16[48,768]{1,0:T(8,128)(2,1)S(1)} %get-tuple-element.85), channel_id=1, source_target_pairs={{0,2},{2,4},{4,6},{6,0},{1,3},{3,5},{5,7},{7,1},{8,10},{10,12},{12... | collective-permute-start | bytes 221192 | tf_op jit(solution)/shard_map/ppermute | solution.py:373
  121.7 6.6 %collective-permute-start.26 = (bf16[48,768]{1,0:T(8,128)(2,1)S(1)}, bf16[48,768]{1,0:T(8,128)(2,1)S(1)}, u32[]{:S(2)}, u32[]{:S(2)}) collective-permute-start(bf16[48,768]{1,0:T(8,128)(2,1)S(1)} %get-tuple-element.84), channel_id=1, source_target_pairs={{0,6},{2,0},{4,2},{6,4},{1,7},{3,1},{5,3},{7,5},{8,14},{10,8},{12,... | collective-permute-start | bytes 221192 | tf_op jit(solution)/shard_map/ppermute | solution.py:373
  124.2 4.8 %collective-permute-start.18 = (bf16[48,768]{1,0:T(8,128)(2,1)S(1)}, bf16[48,768]{1,0:T(8,128)(2,1)S(1)}, u32[]{:S(2)}, u32[]{:S(2)}) collective-permute-start(bf16[48,768]{1,0:T(8,128)(2,1)S(1)} %get-tuple-element.86), channel_id=1, source_target_pairs={{0,16},{8,24},{16,0},{24,8},{1,17},{9,25},{17,1},{25,9},{2,18},{10... | collective-permute-start | bytes 221192 | tf_op jit(solution)/shard_map/ppermute | solution.py:373
  125.6 4.4 %collective-permute-start.19 = (bf16[48,768]{1,0:T(8,128)(2,1)S(1)}, bf16[48,768]{1,0:T(8,128)(2,1)S(1)}, u32[]{:S(2)}, u32[]{:S(2)}) collective-permute-start(bf16[48,768]{1,0:T(8,128)(2,1)S(1)} %get-tuple-element.88), channel_id=1, source_target_pairs={{0,8},{8,16},{16,24},{24,0},{1,9},{9,17},{17,25},{25,1},{2,10},{10... | collective-permute-start | bytes 221192 | tf_op jit(solution)/shard_map/ppermute | solution.py:373
  127.6 4.0 %collective-permute-start.20 = (bf16[48,768]{1,0:T(8,128)(2,1)S(1)}, bf16[48,768]{1,0:T(8,128)(2,1)S(1)}, u32[]{:S(2)}, u32[]{:S(2)}) collective-permute-start(bf16[48,768]{1,0:T(8,128)(2,1)S(1)} %get-tuple-element.87), channel_id=1, source_target_pairs={{0,24},{8,0},{16,8},{24,16},{1,25},{9,1},{17,9},{25,17},{2,26},{10... | collective-permute-start | bytes 221192 | tf_op jit(solution)/shard_map/ppermute | solution.py:373
  131.7 3.3 %collective-permute-start.27 = (bf16[2,24,768]{2,1,0:T(8,128)(2,1)S(1)}, bf16[2,24,768]{2,1,0:T(8,128)(2,1)S(1)}, u32[]{:S(2)}, u32[]{:S(2)}) collective-permute-start(bf16[2,24,768]{2,1,0:T(8,128)(2,1)S(1)} %get-tuple-element.90), channel_id=1, source_target_pairs={{0,1},{1,0},{2,3},{3,2},{4,5},{5,4},{6,7},{7,6},{8,9},{9,8},{10,11... | collective-permute-start | bytes 221192 | tf_op jit(solution)/shard_map/ppermute | solution.py:33
  (15 other events, 82.4 us)

commit v9 on v8

--- a/solution.py
+++ b/solution.py
@@ -13,7 +13,7 @@
 RING = 4
 CORES = 2
 SLOTS = 2
-VMEM_LIMIT = 56 * 2**20
+VMEM_LIMIT = 52 * 2**20
 BF16 = jnp.bfloat16
 F32 = jnp.float32
 NT = (((1,), (1,)), ((), ()))

time: 137 us -> 136 us (level)
  Pallas kernels: 37.7 us -> 35.8 us
    pallas_call x4, Pallas kernels: 12.2 us -> 10.5 us  [pack(): pl.pallas_call(functools.partial(pack_kernel, quarter, dom, which, flip),...]
    unnamed x35 -> x21, local copies, waits for them, and re-layouts: 3.39 us -> 4.17 us
  transfers between devices with their start and end apart: 30 -> 30, of which waited for: 13 -> 13; matrix products, arithmetic and copies ran while one was open for 2% -> 3% of each run, Pallas kernels for 18% -> 17%
where the time goes in v9:
time: 136 us; the launch traced here: 135 us
  starting transfers between devices  57.4 us (42%)
  Pallas kernels  35.8 us (26%)
  waiting for transfers between devices  31.1 us (23%)
  local copies, waits for them, and re-layouts  7.27 us (5%)
  other arithmetic  3.3 us (2%)
    ppermute x14, waiting for transfers between devices, send(): hop(s, key[1])(part)  21.7 us
    ppermute x12, starting transfers between devices, sum_over(): total = total + lax.ppermute(parts[s].astype(BF16), axis, perm).astype(F32)  21.3 us
    ppermute x14, starting transfers between devices, send(): hop(s, key[1])(part)  20.6 us
    pallas_call x2, Pallas kernels, work(): pl.pallas_call(functools.partial(work_kernel, quarter, dom, jobs, finish,...  15.1 us
    pallas_call x4, Pallas kernels, pack(): pl.pallas_call(functools.partial(pack_kernel, quarter, dom, which, flip),...  10.5 us
    ppermute x12, waiting for transfers between devices, sum_over(): total = total + lax.ppermute(parts[s].astype(BF16), axis, perm).astype(F32)  8.4 us
    all_to_all x1, starting transfers between devices, body(): lax.all_to_all(jnp.broadcast_to(both[None], (chips,) + both.shape), ('y',...  6.8 us
    pallas_call x1, Pallas kernels, add_cycle(): pl.pallas_call(functools.partial(cycle_kernel, [[place for _, place in in...  6 us
  transfers between devices with their start and end apart: 30, of which 13 were waited for; matrix products, arithmetic and copies ran while one was open for 3% of the time, Pallas kernels for 17%

profile of v9, /device:TPU:1, one launch (start us, length us, event | category | flops | bytes accessed | tf_op | source)
XLA Modules:
  0.0 135.2 jit_solution(15224507640427648356)
XLA Ops:
  0.9 2.5 %pack_tiles.4 = (bf16[2,128,768]{2,1,0:T(8,128)(2,1)S(1)}, bf16[2,128,768]{2,1,0:T(8,128)(2,1)S(1)}, bf16[2,128,768]{2,1,0:T(8,128)(2,1)S(1)}, bf16[2,128,768]{2,1,0:T(8,128)(2,1)S(1)}) custom-call(s32[100]{0:T(128)S(1)} %concatenate.23.scalars_ref, bf16[1,1024,4096]{2,1,0:T(8,128)(2,1)} %dfint_ref.7), custom_call_target="tpu_custom_call" | custom-call | flops 12000000000 | bytes 1 | tf_op jit(solution)/shard_map/pack_tiles/pallas_call | solution.py:78
  7.1 3.7 %collective-permute-start.10 = (bf16[2,128,768]{2,1,0:T(8,128)(2,1)S(1)}, bf16[2,128,768]{2,1,0:T(8,128)(2,1)S(1)}, u32[]{:S(2)}, u32[]{:S(2)}) collective-permute-start(bf16[2,128,768]{2,1,0:T(8,128)(2,1)S(1)} %get-tuple-element.58), channel_id=1, source_target_pairs={{0,64},{1,65},{32,96},{33,97},{64,0},{65,1},{96,32},{97,33},{2,66}... | collective-permute-start | bytes 1179656 | tf_op jit(solution)/shard_map/ppermute | solution.py:399
  11.5 1.9 %collective-permute-start.9 = (bf16[2,128,768]{2,1,0:T(8,128)(2,1)S(1)}, bf16[2,128,768]{2,1,0:T(8,128)(2,1)}, u32[]{:S(2)}, u32[]{:S(2)}) collective-permute-start(bf16[2,128,768]{2,1,0:T(8,128)(2,1)S(1)} %get-tuple-element.57), channel_id=1, source_target_pairs={{0,96},{1,97},{32,0},{33,1},{64,32},{65,33},{96,64},{97,65},{2,98}... | collective-permute-start | bytes 1179656 | tf_op jit(solution)/shard_map/ppermute | solution.py:399
  13.5 2.6 %pack_tiles.5 = (bf16[2,128,768]{2,1,0:T(8,128)(2,1)}, bf16[2,128,768]{2,1,0:T(8,128)(2,1)S(1)}, bf16[2,128,768]{2,1,0:T(8,128)(2,1)S(1)}, bf16[2,128,768]{2,1,0:T(8,128)(2,1)S(1)}) custom-call(s32[100]{0:T(128)S(1)} %concatenate.23.scalars_ref, bf16[1,1024,4096]{2,1,0:T(8,128)(2,1)} %dfint_ref.7), custom_call_target="tpu_custom_call" | custom-call | flops 12000000000 | bytes 1 | tf_op jit(solution)/shard_map/pack_tiles/pallas_call | solution.py:78
  16.8 2.7 %collective-permute-start.2 = (bf16[2,128,768]{2,1,0:T(8,128)(2,1)S(1)}, bf16[2,128,768]{2,1,0:T(8,128)(2,1)S(1)}, u32[]{:S(2)}, u32[]{:S(2)}) collective-permute-start(bf16[2,128,768]{2,1,0:T(8,128)(2,1)S(1)} %get-tuple-element.49), channel_id=1, source_target_pairs={{0,96},{1,97},{32,0},{33,1},{64,32},{65,33},{96,64},{97,65},{2,98}... | collective-permute-start | bytes 1179656 | tf_op jit(solution)/shard_map/ppermute | solution.py:399
  20.5 1.6 %broadcast_in_dim.34 = bf16[16,2,48,768]{3,2,1,0:T(8,128)(2,1)} broadcast(bf16[2,48,768]{2,1,0:T(8,128)(2,1)S(1)} %maximum_select_fusion), dimensions={1,2,3} | broadcast | bytes 2506752 | tf_op jit(solution)/shard_map/broadcast_in_dim | solution.py:421
  22.1 6.8 %all-to-all-start = ((bf16[16,2,48,768]{3,2,1,0:T(8,128)(2,1)}), bf16[16,2,48,768]{3,2,1,0:T(8,128)(2,1)}, u32[]{:S(2)}, u32[]{:S(2)}) async-start(bf16[16,2,48,768]{3,2,1,0:T(8,128)(2,1)} %broadcast_in_dim.34), calls=%async_computation | async-start | bytes 4718592 | tf_op jit(solution)/shard_map/all_to_all | solution.py:420
  28.9 2.5 %pack_tiles.6 = (bf16[2,128,768]{2,1,0:T(8,128)(2,1)S(1)}, bf16[2,128,768]{2,1,0:T(8,128)(2,1)S(1)}, bf16[2,128,768]{2,1,0:T(8,128)(2,1)S(1)}, bf16[2,128,768]{2,1,0:T(8,128)(2,1)S(1)}) custom-call(s32[100]{0:T(128)S(1)} %concatenate.23.scalars_ref, bf16[1,1024,4096]{2,1,0:T(8,128)(2,1)} %dfint_ref.7), custom_call_target="tpu_custom_call" | custom-call | flops 12000000000 | bytes 1 | tf_op jit(solution)/shard_map/pack_tiles/pallas_call | solution.py:78
  31.5 2.0 %collective-permute-start.4 = (bf16[2,128,768]{2,1,0:T(8,128)(2,1)S(1)}, bf16[2,128,768]{2,1,0:T(8,128)(2,1)S(1)}, u32[]{:S(2)}, u32[]{:S(2)}) collective-permute-start(bf16[2,128,768]{2,1,0:T(8,128)(2,1)S(1)} %get-tuple-element.52), channel_id=1, source_target_pairs={{0,33},{1,32},{32,65},{33,64},{64,97},{65,96},{96,1},{97,0},{2,35}... | collective-permute-start | bytes 1179656 | tf_op jit(solution)/shard_map/ppermute | solution.py:399
  34.6 2.8 %collective-permute-done.1.rest_0_ = bf16[2,128,768]{2,1,0:T(8,128)(2,1)S(1)} collective-permute-done((bf16[2,128,768]{2,1,0:T(8,128)(2,1)}, bf16[2,128,768]{2,1,0:T(8,128)(2,1)S(1)}, u32[]{:S(2)}, u32[]{:S(2)}) %collective-permute-start.1) | collective-permute-done | bytes 393248 | tf_op jit(solution)/shard_map/ppermute | solution.py:399
  37.4 3.3 %collective-permute-start.6 = (bf16[2,128,768]{2,1,0:T(8,128)(2,1)S(1)}, bf16[2,128,768]{2,1,0:T(8,128)(2,1)S(1)}, u32[]{:S(2)}, u32[]{:S(2)}) collective-permute-start(bf16[2,128,768]{2,1,0:T(8,128)(2,1)S(1)} %get-tuple-element.54), channel_id=1, source_target_pairs={{0,65},{1,64},{32,97},{33,96},{64,1},{65,0},{96,33},{97,32},{2,67}... | collective-permute-start | bytes 1179656 | tf_op jit(solution)/shard_map/ppermute | solution.py:399
  40.8 2.9 %pack_tiles.7 = (bf16[2,128,768]{2,1,0:T(8,128)(2,1)}, bf16[2,128,768]{2,1,0:T(8,128)(2,1)}, bf16[2,128,768]{2,1,0:T(8,128)(2,1)}, bf16[2,128,768]{2,1,0:T(8,128)(2,1)}) custom-call(s32[100]{0:T(128)S(1)} %concatenate.23.scalars_ref, bf16[1,1024,4096]{2,1,0:T(8,128)(2,1)} %dfint_ref.7), custom_call_target="tpu_custom_call" | custom-call | flops 12000000000 | bytes 1 | tf_op jit(solution)/shard_map/pack_tiles/pallas_call | solution.py:78
  45.4 2.2 %collective-permute-start.11 = (bf16[2,128,768]{2,1,0:T(8,128)(2,1)}, bf16[2,128,768]{2,1,0:T(8,128)(2,1)S(1)}, u32[]{:S(2)}, u32[]{:S(2)}) collective-permute-start(bf16[2,128,768]{2,1,0:T(8,128)(2,1)} %get-tuple-element.61), channel_id=1, source_target_pairs={{0,33},{1,32},{32,65},{33,64},{64,97},{65,96},{96,1},{97,0},{2,35}... | collective-permute-start | bytes 1179656 | tf_op jit(solution)/shard_map/ppermute | solution.py:399
  47.6 7.3 %collective-permute-done.4.rest_4_ = bf16[2,128,768]{2,1,0:T(8,128)(2,1)S(1)} collective-permute-done((bf16[2,128,768]{2,1,0:T(8,128)(2,1)S(1)}, bf16[2,128,768]{2,1,0:T(8,128)(2,1)S(1)}, u32[]{:S(2)}, u32[]{:S(2)}) %collective-permute-start.4) | collective-permute-done | bytes 393248 | tf_op jit(solution)/shard_map/ppermute | solution.py:399
  55.5 2.8 %collective-permute-start.13 = (bf16[2,128,768]{2,1,0:T(8,128)(2,1)}, bf16[2,128,768]{2,1,0:T(8,128)(2,1)S(1)}, u32[]{:S(2)}, u32[]{:S(2)}) collective-permute-start(bf16[2,128,768]{2,1,0:T(8,128)(2,1)} %get-tuple-element.63), channel_id=1, source_target_pairs={{0,65},{1,64},{32,97},{33,96},{64,1},{65,0},{96,33},{97,32},{2,67}... | collective-permute-start | bytes 1179656 | tf_op jit(solution)/shard_map/ppermute | solution.py:399
  58.3 5.1 %collective-permute-done.6.rest_6_ = bf16[2,128,768]{2,1,0:T(8,128)(2,1)S(1)} collective-permute-done((bf16[2,128,768]{2,1,0:T(8,128)(2,1)S(1)}, bf16[2,128,768]{2,1,0:T(8,128)(2,1)S(1)}, u32[]{:S(2)}, u32[]{:S(2)}) %collective-permute-start.6) | collective-permute-done | bytes 393248 | tf_op jit(solution)/shard_map/ppermute | solution.py:399
  64.1 10.8 %half_and_ladder.1 = (bf16[3,768,768]{2,1,0:T(8,128)(2,1)}, f32[768,768]{1,0:T(8,128)}, f32[768,768]{1,0:T(8,128)}, f32[8,128]{1,0:T(8,128)S(1)}) custom-call(s32[100]{0:T(128)S(1)} %concatenate.23.scalars_ref, bf16[16,2,48,768]{3,2,1,0:T(8,128)(2,1)} %all-to-all-done.amp_ref, bf16[2,128,768]{2,1,0:T(8,128)(2,1)S(1)} %collective-permute-done.1.rest_0_, ...), custom_call_target="tpu_custom_call" | custom-call | flops 1 | bytes 1 | tf_op jit(solution)/shard_map/half_and_ladder/pallas_call | solution.py:202
  75.0 4.3 %collective-permute-done.13.rest_3_ = bf16[2,128,768]{2,1,0:T(8,128)(2,1)S(1)} collective-permute-done((bf16[2,128,768]{2,1,0:T(8,128)(2,1)}, bf16[2,128,768]{2,1,0:T(8,128)(2,1)S(1)}, u32[]{:S(2)}, u32[]{:S(2)}) %collective-permute-start.13) | collective-permute-done | bytes 393248 | tf_op jit(solution)/shard_map/ppermute | solution.py:399
  79.3 4.3 %half_ladder.1 = (bf16[1,768,768]{2,1,0:T(8,128)(2,1)}, bf16[1,768,768]{2,1,0:T(8,128)(2,1)}, f32[8,128]{1,0:T(8,128)}) custom-call(s32[100]{0:T(128)S(1)} %concatenate.23.scalars_ref, bf16[16,2,48,768]{3,2,1,0:T(8,128)(2,1)} %all-to-all-done.amp_ref, f32[8,128]{1,0:T(8,128)S(1)} %get-tuple-element.60.rest_0_, ...), custom_call_target="tpu_custom_call" | custom-call | flops 1 | bytes 1 | tf_op jit(solution)/shard_map/half_ladder/pallas_call | solution.py:202
  83.6 5.0 %all-to-all-start.1 = ((f32[8,1,128]{2,1,0:T(1,128)}), f32[8,1,128]{2,1,0:T(1,128)S(1)}, u32[]{:S(2)}, u32[]{:S(2)}) async-start(f32[8,1,128]{2,1,0:T(1,128)} %bitcast.5), calls=%async_computation.1 | async-start | bytes 8192 | tf_op jit(solution)/shard_map/all_to_all | solution.py:440
  89.9 4.2 %ladder.1.rest_5_ = f32[768,768]{1,0:T(8,128)} custom-call(bf16[1,768,768]{2,1,0:T(8,128)(2,1)S(1)} %copy-done, bf16[1,768,768]{2,1,0:T(8,128)(2,1)} %get-tuple-element.69.half_ref, f32[768,768]{1,0:T(8,128)} %get-tuple-element.70.before_ref), custom_call_target="tpu_custom_call" | custom-call | flops 1 | bytes 1 | tf_op jit(solution)/shard_map/ladder/pallas_call | solution.py:260
  94.1 6.0 %add_cycle.1 = (f32[4,48,768]{2,1,0:T(8,128)}, bf16[4,48,768]{2,1,0:T(8,128)(2,1)S(1)}, bf16[4,48,768]{2,1,0:T(8,128)(2,1)S(1)}, bf16[4,48,768]{2,1,0:T(8,128)(2...) custom-call(s32[100]{0:T(128)S(1)} %concatenate.23.scalars_ref, ...), custom_call_target="tpu_custom_call" | custom-call | flops 1 | bytes 1 | tf_op jit(solution)/shard_map/add_cycle/pallas_call | solution.py:346
  100.1 3.0 %collective-permute-start.21 = (bf16[4,48,768]{2,1,0:T(8,128)(2,1)S(1)}, bf16[4,48,768]{2,1,0:T(8,128)(2,1)S(1)}, u32[]{:S(2)}, u32[]{:S(2)}) collective-permute-start(bf16[4,48,768]{2,1,0:T(8,128)(2,1)S(1)} %get-tuple-element.76), channel_id=1, source_target_pairs={{0,16},{8,24},{16,0},{24,8},{1,17},{9,25},{17,1},{25,9},{2,18},{10... | collective-permute-start | bytes 884744 | tf_op jit(solution)/shard_map/ppermute | solution.py:373
  103.5 2.3 %collective-permute-start.23 = (bf16[4,48,768]{2,1,0:T(8,128)(2,1)S(1)}, bf16[4,48,768]{2,1,0:T(8,128)(2,1)S(1)}, u32[]{:S(2)}, u32[]{:S(2)}) collective-permute-start(bf16[4,48,768]{2,1,0:T(8,128)(2,1)S(1)} %get-tuple-element.78), channel_id=1, source_target_pairs={{0,24},{8,0},{16,8},{24,16},{1,25},{9,1},{17,9},{25,17},{2,26},{10... | collective-permute-start | bytes 884744 | tf_op jit(solution)/shard_map/ppermute | solution.py:373
  105.8 2.7 %collective-permute-start.15 = (bf16[4,48,768]{2,1,0:T(8,128)(2,1)S(1)}, bf16[4,48,768]{2,1,0:T(8,128)(2,1)S(1)}, u32[]{:S(2)}, u32[]{:S(2)}) collective-permute-start(bf16[4,48,768]{2,1,0:T(8,128)(2,1)S(1)} %get-tuple-element.72), channel_id=1, source_target_pairs={{0,4},{2,6},{4,0},{6,2},{1,5},{3,7},{5,1},{7,3},{8,12},{10,14},{12... | collective-permute-start | bytes 884744 | tf_op jit(solution)/shard_map/ppermute | solution.py:373
  110.4 2.5 %collective-permute-start.17 = (bf16[4,48,768]{2,1,0:T(8,128)(2,1)S(1)}, bf16[4,48,768]{2,1,0:T(8,128)(2,1)S(1)}, u32[]{:S(2)}, u32[]{:S(2)}) collective-permute-start(bf16[4,48,768]{2,1,0:T(8,128)(2,1)S(1)} %get-tuple-element.74), channel_id=1, source_target_pairs={{0,6},{2,0},{4,2},{6,4},{1,7},{3,1},{5,3},{7,5},{8,14},{10,8},{12,... | collective-permute-start | bytes 884744 | tf_op jit(solution)/shard_map/ppermute | solution.py:373
  112.9 4.1 %collective-permute-done.22 = bf16[4,48,768]{2,1,0:T(8,128)(2,1)S(1)} collective-permute-done((bf16[4,48,768]{2,1,0:T(8,128)(2,1)S(1)}, bf16[4,48,768]{2,1,0:T(8,128)(2,1)S(1)}, u32[]{:S(2)}, u32[]{:S(2)}) %collective-permute-start.22) | collective-permute-done | bytes 294944 | tf_op jit(solution)/shard_map/ppermute | solution.py:373
  118.3 2.8 %collective-permute-start.24 = (bf16[48,768]{1,0:T(8,128)(2,1)S(1)}, bf16[48,768]{1,0:T(8,128)(2,1)S(1)}, u32[]{:S(2)}, u32[]{:S(2)}) collective-permute-start(bf16[48,768]{1,0:T(8,128)(2,1)S(1)} %get-tuple-element.83), channel_id=1, source_target_pairs={{0,4},{2,6},{4,0},{6,2},{1,5},{3,7},{5,1},{7,3},{8,12},{10,14},{12... | collective-permute-start | bytes 221192 | tf_op jit(solution)/shard_map/ppermute | solution.py:373
  121.4 2.3 %collective-permute-start.26 = (bf16[48,768]{1,0:T(8,128)(2,1)S(1)}, bf16[48,768]{1,0:T(8,128)(2,1)S(1)}, u32[]{:S(2)}, u32[]{:S(2)}) collective-permute-start(bf16[48,768]{1,0:T(8,128)(2,1)S(1)} %get-tuple-element.84), channel_id=1, source_target_pairs={{0,6},{2,0},{4,2},{6,4},{1,7},{3,1},{5,3},{7,5},{8,14},{10,8},{12,... | collective-permute-start | bytes 221192 | tf_op jit(solution)/shard_map/ppermute | solution.py:373
  124.0 1.8 %collective-permute-start.18 = (bf16[48,768]{1,0:T(8,128)(2,1)S(1)}, bf16[48,768]{1,0:T(8,128)(2,1)S(1)}, u32[]{:S(2)}, u32[]{:S(2)}) collective-permute-start(bf16[48,768]{1,0:T(8,128)(2,1)S(1)} %get-tuple-element.86), channel_id=1, source_target_pairs={{0,16},{8,24},{16,0},{24,8},{1,17},{9,25},{17,1},{25,9},{2,18},{10... | collective-permute-start | bytes 221192 | tf_op jit(solution)/shard_map/ppermute | solution.py:373
  128.7 1.9 %collective-permute-done.19 = bf16[48,768]{1,0:T(8,128)(2,1)S(1)} collective-permute-done((bf16[48,768]{1,0:T(8,128)(2,1)S(1)}, bf16[48,768]{1,0:T(8,128)(2,1)S(1)}, u32[]{:S(2)}, u32[]{:S(2)}) %collective-permute-start.19) | collective-permute-done | bytes 73760 | tf_op jit(solution)/shard_map/ppermute | solution.py:373
  131.3 2.4 %collective-permute-start.27 = (bf16[2,24,768]{2,1,0:T(8,128)(2,1)S(1)}, bf16[2,24,768]{2,1,0:T(8,128)(2,1)S(1)}, u32[]{:S(2)}, u32[]{:S(2)}) collective-permute-start(bf16[2,24,768]{2,1,0:T(8,128)(2,1)S(1)} %get-tuple-element.90), channel_id=1, source_target_pairs={{0,1},{1,0},{2,3},{3,2},{4,5},{5,4},{6,7},{7,6},{8,9},{9,8},{10,11... | collective-permute-start | bytes 221192 | tf_op jit(solution)/shard_map/ppermute | solution.py:33
  (79 shorter events, 21.6 us)
Async XLA Ops:
  5.7 10.4 %collective-permute-start = (bf16[2,24,768]{2,1,0:T(8,128)(2,1)S(1)}, bf16[2,24,768]{2,1,0:T(8,128)(2,1)S(1)}, u32[]{:S(2)}, u32[]{:S(2)}) collective-permute-start(bf16[2,24,768]{2,1,0:T(8,128)(2,1)S(1)} %get-tuple-element.92), channel_id=1, source_target_pairs={{0,1},{1,0},{2,3},{3,2},{4,5},{5,4},{6,7},{7,6},{8,9},{9,8},{10,11... | collective-permute-start | bytes 221192 | tf_op jit(solution)/shard_map/ppermute | solution.py:33
  7.1 24.3 %collective-permute-start.10 = (bf16[2,128,768]{2,1,0:T(8,128)(2,1)S(1)}, bf16[2,128,768]{2,1,0:T(8,128)(2,1)S(1)}, u32[]{:S(2)}, u32[]{:S(2)}) collective-permute-start(bf16[2,128,768]{2,1,0:T(8,128)(2,1)S(1)} %get-tuple-element.58), channel_id=1, source_target_pairs={{0,64},{1,65},{32,96},{33,97},{64,0},{65,1},{96,32},{97,33},{2,66}... | collective-permute-start | bytes 1179656 | tf_op jit(solution)/shard_map/ppermute | solution.py:399
  10.8 20.7 %collective-permute-start.8 = (bf16[2,128,768]{2,1,0:T(8,128)(2,1)S(1)}, bf16[2,128,768]{2,1,0:T(8,128)(2,1)}, u32[]{:S(2)}, u32[]{:S(2)}) collective-permute-start(bf16[2,128,768]{2,1,0:T(8,128)(2,1)S(1)} %get-tuple-element.56), channel_id=1, source_target_pairs={{0,32},{1,33},{32,64},{33,65},{64,96},{65,97},{96,0},{97,1},{2,34}... | collective-permute-start | bytes 1179656 | tf_op jit(solution)/shard_map/ppermute | solution.py:399
  11.5 22.0 %collective-permute-start.9 = (bf16[2,128,768]{2,1,0:T(8,128)(2,1)S(1)}, bf16[2,128,768]{2,1,0:T(8,128)(2,1)}, u32[]{:S(2)}, u32[]{:S(2)}) collective-permute-start(bf16[2,128,768]{2,1,0:T(8,128)(2,1)S(1)} %get-tuple-element.57), channel_id=1, source_target_pairs={{0,96},{1,97},{32,0},{33,1},{64,32},{65,33},{96,64},{97,65},{2,98}... | collective-permute-start | bytes 1179656 | tf_op jit(solution)/shard_map/ppermute | solution.py:399
  16.0 21.4 %collective-permute-start.1 = (bf16[2,128,768]{2,1,0:T(8,128)(2,1)}, bf16[2,128,768]{2,1,0:T(8,128)(2,1)S(1)}, u32[]{:S(2)}, u32[]{:S(2)}) collective-permute-start(bf16[2,128,768]{2,1,0:T(8,128)(2,1)} %get-tuple-element.48), channel_id=1, source_target_pairs={{0,32},{1,33},{32,64},{33,65},{64,96},{65,97},{96,0},{97,1},{2,34}... | collective-permute-start | bytes 1179656 | tf_op jit(solution)/shard_map/ppermute | solution.py:399
  16.8 26.9 %collective-permute-start.2 = (bf16[2,128,768]{2,1,0:T(8,128)(2,1)S(1)}, bf16[2,128,768]{2,1,0:T(8,128)(2,1)S(1)}, u32[]{:S(2)}, u32[]{:S(2)}) collective-permute-start(bf16[2,128,768]{2,1,0:T(8,128)(2,1)S(1)} %get-tuple-element.49), channel_id=1, source_target_pairs={{0,96},{1,97},{32,0},{33,1},{64,32},{65,33},{96,64},{97,65},{2,98}... | collective-permute-start | bytes 1179656 | tf_op jit(solution)/shard_map/ppermute | solution.py:399
  22.1 42.0 %all-to-all-start = ((bf16[16,2,48,768]{3,2,1,0:T(8,128)(2,1)}), bf16[16,2,48,768]{3,2,1,0:T(8,128)(2,1)}, u32[]{:S(2)}, u32[]{:S(2)}) async-start(bf16[16,2,48,768]{3,2,1,0:T(8,128)(2,1)} %broadcast_in_dim.34), calls=%async_computation | async-start | bytes 4718592 | tf_op jit(solution)/shard_map/all_to_all | solution.py:420
  31.4 12.3 %copy-start.4 = (bf16[2,128,768]{2,1,0:T(8,128)(2,1)}, bf16[2,128,768]{2,1,0:T(8,128)(2,1)S(1)}, u32[]{:S(2)}) copy-start(bf16[2,128,768]{2,1,0:T(8,128)(2,1)S(1)} %collective-permute-done.10.rest_10_) | copy-start | bytes 1179652
  31.4 14.0 %collective-permute-start.3 = (bf16[2,128,768]{2,1,0:T(8,128)(2,1)S(1)}, bf16[2,128,768]{2,1,0:T(8,128)(2,1)S(1)}, u32[]{:S(2)}, u32[]{:S(2)}) collective-permute-start(bf16[2,128,768]{2,1,0:T(8,128)(2,1)S(1)} %get-tuple-element.50), channel_id=1, source_target_pairs={{0,64},{1,65},{32,96},{33,97},{64,0},{65,1},{96,32},{97,33},{2,66}... | collective-permute-start | bytes 1179656 | tf_op jit(solution)/shard_map/ppermute | solution.py:399
  31.5 23.3 %collective-permute-start.4 = (bf16[2,128,768]{2,1,0:T(8,128)(2,1)S(1)}, bf16[2,128,768]{2,1,0:T(8,128)(2,1)S(1)}, u32[]{:S(2)}, u32[]{:S(2)}) collective-permute-start(bf16[2,128,768]{2,1,0:T(8,128)(2,1)S(1)} %get-tuple-element.52), channel_id=1, source_target_pairs={{0,33},{1,32},{32,65},{33,64},{64,97},{65,96},{96,1},{97,0},{2,35}... | collective-permute-start | bytes 1179656 | tf_op jit(solution)/shard_map/ppermute | solution.py:399
  33.6 21.9 %collective-permute-start.5 = (bf16[2,128,768]{2,1,0:T(8,128)(2,1)S(1)}, bf16[2,128,768]{2,1,0:T(8,128)(2,1)S(1)}, u32[]{:S(2)}, u32[]{:S(2)}) collective-permute-start(bf16[2,128,768]{2,1,0:T(8,128)(2,1)S(1)} %get-tuple-element.53), channel_id=1, source_target_pairs={{0,97},{1,96},{32,1},{33,0},{64,33},{65,32},{96,65},{97,64},{2,99}... | collective-permute-start | bytes 1179656 | tf_op jit(solution)/shard_map/ppermute | solution.py:399
  37.4 25.9 %collective-permute-start.6 = (bf16[2,128,768]{2,1,0:T(8,128)(2,1)S(1)}, bf16[2,128,768]{2,1,0:T(8,128)(2,1)S(1)}, u32[]{:S(2)}, u32[]{:S(2)}) collective-permute-start(bf16[2,128,768]{2,1,0:T(8,128)(2,1)S(1)} %get-tuple-element.54), channel_id=1, source_target_pairs={{0,65},{1,64},{32,97},{33,96},{64,1},{65,0},{96,33},{97,32},{2,67}... | collective-permute-start | bytes 1179656 | tf_op jit(solution)/shard_map/ppermute | solution.py:399
  43.7 20.4 %collective-permute-start.7 = (bf16[2,128,768]{2,1,0:T(8,128)(2,1)S(1)}, bf16[2,128,768]{2,1,0:T(8,128)(2,1)}, u32[]{:S(2)}, u32[]{:S(2)}) collective-permute-start(bf16[2,128,768]{2,1,0:T(8,128)(2,1)S(1)} %get-tuple-element.55), channel_id=1, source_target_pairs={{0,1},{1,0},{32,33},{33,32},{64,65},{65,64},{96,97},{97,96},{2,3},... | collective-permute-start | bytes 1179656 | tf_op jit(solution)/shard_map/ppermute | solution.py:399
  45.4 29.6 %collective-permute-start.11 = (bf16[2,128,768]{2,1,0:T(8,128)(2,1)}, bf16[2,128,768]{2,1,0:T(8,128)(2,1)S(1)}, u32[]{:S(2)}, u32[]{:S(2)}) collective-permute-start(bf16[2,128,768]{2,1,0:T(8,128)(2,1)} %get-tuple-element.61), channel_id=1, source_target_pairs={{0,33},{1,32},{32,65},{33,64},{64,97},{65,96},{96,1},{97,0},{2,35}... | collective-permute-start | bytes 1179656 | tf_op jit(solution)/shard_map/ppermute | solution.py:399
  54.9 20.1 %collective-permute-start.12 = (bf16[2,128,768]{2,1,0:T(8,128)(2,1)}, bf16[2,128,768]{2,1,0:T(8,128)(2,1)S(1)}, u32[]{:S(2)}, u32[]{:S(2)}) collective-permute-start(bf16[2,128,768]{2,1,0:T(8,128)(2,1)} %get-tuple-element.62), channel_id=1, source_target_pairs={{0,97},{1,96},{32,1},{33,0},{64,33},{65,32},{96,65},{97,64},{2,99}... | collective-permute-start | bytes 1179656 | tf_op jit(solution)/shard_map/ppermute | solution.py:399
  55.5 23.8 %collective-permute-start.13 = (bf16[2,128,768]{2,1,0:T(8,128)(2,1)}, bf16[2,128,768]{2,1,0:T(8,128)(2,1)S(1)}, u32[]{:S(2)}, u32[]{:S(2)}) collective-permute-start(bf16[2,128,768]{2,1,0:T(8,128)(2,1)} %get-tuple-element.63), channel_id=1, source_target_pairs={{0,65},{1,64},{32,97},{33,96},{64,1},{65,0},{96,33},{97,32},{2,67}... | collective-permute-start | bytes 1179656 | tf_op jit(solution)/shard_map/ppermute | solution.py:399
  64.1 15.2 %collective-permute-start.14 = (bf16[2,128,768]{2,1,0:T(8,128)(2,1)}, bf16[2,128,768]{2,1,0:T(8,128)(2,1)S(1)}, u32[]{:S(2)}, u32[]{:S(2)}) collective-permute-start(bf16[2,128,768]{2,1,0:T(8,128)(2,1)} %get-tuple-element.64), channel_id=1, source_target_pairs={{0,1},{1,0},{32,33},{33,32},{64,65},{65,64},{96,97},{97,96},{2,3},... | collective-permute-start | bytes 1179656 | tf_op jit(solution)/shard_map/ppermute | solution.py:399
  83.6 10.5 %all-to-all-start.1 = ((f32[8,1,128]{2,1,0:T(1,128)}), f32[8,1,128]{2,1,0:T(1,128)S(1)}, u32[]{:S(2)}, u32[]{:S(2)}) async-start(f32[8,1,128]{2,1,0:T(1,128)} %bitcast.5), calls=%async_computation.1 | async-start | bytes 8192 | tf_op jit(solution)/shard_map/all_to_all | solution.py:440
  100.1 23.7 %copy-start.3 = (f32[4,48,768]{2,1,0:T(8,128)S(1)}, f32[4,48,768]{2,1,0:T(8,128)}, u32[]{:S(2)}) copy-start(f32[4,48,768]{2,1,0:T(8,128)} %get-tuple-element.71) | copy-start | bytes 1769476
  100.1 10.3 %collective-permute-start.21 = (bf16[4,48,768]{2,1,0:T(8,128)(2,1)S(1)}, bf16[4,48,768]{2,1,0:T(8,128)(2,1)S(1)}, u32[]{:S(2)}, u32[]{:S(2)}) collective-permute-start(bf16[4,48,768]{2,1,0:T(8,128)(2,1)S(1)} %get-tuple-element.76), channel_id=1, source_target_pairs={{0,16},{8,24},{16,0},{24,8},{1,17},{9,25},{17,1},{25,9},{2,18},{10... | collective-permute-start | bytes 884744 | tf_op jit(solution)/shard_map/ppermute | solution.py:373
  103.1 13.9 %collective-permute-start.22 = (bf16[4,48,768]{2,1,0:T(8,128)(2,1)S(1)}, bf16[4,48,768]{2,1,0:T(8,128)(2,1)S(1)}, u32[]{:S(2)}, u32[]{:S(2)}) collective-permute-start(bf16[4,48,768]{2,1,0:T(8,128)(2,1)S(1)} %get-tuple-element.77), channel_id=1, source_target_pairs={{0,8},{8,16},{16,24},{24,0},{1,9},{9,17},{17,25},{25,1},{2,10},{10... | collective-permute-start | bytes 884744 | tf_op jit(solution)/shard_map/ppermute | solution.py:373
  103.5 13.5 %collective-permute-start.23 = (bf16[4,48,768]{2,1,0:T(8,128)(2,1)S(1)}, bf16[4,48,768]{2,1,0:T(8,128)(2,1)S(1)}, u32[]{:S(2)}, u32[]{:S(2)}) collective-permute-start(bf16[4,48,768]{2,1,0:T(8,128)(2,1)S(1)} %get-tuple-element.78), channel_id=1, source_target_pairs={{0,24},{8,0},{16,8},{24,16},{1,25},{9,1},{17,9},{25,17},{2,26},{10... | collective-permute-start | bytes 884744 | tf_op jit(solution)/shard_map/ppermute | solution.py:373
  105.8 15.6 %collective-permute-start.15 = (bf16[4,48,768]{2,1,0:T(8,128)(2,1)S(1)}, bf16[4,48,768]{2,1,0:T(8,128)(2,1)S(1)}, u32[]{:S(2)}, u32[]{:S(2)}) collective-permute-start(bf16[4,48,768]{2,1,0:T(8,128)(2,1)S(1)} %get-tuple-element.72), channel_id=1, source_target_pairs={{0,4},{2,6},{4,0},{6,2},{1,5},{3,7},{5,1},{7,3},{8,12},{10,14},{12... | collective-permute-start | bytes 884744 | tf_op jit(solution)/shard_map/ppermute | solution.py:373
  108.5 15.2 %collective-permute-start.16 = (bf16[4,48,768]{2,1,0:T(8,128)(2,1)S(1)}, bf16[4,48,768]{2,1,0:T(8,128)(2,1)S(1)}, u32[]{:S(2)}, u32[]{:S(2)}) collective-permute-start(bf16[4,48,768]{2,1,0:T(8,128)(2,1)S(1)} %get-tuple-element.73), channel_id=1, source_target_pairs={{0,2},{2,4},{4,6},{6,0},{1,3},{3,5},{5,7},{7,1},{8,10},{10,12},{12... | collective-permute-start | bytes 884744 | tf_op jit(solution)/shard_map/ppermute | solution.py:373
  110.4 13.4 %collective-permute-start.17 = (bf16[4,48,768]{2,1,0:T(8,128)(2,1)S(1)}, bf16[4,48,768]{2,1,0:T(8,128)(2,1)S(1)}, u32[]{:S(2)}, u32[]{:S(2)}) collective-permute-start(bf16[4,48,768]{2,1,0:T(8,128)(2,1)S(1)} %get-tuple-element.74), channel_id=1, source_target_pairs={{0,6},{2,0},{4,2},{6,4},{1,7},{3,1},{5,3},{7,5},{8,14},{10,8},{12,... | collective-permute-start | bytes 884744 | tf_op jit(solution)/shard_map/ppermute | solution.py:373
  118.3 9.0 %collective-permute-start.24 = (bf16[48,768]{1,0:T(8,128)(2,1)S(1)}, bf16[48,768]{1,0:T(8,128)(2,1)S(1)}, u32[]{:S(2)}, u32[]{:S(2)}) collective-permute-start(bf16[48,768]{1,0:T(8,128)(2,1)S(1)} %get-tuple-element.83), channel_id=1, source_target_pairs={{0,4},{2,6},{4,0},{6,2},{1,5},{3,7},{5,1},{7,3},{8,12},{10,14},{12... | collective-permute-start | bytes 221192 | tf_op jit(solution)/shard_map/ppermute | solution.py:373
  121.1 7.4 %collective-permute-start.25 = (bf16[48,768]{1,0:T(8,128)(2,1)S(1)}, bf16[48,768]{1,0:T(8,128)(2,1)S(1)}, u32[]{:S(2)}, u32[]{:S(2)}) collective-permute-start(bf16[48,768]{1,0:T(8,128)(2,1)S(1)} %get-tuple-element.85), channel_id=1, source_target_pairs={{0,2},{2,4},{4,6},{6,0},{1,3},{3,5},{5,7},{7,1},{8,10},{10,12},{12... | collective-permute-start | bytes 221192 | tf_op jit(solution)/shard_map/ppermute | solution.py:373
  121.4 7.0 %collective-permute-start.26 = (bf16[48,768]{1,0:T(8,128)(2,1)S(1)}, bf16[48,768]{1,0:T(8,128)(2,1)S(1)}, u32[]{:S(2)}, u32[]{:S(2)}) collective-permute-start(bf16[48,768]{1,0:T(8,128)(2,1)S(1)} %get-tuple-element.84), channel_id=1, source_target_pairs={{0,6},{2,0},{4,2},{6,4},{1,7},{3,1},{5,3},{7,5},{8,14},{10,8},{12,... | collective-permute-start | bytes 221192 | tf_op jit(solution)/shard_map/ppermute | solution.py:373
  124.0 4.8 %collective-permute-start.18 = (bf16[48,768]{1,0:T(8,128)(2,1)S(1)}, bf16[48,768]{1,0:T(8,128)(2,1)S(1)}, u32[]{:S(2)}, u32[]{:S(2)}) collective-permute-start(bf16[48,768]{1,0:T(8,128)(2,1)S(1)} %get-tuple-element.86), channel_id=1, source_target_pairs={{0,16},{8,24},{16,0},{24,8},{1,17},{9,25},{17,1},{25,9},{2,18},{10... | collective-permute-start | bytes 221192 | tf_op jit(solution)/shard_map/ppermute | solution.py:373
  125.8 4.9 %collective-permute-start.19 = (bf16[48,768]{1,0:T(8,128)(2,1)S(1)}, bf16[48,768]{1,0:T(8,128)(2,1)S(1)}, u32[]{:S(2)}, u32[]{:S(2)}) collective-permute-start(bf16[48,768]{1,0:T(8,128)(2,1)S(1)} %get-tuple-element.88), channel_id=1, source_target_pairs={{0,8},{8,16},{16,24},{24,0},{1,9},{9,17},{17,25},{25,1},{2,10},{10... | collective-permute-start | bytes 221192 | tf_op jit(solution)/shard_map/ppermute | solution.py:373
  127.3 4.0 %collective-permute-start.20 = (bf16[48,768]{1,0:T(8,128)(2,1)S(1)}, bf16[48,768]{1,0:T(8,128)(2,1)S(1)}, u32[]{:S(2)}, u32[]{:S(2)}) collective-permute-start(bf16[48,768]{1,0:T(8,128)(2,1)S(1)} %get-tuple-element.87), channel_id=1, source_target_pairs={{0,24},{8,0},{16,8},{24,16},{1,25},{9,1},{17,9},{25,17},{2,26},{10... | collective-permute-start | bytes 221192 | tf_op jit(solution)/shard_map/ppermute | solution.py:373
  131.3 3.3 %collective-permute-start.27 = (bf16[2,24,768]{2,1,0:T(8,128)(2,1)S(1)}, bf16[2,24,768]{2,1,0:T(8,128)(2,1)S(1)}, u32[]{:S(2)}, u32[]{:S(2)}) collective-permute-start(bf16[2,24,768]{2,1,0:T(8,128)(2,1)S(1)} %get-tuple-element.90), channel_id=1, source_target_pairs={{0,1},{1,0},{2,3},{3,2},{4,5},{5,4},{6,7},{7,6},{8,9},{9,8},{10,11... | collective-permute-start | bytes 221192 | tf_op jit(solution)/shard_map/ppermute | solution.py:33
  (8 other events, 22.8 us)
